TPU v7x, 32 devices: a whole 2x2x4 slice. The times are simulated.
32 devices in a mesh: groups: 2 (over y), blk: 4 (over z), eig: 2 (over x), rep: 2 (over core).
Axes of the slice: x: 2, y: 2, z: 4, core: 2. Of those that a mesh axis runs over, the one named last changes fastest.
Arguments:
- acts: bfloat16 [6144, 28672], P(('groups', 'blk'), ('eig', 'rep')), parts along dimension 0, may hold values from -6 to 6
- out_grads: bfloat16 [6144, 8192], P(('groups', 'blk'), ('eig', 'rep')), parts along dimension 0, may hold values from -6 to 6
- basis_in: bfloat16 [256, 28672], P('blk', ('eig', 'rep')), may hold values from -0.03125 to 0.03125
- basis_out: bfloat16 [128, 8192], P(None, ('eig', 'rep')), may hold values from -0.0625 to 0.0625
- eigvals: bfloat16 [256, 128], P('blk'), may hold values from 0.049804688 to 5
- query_out: bfloat16 [8192, 256], P(('eig', 'rep'), 'groups'), parts along dimension 1, may hold values from -0.017944336 to 0.017944336
- query_in: bfloat16 [28672, 256], P(('eig', 'rep'), 'groups'), parts along dimension 1, may hold values from -0.017944336 to 0.017944336
- seq_ids: int32 [6144], P(('groups', 'blk')), parts along dimension 0, may hold values from 0 to 7, never falling along the last dimension, each value on 1 to 1536 neighbouring positions
- owner: int32 [16], P('groups'), parts along dimension 0, may hold values from 0 to 7, each once
Outputs:
- scores: float32 [8, 8], P(('groups', 'eig', 'rep'), 'blk'), parts along dimension 0
There are 2 independent parts, one for each index of `groups`. A program takes and returns all parts, laid end to end along the dimension named above; an argument that names none is the same for every part. Nothing has to cross between parts.
Inputs may be any that keep to these rules, and one draw needn't show every extreme that they name: `seq_ids`: ids never fall along the tokens; every one of the 8 sequences has 1 to 1536 tokens, one exactly 1536. `owner`: a permutation: each column belongs to one sequence.
All inputs are finite; a program needn't handle non-finite values.
Results may differ from a plain program's by a relative error of at most 0.0068.
Values may be sent and summed in bfloat16 or wider, within the bound.
No kernel may reach another device: no remote copies, remote signals or barrier semaphores. Data moves between devices by JAX's collectives and lax.ppermute only.
A program may use at most 64 MiB of HBM per device.

v0:
```python
import jax
import jax.numpy as jnp
from jax import lax
from jax.sharding import PartitionSpec as P

R = 32


damping = 0.05


def contract_last(left_side, right_side):
    return lax.dot_general(
        left_side, right_side, (((1,), (1,)), ((), ())), preferred_element_type=jnp.float32
    )


def precondition(in_rows, eig_rows, out_query):
    row_count = in_rows.shape[0]
    basis_width = out_query.shape[0]
    query_count = out_query.shape[1] // R
    outer_sum = jnp.einsum(
        "jqr,iqr->jqi",
        in_rows.reshape(row_count, query_count, R),
        out_query.reshape(basis_width, query_count, R),
        preferred_element_type=jnp.float32,
    )
    inverse = 1.0 / (eig_rows.astype(jnp.float32) + damping)
    return (
        (outer_sum * inverse[:, None, :])
        .astype(jnp.bfloat16)
        .reshape(row_count * query_count, basis_width)
    )


def score_tokens(grad_proj, weighted, projected):
    token_count = projected.shape[0]
    row_count = projected.shape[1]
    mixed_rows = contract_last(grad_proj, weighted).reshape(token_count, row_count, -1)
    return jnp.sum(mixed_rows * projected[:, :, None], axis=1).T


def on_device(acts, out_grads, basis_in, basis_out, eigvals, query_out, query_in, seq_ids, owner):
    pair_count = query_in.shape[1]
    query_count = pair_count // R
    in_part = jnp.dot(basis_in, query_in, preferred_element_type=jnp.float32)
    out_part = jnp.dot(basis_out, query_out, preferred_element_type=jnp.float32)
    grad_part = contract_last(out_grads, basis_out)
    in_sum, out_sum, grad_sum = lax.psum((in_part, out_part, grad_part), ("eig", "rep"))
    in_query = in_sum.astype(jnp.bfloat16)
    out_query = out_sum.astype(jnp.bfloat16)
    grad_proj = grad_sum.astype(jnp.bfloat16)
    basis_piece = lax.all_gather(basis_in, "blk", axis=0, tiled=True)
    eig_piece = lax.all_gather(eigvals, "blk", axis=0, tiled=True)
    in_piece = lax.all_gather(in_query, "blk", axis=0, tiled=True)
    projected = contract_last(acts, basis_piece)
    folded = (projected, in_piece, eig_piece)
    seq_count = owner.shape[0]
    labels = jnp.arange(seq_count, dtype=jnp.int32)
    column_of = jnp.sum(jnp.where(seq_ids[None, :] == labels[:, None], owner[:, None], 0), axis=0)
    onehot = (labels[:, None] == column_of[None, :]).astype(jnp.float32)
    proj_buf, in_buf, eig_buf = folded
    proj_full = lax.psum(proj_buf, ("eig", "rep"))
    own_queries = query_count // lax.axis_size(("eig", "rep"))
    offset = lax.axis_index(("eig", "rep")) * (own_queries * R)
    in_mine = lax.dynamic_slice_in_dim(in_buf, offset, own_queries * R, 1)
    out_mine = lax.dynamic_slice_in_dim(out_query, offset, own_queries * R, 1)
    weighted = precondition(in_mine, eig_buf, out_mine)
    per_token = score_tokens(grad_proj, weighted, proj_full)
    own_scores = lax.dot_general(
        per_token,
        onehot,
        (((1,), (1,)), ((), ())),
        precision=lax.Precision.HIGHEST,
        preferred_element_type=jnp.float32,
    )
    return lax.psum_scatter(own_scores, "blk", scatter_dimension=1, tiled=True)


def solution(mesh):
    return jax.shard_map(
        on_device,
        mesh=mesh,
        in_specs=(
            P(("groups", "blk"), ("eig", "rep")),
            P(("groups", "blk"), ("eig", "rep")),
            P("blk", ("eig", "rep")),
            P(None, ("eig", "rep")),
            P("blk", None),
            P(("eig", "rep"), "groups"),
            P(("eig", "rep"), "groups"),
            P(("groups", "blk")),
            P("groups"),
        ),
        out_specs=P(("groups", "eig", "rep"), "blk"),
        check_vma=False,
    )
```

profile of v0, /device:TPU:0, one launch (start us, length us, event | category | flops | bytes accessed | tf_op | source)
XLA Modules:
  0.0 150.3 jit_solution(2093662907766512944)
XLA Ops:
  6.5 0.0 copy-start
  6.5 0.0 all-gather.2.cloned.1.call-start
  6.5 0.7 all-gather.2.cloned.1.call-update
  7.3 0.0 all-reduce.5.cloned.1.call-start
  7.3 0.0 copy-start.1
  7.3 0.0 copy-start.3
  7.3 1.1 copy-done
  8.4 0.0 copy-start.2
  8.4 0.0 copy-start.4
  8.4 2.1 %fusion.19 = f32[768,128]{1,0:T(8,128)S(1)} fusion(bf16[768,2048]{1,0:T(8,128)(2,1)S(1)} %copy-done, bf16[128,2048]{1,0:T(8,128)(2,1)} %param.12), kind=kOutput, calls=%fused_computation.24 | convolution fusion | flops 402653184 | bytes 4063232 | tf_op jit(solution)/shard_map/dot_general | solution.py:13
  10.6 0.0 copy-done.1
  10.6 0.0 copy-done.3
  10.6 1.1 fusion.21
  11.6 0.0 copy-done.2
  11.6 0.0 copy-done.4
  11.6 1.0 fusion.20
  12.6 0.0 copy-done.5
  12.6 16.0 %all_gather.10 = bf16[256,128]{1,0:T(8,128)(2,1)} all-gather(bf16[64,128]{1,0:T(8,128)(2,1)S(1)} %copy-done.5), channel_id=1, replica_groups=mesh['groups'=2,'blk'=4,'eig'=2,'rep'=2] {'blk'}, dimensions={0}, use_global_device_ids=true | all-gather | bytes 81920 | tf_op jit(solution)/shard_map/all_gather | solution.py:54
  28.5 1.6 %copy.12 = bf16[256,128]{0,1:T(8,128)(2,1)} copy(bf16[256,128]{1,0:T(8,128)(2,1)} %all_gather.10) | data formatting | bytes 131072 | tf_op jit(solution)/shard_map/all_gather | solution.py:54
  30.1 0.0 copy-done.6
  30.1 0.6 dynamic-slice
  30.7 53.5 %all-gather.2.cloned.1.call-done = bf16[256,7168]{1,0:T(8,128)(2,1)} async-done(((bf16[64,7168]{1,0:T(8,128)(2,1)}), bf16[256,7168]{1,0:T(8,128)(2,1)}) %all-gather.2.cloned.1.call-update) | async-done | bytes 3670032 | tf_op jit(solution)/shard_map/all_gather | solution.py:53
  84.2 9.1 %fusion.22 = f32[768,256]{0,1:T(8,128)} fusion(bf16[768,7168]{1,0:T(8,128)(2,1)} %param.9, bf16[256,7168]{1,0:T(8,128)(2,1)} %all-gather.2.cloned.1.call-done), kind=kOutput, calls=%fused_computation.27 | convolution fusion | flops 2818572288 | bytes 15466496 | tf_op jit(solution)/shard_map/dot_general | solution.py:13
  93.3 0.0 all-reduce.5.cloned.1.call-update
  93.3 21.4 %all-reduce.6 = (bf16[768,128]{1,0:T(8,128)(2,1)}, bf16[64,128]{1,0:T(8,128)(2,1)S(1)}, bf16[128,128]{0,1:T(8,128)(2,1)}) all-reduce(f32[768,128]{1,0:T(8,128)S(1)} %fusion.19, f32[64,128]{1,0:T(8,128)} %fusion.21, f32[128,128]{0,1:T(8,128)} %fusion.20), channel_id=1, replica_groups=mesh['groups'=2,'blk'=4,'eig'=2,'rep'=2] {'eig','rep'}, use_global_device_ids=true, to_apply=%region_0.0 | all-reduce | flops 122880 | bytes 737280 | tf_op jit(solution)/shard_map/psum | solution.py:49
  114.7 13.1 %all_gather.9 = bf16[256,128]{1,0:T(8,128)(2,1)S(1)} all-gather(bf16[64,128]{1,0:T(8,128)(2,1)S(1)} %get-tuple-element.6), channel_id=1, replica_groups=mesh['groups'=2,'blk'=4,'eig'=2,'rep'=2] {'blk'}, dimensions={0}, use_global_device_ids=true | all-gather | bytes 81920 | tf_op jit(solution)/shard_map/all_gather | solution.py:55
  127.8 0.8 select_reduce_fusion
  128.6 0.0 all-reduce.5.cloned.1.call-done
  128.6 1.8 %fusion = f32[768]{0:T(1024)S(1)} fusion(f32[768,256]{0,1:T(8,128)} %all-reduce.5.cloned.1.call-done, bf16[768,128]{1,0:T(8,128)(2,1)} %get-tuple-element.5, bf16[256,128]{0,1:T(8,128)(2,1)} %copy.12, bf16[256,128]{1,0:T(8,128)(2,1)S(1)} %all_gather.9, s32[]{:T(128)S(6)} %select_n.8, bf16[128,128]{0,1:T(8,128)(2,1)} %get-tuple-element.7), kind=kOutput, calls=%fused_computation.1 | convolution fusion | flops 52985088 | bytes 1126400 | tf_op jit(solution)/shard_map/dot_general | solution.py:13
  130.5 0.1 fusion.13
  131.3 11.6 %all-reduce = f32[1,8]{1,0:T(1,128)S(1)} all-reduce(f32[1,8]{1,0:T(1,128)S(1)} %fusion.13), channel_id=2, replica_groups=mesh['groups'=2,'blk'=4,'eig'=2,'rep'=2] {'blk'}, use_global_device_ids=true, to_apply=%region_6.7.clone | all-reduce | flops 8 | bytes 64
  142.9 0.6 constant_dynamic-slice_fusion
  (3 shorter events, 0.0 us)
Async XLA Ops:
  6.5 1.9 %copy-start = (bf16[768,2048]{1,0:T(8,128)(2,1)S(1)}, bf16[768,2048]{1,0:T(8,128)(2,1)}, u32[]{:S(2)}) copy-start(bf16[768,2048]{1,0:T(8,128)(2,1)} %param.10) | copy-start | bytes 9437188
  6.5 77.7 %all-gather.2.cloned.1.call-start = ((), (), s32[]{:S(2)}) async-start(), calls=%async_computation | async-start | bytes 4587520 | tf_op jit(solution)/shard_map/all_gather | solution.py:53
  7.3 121.4 %all-reduce.5.cloned.1.call-start = ((), (), s32[]{:S(2)}) async-start(), calls=%async_computation.1 | async-start | bytes 1572864 | tf_op jit(solution)/shard_map/psum | solution.py:63
  7.3 3.2 %copy-start.1 = (bf16[64,7168]{1,0:T(8,128)(2,1)S(1)}, bf16[64,7168]{1,0:T(8,128)(2,1)}, u32[]{:S(2)}) copy-start(bf16[64,7168]{1,0:T(8,128)(2,1)} %param.11) | copy-start | bytes 2752516
  7.3 3.2 %copy-start.3 = (bf16[7168,128]{1,0:T(8,128)(2,1)S(1)}, bf16[7168,128]{1,0:T(8,128)(2,1)}, u32[]{:S(2)}) copy-start(bf16[7168,128]{1,0:T(8,128)(2,1)} %param.15) | copy-start | bytes 5505028
  8.4 3.2 %copy-start.2 = (bf16[128,2048]{1,0:T(8,128)(2,1)S(1)}, bf16[128,2048]{1,0:T(8,128)(2,1)}, u32[]{:S(2)}) copy-start(bf16[128,2048]{1,0:T(8,128)(2,1)} %param.12) | copy-start | bytes 1572868
  8.4 3.2 %copy-start.4 = (bf16[2048,128]{1,0:T(8,128)(2,1)S(1)}, bf16[2048,128]{1,0:T(8,128)(2,1)}, u32[]{:S(2)}) copy-start(bf16[2048,128]{1,0:T(8,128)(2,1)} %param.14) | copy-start | bytes 1572868
  8.4 4.2 %copy-start.5 = (bf16[64,128]{1,0:T(8,128)(2,1)S(1)}, bf16[64,128]{1,0:T(8,128)(2,1)}, u32[]{:S(2)}) copy-start(bf16[64,128]{1,0:T(8,128)(2,1)} %param.13) | copy-start | bytes 49156
  8.4 21.7 %copy-start.6 = (u32[32]{0:T(128)S(1)}, u32[32]{0:T(128)}, u32[]{:S(2)}) copy-start(u32[32]{0:T(128)} %constant.22) | copy-start | bytes 388
Sparse Core Ops, SparseCore 0:
  8.9 75.2 all-gather.1
  93.5 35.0 all-reduce.4
where the time goes:
time: 151 us; the launch traced here: 150 us
  blocking collectives  62 us (41%)
  waiting for transfers between devices  54.3 us (36%)
  matrix products  15.2 us (10%)
  between operations  14.2 us (9%)
  local copies, waits for them, and re-layouts  3.85 us (3%)
    all_gather x1, waiting for transfers between devices, on_device(): basis_piece = lax.all_gather(basis_in, 'blk', axis=0, tiled=True)  53.5 us
    psum x1, blocking collectives, on_device(): lax.psum((in_part, out_part, grad_part), ('eig', 'rep'))  21.4 us
    all_gather x1, blocking collectives, on_device(): eig_piece = lax.all_gather(eigvals, 'blk', axis=0, tiled=True)  16 us
    all_gather x1, blocking collectives, on_device(): in_piece = lax.all_gather(in_query, 'blk', axis=0, tiled=True)  13.1 us
    dot_general x3, matrix products, contract_last(): lax.dot_general(left_side, right_side, (((1,), (1,)), ((), ())), preferre...  13.1 us
    unnamed x1, blocking collectives  11.6 us
  transfers between devices with their start and end apart: 2, of which 1 were waited for; matrix products, arithmetic and copies ran while one was open for 5% of the time, Pallas kernels for 0%

commit v1 on v0

v1 whole, which is shorter than its diff:
```python
import jax
import jax.numpy as jnp
from jax import lax
from jax.sharding import PartitionSpec as P

R = 32


damping = 0.05


def contract_last(left_side, right_side):
    return lax.dot_general(
        left_side, right_side, (((1,), (1,)), ((), ())), preferred_element_type=jnp.float32
    )


def swap_sum(value, axis, send_as):
    size = lax.axis_size(axis)
    if size & (size - 1):
        return lax.psum(value, axis)
    step = 1
    while step < size:
        pairs = [(i, i ^ step) for i in range(size)]
        value = value + lax.ppermute(value.astype(send_as), axis, pairs).astype(jnp.float32)
        step *= 2
    return value


def by_distance(value):
    size = lax.axis_size("blk")
    return [value] + [
        lax.ppermute(value, "blk", [(i, i ^ k) for i in range(size)]) for k in range(1, size)
    ]


def halves_by_distance(half):
    place = lax.axis_index("blk")
    inner = (place == 1) | (place == 2)
    middle = [(1, 2), (2, 1)]
    outward = [(1, 0), (2, 3)]
    first = lax.ppermute(half, "blk", [(0, 1), (1, 0), (2, 3), (3, 2)])
    across = lax.ppermute(half, "blk", middle)
    across_out = lax.ppermute(across, "blk", outward)
    first_over = lax.ppermute(first, "blk", middle)
    first_out = lax.ppermute(first_over, "blk", outward)
    return [
        first,
        jnp.where(inner, first_over, across_out),
        jnp.where(inner, across, first_out),
    ]


def precondition(in_rows, eig_rows, out_query):
    row_count = in_rows.shape[0]
    basis_width = out_query.shape[0]
    query_count = out_query.shape[1] // R
    outer_sum = jnp.einsum(
        "jqr,iqr->qji",
        in_rows.reshape(row_count, query_count, R),
        out_query.reshape(basis_width, query_count, R),
        preferred_element_type=jnp.float32,
    )
    inverse = 1.0 / (eig_rows.astype(jnp.float32) + damping)
    return (outer_sum * inverse[None, :, :]).astype(jnp.bfloat16)


def on_device(acts, out_grads, basis_in, basis_out, eigvals, query_out, query_in, seq_ids, owner):
    rows = basis_in.shape[0]
    group = lax.axis_index("groups")
    stepped = lax.axis_size("blk") == 4 and lax.axis_size("groups") == 2

    if stepped:
        half = lax.dynamic_slice_in_dim(basis_in, group * (rows // 2), rows // 2, 0)
        own_way = halves_by_distance(half)
        swap = [(0, 1), (1, 0)]
        other_way = [lax.ppermute(piece, "groups", swap) for piece in own_way]

    in_part = jnp.dot(basis_in, query_in, preferred_element_type=jnp.float32)
    out_part = jnp.dot(basis_out, query_out, preferred_element_type=jnp.float32)
    small = jnp.concatenate([in_part, out_part], axis=0)
    small = swap_sum(swap_sum(small, "rep", jnp.float32), "eig", jnp.float32).astype(jnp.bfloat16)
    in_query, out_query = small[:rows], small[rows:]
    grad_part = contract_last(out_grads, basis_out)
    grad_proj = swap_sum(swap_sum(grad_part, "rep", jnp.float32), "eig", jnp.bfloat16)
    grad_proj = grad_proj.astype(jnp.bfloat16)

    if stepped:
        pack = jnp.concatenate([in_query, eigvals], axis=1)
        swapped = jnp.concatenate([pack[rows // 2 :], pack[: rows // 2]], axis=0)
        ordered = jnp.where(group == 0, pack, swapped)
        pack = jnp.concatenate([pack] + by_distance(ordered)[1:], axis=0)
        pieces = [basis_in]
        for mine, theirs in zip(own_way, other_way):
            pieces += [mine, theirs]
    else:
        pack = jnp.concatenate([in_query, eigvals], axis=1)
        pack = lax.all_gather(pack, "blk", axis=0, tiled=True)
        pieces = [lax.all_gather(basis_in, "blk", axis=0, tiled=True)]
    pairs = in_query.shape[1]
    weighted = precondition(pack[:, :pairs], pack[:, pairs:], out_query)
    query_count = weighted.shape[0]
    mixed = [contract_last(grad_proj, weighted[q]) for q in range(query_count)]

    projected = jnp.concatenate([contract_last(acts, piece) for piece in pieces], axis=1)
    per_token = jnp.stack([jnp.sum(projected * mixed[q], axis=1) for q in range(query_count)])

    seq_count = owner.shape[0]
    labels = jnp.arange(seq_count, dtype=jnp.int32)
    column_of = jnp.sum(jnp.where(seq_ids[None, :] == labels[:, None], owner[:, None], 0), axis=0)
    onehot = (labels[:, None] == column_of[None, :]).astype(jnp.float32)
    part_scores = lax.dot_general(
        per_token,
        onehot,
        (((1,), (1,)), ((), ())),
        precision=lax.Precision.HIGHEST,
        preferred_element_type=jnp.float32,
    )
    scores = lax.psum(part_scores, ("blk", "eig", "rep"))
    own_queries = query_count // lax.axis_size(("eig", "rep"))
    own_columns = seq_count // lax.axis_size("blk")
    return lax.dynamic_slice(
        scores,
        (lax.axis_index(("eig", "rep")) * own_queries, lax.axis_index("blk") * own_columns),
        (own_queries, own_columns),
    )


def solution(mesh):
    return jax.shard_map(
        on_device,
        mesh=mesh,
        in_specs=(
            P(("groups", "blk"), ("eig", "rep")),
            P(("groups", "blk"), ("eig", "rep")),
            P("blk", ("eig", "rep")),
            P(None, ("eig", "rep")),
            P("blk", None),
            P(("eig", "rep"), "groups"),
            P(("eig", "rep"), "groups"),
            P(("groups", "blk")),
            P("groups"),
        ),
        out_specs=P(("groups", "eig", "rep"), "blk"),
        check_vma=False,
    )
```

time: 151 us -> 131 us (0.87)
  waiting for transfers between devices: 54.3 us -> 11.4 us
  matrix products: 15.2 us -> 52.5 us
  blocking collectives: 62 us -> 29.5 us
  starting transfers between devices: 0.04 us -> 19.7 us
  between operations: 14.2 us -> 0.28 us
  other arithmetic: 0.78 us -> 7.91 us
  local copies, waits for them, and re-layouts: 3.85 us -> 8.89 us
    all_gather x1 -> x0, waiting for transfers between devices: 53.5 us -> none  [on_device(): basis_piece = lax.all_gather(basis_in, 'blk', axis=0, tiled=True)]
    dot_general x3 -> x12, matrix products: 13.1 us -> 47.5 us  [contract_last(): lax.dot_general(left_side, right_side, (((1,), (1,)), ((), ())), preferre...]
    all_gather x2 -> x0, blocking collectives: 29.1 us -> none  [the longest x1 16 us: on_device(): eig_piece = lax.all_gather(eigvals, 'blk', axis=0, tiled=True)]
    ppermute x0 -> x15, starting transfers between devices: none -> 19.7 us  [the longest x3 5.08 us: by_distance(): lax.ppermute(value, 'blk', [(i, i ^ k) for i in range(size)])]
    unnamed x1 -> x0, blocking collectives: 11.6 us -> none
    ppermute x0 -> x15, waiting for transfers between devices: none -> 11.4 us  [the longest x1 5.7 us: halves_by_distance(): across_out = lax.ppermute(across, 'blk', outward)]
    psum x1, blocking collectives: 21.4 us -> 29.5 us  [on_device(): scores = lax.psum(part_scores, ('blk', 'eig', 'rep'))]
    slice x0 -> x5, local copies, waits for them, and re-layouts: none -> 5.02 us  [the longest x3 2.83 us: on_device(): in_query, out_query = (small[:rows], small[rows:])]
  transfers between devices with their start and end apart: 2 -> 15, of which waited for: 1 -> 4; matrix products, arithmetic and copies ran while one was open for 5% -> 43% of each run, Pallas kernels for 0% -> 0%
where the time goes in v1:
time: 131 us; the launch traced here: 130 us
  matrix products  52.5 us (40%)
  blocking collectives  29.5 us (23%)
  starting transfers between devices  19.7 us (15%)
  waiting for transfers between devices  11.4 us (9%)
  local copies, waits for them, and re-layouts  8.89 us (7%)
  other arithmetic  7.91 us (6%)
    dot_general x12, matrix products, contract_last(): lax.dot_general(left_side, right_side, (((1,), (1,)), ((), ())), preferre...  47.5 us
    psum x1, blocking collectives, on_device(): scores = lax.psum(part_scores, ('blk', 'eig', 'rep'))  29.5 us
    ppermute x1, waiting for transfers between devices, halves_by_distance(): across_out = lax.ppermute(across, 'blk', outward)  5.7 us
    ppermute x3, starting transfers between devices, by_distance(): lax.ppermute(value, 'blk', [(i, i ^ k) for i in range(size)])  5.08 us
    ppermute x3, starting transfers between devices, on_device(): other_way = [lax.ppermute(piece, 'groups', swap) for piece in own_way]  3.61 us
    ppermute x4, starting transfers between devices, swap_sum(): lax.ppermute(value.astype(send_as), axis, pairs).astype(jnp.float32)  3.13 us
    ppermute x4, waiting for transfers between devices, swap_sum(): lax.ppermute(value.astype(send_as), axis, pairs).astype(jnp.float32)  3.03 us
    ppermute x1, starting transfers between devices, halves_by_distance(): first = lax.ppermute(half, 'blk', [(0, 1), (1, 0), (2, 3), (3, 2)])  3.02 us
  transfers between devices with their start and end apart: 15, of which 4 were waited for; matrix products, arithmetic and copies ran while one was open for 43% of the time, Pallas kernels for 0%

profile of v1, /device:TPU:0, one launch (start us, length us, event | category | flops | bytes accessed | tf_op | source)
XLA Modules:
  0.0 130.2 jit_solution(13121964261165894477)
XLA Ops:
  0.0 2.0 %constant_dynamic-slice_fusion = bf16[32,7168]{1,0:T(8,128)(2,1)} fusion(bf16[64,7168]{1,0:T(8,128)(2,1)} %param.11, s32[]{:T(128)S(6)} %select_n.33), kind=kLoop, calls=%fused_computation.54 | loop fusion | bytes 917508 | tf_op jit(solution)/shard_map/dynamic_slice | solution.py:74
  2.0 3.0 %collective-permute-start = (bf16[32,7168]{1,0:T(8,128)(2,1)}, bf16[32,7168]{1,0:T(8,128)(2,1)}, u32[]{:S(2)}, u32[]{:S(2)}) collective-permute-start(bf16[32,7168]{1,0:T(8,128)(2,1)} %constant_dynamic-slice_fusion), channel_id=1, source_target_pairs={{0,4},{4,0},{8,12},{12,8},{1,5},{5,1},{9,13},{13,9},{2,6},{6,2},{1... | collective-permute-start | bytes 1376264 | tf_op jit(solution)/shard_map/ppermute | solution.py:42
  5.0 1.4 %collective-permute-start.3 = (bf16[32,7168]{1,0:T(8,128)(2,1)}, bf16[32,7168]{1,0:T(8,128)(2,1)}, u32[]{:S(2)}, u32[]{:S(2)}) collective-permute-start(bf16[32,7168]{1,0:T(8,128)(2,1)} %constant_dynamic-slice_fusion), channel_id=1, source_target_pairs={{4,8},{8,4},{5,9},{9,5},{6,10},{10,6},{7,11},{11,7},{20,24},{24,20... | collective-permute-start | bytes 1376264 | tf_op jit(solution)/shard_map/ppermute | solution.py:43
  6.4 2.2 %fusion.27 = f32[64,128]{1,0:T(8,128)S(1)} fusion(bf16[64,7168]{1,0:T(8,128)(2,1)} %param.11, bf16[7168,128]{1,0:T(8,128)(2,1)} %param.15), kind=kOutput, calls=%fused_computation.59 | convolution fusion | flops 117440512 | bytes 2785280 | tf_op jit(solution)/shard_map/dot_general | solution.py:79
  8.7 1.5 %fusion.28 = f32[128,128]{1,0:T(8,128)S(1)} fusion(bf16[128,2048]{1,0:T(8,128)(2,1)} %param.12, bf16[2048,128]{1,0:T(8,128)(2,1)} %param.14), kind=kOutput, calls=%fused_computation.60 | convolution fusion | flops 67108864 | bytes 1114112 | tf_op jit(solution)/shard_map/dot_general | solution.py:80
  10.3 8.5 %convolution_dynamic-update-slice_fusion = f32[768,256]{0,1:T(8,128)} fusion(bf16[768,7168]{1,0:T(8,128)(2,1)} %param.9, bf16[64,7168]{1,0:T(8,128)(2,1)} %param.11), kind=kOutput, calls=%fused_computation.10 | convolution fusion | flops 704643072 | bytes 12124160 | tf_op jit(solution)/shard_map/dot_general | solution.py:13
  19.4 1.5 %collective-permute-start.11 = (f32[192,128]{1,0:T(8,128)}, f32[192,128]{1,0:T(8,128)}, u32[]{:S(2)}, u32[]{:S(2)}) collective-permute-start(f32[192,128]{1,0:T(8,128)} %fusion.24), channel_id=1, source_target_pairs={{0,2},{2,0},{1,3},{3,1},{4,6},{6,4},{5,7},{7,5},{8,10},{10,8},{9,1... | collective-permute-start | bytes 294920 | tf_op jit(solution)/shard_map/ppermute | solution.py:25
  21.9 3.0 %collective-permute-done.11 = f32[192,128]{1,0:T(8,128)} collective-permute-done((f32[192,128]{1,0:T(8,128)}, f32[192,128]{1,0:T(8,128)}, u32[]{:S(2)}, u32[]{:S(2)}) %collective-permute-start.11) | collective-permute-done | bytes 98336 | tf_op jit(solution)/shard_map/ppermute | solution.py:25
  27.2 1.3 %fusion.11 = bf16[64,256]{1,0:T(8,128)(2,1)} fusion(bf16[64,128]{1,0:T(8,128)(2,1)} %param.13, bf16[64,128]{1,0:T(8,128)(2,1)S(1)} %slice.40, bf16[32,256]{1,0:T(8,128)(2,1)S(1)} %get-tuple-element.8, bf16[32,256]{1,0:T(8,128)(2,1)S(1)} %get-tuple-element.7, pred[]{:T(512)S(6)} %eq.37), kind=kLoop, calls=%fused_computation.39 | loop fusion | flops 147456 | bytes 98305 | tf_op jit(solution)/shard_map/jit(_where)/select_n | solution.py:91
  28.6 2.5 %collective-permute-start.14 = (bf16[64,256]{1,0:T(8,128)(2,1)}, bf16[64,256]{1,0:T(8,128)(2,1)}, u32[]{:S(2)}, u32[]{:S(2)}) collective-permute-start(bf16[64,256]{1,0:T(8,128)(2,1)} %fusion.11), channel_id=1, source_target_pairs={{0,12},{4,8},{8,4},{12,0},{1,13},{5,9},{9,5},{13,1},{2,14},{6,10},... | collective-permute-start | bytes 98312 | tf_op jit(solution)/shard_map/ppermute | solution.py:33
  31.0 2.6 %collective-permute-start.13 = (bf16[64,256]{1,0:T(8,128)(2,1)}, bf16[64,256]{1,0:T(8,128)(2,1)}, u32[]{:S(2)}, u32[]{:S(2)}) collective-permute-start(bf16[64,256]{1,0:T(8,128)(2,1)} %fusion.11), channel_id=1, source_target_pairs={{0,8},{4,12},{8,0},{12,4},{1,9},{5,13},{9,1},{13,5},{2,10},{6,14},... | collective-permute-start | bytes 98312 | tf_op jit(solution)/shard_map/ppermute | solution.py:33
  33.7 1.4 %select_reduce_fusion = s32[768]{0:T(1024)} fusion(s32[8]{0:T(128)} %param.17, s32[768]{0:T(1024)} %param.16), kind=kLoop, calls=%fused_computation.40 | loop fusion | flops 17664 | bytes 6176 | tf_op jit(solution)/shard_map/reduce_sum | solution.py:110
  35.0 1.4 %slice.46 = bf16[128,128]{1,0:T(8,128)(2,1)} slice(bf16[192,128]{1,0:T(8,128)(2,1)} %copy-done.3), slice={[64:192], [0:128]} | slice | bytes 65536 | tf_op jit(solution)/shard_map/slice | solution.py:83
  36.4 1.5 %copy.15 = bf16[128,128]{0,1:T(8,128)(2,1)} copy(bf16[128,128]{1,0:T(8,128)(2,1)} %slice.46) | data formatting | bytes 65536 | tf_op jit(solution)/shard_map/slice | solution.py:83
  40.0 1.6 %copy.14 = bf16[256,128]{0,1:T(8,128)(2,1)} copy(bf16[256,128]{1,0:T(8,128)(2,1)} %slice.45) | data formatting | bytes 131072 | tf_op jit(solution)/shard_map/slice | solution.py:101
  44.6 1.6 %collective-permute-start.9 = (bf16[768,128]{1,0:T(8,128)(2,1)S(1)}, bf16[768,128]{1,0:T(8,128)(2,1)S(1)}, u32[]{:S(2)}, u32[]{:S(2)}) collective-permute-start(bf16[768,128]{1,0:T(8,128)(2,1)S(1)} %get-tuple-element.5), channel_id=1, source_target_pairs={{0,2},{2,0},{1,3},{3,1},{4,6},{6,4},{5,7},{7,5},{8,10},{10,8},{9,1... | collective-permute-start | bytes 589832 | tf_op jit(solution)/shard_map/ppermute | solution.py:25
  46.2 1.5 %collective-permute-start.1 = (bf16[32,7168]{1,0:T(8,128)(2,1)}, bf16[32,7168]{1,0:T(8,128)(2,1)S(1)}, u32[]{:S(2)}, u32[]{:S(2)}) collective-permute-start(bf16[32,7168]{1,0:T(8,128)(2,1)} %collective-permute-done), channel_id=1, source_target_pairs={{0,16},{16,0},{1,17},{17,1},{2,18},{18,2},{3,19},{19,3},{4,20},{20... | collective-permute-start | bytes 1376264 | tf_op jit(solution)/shard_map/ppermute | solution.py:77
  48.4 1.3 collective-permute-start.4
  49.7 8.3 %fusion.10 = f32[768,256]{0,1:T(8,128)} fusion(f32[768,256]{0,1:T(8,128)} %convolution_dynamic-update-slice_fusion, bf16[32,7168]{1,0:T(8,128)(2,1)} %collective-permute-done, bf16[768,7168]{1,0:T(8,128)(2,1)} %param.9), kind=kOutput, calls=%fused_computation.22 | convolution fusion | flops 352321536 | bytes 11567104 | tf_op jit(solution)/shard_map/dot_general | solution.py:13
  58.1 5.7 %collective-permute-done.4 = bf16[32,7168]{1,0:T(8,128)(2,1)S(1)} collective-permute-done((bf16[32,7168]{1,0:T(8,128)(2,1)}, bf16[32,7168]{1,0:T(8,128)(2,1)S(1)}, u32[]{:S(2)}, u32[]{:S(2)}) %collective-permute-start.4) | collective-permute-done | bytes 458784 | tf_op jit(solution)/shard_map/ppermute | solution.py:44
  64.7 1.5 %collective-permute-start.6 = (bf16[32,7168]{1,0:T(8,128)(2,1)S(1)}, bf16[32,7168]{1,0:T(8,128)(2,1)S(1)}, u32[]{:S(2)}, u32[]{:S(2)}) collective-permute-start(bf16[32,7168]{1,0:T(8,128)(2,1)S(1)} %collective-permute-done.2), channel_id=1, source_target_pairs={{4,0},{8,12},{5,1},{9,13},{6,2},{10,14},{7,3},{11,15},{20,16},{24,... | collective-permute-start | bytes 1376264 | tf_op jit(solution)/shard_map/ppermute | solution.py:46
  66.2 8.1 %fusion.9 = f32[768,256]{0,1:T(8,128)} fusion(f32[768,256]{0,1:T(8,128)} %fusion.10, bf16[32,7168]{1,0:T(8,128)(2,1)S(1)} %collective-permute-done.1, bf16[768,7168]{1,0:T(8,128)(2,1)} %param.9), kind=kOutput, calls=%fused_computation.20 | convolution fusion | flops 352321536 | bytes 11567104 | tf_op jit(solution)/shard_map/dot_general | solution.py:13
  74.3 4.0 %fusion.8 = f32[768,256]{0,1:T(8,128)} fusion(f32[768,256]{0,1:T(8,128)} %fusion.9, bf16[32,7168]{1,0:T(8,128)(2,1)S(1)} %broadcast_select_fusion.1, bf16[768,7168]{1,0:T(8,128)(2,1)S(1)} %bitcast.65), kind=kOutput, calls=%fused_computation.18 | convolution fusion | flops 352321536 | bytes 11567104 | tf_op jit(solution)/shard_map/dot_general | solution.py:13
  79.7 4.0 %fusion.7 = f32[768,256]{0,1:T(8,128)} fusion(f32[768,256]{0,1:T(8,128)} %fusion.8, bf16[32,7168]{1,0:T(8,128)(2,1)S(1)} %collective-permute-done.5, bf16[768,7168]{1,0:T(8,128)(2,1)S(1)} %bitcast.65), kind=kOutput, calls=%fused_computation.16 | convolution fusion | flops 352321536 | bytes 11567104 | tf_op jit(solution)/shard_map/dot_general | solution.py:13
  83.7 4.0 %fusion.6 = f32[768,256]{0,1:T(8,128)} fusion(f32[768,256]{0,1:T(8,128)} %fusion.7, bf16[32,7168]{1,0:T(8,128)(2,1)S(1)} %broadcast_select_fusion, bf16[768,7168]{1,0:T(8,128)(2,1)S(1)} %bitcast.65), kind=kOutput, calls=%fused_computation.14 | convolution fusion | flops 352321536 | bytes 11567104 | tf_op jit(solution)/shard_map/dot_general | solution.py:13
  87.7 2.6 %collective-permute-done.7 = bf16[32,7168]{1,0:T(8,128)(2,1)S(1)} collective-permute-done((bf16[32,7168]{1,0:T(8,128)(2,1)S(1)}, bf16[32,7168]{1,0:T(8,128)(2,1)S(1)}, u32[]{:S(2)}, u32[]{:S(2)}) %collective-permute-start.7) | collective-permute-done | bytes 458784 | tf_op jit(solution)/shard_map/ppermute | solution.py:77
  90.3 4.0 %fusion.5 = f32[768,256]{0,1:T(8,128)} fusion(f32[768,256]{0,1:T(8,128)} %fusion.6, bf16[32,7168]{1,0:T(8,128)(2,1)S(1)} %collective-permute-done.7, bf16[768,7168]{1,0:T(8,128)(2,1)S(1)} %bitcast.65), kind=kOutput, calls=%fused_computation.12 | convolution fusion | flops 352321536 | bytes 11567104 | tf_op jit(solution)/shard_map/dot_general | solution.py:13
  94.2 1.4 %fusion.3 = f32[768]{0:T(1024)S(1)} fusion(f32[768,256]{0,1:T(8,128)} %fusion.5, bf16[768,128]{1,0:T(8,128)(2,1)S(1)} %add_convert_fusion, bf16[4,256,128]{2,1,0:T(8,128)(2,1)S(1)} %fusion.4), kind=kOutput, calls=%fused_computation.8 | convolution fusion | flops 50724096 | bytes 1051648 | tf_op jit(solution)/shard_map/dot_general | solution.py:13
  95.7 1.4 %fusion.2 = f32[768]{0:T(1024)S(1)} fusion(f32[768,256]{0,1:T(8,128)} %fusion.5, bf16[768,128]{1,0:T(8,128)(2,1)S(1)} %add_convert_fusion, bf16[4,256,128]{2,1,0:T(8,128)(2,1)S(1)} %fusion.4), kind=kOutput, calls=%fused_computation.7 | convolution fusion | flops 50724096 | bytes 1051648 | tf_op jit(solution)/shard_map/dot_general | solution.py:13
  97.1 1.4 %fusion.1 = f32[768]{0:T(1024)S(1)} fusion(f32[768,256]{0,1:T(8,128)} %fusion.5, bf16[768,128]{1,0:T(8,128)(2,1)S(1)} %add_convert_fusion, bf16[4,256,128]{2,1,0:T(8,128)(2,1)S(1)} %fusion.4), kind=kOutput, calls=%fused_computation.6 | convolution fusion | flops 50724096 | bytes 1051648 | tf_op jit(solution)/shard_map/dot_general | solution.py:13
  98.5 1.4 %fusion = f32[768]{0:T(1024)S(1)} fusion(f32[768,256]{0,1:T(8,128)} %fusion.5, bf16[768,128]{1,0:T(8,128)(2,1)S(1)} %add_convert_fusion, bf16[4,256,128]{2,1,0:T(8,128)(2,1)S(1)} %fusion.4), kind=kOutput, calls=%fused_computation.5 | convolution fusion | flops 50724096 | bytes 1051648 | tf_op jit(solution)/shard_map/dot_general | solution.py:13
  100.1 29.5 %psum.7 = f32[4,8]{1,0:T(4,128)S(1)} all-reduce(f32[4,8]{1,0:T(4,128)S(1)} %fusion.12), channel_id=1, replica_groups=mesh['groups'=2,'blk'=4,'eig'=2,'rep'=2] {'blk','eig','rep'}, use_global_device_ids=true, to_apply=%region_5.6 | all-reduce | flops 32 | bytes 256 | tf_op jit(solution)/shard_map/psum | solution.py:119
  (55 shorter events, 12.9 us)
Async XLA Ops:
  0.0 20.9 %copy-start = (bf16[768,2048]{1,0:T(8,128)(2,1)S(1)}, bf16[768,2048]{1,0:T(8,128)(2,1)}, u32[]{:S(2)}) copy-start(bf16[768,2048]{1,0:T(8,128)(2,1)} %param.10) | copy-start | bytes 9437188
  0.0 20.9 %copy-start.1 = (bf16[128,2048]{1,0:T(8,128)(2,1)S(1)}, bf16[128,2048]{1,0:T(8,128)(2,1)}, u32[]{:S(2)}) copy-start(bf16[128,2048]{1,0:T(8,128)(2,1)} %param.12) | copy-start | bytes 1572868
  2.0 44.2 %collective-permute-start = (bf16[32,7168]{1,0:T(8,128)(2,1)}, bf16[32,7168]{1,0:T(8,128)(2,1)}, u32[]{:S(2)}, u32[]{:S(2)}) collective-permute-start(bf16[32,7168]{1,0:T(8,128)(2,1)} %constant_dynamic-slice_fusion), channel_id=1, source_target_pairs={{0,4},{4,0},{8,12},{12,8},{1,5},{5,1},{9,13},{13,9},{2,6},{6,2},{1... | collective-permute-start | bytes 1376264 | tf_op jit(solution)/shard_map/ppermute | solution.py:42
  5.0 43.4 %collective-permute-start.3 = (bf16[32,7168]{1,0:T(8,128)(2,1)}, bf16[32,7168]{1,0:T(8,128)(2,1)}, u32[]{:S(2)}, u32[]{:S(2)}) collective-permute-start(bf16[32,7168]{1,0:T(8,128)(2,1)} %constant_dynamic-slice_fusion), channel_id=1, source_target_pairs={{4,8},{8,4},{5,9},{9,5},{6,10},{10,6},{7,11},{11,7},{20,24},{24,20... | collective-permute-start | bytes 1376264 | tf_op jit(solution)/shard_map/ppermute | solution.py:43
  10.2 8.6 %collective-permute-start.10 = (f32[192,128]{1,0:T(8,128)S(1)}, f32[192,128]{1,0:T(8,128)S(1)}, u32[]{:S(2)}, u32[]{:S(2)}) collective-permute-start(f32[192,128]{1,0:T(8,128)S(1)} %pad_maximum_fusion.1), channel_id=1, source_target_pairs={{0,1},{1,0},{2,3},{3,2},{4,5},{5,4},{6,7},{7,6},{8,9},{9,8},{10,11... | collective-permute-start | bytes 294920 | tf_op jit(solution)/shard_map/ppermute | solution.py:25
  19.4 5.5 %collective-permute-start.11 = (f32[192,128]{1,0:T(8,128)}, f32[192,128]{1,0:T(8,128)}, u32[]{:S(2)}, u32[]{:S(2)}) collective-permute-start(f32[192,128]{1,0:T(8,128)} %fusion.24), channel_id=1, source_target_pairs={{0,2},{2,0},{1,3},{3,1},{4,6},{6,4},{5,7},{7,5},{8,10},{10,8},{9,1... | collective-permute-start | bytes 294920 | tf_op jit(solution)/shard_map/ppermute | solution.py:25
  25.9 0.6 copy-start.3
  28.6 9.3 %collective-permute-start.14 = (bf16[64,256]{1,0:T(8,128)(2,1)}, bf16[64,256]{1,0:T(8,128)(2,1)}, u32[]{:S(2)}, u32[]{:S(2)}) collective-permute-start(bf16[64,256]{1,0:T(8,128)(2,1)} %fusion.11), channel_id=1, source_target_pairs={{0,12},{4,8},{8,4},{12,0},{1,13},{5,9},{9,5},{13,1},{2,14},{6,10},... | collective-permute-start | bytes 98312 | tf_op jit(solution)/shard_map/ppermute | solution.py:33
  31.0 6.8 %collective-permute-start.13 = (bf16[64,256]{1,0:T(8,128)(2,1)}, bf16[64,256]{1,0:T(8,128)(2,1)}, u32[]{:S(2)}, u32[]{:S(2)}) collective-permute-start(bf16[64,256]{1,0:T(8,128)(2,1)} %fusion.11), channel_id=1, source_target_pairs={{0,8},{4,12},{8,0},{12,4},{1,9},{5,13},{9,1},{13,5},{2,10},{6,14},... | collective-permute-start | bytes 98312 | tf_op jit(solution)/shard_map/ppermute | solution.py:33
  33.7 4.2 %collective-permute-start.12 = (bf16[64,256]{1,0:T(8,128)(2,1)}, bf16[64,256]{1,0:T(8,128)(2,1)}, u32[]{:S(2)}, u32[]{:S(2)}) collective-permute-start(bf16[64,256]{1,0:T(8,128)(2,1)} %fusion.11), channel_id=1, source_target_pairs={{0,4},{4,0},{8,12},{12,8},{1,5},{5,1},{9,13},{13,9},{2,6},{6,2},{1... | collective-permute-start | bytes 98312 | tf_op jit(solution)/shard_map/ppermute | solution.py:33
  37.9 5.7 %collective-permute-start.8 = (f32[768,128]{1,0:T(8,128)S(1)}, f32[768,128]{1,0:T(8,128)}, u32[]{:S(2)}, u32[]{:S(2)}) collective-permute-start(f32[768,128]{1,0:T(8,128)S(1)} %fusion.26), channel_id=1, source_target_pairs={{0,1},{1,0},{2,3},{3,2},{4,5},{5,4},{6,7},{7,6},{8,9},{9,8},{10,11... | collective-permute-start | bytes 1179656 | tf_op jit(solution)/shard_map/ppermute | solution.py:25
  38.7 0.7 copy-start.2
  44.6 29.7 %slice-start = ((s8[11010048]{0:T(1024)(128)(4,1)}), s8[4194304]{0:T(1024)(128)(4,1)S(1)}, s32[]{:S(2)}) async-start(s8[11010048]{0:T(1024)(128)(4,1)} %bitcast.64), calls=%async_computation | async-start | bytes 8388608
  44.6 29.7 %slice-start.1 = ((s8[11010048]{0:T(1024)(128)(4,1)}), s8[4194304]{0:T(1024)(128)(4,1)S(1)}, s32[]{:S(2)}) async-start(s8[11010048]{0:T(1024)(128)(4,1)} %bitcast.64), calls=%async_computation.1 | async-start | bytes 8388608
  44.6 13.4 %collective-permute-start.9 = (bf16[768,128]{1,0:T(8,128)(2,1)S(1)}, bf16[768,128]{1,0:T(8,128)(2,1)S(1)}, u32[]{:S(2)}, u32[]{:S(2)}) collective-permute-start(bf16[768,128]{1,0:T(8,128)(2,1)S(1)} %get-tuple-element.5), channel_id=1, source_target_pairs={{0,2},{2,0},{1,3},{3,1},{4,6},{6,4},{5,7},{7,5},{8,10},{10,8},{9,1... | collective-permute-start | bytes 589832 | tf_op jit(solution)/shard_map/ppermute | solution.py:25
  46.2 19.9 %collective-permute-start.1 = (bf16[32,7168]{1,0:T(8,128)(2,1)}, bf16[32,7168]{1,0:T(8,128)(2,1)S(1)}, u32[]{:S(2)}, u32[]{:S(2)}) collective-permute-start(bf16[32,7168]{1,0:T(8,128)(2,1)} %collective-permute-done), channel_id=1, source_target_pairs={{0,16},{16,0},{1,17},{17,1},{2,18},{18,2},{3,19},{19,3},{4,20},{20... | collective-permute-start | bytes 1376264 | tf_op jit(solution)/shard_map/ppermute | solution.py:77
  47.7 10.3 %collective-permute-start.2 = (bf16[32,7168]{1,0:T(8,128)(2,1)}, bf16[32,7168]{1,0:T(8,128)(2,1)S(1)}, u32[]{:S(2)}, u32[]{:S(2)}) collective-permute-start(bf16[32,7168]{1,0:T(8,128)(2,1)} %collective-permute-done), channel_id=1, source_target_pairs={{4,8},{8,4},{5,9},{9,5},{6,10},{10,6},{7,11},{11,7},{20,24},{24,20... | collective-permute-start | bytes 1376264 | tf_op jit(solution)/shard_map/ppermute | solution.py:45
  48.4 15.4 %collective-permute-start.4 = (bf16[32,7168]{1,0:T(8,128)(2,1)}, bf16[32,7168]{1,0:T(8,128)(2,1)S(1)}, u32[]{:S(2)}, u32[]{:S(2)}) collective-permute-start(bf16[32,7168]{1,0:T(8,128)(2,1)} %collective-permute-done.3), channel_id=1, source_target_pairs={{4,0},{8,12},{5,1},{9,13},{6,2},{10,14},{7,3},{11,15},{20,16},{24,... | collective-permute-start | bytes 1376264 | tf_op jit(solution)/shard_map/ppermute | solution.py:44
  63.8 10.5 %slice-start.2 = ((s8[11010048]{0:T(1024)(128)(4,1)}), s8[2621440]{0:T(1024)(128)(4,1)S(1)}, s32[]{:S(2)}) async-start(s8[11010048]{0:T(1024)(128)(4,1)} %bitcast.64), calls=%async_computation.2 | async-start | bytes 5242880
  63.8 15.9 %collective-permute-start.5 = (bf16[32,7168]{1,0:T(8,128)(2,1)S(1)}, bf16[32,7168]{1,0:T(8,128)(2,1)S(1)}, u32[]{:S(2)}, u32[]{:S(2)}) collective-permute-start(bf16[32,7168]{1,0:T(8,128)(2,1)S(1)} %broadcast_select_fusion.1), channel_id=1, source_target_pairs={{0,16},{16,0},{1,17},{17,1},{2,18},{18,2},{3,19},{19,3},{4,20},{20... | collective-permute-start | bytes 1376264 | tf_op jit(solution)/shard_map/ppermute | solution.py:77
  64.7 13.7 %collective-permute-start.6 = (bf16[32,7168]{1,0:T(8,128)(2,1)S(1)}, bf16[32,7168]{1,0:T(8,128)(2,1)S(1)}, u32[]{:S(2)}, u32[]{:S(2)}) collective-permute-start(bf16[32,7168]{1,0:T(8,128)(2,1)S(1)} %collective-permute-done.2), channel_id=1, source_target_pairs={{4,0},{8,12},{5,1},{9,13},{6,2},{10,14},{7,3},{11,15},{20,16},{24,... | collective-permute-start | bytes 1376264 | tf_op jit(solution)/shard_map/ppermute | solution.py:46
  78.4 11.8 %collective-permute-start.7 = (bf16[32,7168]{1,0:T(8,128)(2,1)S(1)}, bf16[32,7168]{1,0:T(8,128)(2,1)S(1)}, u32[]{:S(2)}, u32[]{:S(2)}) collective-permute-start(bf16[32,7168]{1,0:T(8,128)(2,1)S(1)} %broadcast_select_fusion), channel_id=1, source_target_pairs={{0,16},{16,0},{1,17},{17,1},{2,18},{18,2},{3,19},{19,3},{4,20},{20... | collective-permute-start | bytes 1376264 | tf_op jit(solution)/shard_map/ppermute | solution.py:77
  83.7 16.3 %copy-start.4 = (s32[768]{0:T(1024)S(1)}, s32[768]{0:T(1024)}, u32[]{:S(2)}) copy-start(s32[768]{0:T(1024)} %select_reduce_fusion) | copy-start | bytes 9220

commit v2 on v1

v2 whole, which is shorter than its diff:
```python
import functools

import jax
import jax.numpy as jnp
from jax import lax
from jax.experimental import pallas as pl
from jax.experimental.pallas import tpu as pltpu
from jax.sharding import PartitionSpec as P

R = 32
LANES = 128
BLOCK = 256
VMEM_LIMIT = 24 * 1024 * 1024
AXES = ("groups", "blk", "eig", "rep")


damping = 0.05


def contract_last(left_side, right_side, precision=None):
    return lax.dot_general(
        left_side,
        right_side,
        (((1,), (1,)), ((), ())),
        precision=precision,
        preferred_element_type=jnp.float32,
    )


def swap_sum(value, axis, send_as):
    size = lax.axis_size(axis)
    if size & (size - 1):
        return lax.psum(value, axis)
    step = 1
    while step < size:
        pairs = [(i, i ^ step) for i in range(size)]
        value = value + lax.ppermute(value.astype(send_as), axis, pairs).astype(jnp.float32)
        step *= 2
    return value


def by_distance(value, axis="blk"):
    size = lax.axis_size(axis)
    return [value] + [
        lax.ppermute(value, axis, [(i, i ^ k) for i in range(size)]) for k in range(1, size)
    ]


def held(value, *until):
    return lax.optimization_barrier((value, *until))[0]


def half_kernel(whole_ref, half_ref, copied):
    columns = half_ref.shape[1]
    start = pl.multiple_of(lax.axis_index("groups") * columns, LANES)
    copy = pltpu.make_async_copy(whole_ref.at[:, pl.ds(start, columns)], half_ref, copied)
    copy.start()
    copy.wait()


def take_half(whole):
    rows, columns = whole.shape
    return pl.pallas_call(
        half_kernel,
        in_specs=[pl.BlockSpec(memory_space=pl.ANY)],
        out_specs=pl.BlockSpec(memory_space=pltpu.VMEM),
        out_shape=jax.ShapeDtypeStruct((rows, columns // 2), whole.dtype),
        scratch_shapes=[pltpu.SemaphoreType.DMA],
    )(whole)


def parts_kernel(in_ref, in_query_ref, out_ref, out_query_ref, grads_ref, sum_ref):
    rows, width = in_ref.shape[0], out_ref.shape[0]
    sum_ref[:rows] = jnp.dot(in_ref[...], in_query_ref[...], preferred_element_type=jnp.float32)
    sum_ref[rows : rows + width] = jnp.dot(
        out_ref[...], out_query_ref[...], preferred_element_type=jnp.float32
    )
    tokens = grads_ref.shape[0]
    block = tokens // 3 if tokens % 48 == 0 else tokens

    @pl.loop(0, tokens // block)
    def _(step):
        start = pl.multiple_of(step * block, 16)
        sum_ref[pl.ds(rows + width + start, block), :] = contract_last(
            grads_ref[pl.ds(start, block), :], out_ref[...]
        )


def small_parts(basis_in, query_in, basis_out, query_out, out_grads):
    high = basis_in.shape[0] + basis_out.shape[0] + out_grads.shape[0]
    return pl.pallas_call(
        parts_kernel,
        out_shape=jax.ShapeDtypeStruct((high, query_in.shape[1]), jnp.float32),
        compiler_params=pltpu.CompilerParams(vmem_limit_bytes=VMEM_LIMIT),
    )(basis_in, query_in, basis_out, query_out, out_grads)


def weigh(query_count, packs, out_query, weighted_ref):
    rows, pairs = packs[0].shape[0], out_query.shape[1]
    query_of = lax.broadcasted_iota(jnp.int32, (rows, pairs), 1) // R
    for slot, pack_ref in enumerate(packs):
        in_query = pack_ref[:, :pairs].astype(jnp.float32)
        inverse = 1.0 / (pack_ref[:, pairs:].astype(jnp.float32) + damping)
        for query in range(query_count):
            own = jnp.where(query_of == query, in_query, 0.0).astype(jnp.bfloat16)
            outer_sum = contract_last(own, out_query)
            weighted_ref[slot, pl.ds(query * rows, rows), :] = (outer_sum * inverse).astype(
                jnp.bfloat16
            )


def score_block(acts_ref, tokens, start, columns, pieces, slots, grad_ref, weighted_ref, onehot_ref):
    rows = pieces[0].shape[0]
    copies = LANES // rows
    stacked = jnp.concatenate([piece[...] for piece in pieces for _ in range(copies)], axis=0)
    projected = contract_last(acts_ref[pl.ds(start, tokens), columns], stacked)
    grad = grad_ref[pl.ds(start, tokens), :]
    onehot = onehot_ref[:, pl.ds(start, tokens)]
    summed = 0.0
    for place, slot in enumerate(slots):
        mixed = contract_last(grad, weighted_ref[slot])
        own = projected[:, place * LANES : (place + 1) * LANES]
        product = jnp.concatenate([own] * (mixed.shape[1] // LANES), axis=1) * mixed
        high = product.astype(jnp.bfloat16)
        low = (product - high.astype(jnp.float32)).astype(jnp.bfloat16)
        summed += jnp.dot(onehot, high, preferred_element_type=jnp.float32)
        summed += jnp.dot(onehot, low, preferred_element_type=jnp.float32)
    return summed


def score_kernel(parts, query_count, make_weights, last, acts_ref, grad_ref, onehot_ref, *refs):
    counts = [len(slots) for slots, _ in parts]
    pieces = [refs[sum(counts[:i]) : sum(counts[: i + 1])] for i in range(len(parts))]
    refs = refs[sum(counts) :]
    if make_weights:
        packs, out_query_ref, out_ref, weighted_ref = refs[:-3], *refs[-3:]
        weigh(query_count, packs, out_query_ref[...], weighted_ref)
        before = jnp.zeros(out_ref.shape, jnp.float32)
    else:
        weighted_ref, before_ref, out_ref = refs
        before = before_ref[...]
    block = BLOCK
    group = lax.axis_index("groups")

    def add_block(step, summed):
        start = pl.multiple_of(step * block, LANES)
        for (slots, which), own in zip(parts, pieces):
            columns = slice(None)
            if which != "all":
                width = own[0].shape[1]
                half = group if which == "here" else 1 - group
                columns = pl.ds(pl.multiple_of(half * width, LANES), width)
            summed = summed + score_block(
                acts_ref, block, start, columns, own, slots, grad_ref, weighted_ref, onehot_ref
            )
        return summed

    summed = lax.fori_loop(0, acts_ref.shape[0] // block, add_block, before)
    if last:
        width = summed.shape[1]
        query_of = lax.broadcasted_iota(jnp.int32, (query_count, width), 1) // (
            width // query_count
        )
        chosen = query_of == lax.broadcasted_iota(jnp.int32, (query_count, width), 0)
        out_ref[...] = contract_last(
            chosen.astype(jnp.float32), summed, precision=lax.Precision.HIGHEST
        )
    else:
        out_ref[...] = summed


def add_scores(acts, grad_proj, onehot, parts, pieces, more, query_count, last=False):
    seq_count = onehot.shape[0]
    first = isinstance(more[0], list)
    rows = pieces[0].shape[0]
    width = query_count * rows
    out_shape = jax.ShapeDtypeStruct((query_count, seq_count) if last else (seq_count, width), jnp.float32)
    if first:
        weights = jax.ShapeDtypeStruct((len(more[0]), width, more[1].shape[0]), jnp.bfloat16)
        out_shape = [out_shape, weights]
        more = [*more[0], more[1]]
    flops = 2 * sum(piece.shape[1] for piece in pieces) * acts.shape[0] * LANES
    return pl.pallas_call(
        functools.partial(score_kernel, parts, query_count, first, last),
        out_shape=out_shape,
        compiler_params=pltpu.CompilerParams(vmem_limit_bytes=VMEM_LIMIT),
        cost_estimate=pl.CostEstimate(flops=flops, bytes_accessed=acts.shape[0] * 1024, transcendentals=0),
    )(acts, grad_proj, onehot, *pieces, *more)


def precondition(in_rows, eig_rows, out_query):
    row_count = in_rows.shape[0]
    basis_width = out_query.shape[0]
    query_count = out_query.shape[1] // R
    outer_sum = jnp.einsum(
        "jqr,iqr->qji",
        in_rows.reshape(row_count, query_count, R),
        out_query.reshape(basis_width, query_count, R),
        preferred_element_type=jnp.float32,
    )
    inverse = 1.0 / (eig_rows.astype(jnp.float32) + damping)
    return (outer_sum * inverse[None, :, :]).astype(jnp.bfloat16)


def plain_scores(acts, basis_in, pack, out_query, grad_proj, onehot):
    pack = lax.all_gather(pack, "blk", axis=0, tiled=True)
    piece = lax.all_gather(basis_in, "blk", axis=0, tiled=True)
    pairs = out_query.shape[1]
    weighted = precondition(pack[:, :pairs], pack[:, pairs:], out_query)
    projected = contract_last(acts, piece)
    per_token = jnp.stack(
        [jnp.sum(projected * contract_last(grad_proj, slab), axis=1) for slab in weighted]
    )
    return contract_last(per_token, onehot, precision=lax.Precision.HIGHEST)


def to_send(part, split):
    high = lax.reduce_precision(part[:split], 8, 7)
    low = part[:split] - high
    return jnp.concatenate([high, low, part[split:]], axis=0).astype(jnp.bfloat16)


def add_sent(part, other, split):
    high, low, rest = other[:split], other[split : 2 * split], other[2 * split :]
    first = part[:split] + high.astype(jnp.float32) + low.astype(jnp.float32)
    return jnp.concatenate([first, part[split:] + rest.astype(jnp.float32)], axis=0)


def stepped_scores(
    acts, out_grads, basis_in, basis_out, eigvals, query_out, query_in, onehot
):
    rows, width = basis_in.shape[0], basis_out.shape[0]
    query_count = query_in.shape[1] // R
    place = lax.axis_index("blk")
    inner = (place == 1) | (place == 2)
    pair = [(0, 1), (1, 0)]
    middle = [(1, 2), (2, 1)]
    outward = [(1, 0), (2, 3)]
    along = functools.partial(lax.ppermute, axis_name="blk")
    swapped = functools.partial(lax.ppermute, axis_name="groups", perm=pair)

    half = take_half(basis_in)
    mine_1 = along(half, perm=[(0, 1), (1, 0), (2, 3), (3, 2)])
    across = along(half, perm=middle)

    split = rows + width
    part = small_parts(held(basis_in, half), query_in, basis_out, query_out, out_grads)
    other = lax.ppermute(to_send(part, split), "rep", pair)
    part = add_sent(part, held(other, mine_1, across), split)
    other = lax.ppermute(to_send(part, split), "eig", pair)
    part = add_sent(part, other, split).astype(jnp.bfloat16)
    in_query, out_query, grad_proj = part[:rows], part[rows:split], part[split:]

    first_over = along(mine_1, perm=middle)
    across_out = along(across, perm=outward)
    theirs_1 = swapped(mine_1)

    in_query = held(in_query, first_over, across_out)
    packs = by_distance(jnp.concatenate([in_query, eigvals], axis=1))

    mine_2 = jnp.where(inner, first_over, held(across_out, theirs_1))
    theirs_2 = swapped(mine_2)
    first_out = along(first_over, perm=outward)

    add = functools.partial(add_scores, acts, grad_proj, onehot, query_count=query_count)
    sums, weights = add([((0,), "all")], [basis_in], (packs, out_query))
    sums = add([((1, 2), "here")], [mine_1, mine_2], (weights, sums))
    mine_3 = jnp.where(inner, across, held(first_out, sums))
    theirs_3 = swapped(mine_3)
    sums = add(
        [((1, 2), "there"), ((3,), "here")], [theirs_1, theirs_2, mine_3], (weights, sums)
    )
    scores = add([((3,), "there")], [theirs_3], (weights, sums), last=True)
    for axis in (("eig", "rep"), "blk"):
        scores = sum(by_distance(scores, axis))
    return scores


def plain_path(acts, out_grads, basis_in, basis_out, eigvals, query_out, query_in, onehot):
    def whole_sum(part, send_as):
        return swap_sum(swap_sum(part, "rep", jnp.float32), "eig", send_as).astype(jnp.bfloat16)

    in_query = whole_sum(jnp.dot(basis_in, query_in, preferred_element_type=jnp.float32), jnp.float32)
    out_query = whole_sum(
        jnp.dot(basis_out, query_out, preferred_element_type=jnp.float32), jnp.float32
    )
    grad_proj = whole_sum(contract_last(out_grads, basis_out), jnp.bfloat16)
    pack = jnp.concatenate([in_query, eigvals], axis=1)
    scores = plain_scores(acts, basis_in, pack, out_query, grad_proj, onehot.astype(jnp.float32))
    return lax.psum(scores, ("blk", "eig", "rep"))


def on_device(acts, out_grads, basis_in, basis_out, eigvals, query_out, query_in, seq_ids, owner):
    rows, features = basis_in.shape
    pairs = query_in.shape[1]
    seq_count = owner.shape[0]
    labels = jnp.arange(seq_count, dtype=jnp.int32)
    column_of = jnp.sum(jnp.where(seq_ids[None, :] == labels[:, None], owner[:, None], 0), axis=0)
    onehot = (labels[:, None] == column_of[None, :]).astype(jnp.bfloat16)
    stepped = (
        all(lax.axis_size(axis) == size for axis, size in zip(AXES, (2, 4, 2, 2)))
        and LANES % rows == 0
        and (pairs // R * rows) % LANES == 0
        and features % (2 * LANES) == 0
        and acts.shape[0] % BLOCK == 0
        and pairs == basis_out.shape[0] == LANES
    )
    way = stepped_scores if stepped else plain_path
    scores = way(acts, out_grads, basis_in, basis_out, eigvals, query_out, query_in, onehot)
    own_queries = pairs // R // lax.axis_size(("eig", "rep"))
    own_columns = seq_count // lax.axis_size("blk")
    return lax.dynamic_slice(
        scores,
        (lax.axis_index(("eig", "rep")) * own_queries, lax.axis_index("blk") * own_columns),
        (own_queries, own_columns),
    )


def solution(mesh):
    return jax.shard_map(
        on_device,
        mesh=mesh,
        in_specs=(
            P(("groups", "blk"), ("eig", "rep")),
            P(("groups", "blk"), ("eig", "rep")),
            P("blk", ("eig", "rep")),
            P(None, ("eig", "rep")),
            P("blk", None),
            P(("eig", "rep"), "groups"),
            P(("eig", "rep"), "groups"),
            P(("groups", "blk")),
            P("groups"),
        ),
        out_specs=P(("groups", "eig", "rep"), "blk"),
        check_vma=False,
    )
```

time: 131 us -> 85.2 us (0.65)
  matrix products: 52.5 us -> 0 us
  blocking collectives: 29.5 us -> 0 us
  Pallas kernels: 0 us -> 22.7 us
  waiting for transfers between devices: 11.4 us -> 21.6 us
  other arithmetic: 7.91 us -> 0.45 us
  local copies, waits for them, and re-layouts: 8.89 us -> 15.6 us
  starting transfers between devices: 19.7 us -> 24.2 us
    dot_general x16 -> x0, matrix products: 52.5 us -> none  [the longest x12 47.5 us: contract_last(): lax.dot_general(left_side, right_side, (((1,), (1,)), ((), ())), preferre...]
    psum x1 -> x0, blocking collectives: 29.5 us -> none  [on_device(): scores = lax.psum(part_scores, ('blk', 'eig', 'rep'))]
    pallas_call x0 -> x6, Pallas kernels: none -> 22.7 us  [the longest x4 18.9 us: add_scores(): pl.pallas_call(functools.partial(score_kernel, parts, query_count, first,...]
    unnamed x16 -> x29, local copies, waits for them, and re-layouts: 1.29 us -> 14.9 us
    ppermute x15 -> x19, waiting for transfers between devices: 11.4 us -> 21.6 us  [the longest x1 10.5 us: stepped_scores(): across_out = along(across, perm=outward)]
    slice x5 -> x3, local copies, waits for them, and re-layouts: 5.02 us -> 0.03 us  [the longest x1 0.02 us: to_send(): part[split:]]
    ppermute x15 -> x19, starting transfers between devices: 19.7 us -> 24.2 us  [the longest x9 10.8 us: by_distance(): lax.ppermute(value, axis, [(i, i ^ k) for i in range(size)])]
    convert_element_type x3 -> x1, other arithmetic: 2.05 us -> 0.01 us  [on_device(): onehot = (labels[:, None] == column_of[None, :]).astype(jnp.bfloat16)]
  transfers between devices with their start and end apart: 15 -> 19, of which waited for: 4 -> 7; matrix products, arithmetic and copies ran while one was open for 43% -> 0% of each run, Pallas kernels for 0% -> 21%
where the time goes in v2:
time: 85.2 us; the launch traced here: 84.8 us
  starting transfers between devices  24.2 us (28%)
  Pallas kernels  22.7 us (27%)
  waiting for transfers between devices  21.6 us (25%)
  local copies, waits for them, and re-layouts  15.6 us (18%)
    pallas_call x4, Pallas kernels, add_scores(): pl.pallas_call(functools.partial(score_kernel, parts, query_count, first,...  18.9 us
    unnamed x29, local copies, waits for them, and re-layouts  14.9 us
    ppermute x9, starting transfers between devices, by_distance(): lax.ppermute(value, axis, [(i, i ^ k) for i in range(size)])  10.8 us
    ppermute x1, waiting for transfers between devices, stepped_scores(): across_out = along(across, perm=outward)  10.5 us
    ppermute x9, waiting for transfers between devices, by_distance(): lax.ppermute(value, axis, [(i, i ^ k) for i in range(size)])  5.63 us
    ppermute x1, waiting for transfers between devices, stepped_scores(): other = lax.ppermute(to_send(part, split), 'eig', pair)  3.85 us
    ppermute x1, starting transfers between devices, stepped_scores(): mine_1 = along(half, perm=[(0, 1), (1, 0), (2, 3), (3, 2)])  3.09 us
    pallas_call x1, Pallas kernels, small_parts(): pl.pallas_call(parts_kernel, out_shape=jax.ShapeDtypeStruct((high, query_...  1.91 us
  transfers between devices with their start and end apart: 19, of which 7 were waited for; matrix products, arithmetic and copies ran while one was open for 0% of the time, Pallas kernels for 21%

profile of v2, /device:TPU:0, one launch (start us, length us, event | category | flops | bytes accessed | tf_op | source)
XLA Modules:
  0.0 84.8 jit_solution(15034081010563732579)
XLA Ops:
  0.0 1.8 %shard_map.91 = bf16[64,3584]{1,0:T(8,128)(2,1)} custom-call(bf16[64,7168]{1,0:T(8,128)(2,1)} %refs_0_.1), custom_call_target="tpu_custom_call" | custom-call | tf_op jit(solution)/shard_map/pallas_call | solution.py:63
  1.8 3.1 %collective-permute-start.1 = (bf16[64,3584]{1,0:T(8,128)(2,1)}, bf16[64,3584]{1,0:T(8,128)(2,1)S(1)}, u32[]{:S(2)}, u32[]{:S(2)}) collective-permute-start(bf16[64,3584]{1,0:T(8,128)(2,1)} %shard_map.91), channel_id=1, source_target_pairs={{0,4},{4,0},{8,12},{12,8},{1,5},{5,1},{9,13},{13,9},{2,6},{6,2},{1... | collective-permute-start | bytes 1376264 | tf_op jit(solution)/shard_map/ppermute | solution.py:243
  5.6 1.2 %copy-done.3 = bf16[64,7168]{1,0:T(8,128)(2,1)S(1)} copy-done((bf16[64,7168]{1,0:T(8,128)(2,1)S(1)}, bf16[64,7168]{1,0:T(8,128)(2,1)}, u32[]{:S(2)}) %copy-start.3) | copy-done | bytes 917528
  6.8 1.9 %copy-done.5 = bf16[768,2048]{1,0:T(8,128)(2,1)S(1)} copy-done((bf16[768,2048]{1,0:T(8,128)(2,1)S(1)}, bf16[768,2048]{1,0:T(8,128)(2,1)}, u32[]{:S(2)}) %copy-start.5) | copy-done | bytes 3145752
  8.7 1.5 %copy-done.6 = bf16[7168,128]{1,0:T(8,128)(2,1)S(1)} copy-done((bf16[7168,128]{1,0:T(8,128)(2,1)S(1)}, bf16[7168,128]{1,0:T(8,128)(2,1)}, u32[]{:S(2)}) %copy-start.6) | copy-done | bytes 1835032
  10.2 1.0 %copy-done.7 = bf16[128,2048]{1,0:T(8,128)(2,1)S(1)} copy-done((bf16[128,2048]{1,0:T(8,128)(2,1)S(1)}, bf16[128,2048]{1,0:T(8,128)(2,1)}, u32[]{:S(2)}) %copy-start.7) | copy-done | bytes 524312
  11.2 1.0 %copy-done.8 = bf16[2048,128]{1,0:T(8,128)(2,1)S(1)} copy-done((bf16[2048,128]{1,0:T(8,128)(2,1)S(1)}, bf16[2048,128]{1,0:T(8,128)(2,1)}, u32[]{:S(2)}) %copy-start.8) | copy-done | bytes 524312
  12.3 1.9 %shard_map.92 = f32[960,128]{1,0:T(8,128)S(1)} custom-call(bf16[64,7168]{1,0:T(8,128)(2,1)S(1)} %copy-done.3, bf16[7168,128]{1,0:T(8,128)(2,1)S(1)} %copy-done.6, bf16[128,2048]{1,0:T(8,128)(2,1)S(1)} %copy-done.7, bf16[2048,128]{1,0:T(8,128)(2,1)S(1)} %copy-done.8, bf16[768,2048]{1,0:T(8,128)(2,1)S(1)} %copy-done.5), custom_call_target="tpu_custom_call" | custom-call | tf_op jit(solution)/shard_map/pallas_call | solution.py:91
  14.4 1.6 %collective-permute-done = bf16[1152,128]{1,0:T(8,128)(2,1)S(1)} collective-permute-done((bf16[1152,128]{1,0:T(8,128)(2,1)S(1)}, bf16[1152,128]{1,0:T(8,128)(2,1)S(1)}, u32[]{:S(2)}, u32[]{:S(2)}) %collective-permute-start) | collective-permute-done | bytes 294944 | tf_op jit(solution)/shard_map/ppermute | solution.py:248
  16.1 1.6 %collective-permute-start.3 = (bf16[1152,128]{1,0:T(8,128)(2,1)S(1)}, bf16[1152,128]{1,0:T(8,128)(2,1)S(1)}, u32[]{:S(2)}, u32[]{:S(2)}) collective-permute-start(bf16[1152,128]{1,0:T(8,128)(2,1)S(1)} %pad_maximum_fusion.1), channel_id=1, source_target_pairs={{0,2},{2,0},{1,3},{3,1},{4,6},{6,4},{5,7},{7,5},{8,10},{10,8},{9,1... | collective-permute-start | bytes 884744 | tf_op jit(solution)/shard_map/ppermute | solution.py:250
  18.4 1.3 %collective-permute-start.6 = (bf16[64,3584]{1,0:T(8,128)(2,1)S(1)}, bf16[64,3584]{1,0:T(8,128)(2,1)S(1)}, u32[]{:S(2)}, u32[]{:S(2)}) collective-permute-start(bf16[64,3584]{1,0:T(8,128)(2,1)S(1)} %collective-permute-done.2), channel_id=1, source_target_pairs={{4,0},{8,12},{5,1},{9,13},{6,2},{10,14},{7,3},{11,15},{20,16},{24,... | collective-permute-start | bytes 1376264 | tf_op jit(solution)/shard_map/ppermute | solution.py:255
  19.7 1.6 %collective-permute-start.7 = (bf16[64,3584]{1,0:T(8,128)(2,1)S(1)}, bf16[64,3584]{1,0:T(8,128)(2,1)S(1)}, u32[]{:S(2)}, u32[]{:S(2)}) collective-permute-start(bf16[64,3584]{1,0:T(8,128)(2,1)S(1)} %collective-permute-done.1.refs_0_), channel_id=1, source_target_pairs={{0,16},{16,0},{1,17},{17,1},{2,18},{18,2},{3,19},{19,3},{4,20},{20... | collective-permute-start | bytes 1376264 | tf_op jit(solution)/shard_map/ppermute | solution.py:256
  21.3 3.9 %collective-permute-done.3 = bf16[1152,128]{1,0:T(8,128)(2,1)S(1)} collective-permute-done((bf16[1152,128]{1,0:T(8,128)(2,1)S(1)}, bf16[1152,128]{1,0:T(8,128)(2,1)S(1)}, u32[]{:S(2)}, u32[]{:S(2)}) %collective-permute-start.3) | collective-permute-done | bytes 294944 | tf_op jit(solution)/shard_map/ppermute | solution.py:250
  25.3 10.5 %collective-permute-done.6 = bf16[64,3584]{1,0:T(8,128)(2,1)S(1)} collective-permute-done((bf16[64,3584]{1,0:T(8,128)(2,1)S(1)}, bf16[64,3584]{1,0:T(8,128)(2,1)S(1)}, u32[]{:S(2)}, u32[]{:S(2)}) %collective-permute-start.6) | collective-permute-done | bytes 458784 | tf_op jit(solution)/shard_map/ppermute | solution.py:255
  35.9 2.7 %collective-permute-start.10 = (bf16[64,256]{1,0:T(8,128)(2,1)S(1)}, bf16[64,256]{1,0:T(8,128)(2,1)S(1)}, u32[]{:S(2)}, u32[]{:S(2)}) collective-permute-start(bf16[64,256]{1,0:T(8,128)(2,1)S(1)} %constant_dynamic-update-slice_fusion.refs_1_), channel_id=1, source_target_pairs={{0,12},{4,8},{8,4},{12,0},{1,13},{5,9},{9,5},{13,1},{2,14},{6,10},... | collective-permute-start | bytes 98312 | tf_op jit(solution)/shard_map/ppermute | solution.py:45
  38.6 1.8 %collective-permute-start.9 = (bf16[64,256]{1,0:T(8,128)(2,1)S(1)}, bf16[64,256]{1,0:T(8,128)(2,1)S(1)}, u32[]{:S(2)}, u32[]{:S(2)}) collective-permute-start(bf16[64,256]{1,0:T(8,128)(2,1)S(1)} %constant_dynamic-update-slice_fusion.refs_1_), channel_id=1, source_target_pairs={{0,8},{4,12},{8,0},{12,4},{1,9},{5,13},{9,1},{13,5},{2,10},{6,14},... | collective-permute-start | bytes 98312 | tf_op jit(solution)/shard_map/ppermute | solution.py:45
  40.4 1.3 %collective-permute-start.5 = (bf16[64,3584]{1,0:T(8,128)(2,1)S(1)}, bf16[64,3584]{1,0:T(8,128)(2,1)S(1)}, u32[]{:S(2)}, u32[]{:S(2)}) collective-permute-start(bf16[64,3584]{1,0:T(8,128)(2,1)S(1)} %collective-permute-done.4), channel_id=1, source_target_pairs={{4,0},{8,12},{5,1},{9,13},{6,2},{10,14},{7,3},{11,15},{20,16},{24,... | collective-permute-start | bytes 1376264 | tf_op jit(solution)/shard_map/ppermute | solution.py:263
  41.7 1.6 %collective-permute-start.12 = (bf16[64,3584]{1,0:T(8,128)(2,1)S(1)}, bf16[64,3584]{1,0:T(8,128)(2,1)S(1)}, u32[]{:S(2)}, u32[]{:S(2)}) collective-permute-start(bf16[64,3584]{1,0:T(8,128)(2,1)S(1)} %broadcast_select_fusion.1.refs_1_), channel_id=1, source_target_pairs={{0,16},{16,0},{1,17},{17,1},{2,18},{18,2},{3,19},{19,3},{4,20},{20... | collective-permute-start | bytes 1376264 | tf_op jit(solution)/shard_map/ppermute | solution.py:262
  43.5 4.1 %copy-done = bf16[768,7168]{1,0:T(8,128)(2,1)S(1)} copy-done((bf16[768,7168]{1,0:T(8,128)(2,1)S(1)}, bf16[768,7168]{1,0:T(8,128)(2,1)}, u32[]{:S(2)}) %copy-start) | copy-done | bytes 11010072
  47.6 4.4 %shard_map.93 = (f32[8,256]{1,0:T(8,128)S(1)}, bf16[4,256,128]{2,1,0:T(8,128)(2,1)S(1)}) custom-call(bf16[768,7168]{1,0:T(8,128)(2,1)S(1)} %copy-done, bf16[768,128]{1,0:T(8,128)(2,1)S(1)} %add_convert_fusion.grad_ref, bf16[8,768]{1,0:T(8,128)(2,1)S(1)} %fusion.3.onehot_ref, bf16[64,7168]{1,0:T(8,128)(2,1)S(1)} %copy-done.4, ...), custom_call_target="tpu_custom_call" | custom-call | flops 1409286144 | bytes 786432 | tf_op jit(solution)/shard_map/pallas_call | solution.py:183
  52.1 3.7 %shard_map.94.refs_4_ = f32[8,256]{1,0:T(8,128)S(1)} custom-call(bf16[768,7168]{1,0:T(8,128)(2,1)S(1)} %copy-done.1, bf16[768,128]{1,0:T(8,128)(2,1)S(1)} %add_convert_fusion.grad_ref, bf16[8,768]{1,0:T(8,128)(2,1)S(1)} %fusion.3.onehot_ref, bf16[64,3584]{1,0:T(8,128)(2,1)S(1)} %collective-permute-done.1.refs_0_, ...), custom_call_target="tpu_custom_call" | custom-call | flops 1409286144 | bytes 786432 | tf_op jit(solution)/shard_map/pallas_call | solution.py:183
  55.8 1.6 %collective-permute-start.11 = (bf16[64,3584]{1,0:T(8,128)(2,1)S(1)}, bf16[64,3584]{1,0:T(8,128)(2,1)S(1)}, u32[]{:S(2)}, u32[]{:S(2)}) collective-permute-start(bf16[64,3584]{1,0:T(8,128)(2,1)S(1)} %broadcast_select_fusion.refs_2_), channel_id=1, source_target_pairs={{0,16},{16,0},{1,17},{17,1},{2,18},{18,2},{3,19},{19,3},{4,20},{20... | collective-permute-start | bytes 1376264 | tf_op jit(solution)/shard_map/ppermute | solution.py:269
  57.4 4.1 %copy-done.2 = bf16[768,7168]{1,0:T(8,128)(2,1)S(1)} copy-done((bf16[768,7168]{1,0:T(8,128)(2,1)S(1)}, bf16[768,7168]{1,0:T(8,128)(2,1)}, u32[]{:S(2)}) %copy-start.2) | copy-done | bytes 11010072
  61.6 8.1 %shard_map.95.refs_2_ = f32[8,256]{1,0:T(8,128)S(1)} custom-call(bf16[768,7168]{1,0:T(8,128)(2,1)S(1)} %copy-done.2, bf16[768,128]{1,0:T(8,128)(2,1)S(1)} %add_convert_fusion.grad_ref, bf16[8,768]{1,0:T(8,128)(2,1)S(1)} %fusion.3.onehot_ref, bf16[64,3584]{1,0:T(8,128)(2,1)S(1)} %collective-permute-done.7.refs_0_, ...), custom_call_target="tpu_custom_call" | custom-call | flops 2113929216 | bytes 786432 | tf_op jit(solution)/shard_map/pallas_call | solution.py:183
  69.7 2.7 %shard_map.96 = f32[4,8]{1,0:T(4,128)S(1)} custom-call(bf16[768,7168]{1,0:T(8,128)(2,1)S(1)} %copy-done.2, bf16[768,128]{1,0:T(8,128)(2,1)S(1)} %add_convert_fusion.grad_ref, bf16[8,768]{1,0:T(8,128)(2,1)S(1)} %fusion.3.onehot_ref, bf16[64,3584]{1,0:T(8,128)(2,1)S(1)} %collective-permute-done.11.refs_0_, ...), custom_call_target="tpu_custom_call" | custom-call | flops 704643072 | bytes 786432 | tf_op jit(solution)/shard_map/pallas_call | solution.py:183
  73.0 1.3 %collective-permute-start.15 = (f32[4,8]{1,0:T(4,128)S(1)}, f32[4,8]{1,0:T(4,128)S(1)}, u32[]{:S(2)}, u32[]{:S(2)}) collective-permute-start(f32[4,8]{1,0:T(4,128)S(1)} %shard_map.96), channel_id=1, source_target_pairs={{0,3},{1,2},{2,1},{3,0},{4,7},{5,6},{6,5},{7,4},{8,11},{9,10},{10,... | collective-permute-start | bytes 392 | tf_op jit(solution)/shard_map/ppermute | solution.py:45
  74.3 1.8 %collective-permute-done.14 = f32[4,8]{1,0:T(4,128)S(1)} collective-permute-done((f32[4,8]{1,0:T(4,128)S(1)}, f32[4,8]{1,0:T(4,128)S(1)}, u32[]{:S(2)}, u32[]{:S(2)}) %collective-permute-start.14) | collective-permute-done | bytes 160 | tf_op jit(solution)/shard_map/ppermute | solution.py:45
  76.0 2.0 %collective-permute-start.16 = (f32[4,8]{1,0:T(4,128)S(1)}, f32[4,8]{1,0:T(4,128)S(1)}, u32[]{:S(2)}, u32[]{:S(2)}) collective-permute-start(f32[4,8]{1,0:T(4,128)S(1)} %add_add_fusion.1), channel_id=1, source_target_pairs={{0,4},{4,0},{8,12},{12,8},{1,5},{5,1},{9,13},{13,9},{2,6},{6,2},{1... | collective-permute-start | bytes 392 | tf_op jit(solution)/shard_map/ppermute | solution.py:45
  78.0 0.8 collective-permute-start.17
  78.8 1.7 %collective-permute-start.18 = (f32[4,8]{1,0:T(4,128)S(1)}, f32[4,8]{1,0:T(4,128)S(1)}, u32[]{:S(2)}, u32[]{:S(2)}) collective-permute-start(f32[4,8]{1,0:T(4,128)S(1)} %add_add_fusion.1), channel_id=1, source_target_pairs={{0,12},{4,8},{8,4},{12,0},{1,13},{5,9},{9,5},{13,1},{2,14},{6,10},... | collective-permute-start | bytes 392 | tf_op jit(solution)/shard_map/ppermute | solution.py:45
  80.5 2.0 %collective-permute-done.17 = f32[4,8]{1,0:T(4,128)S(1)} collective-permute-done((f32[4,8]{1,0:T(4,128)S(1)}, f32[4,8]{1,0:T(4,128)S(1)}, u32[]{:S(2)}, u32[]{:S(2)}) %collective-permute-start.17) | collective-permute-done | bytes 160 | tf_op jit(solution)/shard_map/ppermute | solution.py:45
  82.5 1.7 %collective-permute-done.18 = f32[4,8]{1,0:T(4,128)S(1)} collective-permute-done((f32[4,8]{1,0:T(4,128)S(1)}, f32[4,8]{1,0:T(4,128)S(1)}, u32[]{:S(2)}, u32[]{:S(2)}) %collective-permute-start.18) | collective-permute-done | bytes 160 | tf_op jit(solution)/shard_map/ppermute | solution.py:45
  (59 shorter events, 3.4 us)
Async XLA Ops:
  0.0 17.6 %copy-start.12 = (s32[768]{0:T(1024)S(1)}, s32[768]{0:T(1024)}, u32[]{:S(2)}) copy-start(s32[768]{0:T(1024)} %param.16) | copy-start | bytes 9220
  0.0 17.6 %copy-start.13 = (s32[8]{0:T(128)S(1)}, s32[8]{0:T(128)}, u32[]{:S(2)}) copy-start(s32[8]{0:T(128)} %param.17) | copy-start | bytes 100
  1.8 14.1 %collective-permute-start.1 = (bf16[64,3584]{1,0:T(8,128)(2,1)}, bf16[64,3584]{1,0:T(8,128)(2,1)S(1)}, u32[]{:S(2)}, u32[]{:S(2)}) collective-permute-start(bf16[64,3584]{1,0:T(8,128)(2,1)} %shard_map.91), channel_id=1, source_target_pairs={{0,4},{4,0},{8,12},{12,8},{1,5},{5,1},{9,13},{13,9},{2,6},{6,2},{1... | collective-permute-start | bytes 1376264 | tf_op jit(solution)/shard_map/ppermute | solution.py:243
  4.9 11.0 %collective-permute-start.2 = (bf16[64,3584]{1,0:T(8,128)(2,1)}, bf16[64,3584]{1,0:T(8,128)(2,1)S(1)}, u32[]{:S(2)}, u32[]{:S(2)}) collective-permute-start(bf16[64,3584]{1,0:T(8,128)(2,1)} %shard_map.91), channel_id=1, source_target_pairs={{4,8},{8,4},{5,9},{9,5},{6,10},{10,6},{7,11},{11,7},{20,24},{24,20... | collective-permute-start | bytes 1376264 | tf_op jit(solution)/shard_map/ppermute | solution.py:244
  5.6 1.2 %copy-start.3 = (bf16[64,7168]{1,0:T(8,128)(2,1)S(1)}, bf16[64,7168]{1,0:T(8,128)(2,1)}, u32[]{:S(2)}) copy-start(bf16[64,7168]{1,0:T(8,128)(2,1)} %refs_0_.1) | copy-start | bytes 2752516
  6.8 1.9 %copy-start.5 = (bf16[768,2048]{1,0:T(8,128)(2,1)S(1)}, bf16[768,2048]{1,0:T(8,128)(2,1)}, u32[]{:S(2)}) copy-start(bf16[768,2048]{1,0:T(8,128)(2,1)} %grads_ref.1) | copy-start | bytes 9437188
  8.7 1.5 %copy-start.6 = (bf16[7168,128]{1,0:T(8,128)(2,1)S(1)}, bf16[7168,128]{1,0:T(8,128)(2,1)}, u32[]{:S(2)}) copy-start(bf16[7168,128]{1,0:T(8,128)(2,1)} %in_query_ref.1) | copy-start | bytes 5505028
  10.2 1.0 %copy-start.7 = (bf16[128,2048]{1,0:T(8,128)(2,1)S(1)}, bf16[128,2048]{1,0:T(8,128)(2,1)}, u32[]{:S(2)}) copy-start(bf16[128,2048]{1,0:T(8,128)(2,1)} %out_ref.1) | copy-start | bytes 1572868
  14.2 21.7 %copy-start.11 = (bf16[64,128]{1,0:T(8,128)(2,1)S(1)}, bf16[64,128]{1,0:T(8,128)(2,1)}, u32[]{:S(2)}) copy-start(bf16[64,128]{1,0:T(8,128)(2,1)} %param.13) | copy-start | bytes 49156
  14.2 29.3 %copy-start.4 = (bf16[64,7168]{1,0:T(8,128)(2,1)S(1)}, bf16[64,7168]{1,0:T(8,128)(2,1)}, u32[]{:S(2)}) copy-start(bf16[64,7168]{1,0:T(8,128)(2,1)} %refs_0_.1) | copy-start | bytes 2752516
  14.3 1.6 %collective-permute-start = (bf16[1152,128]{1,0:T(8,128)(2,1)S(1)}, bf16[1152,128]{1,0:T(8,128)(2,1)S(1)}, u32[]{:S(2)}, u32[]{:S(2)}) collective-permute-start(bf16[1152,128]{1,0:T(8,128)(2,1)S(1)} %pad_maximum_fusion), channel_id=1, source_target_pairs={{0,1},{1,0},{2,3},{3,2},{4,5},{5,4},{6,7},{7,6},{8,9},{9,8},{10,11... | collective-permute-start | bytes 884744 | tf_op jit(solution)/shard_map/ppermute | solution.py:248
  16.0 25.7 %copy-start.9 = (bf16[64,3584]{1,0:T(8,128)(2,1)}, bf16[64,3584]{1,0:T(8,128)(2,1)S(1)}, u32[]{:S(2)}) copy-start(bf16[64,3584]{1,0:T(8,128)(2,1)S(1)} %collective-permute-done.2) | copy-start | bytes 1376260
  16.1 9.1 %collective-permute-start.3 = (bf16[1152,128]{1,0:T(8,128)(2,1)S(1)}, bf16[1152,128]{1,0:T(8,128)(2,1)S(1)}, u32[]{:S(2)}, u32[]{:S(2)}) collective-permute-start(bf16[1152,128]{1,0:T(8,128)(2,1)S(1)} %pad_maximum_fusion.1), channel_id=1, source_target_pairs={{0,2},{2,0},{1,3},{3,1},{4,6},{6,4},{5,7},{7,5},{8,10},{10,8},{9,1... | collective-permute-start | bytes 884744 | tf_op jit(solution)/shard_map/ppermute | solution.py:250
  17.7 7.6 %collective-permute-start.4 = (bf16[64,3584]{1,0:T(8,128)(2,1)S(1)}, bf16[64,3584]{1,0:T(8,128)(2,1)S(1)}, u32[]{:S(2)}, u32[]{:S(2)}) collective-permute-start(bf16[64,3584]{1,0:T(8,128)(2,1)S(1)} %collective-permute-done.1.refs_0_), channel_id=1, source_target_pairs={{4,8},{8,4},{5,9},{9,5},{6,10},{10,6},{7,11},{11,7},{20,24},{24,20... | collective-permute-start | bytes 1376264 | tf_op jit(solution)/shard_map/ppermute | solution.py:254
  18.4 17.4 %collective-permute-start.6 = (bf16[64,3584]{1,0:T(8,128)(2,1)S(1)}, bf16[64,3584]{1,0:T(8,128)(2,1)S(1)}, u32[]{:S(2)}, u32[]{:S(2)}) collective-permute-start(bf16[64,3584]{1,0:T(8,128)(2,1)S(1)} %collective-permute-done.2), channel_id=1, source_target_pairs={{4,0},{8,12},{5,1},{9,13},{6,2},{10,14},{7,3},{11,15},{20,16},{24,... | collective-permute-start | bytes 1376264 | tf_op jit(solution)/shard_map/ppermute | solution.py:255
  19.7 20.6 %collective-permute-start.7 = (bf16[64,3584]{1,0:T(8,128)(2,1)S(1)}, bf16[64,3584]{1,0:T(8,128)(2,1)S(1)}, u32[]{:S(2)}, u32[]{:S(2)}) collective-permute-start(bf16[64,3584]{1,0:T(8,128)(2,1)S(1)} %collective-permute-done.1.refs_0_), channel_id=1, source_target_pairs={{0,16},{16,0},{1,17},{17,1},{2,18},{18,2},{3,19},{19,3},{4,20},{20... | collective-permute-start | bytes 1376264 | tf_op jit(solution)/shard_map/ppermute | solution.py:256
  35.9 7.4 %collective-permute-start.10 = (bf16[64,256]{1,0:T(8,128)(2,1)S(1)}, bf16[64,256]{1,0:T(8,128)(2,1)S(1)}, u32[]{:S(2)}, u32[]{:S(2)}) collective-permute-start(bf16[64,256]{1,0:T(8,128)(2,1)S(1)} %constant_dynamic-update-slice_fusion.refs_1_), channel_id=1, source_target_pairs={{0,12},{4,8},{8,4},{12,0},{1,13},{5,9},{9,5},{13,1},{2,14},{6,10},... | collective-permute-start | bytes 98312 | tf_op jit(solution)/shard_map/ppermute | solution.py:45
  38.6 4.8 %collective-permute-start.8 = (bf16[64,256]{1,0:T(8,128)(2,1)S(1)}, bf16[64,256]{1,0:T(8,128)(2,1)S(1)}, u32[]{:S(2)}, u32[]{:S(2)}) collective-permute-start(bf16[64,256]{1,0:T(8,128)(2,1)S(1)} %constant_dynamic-update-slice_fusion.refs_1_), channel_id=1, source_target_pairs={{0,4},{4,0},{8,12},{12,8},{1,5},{5,1},{9,13},{13,9},{2,6},{6,2},{1... | collective-permute-start | bytes 98312 | tf_op jit(solution)/shard_map/ppermute | solution.py:45
  38.6 4.9 %collective-permute-start.9 = (bf16[64,256]{1,0:T(8,128)(2,1)S(1)}, bf16[64,256]{1,0:T(8,128)(2,1)S(1)}, u32[]{:S(2)}, u32[]{:S(2)}) collective-permute-start(bf16[64,256]{1,0:T(8,128)(2,1)S(1)} %constant_dynamic-update-slice_fusion.refs_1_), channel_id=1, source_target_pairs={{0,8},{4,12},{8,0},{12,4},{1,9},{5,13},{9,1},{13,5},{2,10},{6,14},... | collective-permute-start | bytes 98312 | tf_op jit(solution)/shard_map/ppermute | solution.py:45
  40.4 15.4 %collective-permute-start.5 = (bf16[64,3584]{1,0:T(8,128)(2,1)S(1)}, bf16[64,3584]{1,0:T(8,128)(2,1)S(1)}, u32[]{:S(2)}, u32[]{:S(2)}) collective-permute-start(bf16[64,3584]{1,0:T(8,128)(2,1)S(1)} %collective-permute-done.4), channel_id=1, source_target_pairs={{4,0},{8,12},{5,1},{9,13},{6,2},{10,14},{7,3},{11,15},{20,16},{24,... | collective-permute-start | bytes 1376264 | tf_op jit(solution)/shard_map/ppermute | solution.py:263
  41.7 15.7 %collective-permute-start.12 = (bf16[64,3584]{1,0:T(8,128)(2,1)S(1)}, bf16[64,3584]{1,0:T(8,128)(2,1)S(1)}, u32[]{:S(2)}, u32[]{:S(2)}) collective-permute-start(bf16[64,3584]{1,0:T(8,128)(2,1)S(1)} %broadcast_select_fusion.1.refs_1_), channel_id=1, source_target_pairs={{0,16},{16,0},{1,17},{17,1},{2,18},{18,2},{3,19},{19,3},{4,20},{20... | collective-permute-start | bytes 1376264 | tf_op jit(solution)/shard_map/ppermute | solution.py:262
  43.5 4.1 %copy-start = (bf16[768,7168]{1,0:T(8,128)(2,1)S(1)}, bf16[768,7168]{1,0:T(8,128)(2,1)}, u32[]{:S(2)}) copy-start(bf16[768,7168]{1,0:T(8,128)(2,1)} %acts_ref.7) | copy-start | bytes 33030148
  47.6 4.4 %copy-start.1 = (bf16[768,7168]{1,0:T(8,128)(2,1)S(1)}, bf16[768,7168]{1,0:T(8,128)(2,1)}, u32[]{:S(2)}) copy-start(bf16[768,7168]{1,0:T(8,128)(2,1)} %acts_ref.7) | copy-start | bytes 33030148
  52.0 3.7 %copy-start.10 = (bf16[64,3584]{1,0:T(8,128)(2,1)S(1)}, bf16[64,3584]{1,0:T(8,128)(2,1)}, u32[]{:S(2)}) copy-start(bf16[64,3584]{1,0:T(8,128)(2,1)} %copy-done.9) | copy-start | bytes 1376260
  55.8 13.8 %collective-permute-start.11 = (bf16[64,3584]{1,0:T(8,128)(2,1)S(1)}, bf16[64,3584]{1,0:T(8,128)(2,1)S(1)}, u32[]{:S(2)}, u32[]{:S(2)}) collective-permute-start(bf16[64,3584]{1,0:T(8,128)(2,1)S(1)} %broadcast_select_fusion.refs_2_), channel_id=1, source_target_pairs={{0,16},{16,0},{1,17},{17,1},{2,18},{18,2},{3,19},{19,3},{4,20},{20... | collective-permute-start | bytes 1376264 | tf_op jit(solution)/shard_map/ppermute | solution.py:269
  57.4 4.1 %copy-start.2 = (bf16[768,7168]{1,0:T(8,128)(2,1)S(1)}, bf16[768,7168]{1,0:T(8,128)(2,1)}, u32[]{:S(2)}) copy-start(bf16[768,7168]{1,0:T(8,128)(2,1)} %acts_ref.7) | copy-start | bytes 33030148
  72.4 1.9 %collective-permute-start.13 = (f32[4,8]{1,0:T(4,128)S(1)}, f32[4,8]{1,0:T(4,128)S(1)}, u32[]{:S(2)}, u32[]{:S(2)}) collective-permute-start(f32[4,8]{1,0:T(4,128)S(1)} %shard_map.96), channel_id=1, source_target_pairs={{0,1},{1,0},{2,3},{3,2},{4,5},{5,4},{6,7},{7,6},{8,9},{9,8},{10,11... | collective-permute-start | bytes 392 | tf_op jit(solution)/shard_map/ppermute | solution.py:45
  72.4 3.6 %collective-permute-start.14 = (f32[4,8]{1,0:T(4,128)S(1)}, f32[4,8]{1,0:T(4,128)S(1)}, u32[]{:S(2)}, u32[]{:S(2)}) collective-permute-start(f32[4,8]{1,0:T(4,128)S(1)} %shard_map.96), channel_id=1, source_target_pairs={{0,2},{1,3},{2,0},{3,1},{4,6},{5,7},{6,4},{7,5},{8,10},{9,11},{10,... | collective-permute-start | bytes 392 | tf_op jit(solution)/shard_map/ppermute | solution.py:45
  73.0 3.1 %collective-permute-start.15 = (f32[4,8]{1,0:T(4,128)S(1)}, f32[4,8]{1,0:T(4,128)S(1)}, u32[]{:S(2)}, u32[]{:S(2)}) collective-permute-start(f32[4,8]{1,0:T(4,128)S(1)} %shard_map.96), channel_id=1, source_target_pairs={{0,3},{1,2},{2,1},{3,0},{4,7},{5,6},{6,5},{7,4},{8,11},{9,10},{10,... | collective-permute-start | bytes 392 | tf_op jit(solution)/shard_map/ppermute | solution.py:45
  76.0 4.5 %collective-permute-start.16 = (f32[4,8]{1,0:T(4,128)S(1)}, f32[4,8]{1,0:T(4,128)S(1)}, u32[]{:S(2)}, u32[]{:S(2)}) collective-permute-start(f32[4,8]{1,0:T(4,128)S(1)} %add_add_fusion.1), channel_id=1, source_target_pairs={{0,4},{4,0},{8,12},{12,8},{1,5},{5,1},{9,13},{13,9},{2,6},{6,2},{1... | collective-permute-start | bytes 392 | tf_op jit(solution)/shard_map/ppermute | solution.py:45
  78.0 4.5 %collective-permute-start.17 = (f32[4,8]{1,0:T(4,128)S(1)}, f32[4,8]{1,0:T(4,128)S(1)}, u32[]{:S(2)}, u32[]{:S(2)}) collective-permute-start(f32[4,8]{1,0:T(4,128)S(1)} %add_add_fusion.1), channel_id=1, source_target_pairs={{0,8},{4,12},{8,0},{12,4},{1,9},{5,13},{9,1},{13,5},{2,10},{6,14},... | collective-permute-start | bytes 392 | tf_op jit(solution)/shard_map/ppermute | solution.py:45
  78.8 5.4 %collective-permute-start.18 = (f32[4,8]{1,0:T(4,128)S(1)}, f32[4,8]{1,0:T(4,128)S(1)}, u32[]{:S(2)}, u32[]{:S(2)}) collective-permute-start(f32[4,8]{1,0:T(4,128)S(1)} %add_add_fusion.1), channel_id=1, source_target_pairs={{0,12},{4,8},{8,4},{12,0},{1,13},{5,9},{9,5},{13,1},{2,14},{6,10},... | collective-permute-start | bytes 392 | tf_op jit(solution)/shard_map/ppermute | solution.py:45
  (1 other events, 1.0 us)

commit v3 on v2

v3 whole, which is shorter than its diff:
```python
import functools

import jax
import jax.numpy as jnp
from jax import lax
from jax.experimental import pallas as pl
from jax.experimental.pallas import tpu as pltpu
from jax.sharding import PartitionSpec as P

R = 32
LANES = 128
BLOCK = 256
VMEM_LIMIT = 16 * 1024 * 1024
AXES = ("groups", "blk", "eig", "rep")


damping = 0.05


def contract_last(left_side, right_side, precision=None):
    return lax.dot_general(
        left_side,
        right_side,
        (((1,), (1,)), ((), ())),
        precision=precision,
        preferred_element_type=jnp.float32,
    )


def swap_sum(value, axis, send_as):
    size = lax.axis_size(axis)
    if size & (size - 1):
        return lax.psum(value, axis)
    step = 1
    while step < size:
        pairs = [(i, i ^ step) for i in range(size)]
        value = value + lax.ppermute(value.astype(send_as), axis, pairs).astype(jnp.float32)
        step *= 2
    return value


def by_distance(value, axis="blk"):
    size = lax.axis_size(axis)
    return [value] + [
        lax.ppermute(value, axis, [(i, i ^ k) for i in range(size)]) for k in range(1, size)
    ]


def held(value, *until):
    return lax.optimization_barrier((value, *until))[0]


def in_hbm(value):
    return pltpu.with_memory_space_constraint(value, pltpu.HBM)


def parts_kernel(*refs):
    sources, half_ref, sum_ref, copied = refs[:5], refs[5], refs[6], refs[-1]
    held_refs = out_ref, out_query_ref, in_ref, in_query_ref, grads_ref = refs[7:-1]
    columns = half_ref.shape[1]
    begin = pl.multiple_of(lax.axis_index("groups") * columns, LANES)
    moves = [(sources[2].at[:, pl.ds(begin, columns)], half_ref), *zip(sources, held_refs)]
    copies = [
        pltpu.make_async_copy(source, target, copied.at[place])
        for place, (source, target) in enumerate(moves)
    ]
    for copy in copies:
        copy.start()
    rows, width = in_ref.shape[0], out_ref.shape[0]
    copies[1].wait()
    copies[2].wait()
    sum_ref[rows : rows + width] = jnp.dot(
        out_ref[...], out_query_ref[...], preferred_element_type=jnp.float32
    )
    copies[3].wait()
    copies[4].wait()
    sum_ref[:rows] = jnp.dot(in_ref[...], in_query_ref[...], preferred_element_type=jnp.float32)
    copies[5].wait()

    @pl.loop(0, grads_ref.shape[0] // BLOCK)
    def _(step):
        start = pl.multiple_of(step * BLOCK, LANES)
        sum_ref[pl.ds(rows + width + start, BLOCK), :] = contract_last(
            grads_ref[pl.ds(start, BLOCK), :], out_ref[...]
        )

    copies[0].wait()


def small_parts(basis_in, query_in, basis_out, query_out, out_grads):
    rows, features = basis_in.shape
    high = rows + basis_out.shape[0] + out_grads.shape[0]
    sources = (basis_out, query_out, basis_in, query_in, out_grads)
    return pl.pallas_call(
        parts_kernel,
        in_specs=[pl.BlockSpec(memory_space=pl.ANY)] * len(sources),
        out_shape=[
            pltpu.VMEM((rows, features // 2), basis_in.dtype),
            jax.ShapeDtypeStruct((high, query_in.shape[1]), jnp.float32),
        ],
        scratch_shapes=[pltpu.VMEM(source.shape, source.dtype) for source in sources]
        + [pltpu.SemaphoreType.DMA((len(sources) + 1,))],
        compiler_params=pltpu.CompilerParams(vmem_limit_bytes=VMEM_LIMIT),
    )(*[in_hbm(source) for source in sources])


def weigh(query_count, packs, out_query, weighted_ref):
    rows, pairs = packs[0].shape[0], out_query.shape[1]
    query_of = lax.broadcasted_iota(jnp.int32, (rows, pairs), 1) // R
    for slot, pack_ref in enumerate(packs):
        in_query = pack_ref[:, :pairs].astype(jnp.float32)
        inverse = 1.0 / (pack_ref[:, pairs:].astype(jnp.float32) + damping)
        for query in range(query_count):
            own = jnp.where(query_of == query, in_query, 0.0).astype(jnp.bfloat16)
            outer_sum = contract_last(own, out_query)
            weighted_ref[slot, pl.ds(query * rows, rows), :] = (outer_sum * inverse).astype(
                jnp.bfloat16
            )


def project(acts_ref, start, piece, group, first=0):
    rows, width = piece.shape
    columns = slice(None)
    if width < acts_ref.shape[1]:
        half = acts_ref.shape[1] // 2
        columns = pl.ds(pl.multiple_of(group * half + first, LANES), width)
    repeated = jnp.concatenate([piece[...]] * (LANES // rows), axis=0)
    return contract_last(acts_ref[pl.ds(start, BLOCK), columns], repeated)


def mix(start, projected, weights, grad_ref, onehot_ref):
    mixed = contract_last(grad_ref[pl.ds(start, BLOCK), :], weights)
    product = jnp.concatenate([projected] * (mixed.shape[1] // LANES), axis=1) * mixed
    high = product.astype(jnp.bfloat16)
    low = (product - high.astype(jnp.float32)).astype(jnp.bfloat16)
    onehot = onehot_ref[:, pl.ds(start, BLOCK)]
    return jnp.dot(onehot, high, preferred_element_type=jnp.float32) + jnp.dot(
        onehot, low, preferred_element_type=jnp.float32
    )


def blocks(acts_or_projected, body, initial):
    def step(index, carry):
        return body(pl.multiple_of(index * BLOCK, LANES), carry)

    return lax.fori_loop(0, acts_or_projected.shape[0] // BLOCK, step, initial)


def first_kernel(source_ref, own_ref, acts_ref, total_ref, copied):
    copies = [
        pltpu.make_async_copy(
            source_ref.at[pl.ds(start, BLOCK)], acts_ref.at[pl.ds(start, BLOCK)], copied.at[place]
        )
        for place, start in enumerate(range(0, acts_ref.shape[0], BLOCK))
    ]
    for copy in copies:
        copy.start()
    for place, copy in enumerate(copies):
        copy.wait()
        start = place * BLOCK
        total_ref[pl.ds(start, BLOCK), :] = project(acts_ref, start, own_ref, 0)


def weight_kernel(query_count, *refs):
    packs, refs = refs[:4], refs[4:]
    out_query_ref, grad_ref, onehot_ref, total_ref, sums_ref, weights_ref = refs
    weigh(query_count, packs, out_query_ref[...], weights_ref)

    def body(start, sums):
        total = total_ref[pl.ds(start, BLOCK), :]
        return sums + mix(start, total, weights_ref[0], grad_ref, onehot_ref)

    sums_ref[...] = blocks(total_ref, body, jnp.zeros(sums_ref.shape, jnp.float32))


def slot_kernel(
    slot, acts_ref, mine_ref, theirs_ref, weights_ref, grad_ref, onehot_ref, before_ref, sums_ref
):
    group = lax.axis_index("groups")

    def body(start, sums):
        total = project(acts_ref, start, mine_ref, group)
        total = total + project(acts_ref, start, theirs_ref, 1 - group)
        return sums + mix(start, total, weights_ref[slot], grad_ref, onehot_ref)

    sums_ref[...] = blocks(acts_ref, body, before_ref[...])


def mine_kernel(acts_ref, mine_ref, total_ref):
    group = lax.axis_index("groups")

    def body(start, carry):
        total_ref[pl.ds(start, BLOCK), :] = project(acts_ref, start, mine_ref, group)
        return carry

    blocks(acts_ref, body, 0)


def last_kernel(
    acts_ref, left_ref, right_ref, total_ref, weights_ref, grad_ref, onehot_ref, before_ref, out_ref
):
    other = 1 - lax.axis_index("groups")

    def body(start, sums):
        total = total_ref[pl.ds(start, BLOCK), :]
        total = total + project(acts_ref, start, left_ref, other)
        total = total + project(acts_ref, start, right_ref, other, left_ref.shape[1])
        return sums + mix(start, total, weights_ref[3], grad_ref, onehot_ref)

    sums = blocks(acts_ref, body, before_ref[...])
    queries, width = out_ref.shape[0], sums.shape[1]
    query_of = lax.broadcasted_iota(jnp.int32, (queries, width), 1) // (width // queries)
    chosen = query_of == lax.broadcasted_iota(jnp.int32, (queries, width), 0)
    out_ref[...] = contract_last(chosen.astype(jnp.float32), sums, precision=lax.Precision.HIGHEST)


def call(kernel, out_shape, *operands, **options):
    return pl.pallas_call(
        kernel,
        out_shape=out_shape,
        compiler_params=pltpu.CompilerParams(vmem_limit_bytes=VMEM_LIMIT),
        cost_estimate=pl.CostEstimate(flops=1, bytes_accessed=1, transcendentals=0),
        **options,
    )(*operands)


def precondition(in_rows, eig_rows, out_query):
    row_count = in_rows.shape[0]
    basis_width = out_query.shape[0]
    query_count = out_query.shape[1] // R
    outer_sum = jnp.einsum(
        "jqr,iqr->qji",
        in_rows.reshape(row_count, query_count, R),
        out_query.reshape(basis_width, query_count, R),
        preferred_element_type=jnp.float32,
    )
    inverse = 1.0 / (eig_rows.astype(jnp.float32) + damping)
    return (outer_sum * inverse[None, :, :]).astype(jnp.bfloat16)


def plain_scores(acts, basis_in, pack, out_query, grad_proj, onehot):
    pack = lax.all_gather(pack, "blk", axis=0, tiled=True)
    piece = lax.all_gather(basis_in, "blk", axis=0, tiled=True)
    pairs = out_query.shape[1]
    weighted = precondition(pack[:, :pairs], pack[:, pairs:], out_query)
    projected = contract_last(acts, piece)
    per_token = jnp.stack(
        [jnp.sum(projected * contract_last(grad_proj, slab), axis=1) for slab in weighted]
    )
    return contract_last(per_token, onehot, precision=lax.Precision.HIGHEST)


def to_send(part, split):
    high = lax.reduce_precision(part[:split], 8, 7)
    low = part[:split] - high
    return jnp.concatenate([high, low, part[split:]], axis=0).astype(jnp.bfloat16)


def add_sent(part, other, split):
    high, low, rest = other[:split], other[split : 2 * split], other[2 * split :]
    first = part[:split] + high.astype(jnp.float32) + low.astype(jnp.float32)
    return jnp.concatenate([first, part[split:] + rest.astype(jnp.float32)], axis=0)


def stepped_scores(
    acts, out_grads, basis_in, basis_out, eigvals, query_out, query_in, onehot
):
    rows, width = basis_in.shape[0], basis_out.shape[0]
    tokens, seq_count = acts.shape[0], onehot.shape[0]
    query_count = query_in.shape[1] // R
    pair = [(0, 1), (1, 0)]

    def along(value, distance):
        return lax.ppermute(value, "blk", [(i, i ^ distance) for i in range(4)])

    def swapped(value):
        return lax.ppermute(value, "groups", pair)

    half, part = small_parts(basis_in, query_in, basis_out, query_out, out_grads)
    mine_1 = along(half, 1)
    mine_2 = along(half, 2)

    split = rows + width
    other = lax.ppermute(to_send(part, split), "rep", pair)
    part = add_sent(part, held(other, mine_1), split)
    other = lax.ppermute(to_send(part, split), "eig", pair)
    theirs_1 = swapped(mine_1)
    acts, total = call(
        first_kernel,
        [pltpu.VMEM(acts.shape, acts.dtype), jax.ShapeDtypeStruct((tokens, LANES), jnp.float32)],
        in_hbm(held(acts, mine_1)),
        basis_in,
        in_specs=[pl.BlockSpec(memory_space=pl.ANY), pl.BlockSpec(memory_space=pltpu.VMEM)],
        scratch_shapes=[pltpu.SemaphoreType.DMA((tokens // BLOCK,))],
    )
    mine_2 = held(mine_2, theirs_1, other, total)
    part = add_sent(part, held(other, mine_2), split).astype(jnp.bfloat16)
    in_query, out_query, grad_proj = part[:rows], part[rows:split], part[split:]
    packs = by_distance(jnp.concatenate([in_query, eigvals], axis=1))

    theirs_2 = swapped(mine_2)
    mine_3 = along(mine_2, 1)
    sums_shape = jax.ShapeDtypeStruct((seq_count, query_count * rows), jnp.float32)
    weights_shape = jax.ShapeDtypeStruct((4, query_count * rows, width), jnp.bfloat16)
    sums, weights = call(
        functools.partial(weight_kernel, query_count),
        [sums_shape, weights_shape],
        *packs, out_query, grad_proj, onehot, total,
    )
    fixed = (weights, grad_proj, onehot)
    sums = call(
        functools.partial(slot_kernel, 1), sums_shape, acts, mine_1, theirs_1, *fixed, sums
    )

    middle = mine_3.shape[1] // 2
    left_3 = along(held(theirs_2, sums)[:, :middle], 1)
    right_3 = swapped(held(mine_3, sums)[:, middle:])
    sums = call(
        functools.partial(slot_kernel, 2), sums_shape, acts, mine_2, theirs_2, *fixed, sums
    )
    total = call(mine_kernel, jax.ShapeDtypeStruct((tokens, LANES), jnp.float32), acts, mine_3)
    scores = call(
        last_kernel,
        jax.ShapeDtypeStruct((query_count, seq_count), jnp.float32),
        acts, left_3, right_3, total, *fixed, sums,
    )
    return swap_sum(sum(by_distance(scores, ("eig", "rep"))), "blk", jnp.float32)


def plain_path(acts, out_grads, basis_in, basis_out, eigvals, query_out, query_in, onehot):
    def whole_sum(part, send_as):
        return swap_sum(swap_sum(part, "rep", jnp.float32), "eig", send_as).astype(jnp.bfloat16)

    in_query = whole_sum(jnp.dot(basis_in, query_in, preferred_element_type=jnp.float32), jnp.float32)
    out_query = whole_sum(
        jnp.dot(basis_out, query_out, preferred_element_type=jnp.float32), jnp.float32
    )
    grad_proj = whole_sum(contract_last(out_grads, basis_out), jnp.bfloat16)
    pack = jnp.concatenate([in_query, eigvals], axis=1)
    scores = plain_scores(acts, basis_in, pack, out_query, grad_proj, onehot.astype(jnp.float32))
    return lax.psum(scores, ("blk", "eig", "rep"))


def on_device(acts, out_grads, basis_in, basis_out, eigvals, query_out, query_in, seq_ids, owner):
    rows, features = basis_in.shape
    pairs = query_in.shape[1]
    seq_count = owner.shape[0]
    labels = jnp.arange(seq_count, dtype=jnp.int32)
    column_of = jnp.sum(jnp.where(seq_ids[None, :] == labels[:, None], owner[:, None], 0), axis=0)
    onehot = (labels[:, None] == column_of[None, :]).astype(jnp.bfloat16)
    stepped = (
        all(lax.axis_size(axis) == size for axis, size in zip(AXES, (2, 4, 2, 2)))
        and LANES % rows == 0
        and (pairs // R * rows) % LANES == 0
        and features % (4 * LANES) == 0
        and acts.shape[0] % BLOCK == 0
        and pairs == basis_out.shape[0] == LANES
    )
    way = stepped_scores if stepped else plain_path
    scores = way(acts, out_grads, basis_in, basis_out, eigvals, query_out, query_in, onehot)
    own_queries = pairs // R // lax.axis_size(("eig", "rep"))
    own_columns = seq_count // lax.axis_size("blk")
    return lax.dynamic_slice(
        scores,
        (lax.axis_index(("eig", "rep")) * own_queries, lax.axis_index("blk") * own_columns),
        (own_queries, own_columns),
    )


def solution(mesh):
    return jax.shard_map(
        on_device,
        mesh=mesh,
        in_specs=(
            P(("groups", "blk"), ("eig", "rep")),
            P(("groups", "blk"), ("eig", "rep")),
            P("blk", ("eig", "rep")),
            P(None, ("eig", "rep")),
            P("blk", None),
            P(("eig", "rep"), "groups"),
            P(("eig", "rep"), "groups"),
            P(("groups", "blk")),
            P("groups"),
        ),
        out_specs=P(("groups", "eig", "rep"), "blk"),
        check_vma=False,
    )
```

time: 85.2 us -> 89.3 us (1.048)
  waiting for transfers between devices: 21.6 us -> 30.8 us
  local copies, waits for them, and re-layouts: 15.6 us -> 10.2 us
  Pallas kernels: 22.7 us -> 26 us
  starting transfers between devices: 24.2 us -> 20.9 us
    ppermute x8 -> x9, waiting for transfers between devices: 10.6 us -> 21.2 us  [the longest x4 16.4 us: along(): return lax.ppermute(value, 'blk', [(i, i ^ distance) for i in range(4)])]
    unnamed x29 -> x8, local copies, waits for them, and re-layouts: 14.9 us -> 9.53 us
    ppermute x9 -> x6, starting transfers between devices: 10.8 us -> 6.33 us  [by_distance(): lax.ppermute(value, axis, [(i, i ^ k) for i in range(size)])]
    ppermute x9 -> x6, waiting for transfers between devices: 5.63 us -> 9.53 us  [by_distance(): lax.ppermute(value, axis, [(i, i ^ k) for i in range(size)])]
    ppermute x1, waiting for transfers between devices: 3.85 us -> 0.01 us  [stepped_scores(): other = lax.ppermute(to_send(part, split), 'eig', pair)]
    pallas_call x6 -> x7, Pallas kernels: 22.7 us -> 26 us  [the longest x6 21.4 us: call(): pl.pallas_call(kernel, out_shape=out_shape, compiler_params=pltpu.Compile...]
    ppermute x1, waiting for transfers between devices: 1.56 us -> 0.01 us  [stepped_scores(): other = lax.ppermute(to_send(part, split), 'rep', pair)]
    ppermute x8 -> x9, starting transfers between devices: 11.8 us -> 13 us  [the longest x4 6.78 us: along(): return lax.ppermute(value, 'blk', [(i, i ^ distance) for i in range(4)])]
  transfers between devices with their start and end apart: 19 -> 17, of which waited for: 7 -> 6; matrix products, arithmetic and copies ran while one was open for 0% -> 1% of each run, Pallas kernels for 21% -> 21%
where the time goes in v3:
time: 89.3 us; the launch traced here: 89.1 us
  waiting for transfers between devices  30.8 us (34%)
  Pallas kernels  26 us (29%)
  starting transfers between devices  20.9 us (23%)
  local copies, waits for them, and re-layouts  10.2 us (11%)
  other arithmetic  1.06 us (1%)
    pallas_call x6, Pallas kernels, call(): pl.pallas_call(kernel, out_shape=out_shape, compiler_params=pltpu.Compile...  21.4 us
    ppermute x4, waiting for transfers between devices, along(): return lax.ppermute(value, 'blk', [(i, i ^ distance) for i in range(4)])  16.4 us
    unnamed x8, local copies, waits for them, and re-layouts  9.53 us
    ppermute x6, waiting for transfers between devices, by_distance(): lax.ppermute(value, axis, [(i, i ^ k) for i in range(size)])  9.53 us
    ppermute x4, starting transfers between devices, along(): return lax.ppermute(value, 'blk', [(i, i ^ distance) for i in range(4)])  6.78 us
    ppermute x6, starting transfers between devices, by_distance(): lax.ppermute(value, axis, [(i, i ^ k) for i in range(size)])  6.33 us
    ppermute x2, waiting for transfers between devices, swap_sum(): lax.ppermute(value.astype(send_as), axis, pairs).astype(jnp.float32)  4.86 us
    pallas_call x1, Pallas kernels, small_parts(): pl.pallas_call(parts_kernel, in_specs=[pl.BlockSpec(memory_space=pl.ANY)]...  4.56 us
  transfers between devices with their start and end apart: 17, of which 6 were waited for; matrix products, arithmetic and copies ran while one was open for 1% of the time, Pallas kernels for 21%

profile of v3, /device:TPU:0, one launch (start us, length us, event | category | flops | bytes accessed | tf_op | source)
XLA Modules:
  0.0 89.1 jit_solution(6568623400160393354)
XLA Ops:
  0.0 4.6 %shard_map.91 = (bf16[64,3584]{1,0:T(8,128)(2,1)S(1)}, f32[960,128]{1,0:T(8,128)S(1)}) custom-call(bf16[128,2048]{1,0:T(8,128)(2,1)} %refs_0_.1, bf16[2048,128]{1,0:T(8,128)(2,1)} %refs_1_.1, bf16[64,7168]{1,0:T(8,128)(2,1)} %own_ref.1, bf16[7168,128]{1,0:T(8,128)(2,1)} %refs_3_.1, bf16[768,2048]{1,0:T(8,128)(2,1)} %refs_4_.1), custom_call_target="tpu_custom_call" | custom-call | tf_op jit(solution)/shard_map/pallas_call | solution.py:94
  4.6 3.1 %collective-permute-start = (bf16[64,3584]{1,0:T(8,128)(2,1)S(1)}, bf16[64,3584]{1,0:T(8,128)(2,1)S(1)}, u32[]{:S(2)}, u32[]{:S(2)}) collective-permute-start(bf16[64,3584]{1,0:T(8,128)(2,1)S(1)} %get-tuple-element.17), channel_id=1, source_target_pairs={{0,4},{4,0},{8,12},{12,8},{1,5},{5,1},{9,13},{13,9},{2,6},{6,2},{1... | collective-permute-start | bytes 1376264 | tf_op jit(solution)/shard_map/ppermute | solution.py:274
  7.8 2.7 %collective-permute-start.1 = (bf16[64,3584]{1,0:T(8,128)(2,1)S(1)}, bf16[64,3584]{1,0:T(8,128)(2,1)S(1)}, u32[]{:S(2)}, u32[]{:S(2)}) collective-permute-start(bf16[64,3584]{1,0:T(8,128)(2,1)S(1)} %get-tuple-element.17), channel_id=1, source_target_pairs={{0,8},{4,12},{8,0},{12,4},{1,9},{5,13},{9,1},{13,5},{2,10},{6,14},... | collective-permute-start | bytes 1376264 | tf_op jit(solution)/shard_map/ppermute | solution.py:274
  10.5 16.3 %collective-permute-done.mine_ref = bf16[64,3584]{1,0:T(8,128)(2,1)S(1)} collective-permute-done((bf16[64,3584]{1,0:T(8,128)(2,1)S(1)}, bf16[64,3584]{1,0:T(8,128)(2,1)S(1)}, u32[]{:S(2)}, u32[]{:S(2)}) %collective-permute-start) | collective-permute-done | bytes 458784 | tf_op jit(solution)/shard_map/ppermute | solution.py:274
  26.9 1.7 %collective-permute-start.2 = (bf16[64,3584]{1,0:T(8,128)(2,1)S(1)}, bf16[64,3584]{1,0:T(8,128)(2,1)S(1)}, u32[]{:S(2)}, u32[]{:S(2)}) collective-permute-start(bf16[64,3584]{1,0:T(8,128)(2,1)S(1)} %collective-permute-done.mine_ref), channel_id=1, source_target_pairs={{0,16},{16,0},{1,17},{17,1},{2,18},{18,2},{3,19},{19,3},{4,20},{20... | collective-permute-start | bytes 1376264 | tf_op jit(solution)/shard_map/ppermute | solution.py:277
  28.6 1.6 %collective-permute-start.4 = (bf16[1152,128]{1,0:T(8,128)(2,1)S(1)}, bf16[1152,128]{1,0:T(8,128)(2,1)S(1)}, u32[]{:S(2)}, u32[]{:S(2)}) collective-permute-start(bf16[1152,128]{1,0:T(8,128)(2,1)S(1)} %pad_maximum_fusion.1), channel_id=1, source_target_pairs={{0,2},{2,0},{1,3},{3,1},{4,6},{6,4},{5,7},{7,5},{8,10},{10,8},{9,1... | collective-permute-start | bytes 884744 | tf_op jit(solution)/shard_map/ppermute | solution.py:286
  30.2 0.8 select_reduce_fusion
  31.0 1.2 %copy-done.2 = bf16[64,7168]{1,0:T(8,128)(2,1)S(1)} copy-done((bf16[64,7168]{1,0:T(8,128)(2,1)S(1)}, bf16[64,7168]{1,0:T(8,128)(2,1)}, u32[]{:S(2)}) %copy-start.2) | copy-done | bytes 917528
  32.2 7.3 %shard_map.92 = (bf16[768,7168]{1,0:T(8,128)(2,1)S(1)}, f32[768,128]{1,0:T(8,128)S(1)}) custom-call(bf16[768,7168]{1,0:T(8,128)(2,1)} %source_ref, bf16[64,7168]{1,0:T(8,128)(2,1)S(1)} %copy-done.2), custom_call_target="tpu_custom_call" | custom-call | flops 1 | bytes 1 | tf_op jit(solution)/shard_map/pallas_call | solution.py:218
  39.6 0.6 collective-permute-start.5
  40.2 2.5 %collective-permute-start.8 = (bf16[64,256]{1,0:T(8,128)(2,1)S(1)}, bf16[64,256]{1,0:T(8,128)(2,1)S(1)}, u32[]{:S(2)}, u32[]{:S(2)}) collective-permute-start(bf16[64,256]{1,0:T(8,128)(2,1)S(1)} %pad_maximum_fusion.2.refs_0_), channel_id=1, source_target_pairs={{0,12},{4,8},{8,4},{12,0},{1,13},{5,9},{9,5},{13,1},{2,14},{6,10},... | collective-permute-start | bytes 98312 | tf_op jit(solution)/shard_map/ppermute | solution.py:45
  42.7 0.9 %collective-permute-start.7 = (bf16[64,256]{1,0:T(8,128)(2,1)S(1)}, bf16[64,256]{1,0:T(8,128)(2,1)S(1)}, u32[]{:S(2)}, u32[]{:S(2)}) collective-permute-start(bf16[64,256]{1,0:T(8,128)(2,1)S(1)} %pad_maximum_fusion.2.refs_0_), channel_id=1, source_target_pairs={{0,8},{4,12},{8,0},{12,4},{1,9},{5,13},{9,1},{13,5},{2,10},{6,14},... | collective-permute-start | bytes 98312 | tf_op jit(solution)/shard_map/ppermute | solution.py:45
  43.7 1.0 %collective-permute-start.6 = (bf16[64,256]{1,0:T(8,128)(2,1)S(1)}, bf16[64,256]{1,0:T(8,128)(2,1)S(1)}, u32[]{:S(2)}, u32[]{:S(2)}) collective-permute-start(bf16[64,256]{1,0:T(8,128)(2,1)S(1)} %pad_maximum_fusion.2.refs_0_), channel_id=1, source_target_pairs={{0,4},{4,0},{8,12},{12,8},{1,5},{5,1},{9,13},{13,9},{2,6},{6,2},{1... | collective-permute-start | bytes 98312 | tf_op jit(solution)/shard_map/ppermute | solution.py:45
  44.7 7.8 %collective-permute-done.8.refs_3_ = bf16[64,256]{1,0:T(8,128)(2,1)S(1)} collective-permute-done((bf16[64,256]{1,0:T(8,128)(2,1)S(1)}, bf16[64,256]{1,0:T(8,128)(2,1)S(1)}, u32[]{:S(2)}, u32[]{:S(2)}) %collective-permute-start.8) | collective-permute-done | bytes 32800 | tf_op jit(solution)/shard_map/ppermute | solution.py:45
  52.5 1.5 %shard_map.93 = (f32[8,256]{1,0:T(8,128)S(1)}, bf16[4,256,128]{2,1,0:T(8,128)(2,1)S(1)}) custom-call(bf16[64,256]{1,0:T(8,128)(2,1)S(1)} %pad_maximum_fusion.2.refs_0_, bf16[64,256]{1,0:T(8,128)(2,1)S(1)} %collective-permute-done.6.refs_1_, bf16[64,256]{1,0:T(8,128)(2,1)S(1)} %collective-permute-done.7.refs_2_, ...), custom_call_target="tpu_custom_call" | custom-call | flops 1 | bytes 1 | tf_op jit(solution)/shard_map/pallas_call | solution.py:218
  54.0 4.0 %shard_map.94.before_ref = f32[8,256]{1,0:T(8,128)S(1)} custom-call(bf16[768,7168]{1,0:T(8,128)(2,1)S(1)} %get-tuple-element.19.acts_ref, bf16[64,3584]{1,0:T(8,128)(2,1)S(1)} %collective-permute-done.mine_ref, bf16[64,3584]{1,0:T(8,128)(2,1)S(1)} %collective-permute-done.2.theirs_ref, bf16[4,256,128]{2,1,0:T(8,128)(2,1)S(1)} %get-tuple-element.25.weights_ref, ...), custom_call_target="tpu_custom_call" | custom-call | flops 1 | bytes 1 | tf_op jit(solution)/shard_map/pallas_call | solution.py:218
  58.1 4.2 %copy-done = bf16[768,7168]{1,0:T(8,128)(2,1)} copy-done((bf16[768,7168]{1,0:T(8,128)(2,1)}, bf16[768,7168]{1,0:T(8,128)(2,1)S(1)}, u32[]{:S(2)}) %copy-start) | copy-done | bytes 11010072
  62.3 0.6 collective-permute-start.11
  62.9 1.0 %collective-permute-start.9 = (bf16[64,1792]{1,0:T(8,128)(2,1)S(1)}, bf16[64,1792]{1,0:T(8,128)(2,1)S(1)}, u32[]{:S(2)}, u32[]{:S(2)}) collective-permute-start(bf16[64,1792]{1,0:T(8,128)(2,1)S(1)} %slice.55), channel_id=1, source_target_pairs={{0,4},{4,0},{8,12},{12,8},{1,5},{5,1},{9,13},{13,9},{2,6},{6,2},{1... | collective-permute-start | bytes 688136 | tf_op jit(solution)/shard_map/ppermute | solution.py:274
  63.9 4.1 %copy-done.1 = bf16[768,7168]{1,0:T(8,128)(2,1)S(1)} copy-done((bf16[768,7168]{1,0:T(8,128)(2,1)S(1)}, bf16[768,7168]{1,0:T(8,128)(2,1)}, u32[]{:S(2)}) %copy-start.1) | copy-done | bytes 11010072
  68.0 1.9 %shard_map.95.total_ref = f32[768,128]{1,0:T(8,128)S(1)} custom-call(bf16[768,7168]{1,0:T(8,128)(2,1)S(1)} %copy-done.1, bf16[64,3584]{1,0:T(8,128)(2,1)S(1)} %collective-permute-done.10.mine_ref), custom_call_target="tpu_custom_call" | custom-call | flops 1 | bytes 1 | tf_op jit(solution)/shard_map/pallas_call | solution.py:218
  69.9 4.0 %shard_map.96.before_ref = f32[8,256]{1,0:T(8,128)S(1)} custom-call(bf16[768,7168]{1,0:T(8,128)(2,1)S(1)} %copy-done.1, bf16[64,3584]{1,0:T(8,128)(2,1)S(1)} %collective-permute-done.1.mine_ref, bf16[64,3584]{1,0:T(8,128)(2,1)S(1)} %collective-permute-done.5.theirs_ref, bf16[4,256,128]{2,1,0:T(8,128)(2,1)S(1)} %get-tuple-element.25.weights_ref, ...), custom_call_target="tpu_custom_call" | custom-call | flops 1 | bytes 1 | tf_op jit(solution)/shard_map/pallas_call | solution.py:218
  74.0 2.7 %shard_map.97 = f32[4,8]{1,0:T(4,128)S(1)} custom-call(bf16[768,7168]{1,0:T(8,128)(2,1)S(1)} %copy-done.1, bf16[64,1792]{1,0:T(8,128)(2,1)S(1)} %collective-permute-done.9.left_ref, bf16[64,1792]{1,0:T(8,128)(2,1)S(1)} %collective-permute-done.11.right_ref, f32[768,128]{1,0:T(8,128)S(1)} %shard_map.95.total_ref, ...), custom_call_target="tpu_custom_call" | custom-call | flops 1 | bytes 1 | tf_op jit(solution)/shard_map/pallas_call | solution.py:218
  76.7 1.1 %collective-permute-start.13 = (f32[4,8]{1,0:T(4,128)S(1)}, f32[4,8]{1,0:T(4,128)S(1)}, u32[]{:S(2)}, u32[]{:S(2)}) collective-permute-start(f32[4,8]{1,0:T(4,128)S(1)} %shard_map.97), channel_id=1, source_target_pairs={{0,2},{1,3},{2,0},{3,1},{4,6},{5,7},{6,4},{7,5},{8,10},{9,11},{10,... | collective-permute-start | bytes 392 | tf_op jit(solution)/shard_map/ppermute | solution.py:45
  77.9 0.7 collective-permute-start.12
  78.6 1.1 %collective-permute-done.14 = f32[4,8]{1,0:T(4,128)S(1)} collective-permute-done((f32[4,8]{1,0:T(4,128)S(1)}, f32[4,8]{1,0:T(4,128)S(1)}, u32[]{:S(2)}, u32[]{:S(2)}) %collective-permute-start.14) | collective-permute-done | bytes 160 | tf_op jit(solution)/shard_map/ppermute | solution.py:45
  79.7 0.6 collective-permute-done.13
  80.4 1.2 %collective-permute-start.15 = (f32[4,8]{1,0:T(4,128)S(1)}, f32[4,8]{1,0:T(4,128)S(1)}, u32[]{:S(2)}, u32[]{:S(2)}) collective-permute-start(f32[4,8]{1,0:T(4,128)S(1)} %add_add_fusion), channel_id=1, source_target_pairs={{0,4},{4,0},{8,12},{12,8},{1,5},{5,1},{9,13},{13,9},{2,6},{6,2},{1... | collective-permute-start | bytes 392 | tf_op jit(solution)/shard_map/ppermute | solution.py:37
  81.6 2.5 %collective-permute-done.15 = f32[4,8]{1,0:T(4,128)S(1)} collective-permute-done((f32[4,8]{1,0:T(4,128)S(1)}, f32[4,8]{1,0:T(4,128)S(1)}, u32[]{:S(2)}, u32[]{:S(2)}) %collective-permute-start.15) | collective-permute-done | bytes 160 | tf_op jit(solution)/shard_map/ppermute | solution.py:37
  84.0 2.1 %collective-permute-start.16 = (f32[4,8]{1,0:T(4,128)S(1)}, f32[4,8]{1,0:T(4,128)S(1)}, u32[]{:S(2)}, u32[]{:S(2)}) collective-permute-start(f32[4,8]{1,0:T(4,128)S(1)} %add.51), channel_id=1, source_target_pairs={{0,8},{4,12},{8,0},{12,4},{1,9},{5,13},{9,1},{13,5},{2,10},{6,14},... | collective-permute-start | bytes 392 | tf_op jit(solution)/shard_map/ppermute | solution.py:37
  86.1 2.4 %collective-permute-done.16 = f32[4,8]{1,0:T(4,128)S(1)} collective-permute-done((f32[4,8]{1,0:T(4,128)S(1)}, f32[4,8]{1,0:T(4,128)S(1)}, u32[]{:S(2)}, u32[]{:S(2)}) %collective-permute-start.16) | collective-permute-done | bytes 160 | tf_op jit(solution)/shard_map/ppermute | solution.py:37
  88.5 0.6 dynamic_slice.3
  (36 shorter events, 0.6 us)
Async XLA Ops:
  0.0 40.2 %copy-start.3 = (bf16[64,128]{1,0:T(8,128)(2,1)S(1)}, bf16[64,128]{1,0:T(8,128)(2,1)}, u32[]{:S(2)}) copy-start(bf16[64,128]{1,0:T(8,128)(2,1)} %param.13) | copy-start | bytes 49156
  4.6 22.2 %collective-permute-start = (bf16[64,3584]{1,0:T(8,128)(2,1)S(1)}, bf16[64,3584]{1,0:T(8,128)(2,1)S(1)}, u32[]{:S(2)}, u32[]{:S(2)}) collective-permute-start(bf16[64,3584]{1,0:T(8,128)(2,1)S(1)} %get-tuple-element.17), channel_id=1, source_target_pairs={{0,4},{4,0},{8,12},{12,8},{1,5},{5,1},{9,13},{13,9},{2,6},{6,2},{1... | collective-permute-start | bytes 1376264 | tf_op jit(solution)/shard_map/ppermute | solution.py:274
  7.7 2.7 %collective-permute-start.3 = (bf16[1152,128]{1,0:T(8,128)(2,1)S(1)}, bf16[1152,128]{1,0:T(8,128)(2,1)S(1)}, u32[]{:S(2)}, u32[]{:S(2)}) collective-permute-start(bf16[1152,128]{1,0:T(8,128)(2,1)S(1)} %pad_maximum_fusion), channel_id=1, source_target_pairs={{0,1},{1,0},{2,3},{3,2},{4,5},{5,4},{6,7},{7,6},{8,9},{9,8},{10,11... | collective-permute-start | bytes 884744 | tf_op jit(solution)/shard_map/ppermute | solution.py:284
  7.8 31.6 %collective-permute-start.1 = (bf16[64,3584]{1,0:T(8,128)(2,1)S(1)}, bf16[64,3584]{1,0:T(8,128)(2,1)S(1)}, u32[]{:S(2)}, u32[]{:S(2)}) collective-permute-start(bf16[64,3584]{1,0:T(8,128)(2,1)S(1)} %get-tuple-element.17), channel_id=1, source_target_pairs={{0,8},{4,12},{8,0},{12,4},{1,9},{5,13},{9,1},{13,5},{2,10},{6,14},... | collective-permute-start | bytes 1376264 | tf_op jit(solution)/shard_map/ppermute | solution.py:274
  26.9 12.6 %collective-permute-start.2 = (bf16[64,3584]{1,0:T(8,128)(2,1)S(1)}, bf16[64,3584]{1,0:T(8,128)(2,1)S(1)}, u32[]{:S(2)}, u32[]{:S(2)}) collective-permute-start(bf16[64,3584]{1,0:T(8,128)(2,1)S(1)} %collective-permute-done.mine_ref), channel_id=1, source_target_pairs={{0,16},{16,0},{1,17},{17,1},{2,18},{18,2},{3,19},{19,3},{4,20},{20... | collective-permute-start | bytes 1376264 | tf_op jit(solution)/shard_map/ppermute | solution.py:277
  28.6 10.8 %collective-permute-start.4 = (bf16[1152,128]{1,0:T(8,128)(2,1)S(1)}, bf16[1152,128]{1,0:T(8,128)(2,1)S(1)}, u32[]{:S(2)}, u32[]{:S(2)}) collective-permute-start(bf16[1152,128]{1,0:T(8,128)(2,1)S(1)} %pad_maximum_fusion.1), channel_id=1, source_target_pairs={{0,2},{2,0},{1,3},{3,1},{4,6},{6,4},{5,7},{7,5},{8,10},{10,8},{9,1... | collective-permute-start | bytes 884744 | tf_op jit(solution)/shard_map/ppermute | solution.py:286
  31.0 1.2 %copy-start.2 = (bf16[64,7168]{1,0:T(8,128)(2,1)S(1)}, bf16[64,7168]{1,0:T(8,128)(2,1)}, u32[]{:S(2)}) copy-start(bf16[64,7168]{1,0:T(8,128)(2,1)} %own_ref.1) | copy-start | bytes 2752516
  39.5 22.8 %collective-permute-start.10 = (bf16[64,3584]{1,0:T(8,128)(2,1)S(1)}, bf16[64,3584]{1,0:T(8,128)(2,1)S(1)}, u32[]{:S(2)}, u32[]{:S(2)}) collective-permute-start(bf16[64,3584]{1,0:T(8,128)(2,1)S(1)} %collective-permute-done.1.mine_ref), channel_id=1, source_target_pairs={{0,4},{4,0},{8,12},{12,8},{1,5},{5,1},{9,13},{13,9},{2,6},{6,2},{1... | collective-permute-start | bytes 1376264 | tf_op jit(solution)/shard_map/ppermute | solution.py:274
  39.6 23.4 %collective-permute-start.5 = (bf16[64,3584]{1,0:T(8,128)(2,1)S(1)}, bf16[64,3584]{1,0:T(8,128)(2,1)S(1)}, u32[]{:S(2)}, u32[]{:S(2)}) collective-permute-start(bf16[64,3584]{1,0:T(8,128)(2,1)S(1)} %collective-permute-done.1.mine_ref), channel_id=1, source_target_pairs={{0,16},{16,0},{1,17},{17,1},{2,18},{18,2},{3,19},{19,3},{4,20},{20... | collective-permute-start | bytes 1376264 | tf_op jit(solution)/shard_map/ppermute | solution.py:277
  40.2 12.3 %collective-permute-start.8 = (bf16[64,256]{1,0:T(8,128)(2,1)S(1)}, bf16[64,256]{1,0:T(8,128)(2,1)S(1)}, u32[]{:S(2)}, u32[]{:S(2)}) collective-permute-start(bf16[64,256]{1,0:T(8,128)(2,1)S(1)} %pad_maximum_fusion.2.refs_0_), channel_id=1, source_target_pairs={{0,12},{4,8},{8,4},{12,0},{1,13},{5,9},{9,5},{13,1},{2,14},{6,10},... | collective-permute-start | bytes 98312 | tf_op jit(solution)/shard_map/ppermute | solution.py:45
  42.7 9.8 %collective-permute-start.7 = (bf16[64,256]{1,0:T(8,128)(2,1)S(1)}, bf16[64,256]{1,0:T(8,128)(2,1)S(1)}, u32[]{:S(2)}, u32[]{:S(2)}) collective-permute-start(bf16[64,256]{1,0:T(8,128)(2,1)S(1)} %pad_maximum_fusion.2.refs_0_), channel_id=1, source_target_pairs={{0,8},{4,12},{8,0},{12,4},{1,9},{5,13},{9,1},{13,5},{2,10},{6,14},... | collective-permute-start | bytes 98312 | tf_op jit(solution)/shard_map/ppermute | solution.py:45
  43.7 8.8 %collective-permute-start.6 = (bf16[64,256]{1,0:T(8,128)(2,1)S(1)}, bf16[64,256]{1,0:T(8,128)(2,1)S(1)}, u32[]{:S(2)}, u32[]{:S(2)}) collective-permute-start(bf16[64,256]{1,0:T(8,128)(2,1)S(1)} %pad_maximum_fusion.2.refs_0_), channel_id=1, source_target_pairs={{0,4},{4,0},{8,12},{12,8},{1,5},{5,1},{9,13},{13,9},{2,6},{6,2},{1... | collective-permute-start | bytes 98312 | tf_op jit(solution)/shard_map/ppermute | solution.py:45
  58.1 4.2 %copy-start = (bf16[768,7168]{1,0:T(8,128)(2,1)}, bf16[768,7168]{1,0:T(8,128)(2,1)S(1)}, u32[]{:S(2)}) copy-start(bf16[768,7168]{1,0:T(8,128)(2,1)S(1)} %get-tuple-element.19.acts_ref) | copy-start | bytes 33030148
  62.3 11.6 %collective-permute-start.11 = (bf16[64,1792]{1,0:T(8,128)(2,1)S(1)}, bf16[64,1792]{1,0:T(8,128)(2,1)S(1)}, u32[]{:S(2)}, u32[]{:S(2)}) collective-permute-start(bf16[64,1792]{1,0:T(8,128)(2,1)S(1)} %slice.56), channel_id=1, source_target_pairs={{0,16},{16,0},{1,17},{17,1},{2,18},{18,2},{3,19},{19,3},{4,20},{20... | collective-permute-start | bytes 688136 | tf_op jit(solution)/shard_map/ppermute | solution.py:277
  62.9 11.0 %collective-permute-start.9 = (bf16[64,1792]{1,0:T(8,128)(2,1)S(1)}, bf16[64,1792]{1,0:T(8,128)(2,1)S(1)}, u32[]{:S(2)}, u32[]{:S(2)}) collective-permute-start(bf16[64,1792]{1,0:T(8,128)(2,1)S(1)} %slice.55), channel_id=1, source_target_pairs={{0,4},{4,0},{8,12},{12,8},{1,5},{5,1},{9,13},{13,9},{2,6},{6,2},{1... | collective-permute-start | bytes 688136 | tf_op jit(solution)/shard_map/ppermute | solution.py:274
  63.9 4.1 %copy-start.1 = (bf16[768,7168]{1,0:T(8,128)(2,1)S(1)}, bf16[768,7168]{1,0:T(8,128)(2,1)}, u32[]{:S(2)}) copy-start(bf16[768,7168]{1,0:T(8,128)(2,1)} %copy-done) | copy-start | bytes 33030148
  76.7 3.0 %collective-permute-start.14 = (f32[4,8]{1,0:T(4,128)S(1)}, f32[4,8]{1,0:T(4,128)S(1)}, u32[]{:S(2)}, u32[]{:S(2)}) collective-permute-start(f32[4,8]{1,0:T(4,128)S(1)} %shard_map.97), channel_id=1, source_target_pairs={{0,3},{1,2},{2,1},{3,0},{4,7},{5,6},{6,5},{7,4},{8,11},{9,10},{10,... | collective-permute-start | bytes 392 | tf_op jit(solution)/shard_map/ppermute | solution.py:45
  76.7 3.6 %collective-permute-start.13 = (f32[4,8]{1,0:T(4,128)S(1)}, f32[4,8]{1,0:T(4,128)S(1)}, u32[]{:S(2)}, u32[]{:S(2)}) collective-permute-start(f32[4,8]{1,0:T(4,128)S(1)} %shard_map.97), channel_id=1, source_target_pairs={{0,2},{1,3},{2,0},{3,1},{4,6},{5,7},{6,4},{7,5},{8,10},{9,11},{10,... | collective-permute-start | bytes 392 | tf_op jit(solution)/shard_map/ppermute | solution.py:45
  77.9 2.5 %collective-permute-start.12 = (f32[4,8]{1,0:T(4,128)S(1)}, f32[4,8]{1,0:T(4,128)S(1)}, u32[]{:S(2)}, u32[]{:S(2)}) collective-permute-start(f32[4,8]{1,0:T(4,128)S(1)} %shard_map.97), channel_id=1, source_target_pairs={{0,1},{1,0},{2,3},{3,2},{4,5},{5,4},{6,7},{7,6},{8,9},{9,8},{10,11... | collective-permute-start | bytes 392 | tf_op jit(solution)/shard_map/ppermute | solution.py:45
  80.4 3.7 %collective-permute-start.15 = (f32[4,8]{1,0:T(4,128)S(1)}, f32[4,8]{1,0:T(4,128)S(1)}, u32[]{:S(2)}, u32[]{:S(2)}) collective-permute-start(f32[4,8]{1,0:T(4,128)S(1)} %add_add_fusion), channel_id=1, source_target_pairs={{0,4},{4,0},{8,12},{12,8},{1,5},{5,1},{9,13},{13,9},{2,6},{6,2},{1... | collective-permute-start | bytes 392 | tf_op jit(solution)/shard_map/ppermute | solution.py:37
  84.0 4.5 %collective-permute-start.16 = (f32[4,8]{1,0:T(4,128)S(1)}, f32[4,8]{1,0:T(4,128)S(1)}, u32[]{:S(2)}, u32[]{:S(2)}) collective-permute-start(f32[4,8]{1,0:T(4,128)S(1)} %add.51), channel_id=1, source_target_pairs={{0,8},{4,12},{8,0},{12,4},{1,9},{5,13},{9,1},{13,5},{2,10},{6,14},... | collective-permute-start | bytes 392 | tf_op jit(solution)/shard_map/ppermute | solution.py:37

commit v4 on v3

--- a/solution.py
+++ b/solution.py
@@ -1,4 +1,5 @@
 import functools
+import itertools
 
 import jax
 import jax.numpy as jnp
@@ -54,28 +55,63 @@
     return pltpu.with_memory_space_constraint(value, pltpu.HBM)
 
 
+def in_vmem(value):
+    return pltpu.with_memory_space_constraint(value, pltpu.VMEM)
+
+
+def pairing(partner):
+    sizes = [lax.axis_size(axis) for axis in AXES]
+    places = list(itertools.product(*map(range, sizes)))
+    return [(number, places.index(partner(*place))) for number, place in enumerate(places)]
+
+
+def halves_kernel(whole_ref, mine_ref, other_ref, copied):
+    columns = mine_ref.shape[1]
+    group = lax.axis_index("groups")
+    copies = [
+        pltpu.make_async_copy(
+            whole_ref.at[:, pl.ds(pl.multiple_of(half * columns, LANES), columns)],
+            half_ref,
+            copied.at[place],
+        )
+        for place, (half, half_ref) in enumerate([(group, mine_ref), (1 - group, other_ref)])
+    ]
+    for copy in copies:
+        copy.start()
+    for copy in copies:
+        copy.wait()
+
+
+def take_halves(whole):
+    rows, columns = whole.shape
+    half = pltpu.VMEM((rows, columns // 2), whole.dtype)
+    return pl.pallas_call(
+        halves_kernel,
+        in_specs=[pl.BlockSpec(memory_space=pl.ANY)],
+        out_shape=[half, half],
+        scratch_shapes=[pltpu.SemaphoreType.DMA((2,))],
+    )(in_hbm(whole))
+
+
 def parts_kernel(*refs):
-    sources, half_ref, sum_ref, copied = refs[:5], refs[5], refs[6], refs[-1]
-    held_refs = out_ref, out_query_ref, in_ref, in_query_ref, grads_ref = refs[7:-1]
-    columns = half_ref.shape[1]
-    begin = pl.multiple_of(lax.axis_index("groups") * columns, LANES)
-    moves = [(sources[2].at[:, pl.ds(begin, columns)], half_ref), *zip(sources, held_refs)]
+    sources, sum_ref, copied = refs[:5], refs[5], refs[-1]
+    held_refs = out_ref, out_query_ref, in_ref, in_query_ref, grads_ref = refs[6:-1]
     copies = [
         pltpu.make_async_copy(source, target, copied.at[place])
-        for place, (source, target) in enumerate(moves)
+        for place, (source, target) in enumerate(zip(sources, held_refs))
     ]
     for copy in copies:
         copy.start()
     rows, width = in_ref.shape[0], out_ref.shape[0]
+    copies[0].wait()
     copies[1].wait()
-    copies[2].wait()
     sum_ref[rows : rows + width] = jnp.dot(
         out_ref[...], out_query_ref[...], preferred_element_type=jnp.float32
     )
+    copies[2].wait()
     copies[3].wait()
+    sum_ref[:rows] = jnp.dot(in_ref[...], in_query_ref[...], preferred_element_type=jnp.float32)
     copies[4].wait()
-    sum_ref[:rows] = jnp.dot(in_ref[...], in_query_ref[...], preferred_element_type=jnp.float32)
-    copies[5].wait()
 
     @pl.loop(0, grads_ref.shape[0] // BLOCK)
     def _(step):
@@ -84,22 +120,16 @@
             grads_ref[pl.ds(start, BLOCK), :], out_ref[...]
         )
 
-    copies[0].wait()
-
 
 def small_parts(basis_in, query_in, basis_out, query_out, out_grads):
-    rows, features = basis_in.shape
-    high = rows + basis_out.shape[0] + out_grads.shape[0]
+    high = basis_in.shape[0] + basis_out.shape[0] + out_grads.shape[0]
     sources = (basis_out, query_out, basis_in, query_in, out_grads)
     return pl.pallas_call(
         parts_kernel,
         in_specs=[pl.BlockSpec(memory_space=pl.ANY)] * len(sources),
-        out_shape=[
-            pltpu.VMEM((rows, features // 2), basis_in.dtype),
-            jax.ShapeDtypeStruct((high, query_in.shape[1]), jnp.float32),
-        ],
+        out_shape=jax.ShapeDtypeStruct((high, query_in.shape[1]), jnp.float32),
         scratch_shapes=[pltpu.VMEM(source.shape, source.dtype) for source in sources]
-        + [pltpu.SemaphoreType.DMA((len(sources) + 1,))],
+        + [pltpu.SemaphoreType.DMA((len(sources),))],
         compiler_params=pltpu.CompilerParams(vmem_limit_bytes=VMEM_LIMIT),
     )(*[in_hbm(source) for source in sources])
 
@@ -197,7 +227,7 @@
 
 
 def last_kernel(
-    acts_ref, left_ref, right_ref, total_ref, weights_ref, grad_ref, onehot_ref, before_ref, out_ref
+    queries, acts_ref, left_ref, right_ref, total_ref, weights_ref, grad_ref, onehot_ref, before_ref, out_ref
 ):
     other = 1 - lax.axis_index("groups")
 
@@ -208,10 +238,15 @@
         return sums + mix(start, total, weights_ref[3], grad_ref, onehot_ref)
 
     sums = blocks(acts_ref, body, before_ref[...])
-    queries, width = out_ref.shape[0], sums.shape[1]
+    width = sums.shape[1]
     query_of = lax.broadcasted_iota(jnp.int32, (queries, width), 1) // (width // queries)
     chosen = query_of == lax.broadcasted_iota(jnp.int32, (queries, width), 0)
-    out_ref[...] = contract_last(chosen.astype(jnp.float32), sums, precision=lax.Precision.HIGHEST)
+    scores = contract_last(chosen.astype(jnp.float32), sums, precision=lax.Precision.HIGHEST)
+    columns = out_ref.shape[1]
+    for place in range(out_ref.shape[0] // queries):
+        out_ref[pl.ds(place * queries, queries), :] = scores[
+            :, place * columns : (place + 1) * columns
+        ]
 
 
 def call(kernel, out_shape, *operands, **options):
@@ -269,62 +304,79 @@
     tokens, seq_count = acts.shape[0], onehot.shape[0]
     query_count = query_in.shape[1] // R
     pair = [(0, 1), (1, 0)]
-
-    def along(value, distance):
-        return lax.ppermute(value, "blk", [(i, i ^ distance) for i in range(4)])
+    place = lax.axis_index("blk")
+    inner = (place == 1) | (place == 2)
+
+    def along(value):
+        return lax.ppermute(value, "blk", [(i, i ^ 1) for i in range(4)])
 
     def swapped(value):
         return lax.ppermute(value, "groups", pair)
 
-    half, part = small_parts(basis_in, query_in, basis_out, query_out, out_grads)
-    mine_1 = along(half, 1)
-    mine_2 = along(half, 2)
+    def across(value, at_ends):
+        return lax.ppermute(
+            value,
+            AXES,
+            pairing(lambda g, b, e, r: (g, 3 - b, e, r) if b in (1, 2) else at_ends(g, b, e, r)),
+        )
+
+    half, other_half = take_halves(basis_in)
+    mine_1 = along(half)
+    middle_3 = across(half, lambda g, b, e, r: (g, b, e, 1 - r))
 
     split = rows + width
+    part = small_parts(held(basis_in, half), query_in, basis_out, query_out, out_grads)
     other = lax.ppermute(to_send(part, split), "rep", pair)
-    part = add_sent(part, held(other, mine_1), split)
-    other = lax.ppermute(to_send(part, split), "eig", pair)
-    theirs_1 = swapped(mine_1)
+    part = add_sent(part, other, split)
+    sent = to_send(part, split)
+    other = lax.ppermute(sent, "eig", pair)
+    total_shape = jax.ShapeDtypeStruct((tokens, LANES), jnp.float32)
     acts, total = call(
         first_kernel,
-        [pltpu.VMEM(acts.shape, acts.dtype), jax.ShapeDtypeStruct((tokens, LANES), jnp.float32)],
-        in_hbm(held(acts, mine_1)),
+        [pltpu.VMEM(acts.shape, acts.dtype), total_shape],
+        in_hbm(held(acts, sent)),
         basis_in,
         in_specs=[pl.BlockSpec(memory_space=pl.ANY), pl.BlockSpec(memory_space=pltpu.VMEM)],
         scratch_shapes=[pltpu.SemaphoreType.DMA((tokens // BLOCK,))],
     )
-    mine_2 = held(mine_2, theirs_1, other, total)
-    part = add_sent(part, held(other, mine_2), split).astype(jnp.bfloat16)
+    acts = in_vmem(acts)
+
+    middle_3 = held(middle_3, mine_1, total)
+    from_pair = along(jnp.where(inner, middle_3, other_half))
+    from_across = across(held(mine_1, middle_3), lambda g, b, e, r: (1 - g, b, e, r))
+    part = add_sent(part, held(other, mine_1), split).astype(jnp.bfloat16)
     in_query, out_query, grad_proj = part[:rows], part[rows:split], part[split:]
     packs = by_distance(jnp.concatenate([in_query, eigvals], axis=1))
 
+    mine_2 = jnp.where(inner, from_across, from_pair)
     theirs_2 = swapped(mine_2)
-    mine_3 = along(mine_2, 1)
+    mine_3 = along(mine_2)
+    theirs_1 = jnp.where(inner, held(from_pair, mine_2), held(from_across, mine_2))
     sums_shape = jax.ShapeDtypeStruct((seq_count, query_count * rows), jnp.float32)
     weights_shape = jax.ShapeDtypeStruct((4, query_count * rows, width), jnp.bfloat16)
     sums, weights = call(
         functools.partial(weight_kernel, query_count),
         [sums_shape, weights_shape],
-        *packs, out_query, grad_proj, onehot, total,
+        *packs, held(out_query, mine_2), grad_proj, onehot, total,
     )
     fixed = (weights, grad_proj, onehot)
     sums = call(
         functools.partial(slot_kernel, 1), sums_shape, acts, mine_1, theirs_1, *fixed, sums
     )
 
-    middle = mine_3.shape[1] // 2
-    left_3 = along(held(theirs_2, sums)[:, :middle], 1)
-    right_3 = swapped(held(mine_3, sums)[:, middle:])
+    cut = mine_3.shape[1] // 2
+    left_3 = along(held(theirs_2, sums)[:, :cut])
+    right_3 = swapped(held(mine_3, sums)[:, cut:])
     sums = call(
         functools.partial(slot_kernel, 2), sums_shape, acts, mine_2, theirs_2, *fixed, sums
     )
-    total = call(mine_kernel, jax.ShapeDtypeStruct((tokens, LANES), jnp.float32), acts, mine_3)
-    scores = call(
-        last_kernel,
-        jax.ShapeDtypeStruct((query_count, seq_count), jnp.float32),
+    total = call(mine_kernel, total_shape, acts, mine_3)
+    places = lax.axis_size("blk")
+    return call(
+        functools.partial(last_kernel, query_count),
+        jax.ShapeDtypeStruct((places * query_count, seq_count // places), jnp.float32),
         acts, left_3, right_3, total, *fixed, sums,
     )
-    return swap_sum(sum(by_distance(scores, ("eig", "rep"))), "blk", jnp.float32)
 
 
 def plain_path(acts, out_grads, basis_in, basis_out, eigvals, query_out, query_in, onehot):
@@ -338,7 +390,10 @@
     grad_proj = whole_sum(contract_last(out_grads, basis_out), jnp.bfloat16)
     pack = jnp.concatenate([in_query, eigvals], axis=1)
     scores = plain_scores(acts, basis_in, pack, out_query, grad_proj, onehot.astype(jnp.float32))
-    return lax.psum(scores, ("blk", "eig", "rep"))
+    queries, columns = scores.shape
+    places = lax.axis_size("blk")
+    parts = scores.reshape(queries, places, columns // places)
+    return parts.transpose(1, 0, 2).reshape(places * queries, columns // places)
 
 
 def on_device(acts, out_grads, basis_in, basis_out, eigvals, query_out, query_in, seq_ids, owner):
@@ -357,14 +412,11 @@
         and pairs == basis_out.shape[0] == LANES
     )
     way = stepped_scores if stepped else plain_path
-    scores = way(acts, out_grads, basis_in, basis_out, eigvals, query_out, query_in, onehot)
+    parts = way(acts, out_grads, basis_in, basis_out, eigvals, query_out, query_in, onehot)
     own_queries = pairs // R // lax.axis_size(("eig", "rep"))
     own_columns = seq_count // lax.axis_size("blk")
-    return lax.dynamic_slice(
-        scores,
-        (lax.axis_index(("eig", "rep")) * own_queries, lax.axis_index("blk") * own_columns),
-        (own_queries, own_columns),
-    )
+    parts = lax.all_to_all(parts, ("blk", "eig", "rep"), 0, 0, tiled=True)
+    return jnp.sum(parts.reshape(-1, own_queries, own_columns), axis=0)
 
 
 def solution(mesh):

time: 89.3 us -> 68.9 us (0.77)
  waiting for transfers between devices: 30.8 us -> 11.1 us
  local copies, waits for them, and re-layouts: 10.2 us -> 0.07 us
  blocking collectives: 0 us -> 8.98 us
  starting transfers between devices: 20.9 us -> 18.7 us
  other arithmetic: 1.06 us -> 2.45 us
  Pallas kernels: 26 us -> 27.2 us
    ppermute x7, waiting for transfers between devices: 21.2 us -> 10.1 us  [the longest x4 5.22 us: along(): return lax.ppermute(value, 'blk', [(i, i ^ 1) for i in range(4)])]
    unnamed x8 -> x4, local copies, waits for them, and re-layouts: 9.53 us -> 0.01 us
    ppermute x6 -> x3, waiting for transfers between devices: 9.53 us -> 0.01 us  [by_distance(): lax.ppermute(value, axis, [(i, i ^ k) for i in range(size)])]
    all_to_all x0 -> x1, blocking collectives: none -> 8.98 us  [on_device(): parts = lax.all_to_all(parts, ('blk', 'eig', 'rep'), 0, 0, tiled=True)]
    ppermute x6 -> x3, starting transfers between devices: 6.33 us -> 4.45 us  [by_distance(): lax.ppermute(value, axis, [(i, i ^ k) for i in range(size)])]
    pallas_call x0 -> x1, Pallas kernels: none -> 1.25 us  [take_halves(): pl.pallas_call(halves_kernel, in_specs=[pl.BlockSpec(memory_space=pl.ANY)...]
    ppermute x1, waiting for transfers between devices: 0.01 us -> 0.99 us  [stepped_scores(): other = lax.ppermute(to_send(part, split), 'rep', pair)]
    ppermute x3 -> x2, starting transfers between devices: 2.9 us -> 2.8 us  [swapped(): return lax.ppermute(value, 'groups', pair)]
  transfers between devices with their start and end apart: 17 -> 13, of which waited for: 6 -> 4; matrix products, arithmetic and copies ran while one was open for 1% -> 3% of each run, Pallas kernels for 21% -> 34%
where the time goes in v4:
time: 68.9 us; the launch traced here: 68.7 us
  Pallas kernels  27.2 us (39%)
  starting transfers between devices  18.7 us (27%)
  waiting for transfers between devices  11.1 us (16%)
  blocking collectives  8.98 us (13%)
  other arithmetic  2.45 us (4%)
    pallas_call x6, Pallas kernels, call(): pl.pallas_call(kernel, out_shape=out_shape, compiler_params=pltpu.Compile...  21.5 us
    all_to_all x1, blocking collectives, on_device(): parts = lax.all_to_all(parts, ('blk', 'eig', 'rep'), 0, 0, tiled=True)  8.98 us
    ppermute x4, starting transfers between devices, along(): return lax.ppermute(value, 'blk', [(i, i ^ 1) for i in range(4)])  7.8 us
    ppermute x4, waiting for transfers between devices, along(): return lax.ppermute(value, 'blk', [(i, i ^ 1) for i in range(4)])  5.22 us
    ppermute x2, waiting for transfers between devices, across(): lax.ppermute(value, AXES, pairing(lambda g, b, e, r: (g, 3 - b, e, r) if...  4.86 us
    ppermute x3, starting transfers between devices, by_distance(): lax.ppermute(value, axis, [(i, i ^ k) for i in range(size)])  4.45 us
    pallas_call x1, Pallas kernels, small_parts(): pl.pallas_call(parts_kernel, in_specs=[pl.BlockSpec(memory_space=pl.ANY)]...  4.44 us
    ppermute x2, starting transfers between devices, swapped(): return lax.ppermute(value, 'groups', pair)  2.8 us
  transfers between devices with their start and end apart: 13, of which 4 were waited for; matrix products, arithmetic and copies ran while one was open for 3% of the time, Pallas kernels for 34%

profile of v4, /device:TPU:0, one launch (start us, length us, event | category | flops | bytes accessed | tf_op | source)
XLA Modules:
  0.0 68.7 jit_solution(15016000033587841353)
XLA Ops:
  0.0 1.3 %shard_map.91 = (bf16[64,3584]{1,0:T(8,128)(2,1)S(1)}, bf16[64,3584]{1,0:T(8,128)(2,1)S(1)}) custom-call(bf16[64,7168]{1,0:T(8,128)(2,1)} %own_ref.1), custom_call_target="tpu_custom_call" | custom-call | tf_op jit(solution)/shard_map/pallas_call | solution.py:88
  1.3 0.0 copy-start.1
  1.3 0.5 collective-permute-start.2
  1.8 4.1 %collective-permute-start.1 = (bf16[64,3584]{1,0:T(8,128)(2,1)S(1)}, bf16[64,3584]{1,0:T(8,128)(2,1)S(1)}, u32[]{:S(2)}, u32[]{:S(2)}) collective-permute-start(bf16[64,3584]{1,0:T(8,128)(2,1)S(1)} %get-tuple-element.21), channel_id=1, source_target_pairs={{0,4},{4,0},{8,12},{12,8},{1,5},{5,1},{9,13},{13,9},{2,6},{6,2},{1... | collective-permute-start | bytes 1376264 | tf_op jit(solution)/shard_map/ppermute | solution.py:311
  5.9 4.4 %shard_map.92 = f32[960,128]{1,0:T(8,128)S(1)} custom-call(bf16[128,2048]{1,0:T(8,128)(2,1)} %refs_0_.1, bf16[2048,128]{1,0:T(8,128)(2,1)} %refs_1_.1, bf16[64,7168]{1,0:T(8,128)(2,1)} %own_ref.1, bf16[7168,128]{1,0:T(8,128)(2,1)} %refs_3_.1, bf16[768,2048]{1,0:T(8,128)(2,1)} %refs_4_.1), custom_call_target="tpu_custom_call" | custom-call | tf_op jit(solution)/shard_map/pallas_call | solution.py:127
  10.4 0.7 %pad_maximum_fusion = bf16[1152,128]{1,0:T(8,128)(2,1)} fusion(bf16[768,128]{1,0:T(8,128)(2,1)S(1)} %slice.99, bf16[192,128]{1,0:T(8,128)(2,1)S(1)} %get-tuple-element.40, bf16[192,128]{1,0:T(8,128)(2,1)S(1)} %get-tuple-element.39), kind=kLoop, calls=%fused_computation.6 | loop fusion | flops 884736 | bytes 589824 | tf_op jit(solution)/shard_map/concatenate | solution.py:291
  11.2 0.8 %select_reduce_fusion = s32[768]{0:T(1024)S(1)} fusion(s32[8]{0:T(128)} %param.17, s32[768]{0:T(1024)} %param.16), kind=kLoop, calls=%fused_computation.18 | loop fusion | flops 17664 | bytes 6176 | tf_op jit(solution)/shard_map/reduce_sum | solution.py:404
  12.0 1.0 %collective-permute-done = bf16[1152,128]{1,0:T(8,128)(2,1)S(1)} collective-permute-done((bf16[1152,128]{1,0:T(8,128)(2,1)}, bf16[1152,128]{1,0:T(8,128)(2,1)S(1)}, u32[]{:S(2)}, u32[]{:S(2)}) %collective-permute-start) | collective-permute-done | bytes 294944 | tf_op jit(solution)/shard_map/ppermute | solution.py:329
  13.1 1.6 %collective-permute-start.6 = (bf16[1152,128]{1,0:T(8,128)(2,1)S(1)}, bf16[1152,128]{1,0:T(8,128)(2,1)S(1)}, u32[]{:S(2)}, u32[]{:S(2)}) collective-permute-start(bf16[1152,128]{1,0:T(8,128)(2,1)S(1)} %pad_maximum_fusion.1), channel_id=1, source_target_pairs={{0,2},{2,0},{1,3},{3,1},{4,6},{6,4},{5,7},{7,5},{8,10},{10,8},{9,1... | collective-permute-start | bytes 884744 | tf_op jit(solution)/shard_map/ppermute | solution.py:332
  14.6 7.3 %shard_map.93 = (bf16[768,7168]{1,0:T(8,128)(2,1)S(1)}, f32[768,128]{1,0:T(8,128)S(1)}) custom-call(bf16[768,7168]{1,0:T(8,128)(2,1)} %source_ref, bf16[64,7168]{1,0:T(8,128)(2,1)S(1)} %copy-done), custom_call_target="tpu_custom_call" | custom-call | flops 1 | bytes 1 | tf_op jit(solution)/shard_map/pallas_call | solution.py:253
  21.9 1.6 %collective-permute-start.3 = (bf16[64,3584]{1,0:T(8,128)(2,1)S(1)}, bf16[64,3584]{1,0:T(8,128)(2,1)S(1)}, u32[]{:S(2)}, u32[]{:S(2)}) collective-permute-start(bf16[64,3584]{1,0:T(8,128)(2,1)S(1)} %collective-permute-done.1.mine_ref), channel_id=1, source_target_pairs={{0,16},{1,17},{2,18},{3,19},{4,8},{5,9},{6,10},{7,11},{8,4},{9,5},... | collective-permute-start | bytes 1376264 | tf_op jit(solution)/shard_map/ppermute | solution.py:317
  23.5 0.1 broadcast_select_fusion.2
  23.6 1.2 %collective-permute-start.4 = (bf16[64,3584]{1,0:T(8,128)(2,1)S(1)}, bf16[64,3584]{1,0:T(8,128)(2,1)S(1)}, u32[]{:S(2)}, u32[]{:S(2)}) collective-permute-start(bf16[64,3584]{1,0:T(8,128)(2,1)S(1)} %broadcast_select_fusion.2), channel_id=1, source_target_pairs={{0,4},{4,0},{8,12},{12,8},{1,5},{5,1},{9,13},{13,9},{2,6},{6,2},{1... | collective-permute-start | bytes 1376264 | tf_op jit(solution)/shard_map/ppermute | solution.py:311
  24.9 1.3 %collective-permute-start.9 = (bf16[64,256]{1,0:T(8,128)(2,1)S(1)}, bf16[64,256]{1,0:T(8,128)(2,1)S(1)}, u32[]{:S(2)}, u32[]{:S(2)}) collective-permute-start(bf16[64,256]{1,0:T(8,128)(2,1)S(1)} %pad_maximum_fusion.2.refs_0_), channel_id=1, source_target_pairs={{0,12},{4,8},{8,4},{12,0},{1,13},{5,9},{9,5},{13,1},{2,14},{6,10},... | collective-permute-start | bytes 98312 | tf_op jit(solution)/shard_map/ppermute | solution.py:46
  26.2 1.1 %collective-permute-start.8 = (bf16[64,256]{1,0:T(8,128)(2,1)S(1)}, bf16[64,256]{1,0:T(8,128)(2,1)S(1)}, u32[]{:S(2)}, u32[]{:S(2)}) collective-permute-start(bf16[64,256]{1,0:T(8,128)(2,1)S(1)} %pad_maximum_fusion.2.refs_0_), channel_id=1, source_target_pairs={{0,8},{4,12},{8,0},{12,4},{1,9},{5,13},{9,1},{13,5},{2,10},{6,14},... | collective-permute-start | bytes 98312 | tf_op jit(solution)/shard_map/ppermute | solution.py:46
  27.3 2.0 %collective-permute-start.7 = (bf16[64,256]{1,0:T(8,128)(2,1)S(1)}, bf16[64,256]{1,0:T(8,128)(2,1)S(1)}, u32[]{:S(2)}, u32[]{:S(2)}) collective-permute-start(bf16[64,256]{1,0:T(8,128)(2,1)S(1)} %pad_maximum_fusion.2.refs_0_), channel_id=1, source_target_pairs={{0,4},{4,0},{8,12},{12,8},{1,5},{5,1},{9,13},{13,9},{2,6},{6,2},{1... | collective-permute-start | bytes 98312 | tf_op jit(solution)/shard_map/ppermute | solution.py:46
  29.3 0.1 add_convert_fusion.refs_5_.grad_ref
  29.4 4.9 %collective-permute-done.3 = bf16[64,3584]{1,0:T(8,128)(2,1)S(1)} collective-permute-done((bf16[64,3584]{1,0:T(8,128)(2,1)S(1)}, bf16[64,3584]{1,0:T(8,128)(2,1)S(1)}, u32[]{:S(2)}, u32[]{:S(2)}) %collective-permute-start.3) | collective-permute-done | bytes 458784 | tf_op jit(solution)/shard_map/ppermute | solution.py:317
  34.3 2.8 %collective-permute-done.4 = bf16[64,3584]{1,0:T(8,128)(2,1)S(1)} collective-permute-done((bf16[64,3584]{1,0:T(8,128)(2,1)S(1)}, bf16[64,3584]{1,0:T(8,128)(2,1)S(1)}, u32[]{:S(2)}, u32[]{:S(2)}) %collective-permute-start.4) | collective-permute-done | bytes 458784 | tf_op jit(solution)/shard_map/ppermute | solution.py:311
  37.1 0.9 %collective-permute-start.11 = (bf16[64,3584]{1,0:T(8,128)(2,1)S(1)}, bf16[64,3584]{1,0:T(8,128)(2,1)S(1)}, u32[]{:S(2)}, u32[]{:S(2)}) collective-permute-start(bf16[64,3584]{1,0:T(8,128)(2,1)S(1)} %broadcast_select_fusion.1.mine_ref), channel_id=1, source_target_pairs={{0,4},{4,0},{8,12},{12,8},{1,5},{5,1},{9,13},{13,9},{2,6},{6,2},{1... | collective-permute-start | bytes 1376264 | tf_op jit(solution)/shard_map/ppermute | solution.py:311
  38.0 1.5 %collective-permute-start.5 = (bf16[64,3584]{1,0:T(8,128)(2,1)S(1)}, bf16[64,3584]{1,0:T(8,128)(2,1)S(1)}, u32[]{:S(2)}, u32[]{:S(2)}) collective-permute-start(bf16[64,3584]{1,0:T(8,128)(2,1)S(1)} %broadcast_select_fusion.1.mine_ref), channel_id=1, source_target_pairs={{0,16},{16,0},{1,17},{17,1},{2,18},{18,2},{3,19},{19,3},{4,20},{20... | collective-permute-start | bytes 1376264 | tf_op jit(solution)/shard_map/ppermute | solution.py:314
  39.6 1.5 %shard_map.94 = (f32[8,256]{1,0:T(8,128)S(1)}, bf16[4,256,128]{2,1,0:T(8,128)(2,1)S(1)}) custom-call(bf16[64,256]{1,0:T(8,128)(2,1)S(1)} %pad_maximum_fusion.2.refs_0_, bf16[64,256]{1,0:T(8,128)(2,1)S(1)} %collective-permute-done.7.refs_1_, bf16[64,256]{1,0:T(8,128)(2,1)S(1)} %collective-permute-done.8.refs_2_, ...), custom_call_target="tpu_custom_call" | custom-call | flops 1 | bytes 1 | tf_op jit(solution)/shard_map/pallas_call | solution.py:253
  41.1 4.0 %shard_map.95.before_ref = f32[8,256]{1,0:T(8,128)S(1)} custom-call(bf16[768,7168]{1,0:T(8,128)(2,1)S(1)} %get-tuple-element.24.acts_ref, bf16[64,3584]{1,0:T(8,128)(2,1)S(1)} %collective-permute-done.1.mine_ref, bf16[64,3584]{1,0:T(8,128)(2,1)S(1)} %broadcast_select_fusion.theirs_ref, bf16[4,256,128]{2,1,0:T(8,128)(2,1)S(1)} %get-tuple-element.33.weights_ref, ...), custom_call_target="tpu_custom_call" | custom-call | flops 1 | bytes 1 | tf_op jit(solution)/shard_map/pallas_call | solution.py:253
  45.2 2.4 %collective-permute-done.11.mine_ref = bf16[64,3584]{1,0:T(8,128)(2,1)S(1)} collective-permute-done((bf16[64,3584]{1,0:T(8,128)(2,1)S(1)}, bf16[64,3584]{1,0:T(8,128)(2,1)S(1)}, u32[]{:S(2)}, u32[]{:S(2)}) %collective-permute-start.11) | collective-permute-done | bytes 458784 | tf_op jit(solution)/shard_map/ppermute | solution.py:311
  47.6 1.3 %collective-permute-start.12 = (bf16[64,1792]{1,0:T(8,128)(2,1)S(1)}, bf16[64,1792]{1,0:T(8,128)(2,1)S(1)}, u32[]{:S(2)}, u32[]{:S(2)}) collective-permute-start(bf16[64,1792]{1,0:T(8,128)(2,1)S(1)} %slice.56), channel_id=1, source_target_pairs={{0,16},{16,0},{1,17},{17,1},{2,18},{18,2},{3,19},{19,3},{4,20},{20... | collective-permute-start | bytes 688136 | tf_op jit(solution)/shard_map/ppermute | solution.py:314
  48.9 1.5 %collective-permute-start.10 = (bf16[64,1792]{1,0:T(8,128)(2,1)S(1)}, bf16[64,1792]{1,0:T(8,128)(2,1)S(1)}, u32[]{:S(2)}, u32[]{:S(2)}) collective-permute-start(bf16[64,1792]{1,0:T(8,128)(2,1)S(1)} %slice.55), channel_id=1, source_target_pairs={{0,4},{4,0},{8,12},{12,8},{1,5},{5,1},{9,13},{13,9},{2,6},{6,2},{1... | collective-permute-start | bytes 688136 | tf_op jit(solution)/shard_map/ppermute | solution.py:311
  50.4 1.9 %shard_map.96.total_ref = f32[768,128]{1,0:T(8,128)S(1)} custom-call(bf16[768,7168]{1,0:T(8,128)(2,1)S(1)} %get-tuple-element.24.acts_ref, bf16[64,3584]{1,0:T(8,128)(2,1)S(1)} %collective-permute-done.11.mine_ref), custom_call_target="tpu_custom_call" | custom-call | flops 1 | bytes 1 | tf_op jit(solution)/shard_map/pallas_call | solution.py:253
  52.4 4.0 %shard_map.97.before_ref = f32[8,256]{1,0:T(8,128)S(1)} custom-call(bf16[768,7168]{1,0:T(8,128)(2,1)S(1)} %get-tuple-element.24.acts_ref, bf16[64,3584]{1,0:T(8,128)(2,1)S(1)} %broadcast_select_fusion.1.mine_ref, bf16[64,3584]{1,0:T(8,128)(2,1)S(1)} %collective-permute-done.5.theirs_ref, bf16[4,256,128]{2,1,0:T(8,128)(2,1)S(1)} %get-tuple-element.33.weights_ref, ...), custom_call_target="tpu_custom_call" | custom-call | flops 1 | bytes 1 | tf_op jit(solution)/shard_map/pallas_call | solution.py:253
  56.3 0.0 collective-permute-done.10.left_ref
  56.4 2.8 %shard_map.98 = f32[16,2]{1,0:T(8,128)S(1)} custom-call(bf16[768,7168]{1,0:T(8,128)(2,1)S(1)} %get-tuple-element.24.acts_ref, bf16[64,1792]{1,0:T(8,128)(2,1)S(1)} %collective-permute-done.10.left_ref, bf16[64,1792]{1,0:T(8,128)(2,1)S(1)} %collective-permute-done.12.right_ref, f32[768,128]{1,0:T(8,128)S(1)} %shard_map.96.total_ref, ...), custom_call_target="tpu_custom_call" | custom-call | flops 1 | bytes 1 | tf_op jit(solution)/shard_map/pallas_call | solution.py:253
  59.2 9.0 %all_to_all.9 = f32[16,1,2]{2,1,0:T(1,128)S(1)} all-to-all(f32[16,1,2]{2,1,0:T(1,128)S(1)} %bitcast.4), channel_id=1, replica_groups=mesh['groups'=2,'blk'=4,'eig'=2,'rep'=2] {'blk','eig','rep'}, dimensions={0} | all-to-all | bytes 256 | tf_op jit(solution)/shard_map/all_to_all | solution.py:418
  68.1 0.5 reduce_sum.21
  (26 shorter events, 0.4 us)
Async XLA Ops:
  0.0 14.6 %copy-start = (bf16[64,7168]{1,0:T(8,128)(2,1)S(1)}, bf16[64,7168]{1,0:T(8,128)(2,1)}, u32[]{:S(2)}) copy-start(bf16[64,7168]{1,0:T(8,128)(2,1)} %own_ref.1) | copy-start | bytes 2752516
  1.3 23.6 %copy-start.1 = (bf16[64,128]{1,0:T(8,128)(2,1)S(1)}, bf16[64,128]{1,0:T(8,128)(2,1)}, u32[]{:S(2)}) copy-start(bf16[64,128]{1,0:T(8,128)(2,1)} %param.13) | copy-start | bytes 49156
  1.3 20.6 %collective-permute-start.2 = (bf16[64,3584]{1,0:T(8,128)(2,1)S(1)}, bf16[64,3584]{1,0:T(8,128)(2,1)}, u32[]{:S(2)}, u32[]{:S(2)}) collective-permute-start(bf16[64,3584]{1,0:T(8,128)(2,1)S(1)} %get-tuple-element.21), channel_id=1, source_target_pairs={{0,1},{1,0},{2,3},{3,2},{4,8},{5,9},{6,10},{7,11},{8,4},{9,5},{10,... | collective-permute-start | bytes 1376264 | tf_op jit(solution)/shard_map/ppermute | solution.py:317
  1.8 20.1 %collective-permute-start.1 = (bf16[64,3584]{1,0:T(8,128)(2,1)S(1)}, bf16[64,3584]{1,0:T(8,128)(2,1)S(1)}, u32[]{:S(2)}, u32[]{:S(2)}) collective-permute-start(bf16[64,3584]{1,0:T(8,128)(2,1)S(1)} %get-tuple-element.21), channel_id=1, source_target_pairs={{0,4},{4,0},{8,12},{12,8},{1,5},{5,1},{9,13},{13,9},{2,6},{6,2},{1... | collective-permute-start | bytes 1376264 | tf_op jit(solution)/shard_map/ppermute | solution.py:311
  11.2 1.8 %collective-permute-start = (bf16[1152,128]{1,0:T(8,128)(2,1)}, bf16[1152,128]{1,0:T(8,128)(2,1)S(1)}, u32[]{:S(2)}, u32[]{:S(2)}) collective-permute-start(bf16[1152,128]{1,0:T(8,128)(2,1)} %pad_maximum_fusion), channel_id=1, source_target_pairs={{0,1},{1,0},{2,3},{3,2},{4,5},{5,4},{6,7},{7,6},{8,9},{9,8},{10,11... | collective-permute-start | bytes 884744 | tf_op jit(solution)/shard_map/ppermute | solution.py:329
  13.1 11.7 %collective-permute-start.6 = (bf16[1152,128]{1,0:T(8,128)(2,1)S(1)}, bf16[1152,128]{1,0:T(8,128)(2,1)S(1)}, u32[]{:S(2)}, u32[]{:S(2)}) collective-permute-start(bf16[1152,128]{1,0:T(8,128)(2,1)S(1)} %pad_maximum_fusion.1), channel_id=1, source_target_pairs={{0,2},{2,0},{1,3},{3,1},{4,6},{6,4},{5,7},{7,5},{8,10},{10,8},{9,1... | collective-permute-start | bytes 884744 | tf_op jit(solution)/shard_map/ppermute | solution.py:332
  21.9 12.3 %collective-permute-start.3 = (bf16[64,3584]{1,0:T(8,128)(2,1)S(1)}, bf16[64,3584]{1,0:T(8,128)(2,1)S(1)}, u32[]{:S(2)}, u32[]{:S(2)}) collective-permute-start(bf16[64,3584]{1,0:T(8,128)(2,1)S(1)} %collective-permute-done.1.mine_ref), channel_id=1, source_target_pairs={{0,16},{1,17},{2,18},{3,19},{4,8},{5,9},{6,10},{7,11},{8,4},{9,5},... | collective-permute-start | bytes 1376264 | tf_op jit(solution)/shard_map/ppermute | solution.py:317
  23.6 13.5 %collective-permute-start.4 = (bf16[64,3584]{1,0:T(8,128)(2,1)S(1)}, bf16[64,3584]{1,0:T(8,128)(2,1)S(1)}, u32[]{:S(2)}, u32[]{:S(2)}) collective-permute-start(bf16[64,3584]{1,0:T(8,128)(2,1)S(1)} %broadcast_select_fusion.2), channel_id=1, source_target_pairs={{0,4},{4,0},{8,12},{12,8},{1,5},{5,1},{9,13},{13,9},{2,6},{6,2},{1... | collective-permute-start | bytes 1376264 | tf_op jit(solution)/shard_map/ppermute | solution.py:311
  24.9 14.7 %collective-permute-start.9 = (bf16[64,256]{1,0:T(8,128)(2,1)S(1)}, bf16[64,256]{1,0:T(8,128)(2,1)S(1)}, u32[]{:S(2)}, u32[]{:S(2)}) collective-permute-start(bf16[64,256]{1,0:T(8,128)(2,1)S(1)} %pad_maximum_fusion.2.refs_0_), channel_id=1, source_target_pairs={{0,12},{4,8},{8,4},{12,0},{1,13},{5,9},{9,5},{13,1},{2,14},{6,10},... | collective-permute-start | bytes 98312 | tf_op jit(solution)/shard_map/ppermute | solution.py:46
  26.2 13.4 %collective-permute-start.8 = (bf16[64,256]{1,0:T(8,128)(2,1)S(1)}, bf16[64,256]{1,0:T(8,128)(2,1)S(1)}, u32[]{:S(2)}, u32[]{:S(2)}) collective-permute-start(bf16[64,256]{1,0:T(8,128)(2,1)S(1)} %pad_maximum_fusion.2.refs_0_), channel_id=1, source_target_pairs={{0,8},{4,12},{8,0},{12,4},{1,9},{5,13},{9,1},{13,5},{2,10},{6,14},... | collective-permute-start | bytes 98312 | tf_op jit(solution)/shard_map/ppermute | solution.py:46
  27.3 12.3 %collective-permute-start.7 = (bf16[64,256]{1,0:T(8,128)(2,1)S(1)}, bf16[64,256]{1,0:T(8,128)(2,1)S(1)}, u32[]{:S(2)}, u32[]{:S(2)}) collective-permute-start(bf16[64,256]{1,0:T(8,128)(2,1)S(1)} %pad_maximum_fusion.2.refs_0_), channel_id=1, source_target_pairs={{0,4},{4,0},{8,12},{12,8},{1,5},{5,1},{9,13},{13,9},{2,6},{6,2},{1... | collective-permute-start | bytes 98312 | tf_op jit(solution)/shard_map/ppermute | solution.py:46
  37.1 10.5 %collective-permute-start.11 = (bf16[64,3584]{1,0:T(8,128)(2,1)S(1)}, bf16[64,3584]{1,0:T(8,128)(2,1)S(1)}, u32[]{:S(2)}, u32[]{:S(2)}) collective-permute-start(bf16[64,3584]{1,0:T(8,128)(2,1)S(1)} %broadcast_select_fusion.1.mine_ref), channel_id=1, source_target_pairs={{0,4},{4,0},{8,12},{12,8},{1,5},{5,1},{9,13},{13,9},{2,6},{6,2},{1... | collective-permute-start | bytes 1376264 | tf_op jit(solution)/shard_map/ppermute | solution.py:311
  38.0 10.9 %collective-permute-start.5 = (bf16[64,3584]{1,0:T(8,128)(2,1)S(1)}, bf16[64,3584]{1,0:T(8,128)(2,1)S(1)}, u32[]{:S(2)}, u32[]{:S(2)}) collective-permute-start(bf16[64,3584]{1,0:T(8,128)(2,1)S(1)} %broadcast_select_fusion.1.mine_ref), channel_id=1, source_target_pairs={{0,16},{16,0},{1,17},{17,1},{2,18},{18,2},{3,19},{19,3},{4,20},{20... | collective-permute-start | bytes 1376264 | tf_op jit(solution)/shard_map/ppermute | solution.py:314
  47.6 8.7 %collective-permute-start.12 = (bf16[64,1792]{1,0:T(8,128)(2,1)S(1)}, bf16[64,1792]{1,0:T(8,128)(2,1)S(1)}, u32[]{:S(2)}, u32[]{:S(2)}) collective-permute-start(bf16[64,1792]{1,0:T(8,128)(2,1)S(1)} %slice.56), channel_id=1, source_target_pairs={{0,16},{16,0},{1,17},{17,1},{2,18},{18,2},{3,19},{19,3},{4,20},{20... | collective-permute-start | bytes 688136 | tf_op jit(solution)/shard_map/ppermute | solution.py:314
  48.9 7.5 %collective-permute-start.10 = (bf16[64,1792]{1,0:T(8,128)(2,1)S(1)}, bf16[64,1792]{1,0:T(8,128)(2,1)S(1)}, u32[]{:S(2)}, u32[]{:S(2)}) collective-permute-start(bf16[64,1792]{1,0:T(8,128)(2,1)S(1)} %slice.55), channel_id=1, source_target_pairs={{0,4},{4,0},{8,12},{12,8},{1,5},{5,1},{9,13},{13,9},{2,6},{6,2},{1... | collective-permute-start | bytes 688136 | tf_op jit(solution)/shard_map/ppermute | solution.py:311

commit v5 on v4

--- a/solution.py
+++ b/solution.py
@@ -134,7 +134,7 @@
     )(*[in_hbm(source) for source in sources])
 
 
-def weigh(query_count, packs, out_query, weighted_ref):
+def weigh(query_count, packs, out_query, weights_ref):
     rows, pairs = packs[0].shape[0], out_query.shape[1]
     query_of = lax.broadcasted_iota(jnp.int32, (rows, pairs), 1) // R
     for slot, pack_ref in enumerate(packs):
@@ -143,19 +143,17 @@
         for query in range(query_count):
             own = jnp.where(query_of == query, in_query, 0.0).astype(jnp.bfloat16)
             outer_sum = contract_last(own, out_query)
-            weighted_ref[slot, pl.ds(query * rows, rows), :] = (outer_sum * inverse).astype(
-                jnp.bfloat16
-            )
-
-
-def project(acts_ref, start, piece, group, first=0):
-    rows, width = piece.shape
-    columns = slice(None)
-    if width < acts_ref.shape[1]:
-        half = acts_ref.shape[1] // 2
-        columns = pl.ds(pl.multiple_of(group * half + first, LANES), width)
-    repeated = jnp.concatenate([piece[...]] * (LANES // rows), axis=0)
-    return contract_last(acts_ref[pl.ds(start, BLOCK), columns], repeated)
+            weights_ref[slot // 2, pl.ds((2 * query + slot % 2) * rows, rows), :] = (
+                outer_sum * inverse
+            ).astype(jnp.bfloat16)
+
+
+def project(acts_ref, start, pieces, group, first=0):
+    columns = pl.ds(
+        pl.multiple_of(group * (acts_ref.shape[1] // 2) + first, LANES), pieces[0].shape[1]
+    )
+    stacked = jnp.concatenate([piece[...] for piece in pieces], axis=0)
+    return contract_last(acts_ref[pl.ds(start, BLOCK), columns], stacked)
 
 
 def mix(start, projected, weights, grad_ref, onehot_ref):
@@ -169,14 +167,14 @@
     )
 
 
-def blocks(acts_or_projected, body, initial):
+def blocks(tokens, body, initial):
     def step(index, carry):
         return body(pl.multiple_of(index * BLOCK, LANES), carry)
 
-    return lax.fori_loop(0, acts_or_projected.shape[0] // BLOCK, step, initial)
-
-
-def first_kernel(source_ref, own_ref, acts_ref, total_ref, copied):
+    return lax.fori_loop(0, tokens // BLOCK, step, initial)
+
+
+def load_kernel(source_ref, acts_ref, copied):
     copies = [
         pltpu.make_async_copy(
             source_ref.at[pl.ds(start, BLOCK)], acts_ref.at[pl.ds(start, BLOCK)], copied.at[place]
@@ -185,66 +183,66 @@
     ]
     for copy in copies:
         copy.start()
-    for place, copy in enumerate(copies):
+    for copy in copies:
         copy.wait()
-        start = place * BLOCK
-        total_ref[pl.ds(start, BLOCK), :] = project(acts_ref, start, own_ref, 0)
 
 
 def weight_kernel(query_count, *refs):
-    packs, refs = refs[:4], refs[4:]
-    out_query_ref, grad_ref, onehot_ref, total_ref, sums_ref, weights_ref = refs
+    packs, (out_query_ref, weights_ref) = refs[:4], refs[4:]
     weigh(query_count, packs, out_query_ref[...], weights_ref)
+
+
+def first_kernel(
+    acts_ref, half_ref, mine_ref, other_half_ref, theirs_ref, weights_ref, grad_ref, onehot_ref,
+    sums_ref,
+):
+    group = lax.axis_index("groups")
+
+    def body(start, sums):
+        total = project(acts_ref, start, (half_ref, mine_ref), group)
+        total = total + project(acts_ref, start, (other_half_ref, theirs_ref), 1 - group)
+        return sums + mix(start, total, weights_ref[0], grad_ref, onehot_ref)
+
+    sums_ref[...] = blocks(acts_ref.shape[0], body, jnp.zeros(sums_ref.shape, jnp.float32))
+
+
+def mine_kernel(acts_ref, mine_2_ref, mine_3_ref, total_ref):
+    group = lax.axis_index("groups")
+
+    def body(start, carry):
+        total_ref[pl.ds(start, BLOCK), :] = project(
+            acts_ref, start, (mine_2_ref, mine_3_ref), group
+        )
+        return carry
+
+    blocks(acts_ref.shape[0], body, 0)
+
+
+def last_kernel(
+    query_count, acts_ref, theirs_2_ref, left_ref, right_ref, total_ref, weights_ref, grad_ref,
+    onehot_ref, before_ref, out_ref,
+):
+    other = 1 - lax.axis_index("groups")
+    cut = left_ref.shape[1]
 
     def body(start, sums):
         total = total_ref[pl.ds(start, BLOCK), :]
-        return sums + mix(start, total, weights_ref[0], grad_ref, onehot_ref)
-
-    sums_ref[...] = blocks(total_ref, body, jnp.zeros(sums_ref.shape, jnp.float32))
-
-
-def slot_kernel(
-    slot, acts_ref, mine_ref, theirs_ref, weights_ref, grad_ref, onehot_ref, before_ref, sums_ref
-):
-    group = lax.axis_index("groups")
-
-    def body(start, sums):
-        total = project(acts_ref, start, mine_ref, group)
-        total = total + project(acts_ref, start, theirs_ref, 1 - group)
-        return sums + mix(start, total, weights_ref[slot], grad_ref, onehot_ref)
-
-    sums_ref[...] = blocks(acts_ref, body, before_ref[...])
-
-
-def mine_kernel(acts_ref, mine_ref, total_ref):
-    group = lax.axis_index("groups")
-
-    def body(start, carry):
-        total_ref[pl.ds(start, BLOCK), :] = project(acts_ref, start, mine_ref, group)
-        return carry
-
-    blocks(acts_ref, body, 0)
-
-
-def last_kernel(
-    queries, acts_ref, left_ref, right_ref, total_ref, weights_ref, grad_ref, onehot_ref, before_ref, out_ref
-):
-    other = 1 - lax.axis_index("groups")
-
-    def body(start, sums):
-        total = total_ref[pl.ds(start, BLOCK), :]
-        total = total + project(acts_ref, start, left_ref, other)
-        total = total + project(acts_ref, start, right_ref, other, left_ref.shape[1])
-        return sums + mix(start, total, weights_ref[3], grad_ref, onehot_ref)
-
-    sums = blocks(acts_ref, body, before_ref[...])
+        total = total + project(
+            acts_ref, start, (theirs_2_ref.at[:, :cut], left_ref), other
+        )
+        total = total + project(
+            acts_ref, start, (theirs_2_ref.at[:, cut:], right_ref), other, cut
+        )
+        return sums + mix(start, total, weights_ref[1], grad_ref, onehot_ref)
+
+    sums = blocks(acts_ref.shape[0], body, before_ref[...])
     width = sums.shape[1]
-    query_of = lax.broadcasted_iota(jnp.int32, (queries, width), 1) // (width // queries)
-    chosen = query_of == lax.broadcasted_iota(jnp.int32, (queries, width), 0)
+    query_of = lax.broadcasted_iota(jnp.int32, (query_count, width), 1) // (width // query_count)
+    chosen = query_of == lax.broadcasted_iota(jnp.int32, (query_count, width), 0)
     scores = contract_last(chosen.astype(jnp.float32), sums, precision=lax.Precision.HIGHEST)
     columns = out_ref.shape[1]
-    for place in range(out_ref.shape[0] // queries):
-        out_ref[pl.ds(place * queries, queries), :] = scores[
+    for place in range(out_ref.shape[0] // query_count):
+        out_ref[pl.ds(place * query_count, query_count), :] = scores[
             :, place * columns : (place + 1) * columns
         ]
 
@@ -328,54 +326,49 @@
     part = small_parts(held(basis_in, half), query_in, basis_out, query_out, out_grads)
     other = lax.ppermute(to_send(part, split), "rep", pair)
     part = add_sent(part, other, split)
-    sent = to_send(part, split)
-    other = lax.ppermute(sent, "eig", pair)
-    total_shape = jax.ShapeDtypeStruct((tokens, LANES), jnp.float32)
-    acts, total = call(
-        first_kernel,
-        [pltpu.VMEM(acts.shape, acts.dtype), total_shape],
-        in_hbm(held(acts, sent)),
-        basis_in,
-        in_specs=[pl.BlockSpec(memory_space=pl.ANY), pl.BlockSpec(memory_space=pltpu.VMEM)],
-        scratch_shapes=[pltpu.SemaphoreType.DMA((tokens // BLOCK,))],
-    )
-    acts = in_vmem(acts)
-
-    middle_3 = held(middle_3, mine_1, total)
+    other = lax.ppermute(to_send(part, split), "eig", pair)
+    middle_3 = held(middle_3, mine_1)
     from_pair = along(jnp.where(inner, middle_3, other_half))
     from_across = across(held(mine_1, middle_3), lambda g, b, e, r: (1 - g, b, e, r))
     part = add_sent(part, held(other, mine_1), split).astype(jnp.bfloat16)
     in_query, out_query, grad_proj = part[:rows], part[rows:split], part[split:]
-    packs = by_distance(jnp.concatenate([in_query, eigvals], axis=1))
-
+    pack = jnp.concatenate([in_query, eigvals], axis=1)
+    packs = by_distance(pack)
+    acts = call(
+        load_kernel,
+        pltpu.VMEM(acts.shape, acts.dtype),
+        in_hbm(held(acts, pack)),
+        in_specs=[pl.BlockSpec(memory_space=pl.ANY)],
+        scratch_shapes=[pltpu.SemaphoreType.DMA((tokens // BLOCK,))],
+    )
+    acts = in_vmem(acts)
+
+    from_across = held(from_across, acts)
     mine_2 = jnp.where(inner, from_across, from_pair)
     theirs_2 = swapped(mine_2)
     mine_3 = along(mine_2)
     theirs_1 = jnp.where(inner, held(from_pair, mine_2), held(from_across, mine_2))
-    sums_shape = jax.ShapeDtypeStruct((seq_count, query_count * rows), jnp.float32)
-    weights_shape = jax.ShapeDtypeStruct((4, query_count * rows, width), jnp.bfloat16)
-    sums, weights = call(
+    weights = call(
         functools.partial(weight_kernel, query_count),
-        [sums_shape, weights_shape],
-        *packs, held(out_query, mine_2), grad_proj, onehot, total,
+        jax.ShapeDtypeStruct((2, 2 * query_count * rows, width), jnp.bfloat16),
+        *packs, held(out_query, mine_2),
     )
     fixed = (weights, grad_proj, onehot)
     sums = call(
-        functools.partial(slot_kernel, 1), sums_shape, acts, mine_1, theirs_1, *fixed, sums
+        first_kernel,
+        jax.ShapeDtypeStruct((seq_count, 2 * query_count * rows), jnp.float32),
+        acts, half, mine_1, other_half, theirs_1, *fixed,
     )
 
     cut = mine_3.shape[1] // 2
     left_3 = along(held(theirs_2, sums)[:, :cut])
     right_3 = swapped(held(mine_3, sums)[:, cut:])
-    sums = call(
-        functools.partial(slot_kernel, 2), sums_shape, acts, mine_2, theirs_2, *fixed, sums
-    )
-    total = call(mine_kernel, total_shape, acts, mine_3)
+    total = call(mine_kernel, jax.ShapeDtypeStruct((tokens, LANES), jnp.float32), acts, mine_2, mine_3)
     places = lax.axis_size("blk")
     return call(
         functools.partial(last_kernel, query_count),
         jax.ShapeDtypeStruct((places * query_count, seq_count // places), jnp.float32),
-        acts, left_3, right_3, total, *fixed, sums,
+        acts, theirs_2, left_3, right_3, total, *fixed, sums,
     )
 
 
@@ -405,8 +398,7 @@
     onehot = (labels[:, None] == column_of[None, :]).astype(jnp.bfloat16)
     stepped = (
         all(lax.axis_size(axis) == size for axis, size in zip(AXES, (2, 4, 2, 2)))
-        and LANES % rows == 0
-        and (pairs // R * rows) % LANES == 0
+        and 2 * rows == LANES
         and features % (4 * LANES) == 0
         and acts.shape[0] % BLOCK == 0
         and pairs == basis_out.shape[0] == LANES

time: 68.9 us -> 64.4 us (0.935)
  Pallas kernels: 27.2 us -> 19.9 us
  starting transfers between devices: 18.7 us -> 21.3 us
  blocking collectives: 8.98 us -> 11.3 us
  waiting for transfers between devices: 11.1 us -> 9.76 us
  other arithmetic: 2.45 us -> 1.73 us
    pallas_call x6 -> x5, Pallas kernels: 21.5 us -> 14.2 us  [call(): pl.pallas_call(kernel, out_shape=out_shape, compiler_params=pltpu.Compile...]
    ppermute x2, waiting for transfers between devices: 4.86 us -> 0.01 us  [across(): lax.ppermute(value, AXES, pairing(lambda g, b, e, r: (g, 3 - b, e, r) if...]
    ppermute x4, starting transfers between devices: 7.8 us -> 10.1 us  [along(): return lax.ppermute(value, 'blk', [(i, i ^ 1) for i in range(4)])]
    all_to_all x1, blocking collectives: 8.98 us -> 11.3 us  [on_device(): parts = lax.all_to_all(parts, ('blk', 'eig', 'rep'), 0, 0, tiled=True)]
    ppermute x1, waiting for transfers between devices: 0.01 us -> 1.79 us  [stepped_scores(): other = lax.ppermute(to_send(part, split), 'eig', pair)]
    ppermute x2, waiting for transfers between devices: 0.01 us -> 1 us  [swapped(): return lax.ppermute(value, 'groups', pair)]
    ppermute x4, waiting for transfers between devices: 5.22 us -> 6.19 us  [along(): return lax.ppermute(value, 'blk', [(i, i ^ 1) for i in range(4)])]
    concatenate x2, other arithmetic: 0.75 us -> 0.04 us  [to_send(): jnp.concatenate([high, low, part[split:]], axis=0).astype(jnp.bfloat16)]
  transfers between devices with their start and end apart: 13 -> 13, of which waited for: 4 -> 6; matrix products, arithmetic and copies ran while one was open for 3% -> 2% of each run, Pallas kernels for 34% -> 24%
where the time goes in v5:
time: 64.4 us; the launch traced here: 64.2 us
  starting transfers between devices  21.3 us (33%)
  Pallas kernels  19.9 us (31%)
  blocking collectives  11.3 us (18%)
  waiting for transfers between devices  9.76 us (15%)
  other arithmetic  1.73 us (3%)
    pallas_call x5, Pallas kernels, call(): pl.pallas_call(kernel, out_shape=out_shape, compiler_params=pltpu.Compile...  14.2 us
    all_to_all x1, blocking collectives, on_device(): parts = lax.all_to_all(parts, ('blk', 'eig', 'rep'), 0, 0, tiled=True)  11.3 us
    ppermute x4, starting transfers between devices, along(): return lax.ppermute(value, 'blk', [(i, i ^ 1) for i in range(4)])  10.1 us
    ppermute x4, waiting for transfers between devices, along(): return lax.ppermute(value, 'blk', [(i, i ^ 1) for i in range(4)])  6.19 us
    ppermute x3, starting transfers between devices, by_distance(): lax.ppermute(value, axis, [(i, i ^ k) for i in range(size)])  4.45 us
    pallas_call x1, Pallas kernels, small_parts(): pl.pallas_call(parts_kernel, in_specs=[pl.BlockSpec(memory_space=pl.ANY)]...  4.44 us
    ppermute x2, starting transfers between devices, swapped(): return lax.ppermute(value, 'groups', pair)  3.1 us
    ppermute x2, starting transfers between devices, across(): lax.ppermute(value, AXES, pairing(lambda g, b, e, r: (g, 3 - b, e, r) if...  2.04 us
  transfers between devices with their start and end apart: 13, of which 6 were waited for; matrix products, arithmetic and copies ran while one was open for 2% of the time, Pallas kernels for 24%

profile of v5, /device:TPU:0, one launch (start us, length us, event | category | flops | bytes accessed | tf_op | source)
XLA Modules:
  0.0 64.2 jit_solution(17895164314286454622)
XLA Ops:
  0.0 1.2 %shard_map.91 = (bf16[64,3584]{1,0:T(8,128)(2,1)S(1)}, bf16[64,3584]{1,0:T(8,128)(2,1)S(1)}) custom-call(bf16[64,7168]{1,0:T(8,128)(2,1)} %refs_2_), custom_call_target="tpu_custom_call" | custom-call | tf_op jit(solution)/shard_map/pallas_call | solution.py:88
  1.2 0.5 collective-permute-start.3
  1.7 4.1 %collective-permute-start.2 = (bf16[64,3584]{1,0:T(8,128)(2,1)S(1)}, bf16[64,3584]{1,0:T(8,128)(2,1)S(1)}, u32[]{:S(2)}, u32[]{:S(2)}) collective-permute-start(bf16[64,3584]{1,0:T(8,128)(2,1)S(1)} %get-tuple-element.18.half_ref), channel_id=1, source_target_pairs={{0,4},{4,0},{8,12},{12,8},{1,5},{5,1},{9,13},{13,9},{2,6},{6,2},{1... | collective-permute-start | bytes 1376264 | tf_op jit(solution)/shard_map/ppermute | solution.py:309
  5.9 4.4 %shard_map.92 = f32[960,128]{1,0:T(8,128)S(1)} custom-call(bf16[128,2048]{1,0:T(8,128)(2,1)} %refs_0_.1, bf16[2048,128]{1,0:T(8,128)(2,1)} %refs_1_.1, bf16[64,7168]{1,0:T(8,128)(2,1)} %refs_2_, bf16[7168,128]{1,0:T(8,128)(2,1)} %refs_3_.1, bf16[768,2048]{1,0:T(8,128)(2,1)} %refs_4_.1), custom_call_target="tpu_custom_call" | custom-call | tf_op jit(solution)/shard_map/pallas_call | solution.py:127
  10.4 0.1 collective-permute-start
  10.5 0.8 %select_reduce_fusion = s32[768]{0:T(1024)S(1)} fusion(s32[8]{0:T(128)} %param.17, s32[768]{0:T(1024)} %param.16), kind=kLoop, calls=%fused_computation.18 | loop fusion | flops 17664 | bytes 6176 | tf_op jit(solution)/shard_map/reduce_sum | solution.py:397
  11.3 0.8 %collective-permute-done = bf16[1152,128]{1,0:T(8,128)(2,1)S(1)} collective-permute-done((bf16[1152,128]{1,0:T(8,128)(2,1)S(1)}, bf16[1152,128]{1,0:T(8,128)(2,1)S(1)}, u32[]{:S(2)}, u32[]{:S(2)}) %collective-permute-start) | collective-permute-done | bytes 294944 | tf_op jit(solution)/shard_map/ppermute | solution.py:327
  12.2 1.6 %collective-permute-start.1 = (bf16[1152,128]{1,0:T(8,128)(2,1)S(1)}, bf16[1152,128]{1,0:T(8,128)(2,1)S(1)}, u32[]{:S(2)}, u32[]{:S(2)}) collective-permute-start(bf16[1152,128]{1,0:T(8,128)(2,1)S(1)} %pad_maximum_fusion.1), channel_id=1, source_target_pairs={{0,2},{2,0},{1,3},{3,1},{4,6},{6,4},{5,7},{7,5},{8,10},{10,8},{9,1... | collective-permute-start | bytes 884744 | tf_op jit(solution)/shard_map/ppermute | solution.py:329
  13.7 2.4 %collective-permute-done.2.mine_ref = bf16[64,3584]{1,0:T(8,128)(2,1)S(1)} collective-permute-done((bf16[64,3584]{1,0:T(8,128)(2,1)S(1)}, bf16[64,3584]{1,0:T(8,128)(2,1)S(1)}, u32[]{:S(2)}, u32[]{:S(2)}) %collective-permute-start.2) | collective-permute-done | bytes 458784 | tf_op jit(solution)/shard_map/ppermute | solution.py:309
  16.1 1.8 %collective-permute-start.5 = (bf16[64,3584]{1,0:T(8,128)(2,1)S(1)}, bf16[64,3584]{1,0:T(8,128)(2,1)S(1)}, u32[]{:S(2)}, u32[]{:S(2)}) collective-permute-start(bf16[64,3584]{1,0:T(8,128)(2,1)S(1)} %broadcast_select_fusion.2), channel_id=1, source_target_pairs={{0,4},{4,0},{8,12},{12,8},{1,5},{5,1},{9,13},{13,9},{2,6},{6,2},{1... | collective-permute-start | bytes 1376264 | tf_op jit(solution)/shard_map/ppermute | solution.py:309
  18.0 1.5 %collective-permute-start.4 = (bf16[64,3584]{1,0:T(8,128)(2,1)S(1)}, bf16[64,3584]{1,0:T(8,128)(2,1)S(1)}, u32[]{:S(2)}, u32[]{:S(2)}) collective-permute-start(bf16[64,3584]{1,0:T(8,128)(2,1)S(1)} %collective-permute-done.2.mine_ref), channel_id=1, source_target_pairs={{0,16},{1,17},{2,18},{3,19},{4,8},{5,9},{6,10},{7,11},{8,4},{9,5},... | collective-permute-start | bytes 1376264 | tf_op jit(solution)/shard_map/ppermute | solution.py:315
  19.5 1.8 %collective-permute-done.1 = bf16[1152,128]{1,0:T(8,128)(2,1)S(1)} collective-permute-done((bf16[1152,128]{1,0:T(8,128)(2,1)S(1)}, bf16[1152,128]{1,0:T(8,128)(2,1)S(1)}, u32[]{:S(2)}, u32[]{:S(2)}) %collective-permute-start.1) | collective-permute-done | bytes 294944 | tf_op jit(solution)/shard_map/ppermute | solution.py:329
  21.4 1.4 %collective-permute-start.9 = (bf16[64,256]{1,0:T(8,128)(2,1)S(1)}, bf16[64,256]{1,0:T(8,128)(2,1)S(1)}, u32[]{:S(2)}, u32[]{:S(2)}) collective-permute-start(bf16[64,256]{1,0:T(8,128)(2,1)S(1)} %pad_maximum_fusion.2.refs_0_), channel_id=1, source_target_pairs={{0,12},{4,8},{8,4},{12,0},{1,13},{5,9},{9,5},{13,1},{2,14},{6,10},... | collective-permute-start | bytes 98312 | tf_op jit(solution)/shard_map/ppermute | solution.py:46
  22.8 0.1 collective-permute-start.8
  22.9 2.9 %collective-permute-start.7 = (bf16[64,256]{1,0:T(8,128)(2,1)S(1)}, bf16[64,256]{1,0:T(8,128)(2,1)S(1)}, u32[]{:S(2)}, u32[]{:S(2)}) collective-permute-start(bf16[64,256]{1,0:T(8,128)(2,1)S(1)} %pad_maximum_fusion.2.refs_0_), channel_id=1, source_target_pairs={{0,4},{4,0},{8,12},{12,8},{1,5},{5,1},{9,13},{13,9},{2,6},{6,2},{1... | collective-permute-start | bytes 98312 | tf_op jit(solution)/shard_map/ppermute | solution.py:46
  25.8 4.2 %shard_map.93.acts_ref = bf16[768,7168]{1,0:T(8,128)(2,1)S(1)} custom-call(bf16[768,7168]{1,0:T(8,128)(2,1)} %source_ref), custom_call_target="tpu_custom_call" | custom-call | flops 1 | bytes 1 | tf_op jit(solution)/shard_map/pallas_call | solution.py:251
  30.0 0.1 add_convert_fusion.grad_ref
  30.1 0.1 broadcast_select_fusion.1.mine_2_ref
  30.2 2.6 %collective-permute-start.11 = (bf16[64,3584]{1,0:T(8,128)(2,1)S(1)}, bf16[64,3584]{1,0:T(8,128)(2,1)S(1)}, u32[]{:S(2)}, u32[]{:S(2)}) collective-permute-start(bf16[64,3584]{1,0:T(8,128)(2,1)S(1)} %broadcast_select_fusion.1.mine_2_ref), channel_id=1, source_target_pairs={{0,4},{4,0},{8,12},{12,8},{1,5},{5,1},{9,13},{13,9},{2,6},{6,2},{1... | collective-permute-start | bytes 1376264 | tf_op jit(solution)/shard_map/ppermute | solution.py:309
  32.8 1.5 %collective-permute-start.6 = (bf16[64,3584]{1,0:T(8,128)(2,1)S(1)}, bf16[64,3584]{1,0:T(8,128)(2,1)S(1)}, u32[]{:S(2)}, u32[]{:S(2)}) collective-permute-start(bf16[64,3584]{1,0:T(8,128)(2,1)S(1)} %broadcast_select_fusion.1.mine_2_ref), channel_id=1, source_target_pairs={{0,16},{16,0},{1,17},{17,1},{2,18},{18,2},{3,19},{19,3},{4,20},{20... | collective-permute-start | bytes 1376264 | tf_op jit(solution)/shard_map/ppermute | solution.py:312
  34.4 0.0 collective-permute-done.9.refs_3_
  34.4 0.5 shard_map.94.weights_ref
  34.9 4.5 %shard_map.95.before_ref = f32[8,512]{1,0:T(8,128)S(1)} custom-call(bf16[768,7168]{1,0:T(8,128)(2,1)S(1)} %shard_map.93.acts_ref, bf16[64,3584]{1,0:T(8,128)(2,1)S(1)} %get-tuple-element.18.half_ref, bf16[64,3584]{1,0:T(8,128)(2,1)S(1)} %collective-permute-done.2.mine_ref, bf16[64,3584]{1,0:T(8,128)(2,1)S(1)} %get-tuple-element.25.other_half_ref, ...), custom_call_target="tpu_custom_call" | custom-call | flops 1 | bytes 1 | tf_op jit(solution)/shard_map/pallas_call | solution.py:251
  39.3 2.2 %collective-permute-done.11.mine_3_ref = bf16[64,3584]{1,0:T(8,128)(2,1)S(1)} collective-permute-done((bf16[64,3584]{1,0:T(8,128)(2,1)S(1)}, bf16[64,3584]{1,0:T(8,128)(2,1)S(1)}, u32[]{:S(2)}, u32[]{:S(2)}) %collective-permute-start.11) | collective-permute-done | bytes 458784 | tf_op jit(solution)/shard_map/ppermute | solution.py:309
  41.5 1.6 %collective-permute-start.12 = (bf16[64,1792]{1,0:T(8,128)(2,1)S(1)}, bf16[64,1792]{1,0:T(8,128)(2,1)S(1)}, u32[]{:S(2)}, u32[]{:S(2)}) collective-permute-start(bf16[64,1792]{1,0:T(8,128)(2,1)S(1)} %slice.56), channel_id=1, source_target_pairs={{0,16},{16,0},{1,17},{17,1},{2,18},{18,2},{3,19},{19,3},{4,20},{20... | collective-permute-start | bytes 688136 | tf_op jit(solution)/shard_map/ppermute | solution.py:312
  43.1 1.6 %collective-permute-start.10 = (bf16[64,1792]{1,0:T(8,128)(2,1)S(1)}, bf16[64,1792]{1,0:T(8,128)(2,1)S(1)}, u32[]{:S(2)}, u32[]{:S(2)}) collective-permute-start(bf16[64,1792]{1,0:T(8,128)(2,1)S(1)} %slice.55), channel_id=1, source_target_pairs={{0,4},{4,0},{8,12},{12,8},{1,5},{5,1},{9,13},{13,9},{2,6},{6,2},{1... | collective-permute-start | bytes 688136 | tf_op jit(solution)/shard_map/ppermute | solution.py:309
  44.7 1.9 %shard_map.96.total_ref = f32[768,128]{1,0:T(8,128)S(1)} custom-call(bf16[768,7168]{1,0:T(8,128)(2,1)S(1)} %shard_map.93.acts_ref, bf16[64,3584]{1,0:T(8,128)(2,1)S(1)} %broadcast_select_fusion.1.mine_2_ref, bf16[64,3584]{1,0:T(8,128)(2,1)S(1)} %collective-permute-done.11.mine_3_ref), custom_call_target="tpu_custom_call" | custom-call | flops 1 | bytes 1 | tf_op jit(solution)/shard_map/pallas_call | solution.py:251
  46.6 1.0 %collective-permute-done.12.right_ref = bf16[64,1792]{1,0:T(8,128)(2,1)S(1)} collective-permute-done((bf16[64,1792]{1,0:T(8,128)(2,1)S(1)}, bf16[64,1792]{1,0:T(8,128)(2,1)S(1)}, u32[]{:S(2)}, u32[]{:S(2)}) %collective-permute-start.12) | collective-permute-done | bytes 229408 | tf_op jit(solution)/shard_map/ppermute | solution.py:312
  47.6 1.6 %collective-permute-done.10.left_ref = bf16[64,1792]{1,0:T(8,128)(2,1)S(1)} collective-permute-done((bf16[64,1792]{1,0:T(8,128)(2,1)S(1)}, bf16[64,1792]{1,0:T(8,128)(2,1)S(1)}, u32[]{:S(2)}, u32[]{:S(2)}) %collective-permute-start.10) | collective-permute-done | bytes 229408 | tf_op jit(solution)/shard_map/ppermute | solution.py:309
  49.2 3.2 %shard_map.97 = f32[16,2]{1,0:T(8,128)S(1)} custom-call(bf16[768,7168]{1,0:T(8,128)(2,1)S(1)} %shard_map.93.acts_ref, bf16[64,3584]{1,0:T(8,128)(2,1)S(1)} %collective-permute-done.6.theirs_2_ref, bf16[64,1792]{1,0:T(8,128)(2,1)S(1)} %collective-permute-done.10.left_ref, bf16[64,1792]{1,0:T(8,128)(2,1)S(1)} %collective-permute-done.12.right_ref, ...), custom_call_target="tpu_custom_call" | custom-call | flops 1 | bytes 1 | tf_op jit(solution)/shard_map/pallas_call | solution.py:251
  52.4 11.3 %all_to_all.9 = f32[16,1,2]{2,1,0:T(1,128)S(1)} all-to-all(f32[16,1,2]{2,1,0:T(1,128)S(1)} %bitcast.4), channel_id=1, replica_groups=mesh['groups'=2,'blk'=4,'eig'=2,'rep'=2] {'blk','eig','rep'}, dimensions={0} | all-to-all | bytes 256 | tf_op jit(solution)/shard_map/all_to_all | solution.py:410
  63.7 0.5 reduce_sum.21
  (23 shorter events, 0.4 us)
Async XLA Ops:
  0.0 21.3 %copy-start = (bf16[64,128]{1,0:T(8,128)(2,1)S(1)}, bf16[64,128]{1,0:T(8,128)(2,1)}, u32[]{:S(2)}) copy-start(bf16[64,128]{1,0:T(8,128)(2,1)} %param.13) | copy-start | bytes 49156
  1.2 12.5 %collective-permute-start.3 = (bf16[64,3584]{1,0:T(8,128)(2,1)S(1)}, bf16[64,3584]{1,0:T(8,128)(2,1)S(1)}, u32[]{:S(2)}, u32[]{:S(2)}) collective-permute-start(bf16[64,3584]{1,0:T(8,128)(2,1)S(1)} %get-tuple-element.18.half_ref), channel_id=1, source_target_pairs={{0,1},{1,0},{2,3},{3,2},{4,8},{5,9},{6,10},{7,11},{8,4},{9,5},{10,... | collective-permute-start | bytes 1376264 | tf_op jit(solution)/shard_map/ppermute | solution.py:315
  1.7 14.4 %collective-permute-start.2 = (bf16[64,3584]{1,0:T(8,128)(2,1)S(1)}, bf16[64,3584]{1,0:T(8,128)(2,1)S(1)}, u32[]{:S(2)}, u32[]{:S(2)}) collective-permute-start(bf16[64,3584]{1,0:T(8,128)(2,1)S(1)} %get-tuple-element.18.half_ref), channel_id=1, source_target_pairs={{0,4},{4,0},{8,12},{12,8},{1,5},{5,1},{9,13},{13,9},{2,6},{6,2},{1... | collective-permute-start | bytes 1376264 | tf_op jit(solution)/shard_map/ppermute | solution.py:309
  10.4 1.6 %collective-permute-start = (bf16[1152,128]{1,0:T(8,128)(2,1)S(1)}, bf16[1152,128]{1,0:T(8,128)(2,1)S(1)}, u32[]{:S(2)}, u32[]{:S(2)}) collective-permute-start(bf16[1152,128]{1,0:T(8,128)(2,1)S(1)} %pad_maximum_fusion), channel_id=1, source_target_pairs={{0,1},{1,0},{2,3},{3,2},{4,5},{5,4},{6,7},{7,6},{8,9},{9,8},{10,11... | collective-permute-start | bytes 884744 | tf_op jit(solution)/shard_map/ppermute | solution.py:327
  12.2 9.1 %collective-permute-start.1 = (bf16[1152,128]{1,0:T(8,128)(2,1)S(1)}, bf16[1152,128]{1,0:T(8,128)(2,1)S(1)}, u32[]{:S(2)}, u32[]{:S(2)}) collective-permute-start(bf16[1152,128]{1,0:T(8,128)(2,1)S(1)} %pad_maximum_fusion.1), channel_id=1, source_target_pairs={{0,2},{2,0},{1,3},{3,1},{4,6},{6,4},{5,7},{7,5},{8,10},{10,8},{9,1... | collective-permute-start | bytes 884744 | tf_op jit(solution)/shard_map/ppermute | solution.py:329
  16.1 14.0 %collective-permute-start.5 = (bf16[64,3584]{1,0:T(8,128)(2,1)S(1)}, bf16[64,3584]{1,0:T(8,128)(2,1)S(1)}, u32[]{:S(2)}, u32[]{:S(2)}) collective-permute-start(bf16[64,3584]{1,0:T(8,128)(2,1)S(1)} %broadcast_select_fusion.2), channel_id=1, source_target_pairs={{0,4},{4,0},{8,12},{12,8},{1,5},{5,1},{9,13},{13,9},{2,6},{6,2},{1... | collective-permute-start | bytes 1376264 | tf_op jit(solution)/shard_map/ppermute | solution.py:309
  18.0 12.2 %collective-permute-start.4 = (bf16[64,3584]{1,0:T(8,128)(2,1)S(1)}, bf16[64,3584]{1,0:T(8,128)(2,1)S(1)}, u32[]{:S(2)}, u32[]{:S(2)}) collective-permute-start(bf16[64,3584]{1,0:T(8,128)(2,1)S(1)} %collective-permute-done.2.mine_ref), channel_id=1, source_target_pairs={{0,16},{1,17},{2,18},{3,19},{4,8},{5,9},{6,10},{7,11},{8,4},{9,5},... | collective-permute-start | bytes 1376264 | tf_op jit(solution)/shard_map/ppermute | solution.py:315
  21.4 13.0 %collective-permute-start.9 = (bf16[64,256]{1,0:T(8,128)(2,1)S(1)}, bf16[64,256]{1,0:T(8,128)(2,1)S(1)}, u32[]{:S(2)}, u32[]{:S(2)}) collective-permute-start(bf16[64,256]{1,0:T(8,128)(2,1)S(1)} %pad_maximum_fusion.2.refs_0_), channel_id=1, source_target_pairs={{0,12},{4,8},{8,4},{12,0},{1,13},{5,9},{9,5},{13,1},{2,14},{6,10},... | collective-permute-start | bytes 98312 | tf_op jit(solution)/shard_map/ppermute | solution.py:46
  22.8 11.6 %collective-permute-start.8 = (bf16[64,256]{1,0:T(8,128)(2,1)S(1)}, bf16[64,256]{1,0:T(8,128)(2,1)S(1)}, u32[]{:S(2)}, u32[]{:S(2)}) collective-permute-start(bf16[64,256]{1,0:T(8,128)(2,1)S(1)} %pad_maximum_fusion.2.refs_0_), channel_id=1, source_target_pairs={{0,8},{4,12},{8,0},{12,4},{1,9},{5,13},{9,1},{13,5},{2,10},{6,14},... | collective-permute-start | bytes 98312 | tf_op jit(solution)/shard_map/ppermute | solution.py:46
  22.9 11.5 %collective-permute-start.7 = (bf16[64,256]{1,0:T(8,128)(2,1)S(1)}, bf16[64,256]{1,0:T(8,128)(2,1)S(1)}, u32[]{:S(2)}, u32[]{:S(2)}) collective-permute-start(bf16[64,256]{1,0:T(8,128)(2,1)S(1)} %pad_maximum_fusion.2.refs_0_), channel_id=1, source_target_pairs={{0,4},{4,0},{8,12},{12,8},{1,5},{5,1},{9,13},{13,9},{2,6},{6,2},{1... | collective-permute-start | bytes 98312 | tf_op jit(solution)/shard_map/ppermute | solution.py:46
  30.2 11.3 %collective-permute-start.11 = (bf16[64,3584]{1,0:T(8,128)(2,1)S(1)}, bf16[64,3584]{1,0:T(8,128)(2,1)S(1)}, u32[]{:S(2)}, u32[]{:S(2)}) collective-permute-start(bf16[64,3584]{1,0:T(8,128)(2,1)S(1)} %broadcast_select_fusion.1.mine_2_ref), channel_id=1, source_target_pairs={{0,4},{4,0},{8,12},{12,8},{1,5},{5,1},{9,13},{13,9},{2,6},{6,2},{1... | collective-permute-start | bytes 1376264 | tf_op jit(solution)/shard_map/ppermute | solution.py:309
  32.8 10.3 %collective-permute-start.6 = (bf16[64,3584]{1,0:T(8,128)(2,1)S(1)}, bf16[64,3584]{1,0:T(8,128)(2,1)S(1)}, u32[]{:S(2)}, u32[]{:S(2)}) collective-permute-start(bf16[64,3584]{1,0:T(8,128)(2,1)S(1)} %broadcast_select_fusion.1.mine_2_ref), channel_id=1, source_target_pairs={{0,16},{16,0},{1,17},{17,1},{2,18},{18,2},{3,19},{19,3},{4,20},{20... | collective-permute-start | bytes 1376264 | tf_op jit(solution)/shard_map/ppermute | solution.py:312
  41.5 6.1 %collective-permute-start.12 = (bf16[64,1792]{1,0:T(8,128)(2,1)S(1)}, bf16[64,1792]{1,0:T(8,128)(2,1)S(1)}, u32[]{:S(2)}, u32[]{:S(2)}) collective-permute-start(bf16[64,1792]{1,0:T(8,128)(2,1)S(1)} %slice.56), channel_id=1, source_target_pairs={{0,16},{16,0},{1,17},{17,1},{2,18},{18,2},{3,19},{19,3},{4,20},{20... | collective-permute-start | bytes 688136 | tf_op jit(solution)/shard_map/ppermute | solution.py:312
  43.1 6.1 %collective-permute-start.10 = (bf16[64,1792]{1,0:T(8,128)(2,1)S(1)}, bf16[64,1792]{1,0:T(8,128)(2,1)S(1)}, u32[]{:S(2)}, u32[]{:S(2)}) collective-permute-start(bf16[64,1792]{1,0:T(8,128)(2,1)S(1)} %slice.55), channel_id=1, source_target_pairs={{0,4},{4,0},{8,12},{12,8},{1,5},{5,1},{9,13},{13,9},{2,6},{6,2},{1... | collective-permute-start | bytes 688136 | tf_op jit(solution)/shard_map/ppermute | solution.py:309

commit v6 on v5

--- a/solution.py
+++ b/solution.py
@@ -156,8 +156,11 @@
     return contract_last(acts_ref[pl.ds(start, BLOCK), columns], stacked)
 
 
-def mix(start, projected, weights, grad_ref, onehot_ref):
-    mixed = contract_last(grad_ref[pl.ds(start, BLOCK), :], weights)
+def mixing(start, weights, grad_ref):
+    return contract_last(grad_ref[pl.ds(start, BLOCK), :], weights)
+
+
+def mix(start, projected, mixed, onehot_ref):
     product = jnp.concatenate([projected] * (mixed.shape[1] // LANES), axis=1) * mixed
     high = product.astype(jnp.bfloat16)
     low = (product - high.astype(jnp.float32)).astype(jnp.bfloat16)
@@ -171,10 +174,19 @@
     def step(index, carry):
         return body(pl.multiple_of(index * BLOCK, LANES), carry)
 
-    return lax.fori_loop(0, tokens // BLOCK, step, initial)
-
-
-def load_kernel(source_ref, acts_ref, copied):
+    return lax.fori_loop(0, tokens // BLOCK, step, initial, unroll=True)
+
+
+def weight_kernel(query_count, *refs):
+    packs, (out_query_ref, weights_ref) = refs[:4], refs[4:]
+    weigh(query_count, packs, out_query_ref[...], weights_ref)
+
+
+def first_kernel(
+    source_ref, half_ref, mine_ref, other_half_ref, theirs_ref, weights_ref, grad_ref, onehot_ref,
+    sums_ref, acts_ref, copied,
+):
+    group = lax.axis_index("groups")
     copies = [
         pltpu.make_async_copy(
             source_ref.at[pl.ds(start, BLOCK)], acts_ref.at[pl.ds(start, BLOCK)], copied.at[place]
@@ -183,44 +195,33 @@
     ]
     for copy in copies:
         copy.start()
-    for copy in copies:
+    sums = jnp.zeros(sums_ref.shape, jnp.float32)
+    for place, copy in enumerate(copies):
+        start = place * BLOCK
+        mixed = mixing(start, weights_ref[0], grad_ref)
         copy.wait()
-
-
-def weight_kernel(query_count, *refs):
-    packs, (out_query_ref, weights_ref) = refs[:4], refs[4:]
-    weigh(query_count, packs, out_query_ref[...], weights_ref)
-
-
-def first_kernel(
-    acts_ref, half_ref, mine_ref, other_half_ref, theirs_ref, weights_ref, grad_ref, onehot_ref,
-    sums_ref,
-):
-    group = lax.axis_index("groups")
-
-    def body(start, sums):
         total = project(acts_ref, start, (half_ref, mine_ref), group)
         total = total + project(acts_ref, start, (other_half_ref, theirs_ref), 1 - group)
-        return sums + mix(start, total, weights_ref[0], grad_ref, onehot_ref)
-
-    sums_ref[...] = blocks(acts_ref.shape[0], body, jnp.zeros(sums_ref.shape, jnp.float32))
-
-
-def mine_kernel(acts_ref, mine_2_ref, mine_3_ref, total_ref):
+        sums = sums + mix(start, total, mixed, onehot_ref)
+    sums_ref[...] = sums
+
+
+def mine_kernel(acts_ref, mine_2_ref, mine_3_ref, weights_ref, grad_ref, total_ref, mixed_ref):
     group = lax.axis_index("groups")
 
     def body(start, carry):
         total_ref[pl.ds(start, BLOCK), :] = project(
             acts_ref, start, (mine_2_ref, mine_3_ref), group
         )
+        mixed_ref[pl.ds(start, BLOCK), :] = mixing(start, weights_ref[1], grad_ref)
         return carry
 
     blocks(acts_ref.shape[0], body, 0)
 
 
 def last_kernel(
-    query_count, acts_ref, theirs_2_ref, left_ref, right_ref, total_ref, weights_ref, grad_ref,
-    onehot_ref, before_ref, out_ref,
+    query_count, acts_ref, theirs_2_ref, left_ref, right_ref, total_ref, mixed_ref, onehot_ref,
+    before_ref, out_ref,
 ):
     other = 1 - lax.axis_index("groups")
     cut = left_ref.shape[1]
@@ -233,7 +234,7 @@
         total = total + project(
             acts_ref, start, (theirs_2_ref.at[:, cut:], right_ref), other, cut
         )
-        return sums + mix(start, total, weights_ref[1], grad_ref, onehot_ref)
+        return sums + mix(start, total, mixed_ref[pl.ds(start, BLOCK), :], onehot_ref)
 
     sums = blocks(acts_ref.shape[0], body, before_ref[...])
     width = sums.shape[1]
@@ -334,16 +335,6 @@
     in_query, out_query, grad_proj = part[:rows], part[rows:split], part[split:]
     pack = jnp.concatenate([in_query, eigvals], axis=1)
     packs = by_distance(pack)
-    acts = call(
-        load_kernel,
-        pltpu.VMEM(acts.shape, acts.dtype),
-        in_hbm(held(acts, pack)),
-        in_specs=[pl.BlockSpec(memory_space=pl.ANY)],
-        scratch_shapes=[pltpu.SemaphoreType.DMA((tokens // BLOCK,))],
-    )
-    acts = in_vmem(acts)
-
-    from_across = held(from_across, acts)
     mine_2 = jnp.where(inner, from_across, from_pair)
     theirs_2 = swapped(mine_2)
     mine_3 = along(mine_2)
@@ -353,22 +344,33 @@
         jax.ShapeDtypeStruct((2, 2 * query_count * rows, width), jnp.bfloat16),
         *packs, held(out_query, mine_2),
     )
-    fixed = (weights, grad_proj, onehot)
-    sums = call(
+    mixed_width = 2 * query_count * rows
+    sums, acts = call(
         first_kernel,
-        jax.ShapeDtypeStruct((seq_count, 2 * query_count * rows), jnp.float32),
-        acts, half, mine_1, other_half, theirs_1, *fixed,
-    )
+        [
+            jax.ShapeDtypeStruct((seq_count, mixed_width), jnp.float32),
+            pltpu.VMEM(acts.shape, acts.dtype),
+        ],
+        in_hbm(acts), half, mine_1, other_half, theirs_1, weights, grad_proj, onehot,
+        in_specs=[pl.BlockSpec(memory_space=pl.ANY)]
+        + [pl.BlockSpec(memory_space=pltpu.VMEM)] * 7,
+        scratch_shapes=[pltpu.SemaphoreType.DMA((tokens // BLOCK,))],
+    )
+    acts = in_vmem(acts)
 
     cut = mine_3.shape[1] // 2
     left_3 = along(held(theirs_2, sums)[:, :cut])
     right_3 = swapped(held(mine_3, sums)[:, cut:])
-    total = call(mine_kernel, jax.ShapeDtypeStruct((tokens, LANES), jnp.float32), acts, mine_2, mine_3)
+    total, mixed = call(
+        mine_kernel,
+        [jax.ShapeDtypeStruct((tokens, size), jnp.float32) for size in (LANES, mixed_width)],
+        acts, mine_2, mine_3, weights, grad_proj,
+    )
     places = lax.axis_size("blk")
     return call(
         functools.partial(last_kernel, query_count),
         jax.ShapeDtypeStruct((places * query_count, seq_count // places), jnp.float32),
-        acts, theirs_2, left_3, right_3, total, *fixed, sums,
+        acts, theirs_2, left_3, right_3, total, mixed, onehot, sums,
     )
 
 

time: 64.4 us -> 64.4 us (level)
  waiting for transfers between devices: 9.76 us -> 12.4 us
  Pallas kernels: 19.9 us -> 18.7 us
  other arithmetic: 1.73 us -> 1.02 us
    ppermute x2, waiting for transfers between devices: 1 us -> 2.66 us  [swapped(): return lax.ppermute(value, 'groups', pair)]
    ppermute x1, waiting for transfers between devices: 1.79 us -> 0.54 us  [stepped_scores(): other = lax.ppermute(to_send(part, split), 'eig', pair)]
    ppermute x4, starting transfers between devices: 10.1 us -> 8.9 us  [along(): return lax.ppermute(value, 'blk', [(i, i ^ 1) for i in range(4)])]
    pallas_call x5 -> x4, Pallas kernels: 14.2 us -> 13.1 us  [call(): pl.pallas_call(kernel, out_shape=out_shape, compiler_params=pltpu.Compile...]
    ppermute x2, waiting for transfers between devices: 0.01 us -> 0.99 us  [across(): lax.ppermute(value, AXES, pairing(lambda g, b, e, r: (g, 3 - b, e, r) if...]
    ppermute x4, waiting for transfers between devices: 6.19 us -> 7.07 us  [along(): return lax.ppermute(value, 'blk', [(i, i ^ 1) for i in range(4)])]
    ppermute x3, starting transfers between devices: 4.45 us -> 5.29 us  [by_distance(): lax.ppermute(value, axis, [(i, i ^ k) for i in range(size)])]
    reduce_sum x1, other arithmetic: 0.78 us -> 0.08 us  [on_device(): jnp.sum(jnp.where(seq_ids[None, :] == labels[:, None], owner[:, None], 0)...]
  transfers between devices with their start and end apart: 13 -> 13, of which waited for: 6 -> 7; matrix products, arithmetic and copies ran while one was open for 2% -> 1% of each run, Pallas kernels for 24% -> 23%
where the time goes in v6:
time: 64.4 us; the launch traced here: 64.2 us
  starting transfers between devices  20.7 us (32%)
  Pallas kernels  18.7 us (29%)
  waiting for transfers between devices  12.4 us (19%)
  blocking collectives  11.2 us (17%)
  other arithmetic  1.02 us (2%)
    pallas_call x4, Pallas kernels, call(): pl.pallas_call(kernel, out_shape=out_shape, compiler_params=pltpu.Compile...  13.1 us
    all_to_all x1, blocking collectives, on_device(): parts = lax.all_to_all(parts, ('blk', 'eig', 'rep'), 0, 0, tiled=True)  11.2 us
    ppermute x4, starting transfers between devices, along(): return lax.ppermute(value, 'blk', [(i, i ^ 1) for i in range(4)])  8.9 us
    ppermute x4, waiting for transfers between devices, along(): return lax.ppermute(value, 'blk', [(i, i ^ 1) for i in range(4)])  7.07 us
    ppermute x3, starting transfers between devices, by_distance(): lax.ppermute(value, axis, [(i, i ^ k) for i in range(size)])  5.29 us
    pallas_call x1, Pallas kernels, small_parts(): pl.pallas_call(parts_kernel, in_specs=[pl.BlockSpec(memory_space=pl.ANY)]...  4.44 us
    ppermute x2, waiting for transfers between devices, swapped(): return lax.ppermute(value, 'groups', pair)  2.66 us
    ppermute x2, starting transfers between devices, swapped(): return lax.ppermute(value, 'groups', pair)  2.65 us
  transfers between devices with their start and end apart: 13, of which 7 were waited for; matrix products, arithmetic and copies ran while one was open for 1% of the time, Pallas kernels for 23%

profile of v6, /device:TPU:0, one launch (start us, length us, event | category | flops | bytes accessed | tf_op | source)
XLA Modules:
  0.0 64.2 jit_solution(2521637117743449528)
XLA Ops:
  0.0 1.2 %shard_map.91 = (bf16[64,3584]{1,0:T(8,128)(2,1)S(1)}, bf16[64,3584]{1,0:T(8,128)(2,1)S(1)}) custom-call(bf16[64,7168]{1,0:T(8,128)(2,1)} %refs_2_), custom_call_target="tpu_custom_call" | custom-call | tf_op jit(solution)/shard_map/pallas_call | solution.py:88
  1.2 0.0 copy-start.1
  1.2 0.0 copy-start.2
  1.2 3.1 %collective-permute-start = (bf16[64,3584]{1,0:T(8,128)(2,1)S(1)}, bf16[64,3584]{1,0:T(8,128)(2,1)S(1)}, u32[]{:S(2)}, u32[]{:S(2)}) collective-permute-start(bf16[64,3584]{1,0:T(8,128)(2,1)S(1)} %get-tuple-element.20.half_ref), channel_id=1, source_target_pairs={{0,4},{4,0},{8,12},{12,8},{1,5},{5,1},{9,13},{13,9},{2,6},{6,2},{1... | collective-permute-start | bytes 1376264 | tf_op jit(solution)/shard_map/ppermute | solution.py:310
  4.3 4.4 %shard_map.92 = f32[960,128]{1,0:T(8,128)S(1)} custom-call(bf16[128,2048]{1,0:T(8,128)(2,1)} %refs_0_.1, bf16[2048,128]{1,0:T(8,128)(2,1)} %refs_1_.1, bf16[64,7168]{1,0:T(8,128)(2,1)} %refs_2_, bf16[7168,128]{1,0:T(8,128)(2,1)} %refs_3_.1, bf16[768,2048]{1,0:T(8,128)(2,1)} %refs_4_.1), custom_call_target="tpu_custom_call" | custom-call | tf_op jit(solution)/shard_map/pallas_call | solution.py:127
  8.7 0.0 copy-start
  8.8 0.6 collective-permute-start.4
  9.4 0.1 select_reduce_fusion
  9.5 1.1 %collective-permute-done.4 = bf16[1152,128]{1,0:T(8,128)(2,1)S(1)} collective-permute-done((bf16[1152,128]{1,0:T(8,128)(2,1)S(1)}, bf16[1152,128]{1,0:T(8,128)(2,1)S(1)}, u32[]{:S(2)}, u32[]{:S(2)}) %collective-permute-start.4) | collective-permute-done | bytes 294944 | tf_op jit(solution)/shard_map/ppermute | solution.py:328
  10.7 1.6 %collective-permute-start.5 = (bf16[1152,128]{1,0:T(8,128)(2,1)S(1)}, bf16[1152,128]{1,0:T(8,128)(2,1)S(1)}, u32[]{:S(2)}, u32[]{:S(2)}) collective-permute-start(bf16[1152,128]{1,0:T(8,128)(2,1)S(1)} %pad_maximum_fusion.1), channel_id=1, source_target_pairs={{0,2},{2,0},{1,3},{3,1},{4,6},{6,4},{5,7},{7,5},{8,10},{10,8},{9,1... | collective-permute-start | bytes 884744 | tf_op jit(solution)/shard_map/ppermute | solution.py:330
  12.3 2.5 %collective-permute-done.mine_ref = bf16[64,3584]{1,0:T(8,128)(2,1)S(1)} collective-permute-done((bf16[64,3584]{1,0:T(8,128)(2,1)S(1)}, bf16[64,3584]{1,0:T(8,128)(2,1)S(1)}, u32[]{:S(2)}, u32[]{:S(2)}) %collective-permute-start) | collective-permute-done | bytes 458784 | tf_op jit(solution)/shard_map/ppermute | solution.py:310
  14.8 1.7 %collective-permute-start.3 = (bf16[64,3584]{1,0:T(8,128)(2,1)S(1)}, bf16[64,3584]{1,0:T(8,128)(2,1)S(1)}, u32[]{:S(2)}, u32[]{:S(2)}) collective-permute-start(bf16[64,3584]{1,0:T(8,128)(2,1)S(1)} %collective-permute-done.mine_ref), channel_id=1, source_target_pairs={{0,16},{1,17},{2,18},{3,19},{4,8},{5,9},{6,10},{7,11},{8,4},{9,5},... | collective-permute-start | bytes 1376264 | tf_op jit(solution)/shard_map/ppermute | solution.py:316
  16.6 3.0 %collective-permute-start.2 = (bf16[64,3584]{1,0:T(8,128)(2,1)S(1)}, bf16[64,3584]{1,0:T(8,128)(2,1)S(1)}, u32[]{:S(2)}, u32[]{:S(2)}) collective-permute-start(bf16[64,3584]{1,0:T(8,128)(2,1)S(1)} %broadcast_select_fusion.2), channel_id=1, source_target_pairs={{0,4},{4,0},{8,12},{12,8},{1,5},{5,1},{9,13},{13,9},{2,6},{6,2},{1... | collective-permute-start | bytes 1376264 | tf_op jit(solution)/shard_map/ppermute | solution.py:310
  19.5 0.5 collective-permute-done.5
  20.2 2.8 %collective-permute-start.6 = (bf16[64,256]{1,0:T(8,128)(2,1)S(1)}, bf16[64,256]{1,0:T(8,128)(2,1)S(1)}, u32[]{:S(2)}, u32[]{:S(2)}) collective-permute-start(bf16[64,256]{1,0:T(8,128)(2,1)S(1)} %pad_maximum_fusion.2.refs_0_), channel_id=1, source_target_pairs={{0,4},{4,0},{8,12},{12,8},{1,5},{5,1},{9,13},{13,9},{2,6},{6,2},{1... | collective-permute-start | bytes 98312 | tf_op jit(solution)/shard_map/ppermute | solution.py:46
  23.0 0.3 collective-permute-start.7
  23.3 2.2 %collective-permute-start.8 = (bf16[64,256]{1,0:T(8,128)(2,1)S(1)}, bf16[64,256]{1,0:T(8,128)(2,1)S(1)}, u32[]{:S(2)}, u32[]{:S(2)}) collective-permute-start(bf16[64,256]{1,0:T(8,128)(2,1)S(1)} %pad_maximum_fusion.2.refs_0_), channel_id=1, source_target_pairs={{0,12},{4,8},{8,4},{12,0},{1,13},{5,9},{9,5},{13,1},{2,14},{6,10},... | collective-permute-start | bytes 98312 | tf_op jit(solution)/shard_map/ppermute | solution.py:46
  25.5 0.1 add_convert_fusion.grad_ref
  25.5 1.0 %collective-permute-done.3 = bf16[64,3584]{1,0:T(8,128)(2,1)S(1)} collective-permute-done((bf16[64,3584]{1,0:T(8,128)(2,1)S(1)}, bf16[64,3584]{1,0:T(8,128)(2,1)S(1)}, u32[]{:S(2)}, u32[]{:S(2)}) %collective-permute-start.3) | collective-permute-done | bytes 458784 | tf_op jit(solution)/shard_map/ppermute | solution.py:316
  26.5 3.4 %collective-permute-done.2 = bf16[64,3584]{1,0:T(8,128)(2,1)S(1)} collective-permute-done((bf16[64,3584]{1,0:T(8,128)(2,1)S(1)}, bf16[64,3584]{1,0:T(8,128)(2,1)S(1)}, u32[]{:S(2)}, u32[]{:S(2)}) %collective-permute-start.2) | collective-permute-done | bytes 458784 | tf_op jit(solution)/shard_map/ppermute | solution.py:310
  30.0 2.3 %collective-permute-start.11 = (bf16[64,3584]{1,0:T(8,128)(2,1)S(1)}, bf16[64,3584]{1,0:T(8,128)(2,1)S(1)}, u32[]{:S(2)}, u32[]{:S(2)}) collective-permute-start(bf16[64,3584]{1,0:T(8,128)(2,1)S(1)} %broadcast_select_fusion.1.mine_2_ref), channel_id=1, source_target_pairs={{0,4},{4,0},{8,12},{12,8},{1,5},{5,1},{9,13},{13,9},{2,6},{6,2},{1... | collective-permute-start | bytes 1376264 | tf_op jit(solution)/shard_map/ppermute | solution.py:310
  32.3 1.5 %collective-permute-start.9 = (bf16[64,3584]{1,0:T(8,128)(2,1)S(1)}, bf16[64,3584]{1,0:T(8,128)(2,1)S(1)}, u32[]{:S(2)}, u32[]{:S(2)}) collective-permute-start(bf16[64,3584]{1,0:T(8,128)(2,1)S(1)} %broadcast_select_fusion.1.mine_2_ref), channel_id=1, source_target_pairs={{0,16},{16,0},{1,17},{17,1},{2,18},{18,2},{3,19},{19,3},{4,20},{20... | collective-permute-start | bytes 1376264 | tf_op jit(solution)/shard_map/ppermute | solution.py:313
  33.9 0.5 shard_map.93.weights_ref
  34.4 8.2 %shard_map.94 = (f32[8,512]{1,0:T(8,128)S(1)}, bf16[768,7168]{1,0:T(8,128)(2,1)S(1)}) custom-call(bf16[768,7168]{1,0:T(8,128)(2,1)} %source_ref.1, bf16[64,3584]{1,0:T(8,128)(2,1)S(1)} %get-tuple-element.20.half_ref, bf16[64,3584]{1,0:T(8,128)(2,1)S(1)} %collective-permute-done.mine_ref, bf16[64,3584]{1,0:T(8,128)(2,1)S(1)} %get-tuple-element.21.other_half_ref, ...), custom_call_target="tpu_custom_call" | custom-call | flops 1 | bytes 1 | tf_op jit(solution)/shard_map/pallas_call | solution.py:252
  42.7 1.1 %collective-permute-start.12 = (bf16[64,1792]{1,0:T(8,128)(2,1)S(1)}, bf16[64,1792]{1,0:T(8,128)(2,1)S(1)}, u32[]{:S(2)}, u32[]{:S(2)}) collective-permute-start(bf16[64,1792]{1,0:T(8,128)(2,1)S(1)} %slice.56), channel_id=1, source_target_pairs={{0,16},{16,0},{1,17},{17,1},{2,18},{18,2},{3,19},{19,3},{4,20},{20... | collective-permute-start | bytes 688136 | tf_op jit(solution)/shard_map/ppermute | solution.py:313
  43.8 0.5 collective-permute-start.10
  44.3 1.8 %shard_map.95 = (f32[768,128]{1,0:T(8,128)S(1)}, f32[768,512]{1,0:T(8,128)S(1)}) custom-call(bf16[768,7168]{1,0:T(8,128)(2,1)S(1)} %get-tuple-element.29.acts_ref, bf16[64,3584]{1,0:T(8,128)(2,1)S(1)} %broadcast_select_fusion.1.mine_2_ref, bf16[64,3584]{1,0:T(8,128)(2,1)S(1)} %collective-permute-done.11.mine_3_ref, ...), custom_call_target="tpu_custom_call" | custom-call | flops 1 | bytes 1 | tf_op jit(solution)/shard_map/pallas_call | solution.py:252
  46.1 2.7 %collective-permute-done.12.right_ref = bf16[64,1792]{1,0:T(8,128)(2,1)S(1)} collective-permute-done((bf16[64,1792]{1,0:T(8,128)(2,1)S(1)}, bf16[64,1792]{1,0:T(8,128)(2,1)S(1)}, u32[]{:S(2)}, u32[]{:S(2)}) %collective-permute-start.12) | collective-permute-done | bytes 229408 | tf_op jit(solution)/shard_map/ppermute | solution.py:313
  48.8 1.2 %collective-permute-done.10.left_ref = bf16[64,1792]{1,0:T(8,128)(2,1)S(1)} collective-permute-done((bf16[64,1792]{1,0:T(8,128)(2,1)S(1)}, bf16[64,1792]{1,0:T(8,128)(2,1)S(1)}, u32[]{:S(2)}, u32[]{:S(2)}) %collective-permute-start.10) | collective-permute-done | bytes 229408 | tf_op jit(solution)/shard_map/ppermute | solution.py:310
  49.9 2.6 %shard_map.96 = f32[16,2]{1,0:T(8,128)S(1)} custom-call(bf16[768,7168]{1,0:T(8,128)(2,1)S(1)} %get-tuple-element.29.acts_ref, bf16[64,3584]{1,0:T(8,128)(2,1)S(1)} %collective-permute-done.9.theirs_2_ref, bf16[64,1792]{1,0:T(8,128)(2,1)S(1)} %collective-permute-done.10.left_ref, bf16[64,1792]{1,0:T(8,128)(2,1)S(1)} %collective-permute-done.12.right_ref, ...), custom_call_target="tpu_custom_call" | custom-call | flops 1 | bytes 1 | tf_op jit(solution)/shard_map/pallas_call | solution.py:252
  52.5 11.2 %all_to_all.9 = f32[16,1,2]{2,1,0:T(1,128)S(1)} all-to-all(f32[16,1,2]{2,1,0:T(1,128)S(1)} %bitcast.4), channel_id=1, replica_groups=mesh['groups'=2,'blk'=4,'eig'=2,'rep'=2] {'blk','eig','rep'}, dimensions={0} | all-to-all | bytes 256 | tf_op jit(solution)/shard_map/all_to_all | solution.py:412
  63.7 0.5 reduce_sum.21
  (26 shorter events, 0.4 us)
Async XLA Ops:
  1.2 8.2 %copy-start.1 = (s32[768]{0:T(1024)S(1)}, s32[768]{0:T(1024)}, u32[]{:S(2)}) copy-start(s32[768]{0:T(1024)} %param.16) | copy-start | bytes 9220
  1.2 8.2 %copy-start.2 = (s32[8]{0:T(128)S(1)}, s32[8]{0:T(128)}, u32[]{:S(2)}) copy-start(s32[8]{0:T(128)} %param.17) | copy-start | bytes 100
  1.2 13.6 %collective-permute-start = (bf16[64,3584]{1,0:T(8,128)(2,1)S(1)}, bf16[64,3584]{1,0:T(8,128)(2,1)S(1)}, u32[]{:S(2)}, u32[]{:S(2)}) collective-permute-start(bf16[64,3584]{1,0:T(8,128)(2,1)S(1)} %get-tuple-element.20.half_ref), channel_id=1, source_target_pairs={{0,4},{4,0},{8,12},{12,8},{1,5},{5,1},{9,13},{13,9},{2,6},{6,2},{1... | collective-permute-start | bytes 1376264 | tf_op jit(solution)/shard_map/ppermute | solution.py:310
  4.3 10.5 %collective-permute-start.1 = (bf16[64,3584]{1,0:T(8,128)(2,1)S(1)}, bf16[64,3584]{1,0:T(8,128)(2,1)S(1)}, u32[]{:S(2)}, u32[]{:S(2)}) collective-permute-start(bf16[64,3584]{1,0:T(8,128)(2,1)S(1)} %get-tuple-element.20.half_ref), channel_id=1, source_target_pairs={{0,1},{1,0},{2,3},{3,2},{4,8},{5,9},{6,10},{7,11},{8,4},{9,5},{10,... | collective-permute-start | bytes 1376264 | tf_op jit(solution)/shard_map/ppermute | solution.py:316
  8.7 11.4 %copy-start = (bf16[64,128]{1,0:T(8,128)(2,1)S(1)}, bf16[64,128]{1,0:T(8,128)(2,1)}, u32[]{:S(2)}) copy-start(bf16[64,128]{1,0:T(8,128)(2,1)} %param.13) | copy-start | bytes 49156
  8.8 1.8 %collective-permute-start.4 = (bf16[1152,128]{1,0:T(8,128)(2,1)S(1)}, bf16[1152,128]{1,0:T(8,128)(2,1)S(1)}, u32[]{:S(2)}, u32[]{:S(2)}) collective-permute-start(bf16[1152,128]{1,0:T(8,128)(2,1)S(1)} %pad_maximum_fusion), channel_id=1, source_target_pairs={{0,1},{1,0},{2,3},{3,2},{4,5},{5,4},{6,7},{7,6},{8,9},{9,8},{10,11... | collective-permute-start | bytes 884744 | tf_op jit(solution)/shard_map/ppermute | solution.py:328
  10.7 9.4 %collective-permute-start.5 = (bf16[1152,128]{1,0:T(8,128)(2,1)S(1)}, bf16[1152,128]{1,0:T(8,128)(2,1)S(1)}, u32[]{:S(2)}, u32[]{:S(2)}) collective-permute-start(bf16[1152,128]{1,0:T(8,128)(2,1)S(1)} %pad_maximum_fusion.1), channel_id=1, source_target_pairs={{0,2},{2,0},{1,3},{3,1},{4,6},{6,4},{5,7},{7,5},{8,10},{10,8},{9,1... | collective-permute-start | bytes 884744 | tf_op jit(solution)/shard_map/ppermute | solution.py:330
  14.8 11.7 %collective-permute-start.3 = (bf16[64,3584]{1,0:T(8,128)(2,1)S(1)}, bf16[64,3584]{1,0:T(8,128)(2,1)S(1)}, u32[]{:S(2)}, u32[]{:S(2)}) collective-permute-start(bf16[64,3584]{1,0:T(8,128)(2,1)S(1)} %collective-permute-done.mine_ref), channel_id=1, source_target_pairs={{0,16},{1,17},{2,18},{3,19},{4,8},{5,9},{6,10},{7,11},{8,4},{9,5},... | collective-permute-start | bytes 1376264 | tf_op jit(solution)/shard_map/ppermute | solution.py:316
  16.6 13.4 %collective-permute-start.2 = (bf16[64,3584]{1,0:T(8,128)(2,1)S(1)}, bf16[64,3584]{1,0:T(8,128)(2,1)S(1)}, u32[]{:S(2)}, u32[]{:S(2)}) collective-permute-start(bf16[64,3584]{1,0:T(8,128)(2,1)S(1)} %broadcast_select_fusion.2), channel_id=1, source_target_pairs={{0,4},{4,0},{8,12},{12,8},{1,5},{5,1},{9,13},{13,9},{2,6},{6,2},{1... | collective-permute-start | bytes 1376264 | tf_op jit(solution)/shard_map/ppermute | solution.py:310
  20.2 13.7 %collective-permute-start.6 = (bf16[64,256]{1,0:T(8,128)(2,1)S(1)}, bf16[64,256]{1,0:T(8,128)(2,1)S(1)}, u32[]{:S(2)}, u32[]{:S(2)}) collective-permute-start(bf16[64,256]{1,0:T(8,128)(2,1)S(1)} %pad_maximum_fusion.2.refs_0_), channel_id=1, source_target_pairs={{0,4},{4,0},{8,12},{12,8},{1,5},{5,1},{9,13},{13,9},{2,6},{6,2},{1... | collective-permute-start | bytes 98312 | tf_op jit(solution)/shard_map/ppermute | solution.py:46
  23.0 10.9 %collective-permute-start.7 = (bf16[64,256]{1,0:T(8,128)(2,1)S(1)}, bf16[64,256]{1,0:T(8,128)(2,1)S(1)}, u32[]{:S(2)}, u32[]{:S(2)}) collective-permute-start(bf16[64,256]{1,0:T(8,128)(2,1)S(1)} %pad_maximum_fusion.2.refs_0_), channel_id=1, source_target_pairs={{0,8},{4,12},{8,0},{12,4},{1,9},{5,13},{9,1},{13,5},{2,10},{6,14},... | collective-permute-start | bytes 98312 | tf_op jit(solution)/shard_map/ppermute | solution.py:46
  23.3 10.7 %collective-permute-start.8 = (bf16[64,256]{1,0:T(8,128)(2,1)S(1)}, bf16[64,256]{1,0:T(8,128)(2,1)S(1)}, u32[]{:S(2)}, u32[]{:S(2)}) collective-permute-start(bf16[64,256]{1,0:T(8,128)(2,1)S(1)} %pad_maximum_fusion.2.refs_0_), channel_id=1, source_target_pairs={{0,12},{4,8},{8,4},{12,0},{1,13},{5,9},{9,5},{13,1},{2,14},{6,10},... | collective-permute-start | bytes 98312 | tf_op jit(solution)/shard_map/ppermute | solution.py:46
  30.0 12.7 %collective-permute-start.11 = (bf16[64,3584]{1,0:T(8,128)(2,1)S(1)}, bf16[64,3584]{1,0:T(8,128)(2,1)S(1)}, u32[]{:S(2)}, u32[]{:S(2)}) collective-permute-start(bf16[64,3584]{1,0:T(8,128)(2,1)S(1)} %broadcast_select_fusion.1.mine_2_ref), channel_id=1, source_target_pairs={{0,4},{4,0},{8,12},{12,8},{1,5},{5,1},{9,13},{13,9},{2,6},{6,2},{1... | collective-permute-start | bytes 1376264 | tf_op jit(solution)/shard_map/ppermute | solution.py:310
  32.3 11.5 %collective-permute-start.9 = (bf16[64,3584]{1,0:T(8,128)(2,1)S(1)}, bf16[64,3584]{1,0:T(8,128)(2,1)S(1)}, u32[]{:S(2)}, u32[]{:S(2)}) collective-permute-start(bf16[64,3584]{1,0:T(8,128)(2,1)S(1)} %broadcast_select_fusion.1.mine_2_ref), channel_id=1, source_target_pairs={{0,16},{16,0},{1,17},{17,1},{2,18},{18,2},{3,19},{19,3},{4,20},{20... | collective-permute-start | bytes 1376264 | tf_op jit(solution)/shard_map/ppermute | solution.py:313
  42.7 6.1 %collective-permute-start.12 = (bf16[64,1792]{1,0:T(8,128)(2,1)S(1)}, bf16[64,1792]{1,0:T(8,128)(2,1)S(1)}, u32[]{:S(2)}, u32[]{:S(2)}) collective-permute-start(bf16[64,1792]{1,0:T(8,128)(2,1)S(1)} %slice.56), channel_id=1, source_target_pairs={{0,16},{16,0},{1,17},{17,1},{2,18},{18,2},{3,19},{19,3},{4,20},{20... | collective-permute-start | bytes 688136 | tf_op jit(solution)/shard_map/ppermute | solution.py:313
  43.8 6.1 %collective-permute-start.10 = (bf16[64,1792]{1,0:T(8,128)(2,1)S(1)}, bf16[64,1792]{1,0:T(8,128)(2,1)S(1)}, u32[]{:S(2)}, u32[]{:S(2)}) collective-permute-start(bf16[64,1792]{1,0:T(8,128)(2,1)S(1)} %slice.55), channel_id=1, source_target_pairs={{0,4},{4,0},{8,12},{12,8},{1,5},{5,1},{9,13},{13,9},{2,6},{6,2},{1... | collective-permute-start | bytes 688136 | tf_op jit(solution)/shard_map/ppermute | solution.py:310

commit v7 on v6

--- a/solution.py
+++ b/solution.py
@@ -65,31 +65,29 @@
     return [(number, places.index(partner(*place))) for number, place in enumerate(places)]
 
 
-def halves_kernel(whole_ref, mine_ref, other_ref, copied):
-    columns = mine_ref.shape[1]
+def chunks_kernel(whole_ref, *refs):
+    chunk_refs, copied = refs[:4], refs[4]
+    columns = chunk_refs[0].shape[1]
     group = lax.axis_index("groups")
-    copies = [
-        pltpu.make_async_copy(
-            whole_ref.at[:, pl.ds(pl.multiple_of(half * columns, LANES), columns)],
-            half_ref,
-            copied.at[place],
-        )
-        for place, (half, half_ref) in enumerate([(group, mine_ref), (1 - group, other_ref)])
-    ]
+    copies = []
+    for place, chunk_ref in enumerate(chunk_refs):
+        half = group if place < 2 else 1 - group
+        begin = pl.multiple_of((2 * half + place % 2) * columns, LANES)
+        source = whole_ref.at[:, pl.ds(begin, columns)]
+        copies.append(pltpu.make_async_copy(source, chunk_ref, copied.at[place]))
     for copy in copies:
         copy.start()
     for copy in copies:
         copy.wait()
 
 
-def take_halves(whole):
+def take_chunks(whole):
     rows, columns = whole.shape
-    half = pltpu.VMEM((rows, columns // 2), whole.dtype)
     return pl.pallas_call(
-        halves_kernel,
+        chunks_kernel,
         in_specs=[pl.BlockSpec(memory_space=pl.ANY)],
-        out_shape=[half, half],
-        scratch_shapes=[pltpu.SemaphoreType.DMA((2,))],
+        out_shape=[pltpu.VMEM((rows, columns // 4), whole.dtype)] * 4,
+        scratch_shapes=[pltpu.SemaphoreType.DMA((4,))],
     )(in_hbm(whole))
 
 
@@ -182,11 +180,7 @@
     weigh(query_count, packs, out_query_ref[...], weights_ref)
 
 
-def first_kernel(
-    source_ref, half_ref, mine_ref, other_half_ref, theirs_ref, weights_ref, grad_ref, onehot_ref,
-    sums_ref, acts_ref, copied,
-):
-    group = lax.axis_index("groups")
+def load_kernel(source_ref, acts_ref, copied):
     copies = [
         pltpu.make_async_copy(
             source_ref.at[pl.ds(start, BLOCK)], acts_ref.at[pl.ds(start, BLOCK)], copied.at[place]
@@ -195,15 +189,25 @@
     ]
     for copy in copies:
         copy.start()
-    sums = jnp.zeros(sums_ref.shape, jnp.float32)
-    for place, copy in enumerate(copies):
-        start = place * BLOCK
-        mixed = mixing(start, weights_ref[0], grad_ref)
+    for copy in copies:
         copy.wait()
-        total = project(acts_ref, start, (half_ref, mine_ref), group)
-        total = total + project(acts_ref, start, (other_half_ref, theirs_ref), 1 - group)
-        sums = sums + mix(start, total, mixed, onehot_ref)
-    sums_ref[...] = sums
+
+
+def first_kernel(acts_ref, *refs):
+    slots, (weights_ref, grad_ref, onehot_ref, sums_ref) = refs[:8], refs[8:]
+    columns = slots[0].shape[1]
+    group = lax.axis_index("groups")
+
+    def body(start, sums):
+        total = 0.0
+        for place in range(4):
+            half = group if place < 2 else 1 - group
+            total = total + project(
+                acts_ref, start, (slots[place], slots[4 + place]), half, place % 2 * columns
+            )
+        return sums + mix(start, total, mixing(start, weights_ref[0], grad_ref), onehot_ref)
+
+    sums_ref[...] = blocks(acts_ref.shape[0], body, jnp.zeros(sums_ref.shape, jnp.float32))
 
 
 def mine_kernel(acts_ref, mine_2_ref, mine_3_ref, weights_ref, grad_ref, total_ref, mixed_ref):
@@ -319,44 +323,60 @@
             pairing(lambda g, b, e, r: (g, 3 - b, e, r) if b in (1, 2) else at_ends(g, b, e, r)),
         )
 
-    half, other_half = take_halves(basis_in)
-    mine_1 = along(half)
-    middle_3 = across(half, lambda g, b, e, r: (g, b, e, 1 - r))
+    chunks = take_chunks(basis_in)
+    half, other_half = chunks[:2], chunks[2:]
+    to_core = lambda g, b, e, r: (g, b, e, 1 - r)
+    over_y = lambda g, b, e, r: (1 - g, b, e, r)
+    mine_1, middle_3 = [], []
+    for chunk in half:
+        middle_3.append(across(chunk, to_core))
+        mine_1.append(along(chunk))
 
     split = rows + width
-    part = small_parts(held(basis_in, half), query_in, basis_out, query_out, out_grads)
+    part = small_parts(held(basis_in, *half), query_in, basis_out, query_out, out_grads)
     other = lax.ppermute(to_send(part, split), "rep", pair)
-    part = add_sent(part, other, split)
-    other = lax.ppermute(to_send(part, split), "eig", pair)
-    middle_3 = held(middle_3, mine_1)
-    from_pair = along(jnp.where(inner, middle_3, other_half))
-    from_across = across(held(mine_1, middle_3), lambda g, b, e, r: (1 - g, b, e, r))
-    part = add_sent(part, held(other, mine_1), split).astype(jnp.bfloat16)
-    in_query, out_query, grad_proj = part[:rows], part[rows:split], part[split:]
-    pack = jnp.concatenate([in_query, eigvals], axis=1)
-    packs = by_distance(pack)
-    mine_2 = jnp.where(inner, from_across, from_pair)
+    part = add_sent(part, held(other, *mine_1, *middle_3), split)
+    sent = to_send(part, split)
+    other = lax.ppermute(sent, "eig", pair)
+    acts = call(
+        load_kernel,
+        pltpu.VMEM(acts.shape, acts.dtype),
+        in_hbm(held(acts, sent)),
+        in_specs=[pl.BlockSpec(memory_space=pl.ANY)],
+        scratch_shapes=[pltpu.SemaphoreType.DMA((tokens // BLOCK,))],
+    )
+    acts = in_vmem(acts)
+
+    mine_2, theirs_1 = [], []
+    for first, middle, rest in zip(mine_1, middle_3, other_half):
+        from_pair = along(jnp.where(inner, middle, held(rest, first)))
+        from_across = across(held(first, middle), over_y)
+        mine_2.append((from_across, from_pair))
+    arrived = [chunk for both in mine_2 for chunk in both] + [acts]
+    mine_2 = jnp.concatenate(
+        [jnp.where(inner, held(here, *arrived), there) for here, there in mine_2], axis=1
+    )
+    theirs_1 = [
+        jnp.where(inner, held(there, mine_2), held(here, mine_2))
+        for here, there in zip(arrived[0:4:2], arrived[1:4:2])
+    ]
     theirs_2 = swapped(mine_2)
     mine_3 = along(mine_2)
-    theirs_1 = jnp.where(inner, held(from_pair, mine_2), held(from_across, mine_2))
+
+    part = add_sent(part, held(other, mine_2), split).astype(jnp.bfloat16)
+    in_query, out_query, grad_proj = part[:rows], part[rows:split], part[split:]
+    packs = by_distance(jnp.concatenate([in_query, eigvals], axis=1))
     weights = call(
         functools.partial(weight_kernel, query_count),
         jax.ShapeDtypeStruct((2, 2 * query_count * rows, width), jnp.bfloat16),
-        *packs, held(out_query, mine_2),
+        *packs, out_query,
     )
     mixed_width = 2 * query_count * rows
-    sums, acts = call(
+    sums = call(
         first_kernel,
-        [
-            jax.ShapeDtypeStruct((seq_count, mixed_width), jnp.float32),
-            pltpu.VMEM(acts.shape, acts.dtype),
-        ],
-        in_hbm(acts), half, mine_1, other_half, theirs_1, weights, grad_proj, onehot,
-        in_specs=[pl.BlockSpec(memory_space=pl.ANY)]
-        + [pl.BlockSpec(memory_space=pltpu.VMEM)] * 7,
-        scratch_shapes=[pltpu.SemaphoreType.DMA((tokens // BLOCK,))],
-    )
-    acts = in_vmem(acts)
+        jax.ShapeDtypeStruct((seq_count, mixed_width), jnp.float32),
+        acts, *half, *other_half, *mine_1, *theirs_1, weights, grad_proj, onehot,
+    )
 
     cut = mine_3.shape[1] // 2
     left_3 = along(held(theirs_2, sums)[:, :cut])

time: 64.4 us -> 67.8 us (1.053)
  starting transfers between devices: 20.7 us -> 25 us
  waiting for transfers between devices: 12.4 us -> 11.2 us
    ppermute x3, waiting for transfers between devices: 0.01 us -> 6.96 us  [by_distance(): lax.ppermute(value, axis, [(i, i ^ k) for i in range(size)])]
    ppermute x4 -> x6, waiting for transfers between devices: 7.07 us -> 2.49 us  [along(): return lax.ppermute(value, 'blk', [(i, i ^ 1) for i in range(4)])]
    ppermute x4 -> x6, starting transfers between devices: 8.9 us -> 12.3 us  [along(): return lax.ppermute(value, 'blk', [(i, i ^ 1) for i in range(4)])]
    ppermute x2 -> x4, starting transfers between devices: 1.69 us -> 3.56 us  [across(): lax.ppermute(value, AXES, pairing(lambda g, b, e, r: (g, 3 - b, e, r) if...]
    ppermute x1, waiting for transfers between devices: 1.11 us -> 0.01 us  [stepped_scores(): other = lax.ppermute(to_send(part, split), 'rep', pair)]
    ppermute x2 -> x4, waiting for transfers between devices: 0.99 us -> 0.01 us  [across(): lax.ppermute(value, AXES, pairing(lambda g, b, e, r: (g, 3 - b, e, r) if...]
    ppermute x2, waiting for transfers between devices: 2.66 us -> 1.71 us  [swapped(): return lax.ppermute(value, 'groups', pair)]
    ppermute x3, starting transfers between devices: 5.29 us -> 4.45 us  [by_distance(): lax.ppermute(value, axis, [(i, i ^ k) for i in range(size)])]
  transfers between devices with their start and end apart: 13 -> 17, of which waited for: 7 -> 5; matrix products, arithmetic and copies ran while one was open for 1% -> 1% of each run, Pallas kernels for 23% -> 22%
where the time goes in v7:
time: 67.8 us; the launch traced here: 67.6 us
  starting transfers between devices  25 us (37%)
  Pallas kernels  19 us (28%)
  waiting for transfers between devices  11.2 us (17%)
  blocking collectives  11 us (16%)
  other arithmetic  1.09 us (2%)
    pallas_call x5, Pallas kernels, call(): pl.pallas_call(kernel, out_shape=out_shape, compiler_params=pltpu.Compile...  13.2 us
    ppermute x6, starting transfers between devices, along(): return lax.ppermute(value, 'blk', [(i, i ^ 1) for i in range(4)])  12.3 us
    all_to_all x1, blocking collectives, on_device(): parts = lax.all_to_all(parts, ('blk', 'eig', 'rep'), 0, 0, tiled=True)  11 us
    ppermute x3, waiting for transfers between devices, by_distance(): lax.ppermute(value, axis, [(i, i ^ k) for i in range(size)])  6.96 us
    ppermute x3, starting transfers between devices, by_distance(): lax.ppermute(value, axis, [(i, i ^ k) for i in range(size)])  4.45 us
    pallas_call x1, Pallas kernels, small_parts(): pl.pallas_call(parts_kernel, in_specs=[pl.BlockSpec(memory_space=pl.ANY)]...  4.44 us
    ppermute x4, starting transfers between devices, across(): lax.ppermute(value, AXES, pairing(lambda g, b, e, r: (g, 3 - b, e, r) if...  3.56 us
    ppermute x2, starting transfers between devices, swapped(): return lax.ppermute(value, 'groups', pair)  3.1 us
  transfers between devices with their start and end apart: 17, of which 5 were waited for; matrix products, arithmetic and copies ran while one was open for 1% of the time, Pallas kernels for 22%

profile of v7, /device:TPU:0, one launch (start us, length us, event | category | flops | bytes accessed | tf_op | source)
XLA Modules:
  0.0 67.6 jit_solution(8108051570012048618)
XLA Ops:
  0.0 1.3 %shard_map.91 = (bf16[64,1792]{1,0:T(8,128)(2,1)S(1)}, bf16[64,1792]{1,0:T(8,128)(2,1)S(1)}, bf16[64,1792]{1,0:T(8,128)(2,1)S(1)}, bf16[64,1792]{1,0:T(8,128)(2,1)S(1)}) custom-call(bf16[64,7168]{1,0:T(8,128)(2,1)} %refs_2_), custom_call_target="tpu_custom_call" | custom-call | tf_op jit(solution)/shard_map/pallas_call | solution.py:86
  1.3 0.5 collective-permute-start.3
  1.8 4.1 %collective-permute-start.1 = (bf16[64,1792]{1,0:T(8,128)(2,1)S(1)}, bf16[64,1792]{1,0:T(8,128)(2,1)S(1)}, u32[]{:S(2)}, u32[]{:S(2)}) collective-permute-start(bf16[64,1792]{1,0:T(8,128)(2,1)S(1)} %get-tuple-element.27.refs_0_), channel_id=1, source_target_pairs={{0,4},{4,0},{8,12},{12,8},{1,5},{5,1},{9,13},{13,9},{2,6},{6,2},{1... | collective-permute-start | bytes 688136 | tf_op jit(solution)/shard_map/ppermute | solution.py:314
  6.0 1.7 %collective-permute-start.2 = (bf16[64,1792]{1,0:T(8,128)(2,1)S(1)}, bf16[64,1792]{1,0:T(8,128)(2,1)S(1)}, u32[]{:S(2)}, u32[]{:S(2)}) collective-permute-start(bf16[64,1792]{1,0:T(8,128)(2,1)S(1)} %get-tuple-element.28.refs_1_), channel_id=1, source_target_pairs={{0,4},{4,0},{8,12},{12,8},{1,5},{5,1},{9,13},{13,9},{2,6},{6,2},{1... | collective-permute-start | bytes 688136 | tf_op jit(solution)/shard_map/ppermute | solution.py:314
  7.6 4.4 %shard_map.92 = f32[960,128]{1,0:T(8,128)S(1)} custom-call(bf16[128,2048]{1,0:T(8,128)(2,1)} %refs_0_.1, bf16[2048,128]{1,0:T(8,128)(2,1)} %refs_1_.1, bf16[64,7168]{1,0:T(8,128)(2,1)} %refs_2_, bf16[7168,128]{1,0:T(8,128)(2,1)} %refs_3_.1, bf16[768,2048]{1,0:T(8,128)(2,1)} %refs_4_.1), custom_call_target="tpu_custom_call" | custom-call | tf_op jit(solution)/shard_map/pallas_call | solution.py:125
  12.2 0.1 collective-permute-start
  12.3 0.1 select_reduce_fusion
  12.5 2.1 %collective-permute-start.6 = (bf16[64,1792]{1,0:T(8,128)(2,1)S(1)}, bf16[64,1792]{1,0:T(8,128)(2,1)S(1)}, u32[]{:S(2)}, u32[]{:S(2)}) collective-permute-start(bf16[64,1792]{1,0:T(8,128)(2,1)S(1)} %broadcast_select_fusion.5), channel_id=1, source_target_pairs={{0,4},{4,0},{8,12},{12,8},{1,5},{5,1},{9,13},{13,9},{2,6},{6,2},{1... | collective-permute-start | bytes 688136 | tf_op jit(solution)/shard_map/ppermute | solution.py:314
  14.6 1.5 %collective-permute-start.5 = (bf16[64,1792]{1,0:T(8,128)(2,1)S(1)}, bf16[64,1792]{1,0:T(8,128)(2,1)S(1)}, u32[]{:S(2)}, u32[]{:S(2)}) collective-permute-start(bf16[64,1792]{1,0:T(8,128)(2,1)S(1)} %collective-permute-done.1.refs_4_), channel_id=1, source_target_pairs={{0,16},{1,17},{2,18},{3,19},{4,8},{5,9},{6,10},{7,11},{8,4},{9,5},... | collective-permute-start | bytes 688136 | tf_op jit(solution)/shard_map/ppermute | solution.py:320
  16.1 0.8 %collective-permute-done.2.refs_5_ = bf16[64,1792]{1,0:T(8,128)(2,1)S(1)} collective-permute-done((bf16[64,1792]{1,0:T(8,128)(2,1)S(1)}, bf16[64,1792]{1,0:T(8,128)(2,1)S(1)}, u32[]{:S(2)}, u32[]{:S(2)}) %collective-permute-start.2) | collective-permute-done | bytes 229408 | tf_op jit(solution)/shard_map/ppermute | solution.py:314
  17.0 2.5 %collective-permute-start.8 = (bf16[64,1792]{1,0:T(8,128)(2,1)S(1)}, bf16[64,1792]{1,0:T(8,128)(2,1)S(1)}, u32[]{:S(2)}, u32[]{:S(2)}) collective-permute-start(bf16[64,1792]{1,0:T(8,128)(2,1)S(1)} %broadcast_select_fusion.4), channel_id=1, source_target_pairs={{0,4},{4,0},{8,12},{12,8},{1,5},{5,1},{9,13},{13,9},{2,6},{6,2},{1... | collective-permute-start | bytes 688136 | tf_op jit(solution)/shard_map/ppermute | solution.py:314
  19.5 1.5 %collective-permute-start.7 = (bf16[64,1792]{1,0:T(8,128)(2,1)S(1)}, bf16[64,1792]{1,0:T(8,128)(2,1)S(1)}, u32[]{:S(2)}, u32[]{:S(2)}) collective-permute-start(bf16[64,1792]{1,0:T(8,128)(2,1)S(1)} %collective-permute-done.2.refs_5_), channel_id=1, source_target_pairs={{0,16},{1,17},{2,18},{3,19},{4,8},{5,9},{6,10},{7,11},{8,4},{9,5},... | collective-permute-start | bytes 688136 | tf_op jit(solution)/shard_map/ppermute | solution.py:320
  21.2 1.6 %collective-permute-start.10 = (bf16[1152,128]{1,0:T(8,128)(2,1)S(1)}, bf16[1152,128]{1,0:T(8,128)(2,1)S(1)}, u32[]{:S(2)}, u32[]{:S(2)}) collective-permute-start(bf16[1152,128]{1,0:T(8,128)(2,1)S(1)} %pad_maximum_fusion.2), channel_id=1, source_target_pairs={{0,2},{2,0},{1,3},{3,1},{4,6},{6,4},{5,7},{7,5},{8,10},{10,8},{9,1... | collective-permute-start | bytes 884744 | tf_op jit(solution)/shard_map/ppermute | solution.py:340
  22.7 4.2 %shard_map.93.acts_ref = bf16[768,7168]{1,0:T(8,128)(2,1)S(1)} custom-call(bf16[768,7168]{1,0:T(8,128)(2,1)} %source_ref), custom_call_target="tpu_custom_call" | custom-call | flops 1 | bytes 1 | tf_op jit(solution)/shard_map/pallas_call | solution.py:256
  27.1 0.9 %collective-permute-start.15 = (bf16[64,3584]{1,0:T(8,128)(2,1)S(1)}, bf16[64,3584]{1,0:T(8,128)(2,1)S(1)}, u32[]{:S(2)}, u32[]{:S(2)}) collective-permute-start(bf16[64,3584]{1,0:T(8,128)(2,1)S(1)} %pad_maximum_fusion.mine_2_ref), channel_id=1, source_target_pairs={{0,4},{4,0},{8,12},{12,8},{1,5},{5,1},{9,13},{13,9},{2,6},{6,2},{1... | collective-permute-start | bytes 1376264 | tf_op jit(solution)/shard_map/ppermute | solution.py:314
  28.0 1.5 %collective-permute-start.9 = (bf16[64,3584]{1,0:T(8,128)(2,1)S(1)}, bf16[64,3584]{1,0:T(8,128)(2,1)S(1)}, u32[]{:S(2)}, u32[]{:S(2)}) collective-permute-start(bf16[64,3584]{1,0:T(8,128)(2,1)S(1)} %pad_maximum_fusion.mine_2_ref), channel_id=1, source_target_pairs={{0,16},{16,0},{1,17},{17,1},{2,18},{18,2},{3,19},{19,3},{4,20},{20... | collective-permute-start | bytes 1376264 | tf_op jit(solution)/shard_map/ppermute | solution.py:317
  29.5 0.1 broadcast_select_fusion
  29.7 1.8 %collective-permute-start.13 = (bf16[64,256]{1,0:T(8,128)(2,1)S(1)}, bf16[64,256]{1,0:T(8,128)(2,1)S(1)}, u32[]{:S(2)}, u32[]{:S(2)}) collective-permute-start(bf16[64,256]{1,0:T(8,128)(2,1)S(1)} %pad_maximum_fusion.3.refs_0_), channel_id=1, source_target_pairs={{0,12},{4,8},{8,4},{12,0},{1,13},{5,9},{9,5},{13,1},{2,14},{6,10},... | collective-permute-start | bytes 98312 | tf_op jit(solution)/shard_map/ppermute | solution.py:46
  31.4 0.4 collective-permute-start.12
  31.8 2.3 %collective-permute-start.11 = (bf16[64,256]{1,0:T(8,128)(2,1)S(1)}, bf16[64,256]{1,0:T(8,128)(2,1)S(1)}, u32[]{:S(2)}, u32[]{:S(2)}) collective-permute-start(bf16[64,256]{1,0:T(8,128)(2,1)S(1)} %pad_maximum_fusion.3.refs_0_), channel_id=1, source_target_pairs={{0,4},{4,0},{8,12},{12,8},{1,5},{5,1},{9,13},{13,9},{2,6},{6,2},{1... | collective-permute-start | bytes 98312 | tf_op jit(solution)/shard_map/ppermute | solution.py:46
  34.1 0.1 add_convert_fusion.refs_9_.grad_ref
  34.2 7.0 %collective-permute-done.13.refs_3_ = bf16[64,256]{1,0:T(8,128)(2,1)S(1)} collective-permute-done((bf16[64,256]{1,0:T(8,128)(2,1)S(1)}, bf16[64,256]{1,0:T(8,128)(2,1)S(1)}, u32[]{:S(2)}, u32[]{:S(2)}) %collective-permute-start.13) | collective-permute-done | bytes 32800 | tf_op jit(solution)/shard_map/ppermute | solution.py:46
  41.2 0.5 shard_map.94.refs_8_.weights_ref
  41.6 4.1 %shard_map.95.before_ref = f32[8,512]{1,0:T(8,128)S(1)} custom-call(bf16[768,7168]{1,0:T(8,128)(2,1)S(1)} %shard_map.93.acts_ref, bf16[64,1792]{1,0:T(8,128)(2,1)S(1)} %get-tuple-element.27.refs_0_, bf16[64,1792]{1,0:T(8,128)(2,1)S(1)} %get-tuple-element.28.refs_1_, bf16[64,1792]{1,0:T(8,128)(2,1)S(1)} %get-tuple-element.34.refs_2_, ...), custom_call_target="tpu_custom_call" | custom-call | flops 1 | bytes 1 | tf_op jit(solution)/shard_map/pallas_call | solution.py:256
  45.8 1.6 %collective-permute-start.16 = (bf16[64,1792]{1,0:T(8,128)(2,1)S(1)}, bf16[64,1792]{1,0:T(8,128)(2,1)S(1)}, u32[]{:S(2)}, u32[]{:S(2)}) collective-permute-start(bf16[64,1792]{1,0:T(8,128)(2,1)S(1)} %slice.56), channel_id=1, source_target_pairs={{0,16},{16,0},{1,17},{17,1},{2,18},{18,2},{3,19},{19,3},{4,20},{20... | collective-permute-start | bytes 688136 | tf_op jit(solution)/shard_map/ppermute | solution.py:317
  47.4 1.0 %collective-permute-start.14 = (bf16[64,1792]{1,0:T(8,128)(2,1)S(1)}, bf16[64,1792]{1,0:T(8,128)(2,1)S(1)}, u32[]{:S(2)}, u32[]{:S(2)}) collective-permute-start(bf16[64,1792]{1,0:T(8,128)(2,1)S(1)} %slice.55), channel_id=1, source_target_pairs={{0,4},{4,0},{8,12},{12,8},{1,5},{5,1},{9,13},{13,9},{2,6},{6,2},{1... | collective-permute-start | bytes 688136 | tf_op jit(solution)/shard_map/ppermute | solution.py:314
  48.4 1.8 %shard_map.96 = (f32[768,128]{1,0:T(8,128)S(1)}, f32[768,512]{1,0:T(8,128)S(1)}) custom-call(bf16[768,7168]{1,0:T(8,128)(2,1)S(1)} %shard_map.93.acts_ref, bf16[64,3584]{1,0:T(8,128)(2,1)S(1)} %pad_maximum_fusion.mine_2_ref, bf16[64,3584]{1,0:T(8,128)(2,1)S(1)} %collective-permute-done.15.mine_3_ref, bf16[2,512,128]{2,1,0:T(8,128)(2,1)S(1)} %shard_map.94.refs_8_.weights_ref, ...), custom_call_target="tpu_custom_call" | custom-call | flops 1 | bytes 1 | tf_op jit(solution)/shard_map/pallas_call | solution.py:256
  50.2 1.7 %collective-permute-done.16.right_ref = bf16[64,1792]{1,0:T(8,128)(2,1)S(1)} collective-permute-done((bf16[64,1792]{1,0:T(8,128)(2,1)S(1)}, bf16[64,1792]{1,0:T(8,128)(2,1)S(1)}, u32[]{:S(2)}, u32[]{:S(2)}) %collective-permute-start.16) | collective-permute-done | bytes 229408 | tf_op jit(solution)/shard_map/ppermute | solution.py:317
  51.9 1.6 %collective-permute-done.14.left_ref = bf16[64,1792]{1,0:T(8,128)(2,1)S(1)} collective-permute-done((bf16[64,1792]{1,0:T(8,128)(2,1)S(1)}, bf16[64,1792]{1,0:T(8,128)(2,1)S(1)}, u32[]{:S(2)}, u32[]{:S(2)}) %collective-permute-start.14) | collective-permute-done | bytes 229408 | tf_op jit(solution)/shard_map/ppermute | solution.py:314
  53.5 2.6 %shard_map.97 = f32[16,2]{1,0:T(8,128)S(1)} custom-call(bf16[768,7168]{1,0:T(8,128)(2,1)S(1)} %shard_map.93.acts_ref, bf16[64,3584]{1,0:T(8,128)(2,1)S(1)} %collective-permute-done.9.theirs_2_ref, bf16[64,1792]{1,0:T(8,128)(2,1)S(1)} %collective-permute-done.14.left_ref, bf16[64,1792]{1,0:T(8,128)(2,1)S(1)} %collective-permute-done.16.right_ref, ...), custom_call_target="tpu_custom_call" | custom-call | flops 1 | bytes 1 | tf_op jit(solution)/shard_map/pallas_call | solution.py:256
  56.1 11.0 %all_to_all.9 = f32[16,1,2]{2,1,0:T(1,128)S(1)} all-to-all(f32[16,1,2]{2,1,0:T(1,128)S(1)} %bitcast.4), channel_id=1, replica_groups=mesh['groups'=2,'blk'=4,'eig'=2,'rep'=2] {'blk','eig','rep'}, dimensions={0} | all-to-all | bytes 256 | tf_op jit(solution)/shard_map/all_to_all | solution.py:432
  67.0 0.5 reduce_sum.21
  (38 shorter events, 0.5 us)
Async XLA Ops:
  1.3 11.1 %collective-permute-start.3 = (bf16[64,1792]{1,0:T(8,128)(2,1)S(1)}, bf16[64,1792]{1,0:T(8,128)(2,1)S(1)}, u32[]{:S(2)}, u32[]{:S(2)}) collective-permute-start(bf16[64,1792]{1,0:T(8,128)(2,1)S(1)} %get-tuple-element.27.refs_0_), channel_id=1, source_target_pairs={{0,1},{1,0},{2,3},{3,2},{4,8},{5,9},{6,10},{7,11},{8,4},{9,5},{10,... | collective-permute-start | bytes 688136 | tf_op jit(solution)/shard_map/ppermute | solution.py:320
  1.8 10.6 %collective-permute-start.1 = (bf16[64,1792]{1,0:T(8,128)(2,1)S(1)}, bf16[64,1792]{1,0:T(8,128)(2,1)S(1)}, u32[]{:S(2)}, u32[]{:S(2)}) collective-permute-start(bf16[64,1792]{1,0:T(8,128)(2,1)S(1)} %get-tuple-element.27.refs_0_), channel_id=1, source_target_pairs={{0,4},{4,0},{8,12},{12,8},{1,5},{5,1},{9,13},{13,9},{2,6},{6,2},{1... | collective-permute-start | bytes 688136 | tf_op jit(solution)/shard_map/ppermute | solution.py:314
  6.0 6.3 %copy-start.1 = (s32[768]{0:T(1024)S(1)}, s32[768]{0:T(1024)}, u32[]{:S(2)}) copy-start(s32[768]{0:T(1024)} %param.16) | copy-start | bytes 9220
  6.0 6.3 %copy-start.2 = (s32[8]{0:T(128)S(1)}, s32[8]{0:T(128)}, u32[]{:S(2)}) copy-start(s32[8]{0:T(128)} %param.17) | copy-start | bytes 100
  6.0 11.0 %collective-permute-start.4 = (bf16[64,1792]{1,0:T(8,128)(2,1)S(1)}, bf16[64,1792]{1,0:T(8,128)(2,1)S(1)}, u32[]{:S(2)}, u32[]{:S(2)}) collective-permute-start(bf16[64,1792]{1,0:T(8,128)(2,1)S(1)} %get-tuple-element.28.refs_1_), channel_id=1, source_target_pairs={{0,1},{1,0},{2,3},{3,2},{4,8},{5,9},{6,10},{7,11},{8,4},{9,5},{10,... | collective-permute-start | bytes 688136 | tf_op jit(solution)/shard_map/ppermute | solution.py:320
  6.0 11.0 %collective-permute-start.2 = (bf16[64,1792]{1,0:T(8,128)(2,1)S(1)}, bf16[64,1792]{1,0:T(8,128)(2,1)S(1)}, u32[]{:S(2)}, u32[]{:S(2)}) collective-permute-start(bf16[64,1792]{1,0:T(8,128)(2,1)S(1)} %get-tuple-element.28.refs_1_), channel_id=1, source_target_pairs={{0,4},{4,0},{8,12},{12,8},{1,5},{5,1},{9,13},{13,9},{2,6},{6,2},{1... | collective-permute-start | bytes 688136 | tf_op jit(solution)/shard_map/ppermute | solution.py:314
  12.2 8.9 %collective-permute-start = (bf16[1152,128]{1,0:T(8,128)(2,1)S(1)}, bf16[1152,128]{1,0:T(8,128)(2,1)S(1)}, u32[]{:S(2)}, u32[]{:S(2)}) collective-permute-start(bf16[1152,128]{1,0:T(8,128)(2,1)S(1)} %pad_maximum_fusion.1), channel_id=1, source_target_pairs={{0,1},{1,0},{2,3},{3,2},{4,5},{5,4},{6,7},{7,6},{8,9},{9,8},{10,11... | collective-permute-start | bytes 884744 | tf_op jit(solution)/shard_map/ppermute | solution.py:337
  12.5 14.5 %collective-permute-start.6 = (bf16[64,1792]{1,0:T(8,128)(2,1)S(1)}, bf16[64,1792]{1,0:T(8,128)(2,1)S(1)}, u32[]{:S(2)}, u32[]{:S(2)}) collective-permute-start(bf16[64,1792]{1,0:T(8,128)(2,1)S(1)} %broadcast_select_fusion.5), channel_id=1, source_target_pairs={{0,4},{4,0},{8,12},{12,8},{1,5},{5,1},{9,13},{13,9},{2,6},{6,2},{1... | collective-permute-start | bytes 688136 | tf_op jit(solution)/shard_map/ppermute | solution.py:314
  14.6 12.4 %collective-permute-start.5 = (bf16[64,1792]{1,0:T(8,128)(2,1)S(1)}, bf16[64,1792]{1,0:T(8,128)(2,1)S(1)}, u32[]{:S(2)}, u32[]{:S(2)}) collective-permute-start(bf16[64,1792]{1,0:T(8,128)(2,1)S(1)} %collective-permute-done.1.refs_4_), channel_id=1, source_target_pairs={{0,16},{1,17},{2,18},{3,19},{4,8},{5,9},{6,10},{7,11},{8,4},{9,5},... | collective-permute-start | bytes 688136 | tf_op jit(solution)/shard_map/ppermute | solution.py:320
  17.0 10.0 %collective-permute-start.8 = (bf16[64,1792]{1,0:T(8,128)(2,1)S(1)}, bf16[64,1792]{1,0:T(8,128)(2,1)S(1)}, u32[]{:S(2)}, u32[]{:S(2)}) collective-permute-start(bf16[64,1792]{1,0:T(8,128)(2,1)S(1)} %broadcast_select_fusion.4), channel_id=1, source_target_pairs={{0,4},{4,0},{8,12},{12,8},{1,5},{5,1},{9,13},{13,9},{2,6},{6,2},{1... | collective-permute-start | bytes 688136 | tf_op jit(solution)/shard_map/ppermute | solution.py:314
  19.5 7.5 %collective-permute-start.7 = (bf16[64,1792]{1,0:T(8,128)(2,1)S(1)}, bf16[64,1792]{1,0:T(8,128)(2,1)S(1)}, u32[]{:S(2)}, u32[]{:S(2)}) collective-permute-start(bf16[64,1792]{1,0:T(8,128)(2,1)S(1)} %collective-permute-done.2.refs_5_), channel_id=1, source_target_pairs={{0,16},{1,17},{2,18},{3,19},{4,8},{5,9},{6,10},{7,11},{8,4},{9,5},... | collective-permute-start | bytes 688136 | tf_op jit(solution)/shard_map/ppermute | solution.py:320
  21.2 8.4 %collective-permute-start.10 = (bf16[1152,128]{1,0:T(8,128)(2,1)S(1)}, bf16[1152,128]{1,0:T(8,128)(2,1)S(1)}, u32[]{:S(2)}, u32[]{:S(2)}) collective-permute-start(bf16[1152,128]{1,0:T(8,128)(2,1)S(1)} %pad_maximum_fusion.2), channel_id=1, source_target_pairs={{0,2},{2,0},{1,3},{3,1},{4,6},{6,4},{5,7},{7,5},{8,10},{10,8},{9,1... | collective-permute-start | bytes 884744 | tf_op jit(solution)/shard_map/ppermute | solution.py:340
  27.0 2.7 %copy-start = (bf16[64,128]{1,0:T(8,128)(2,1)S(1)}, bf16[64,128]{1,0:T(8,128)(2,1)}, u32[]{:S(2)}) copy-start(bf16[64,128]{1,0:T(8,128)(2,1)} %param.13) | copy-start | bytes 49156
  27.1 18.6 %collective-permute-start.15 = (bf16[64,3584]{1,0:T(8,128)(2,1)S(1)}, bf16[64,3584]{1,0:T(8,128)(2,1)S(1)}, u32[]{:S(2)}, u32[]{:S(2)}) collective-permute-start(bf16[64,3584]{1,0:T(8,128)(2,1)S(1)} %pad_maximum_fusion.mine_2_ref), channel_id=1, source_target_pairs={{0,4},{4,0},{8,12},{12,8},{1,5},{5,1},{9,13},{13,9},{2,6},{6,2},{1... | collective-permute-start | bytes 1376264 | tf_op jit(solution)/shard_map/ppermute | solution.py:314
  28.0 19.4 %collective-permute-start.9 = (bf16[64,3584]{1,0:T(8,128)(2,1)S(1)}, bf16[64,3584]{1,0:T(8,128)(2,1)S(1)}, u32[]{:S(2)}, u32[]{:S(2)}) collective-permute-start(bf16[64,3584]{1,0:T(8,128)(2,1)S(1)} %pad_maximum_fusion.mine_2_ref), channel_id=1, source_target_pairs={{0,16},{16,0},{1,17},{17,1},{2,18},{18,2},{3,19},{19,3},{4,20},{20... | collective-permute-start | bytes 1376264 | tf_op jit(solution)/shard_map/ppermute | solution.py:317
  29.7 11.5 %collective-permute-start.13 = (bf16[64,256]{1,0:T(8,128)(2,1)S(1)}, bf16[64,256]{1,0:T(8,128)(2,1)S(1)}, u32[]{:S(2)}, u32[]{:S(2)}) collective-permute-start(bf16[64,256]{1,0:T(8,128)(2,1)S(1)} %pad_maximum_fusion.3.refs_0_), channel_id=1, source_target_pairs={{0,12},{4,8},{8,4},{12,0},{1,13},{5,9},{9,5},{13,1},{2,14},{6,10},... | collective-permute-start | bytes 98312 | tf_op jit(solution)/shard_map/ppermute | solution.py:46
  31.4 9.7 %collective-permute-start.12 = (bf16[64,256]{1,0:T(8,128)(2,1)S(1)}, bf16[64,256]{1,0:T(8,128)(2,1)S(1)}, u32[]{:S(2)}, u32[]{:S(2)}) collective-permute-start(bf16[64,256]{1,0:T(8,128)(2,1)S(1)} %pad_maximum_fusion.3.refs_0_), channel_id=1, source_target_pairs={{0,8},{4,12},{8,0},{12,4},{1,9},{5,13},{9,1},{13,5},{2,10},{6,14},... | collective-permute-start | bytes 98312 | tf_op jit(solution)/shard_map/ppermute | solution.py:46
  31.8 9.4 %collective-permute-start.11 = (bf16[64,256]{1,0:T(8,128)(2,1)S(1)}, bf16[64,256]{1,0:T(8,128)(2,1)S(1)}, u32[]{:S(2)}, u32[]{:S(2)}) collective-permute-start(bf16[64,256]{1,0:T(8,128)(2,1)S(1)} %pad_maximum_fusion.3.refs_0_), channel_id=1, source_target_pairs={{0,4},{4,0},{8,12},{12,8},{1,5},{5,1},{9,13},{13,9},{2,6},{6,2},{1... | collective-permute-start | bytes 98312 | tf_op jit(solution)/shard_map/ppermute | solution.py:46
  45.8 6.1 %collective-permute-start.16 = (bf16[64,1792]{1,0:T(8,128)(2,1)S(1)}, bf16[64,1792]{1,0:T(8,128)(2,1)S(1)}, u32[]{:S(2)}, u32[]{:S(2)}) collective-permute-start(bf16[64,1792]{1,0:T(8,128)(2,1)S(1)} %slice.56), channel_id=1, source_target_pairs={{0,16},{16,0},{1,17},{17,1},{2,18},{18,2},{3,19},{19,3},{4,20},{20... | collective-permute-start | bytes 688136 | tf_op jit(solution)/shard_map/ppermute | solution.py:317
  47.4 6.1 %collective-permute-start.14 = (bf16[64,1792]{1,0:T(8,128)(2,1)S(1)}, bf16[64,1792]{1,0:T(8,128)(2,1)S(1)}, u32[]{:S(2)}, u32[]{:S(2)}) collective-permute-start(bf16[64,1792]{1,0:T(8,128)(2,1)S(1)} %slice.55), channel_id=1, source_target_pairs={{0,4},{4,0},{8,12},{12,8},{1,5},{5,1},{9,13},{13,9},{2,6},{6,2},{1... | collective-permute-start | bytes 688136 | tf_op jit(solution)/shard_map/ppermute | solution.py:314

commit v8 on v7

--- a/solution.py
+++ b/solution.py
@@ -28,14 +28,14 @@
     )
 
 
-def swap_sum(value, axis, send_as):
+def swap_sum(value, axis):
     size = lax.axis_size(axis)
     if size & (size - 1):
         return lax.psum(value, axis)
     step = 1
     while step < size:
         pairs = [(i, i ^ step) for i in range(size)]
-        value = value + lax.ppermute(value.astype(send_as), axis, pairs).astype(jnp.float32)
+        value = value + lax.ppermute(value, axis, pairs)
         step *= 2
     return value
 
@@ -92,8 +92,9 @@
 
 
 def parts_kernel(*refs):
-    sources, sum_ref, copied = refs[:5], refs[5], refs[-1]
-    held_refs = out_ref, out_query_ref, in_ref, in_query_ref, grads_ref = refs[6:-1]
+    sources, keep_ref, send_ref, copied = refs[:5], refs[5], refs[6], refs[-1]
+    held_refs = out_ref, out_query_ref, in_ref, in_query_ref, grads_ref = refs[7:-2]
+    sum_ref = refs[-2]
     copies = [
         pltpu.make_async_copy(source, target, copied.at[place])
         for place, (source, target) in enumerate(zip(sources, held_refs))
@@ -118,16 +119,25 @@
             grads_ref[pl.ds(start, BLOCK), :], out_ref[...]
         )
 
+    core, split = lax.axis_index("rep"), rows + width
+    half = grads_ref.shape[0] // 2
+    for part_ref, whose in ((keep_ref, core), (send_ref, 1 - core)):
+        part_ref[:split] = sum_ref[:split]
+        start = pl.multiple_of(split + whose * half, 8)
+        part_ref[split:] = sum_ref[pl.ds(start, half), :]
+
 
 def small_parts(basis_in, query_in, basis_out, query_out, out_grads):
-    high = basis_in.shape[0] + basis_out.shape[0] + out_grads.shape[0]
+    split, tokens, pairs = basis_in.shape[0] + basis_out.shape[0], out_grads.shape[0], query_in.shape[1]
+    high = split + tokens
     sources = (basis_out, query_out, basis_in, query_in, out_grads)
+    half = jax.ShapeDtypeStruct((split + tokens // 2, pairs), jnp.float32)
     return pl.pallas_call(
         parts_kernel,
         in_specs=[pl.BlockSpec(memory_space=pl.ANY)] * len(sources),
-        out_shape=jax.ShapeDtypeStruct((high, query_in.shape[1]), jnp.float32),
+        out_shape=[half, half],
         scratch_shapes=[pltpu.VMEM(source.shape, source.dtype) for source in sources]
-        + [pltpu.SemaphoreType.DMA((len(sources),))],
+        + [pltpu.VMEM((high, pairs), jnp.float32), pltpu.SemaphoreType.DMA((len(sources),))],
         compiler_params=pltpu.CompilerParams(vmem_limit_bytes=VMEM_LIMIT),
     )(*[in_hbm(source) for source in sources])
 
@@ -180,47 +190,53 @@
     weigh(query_count, packs, out_query_ref[...], weights_ref)
 
 
-def load_kernel(source_ref, acts_ref, copied):
-    copies = [
-        pltpu.make_async_copy(
-            source_ref.at[pl.ds(start, BLOCK)], acts_ref.at[pl.ds(start, BLOCK)], copied.at[place]
-        )
-        for place, start in enumerate(range(0, acts_ref.shape[0], BLOCK))
-    ]
-    for copy in copies:
-        copy.start()
-    for copy in copies:
-        copy.wait()
-
-
-def first_kernel(acts_ref, *refs):
-    slots, (weights_ref, grad_ref, onehot_ref, sums_ref) = refs[:8], refs[8:]
+def first_kernel(source_ref, *refs):
+    slots, (total_ref, acts_ref, copied) = refs[:8], refs[8:]
     columns = slots[0].shape[1]
     group = lax.axis_index("groups")
-
-    def body(start, sums):
+    steps = acts_ref.shape[0] // BLOCK
+    parts = 2
+
+    def copies(step):
+        size = BLOCK // parts
+        places = [pl.ds(step * BLOCK + part * size, size) for part in range(parts)]
+        return [
+            pltpu.make_async_copy(source_ref.at[place], acts_ref.at[place], copied.at[step, part])
+            for part, place in enumerate(places)
+        ]
+
+    for copy in copies(0):
+        copy.start()
+    for step in range(steps):
+        for copy in copies(step):
+            copy.wait()
+        if step + 1 < steps:
+            for copy in copies(step + 1):
+                copy.start()
+        start = step * BLOCK
         total = 0.0
         for place in range(4):
             half = group if place < 2 else 1 - group
             total = total + project(
                 acts_ref, start, (slots[place], slots[4 + place]), half, place % 2 * columns
             )
-        return sums + mix(start, total, mixing(start, weights_ref[0], grad_ref), onehot_ref)
+        total_ref[pl.ds(start, BLOCK), :] = total
+
+
+def mine_kernel(
+    acts_ref, mine_2_ref, mine_3_ref, first_ref, weights_ref, grad_ref, onehot_ref,
+    total_ref, mixed_ref, sums_ref,
+):
+    group = lax.axis_index("groups")
+
+    def body(start, sums):
+        rows = pl.ds(start, BLOCK)
+        total_ref[rows, :] = project(acts_ref, start, (mine_2_ref, mine_3_ref), group)
+        mixed_ref[rows, :] = mixing(start, weights_ref[1], grad_ref)
+        mixed = mixing(start, weights_ref[0], grad_ref)
+        return sums + mix(start, first_ref[rows, :], mixed, onehot_ref)
 
     sums_ref[...] = blocks(acts_ref.shape[0], body, jnp.zeros(sums_ref.shape, jnp.float32))
-
-
-def mine_kernel(acts_ref, mine_2_ref, mine_3_ref, weights_ref, grad_ref, total_ref, mixed_ref):
-    group = lax.axis_index("groups")
-
-    def body(start, carry):
-        total_ref[pl.ds(start, BLOCK), :] = project(
-            acts_ref, start, (mine_2_ref, mine_3_ref), group
-        )
-        mixed_ref[pl.ds(start, BLOCK), :] = mixing(start, weights_ref[1], grad_ref)
-        return carry
-
-    blocks(acts_ref.shape[0], body, 0)
 
 
 def last_kernel(
@@ -288,18 +304,6 @@
     return contract_last(per_token, onehot, precision=lax.Precision.HIGHEST)
 
 
-def to_send(part, split):
-    high = lax.reduce_precision(part[:split], 8, 7)
-    low = part[:split] - high
-    return jnp.concatenate([high, low, part[split:]], axis=0).astype(jnp.bfloat16)
-
-
-def add_sent(part, other, split):
-    high, low, rest = other[:split], other[split : 2 * split], other[2 * split :]
-    first = part[:split] + high.astype(jnp.float32) + low.astype(jnp.float32)
-    return jnp.concatenate([first, part[split:] + rest.astype(jnp.float32)], axis=0)
-
-
 def stepped_scores(
     acts, out_grads, basis_in, basis_out, eigvals, query_out, query_in, onehot
 ):
@@ -333,58 +337,71 @@
         mine_1.append(along(chunk))
 
     split = rows + width
-    part = small_parts(held(basis_in, *half), query_in, basis_out, query_out, out_grads)
-    other = lax.ppermute(to_send(part, split), "rep", pair)
-    part = add_sent(part, held(other, *mine_1, *middle_3), split)
-    sent = to_send(part, split)
-    other = lax.ppermute(sent, "eig", pair)
-    acts = call(
-        load_kernel,
-        pltpu.VMEM(acts.shape, acts.dtype),
-        in_hbm(held(acts, sent)),
-        in_specs=[pl.BlockSpec(memory_space=pl.ANY)],
-        scratch_shapes=[pltpu.SemaphoreType.DMA((tokens // BLOCK,))],
-    )
-    acts = in_vmem(acts)
-
-    mine_2, theirs_1 = [], []
-    for first, middle, rest in zip(mine_1, middle_3, other_half):
-        from_pair = along(jnp.where(inner, middle, held(rest, first)))
-        from_across = across(held(first, middle), over_y)
-        mine_2.append((from_across, from_pair))
-    arrived = [chunk for both in mine_2 for chunk in both] + [acts]
+    keep, send = small_parts(held(basis_in, *half), query_in, basis_out, query_out, out_grads)
+    other = lax.ppermute(send, "rep", pair)
+    keep = keep + held(other, *mine_1, *middle_3)
+    small, grad_half = keep[:split], keep[split:]
+    small_other = lax.ppermute(small, "eig", pair)
+    grad_other = lax.ppermute(grad_half, "eig", pair)
+
+    arrived = []
+    for after, first, middle, rest in zip((half[0], keep), mine_1, middle_3, other_half):
+        from_pair = along(jnp.where(inner, middle, held(rest, first, after)))
+        from_across = across(held(first, middle, after), over_y)
+        arrived.append((from_pair, from_across))
+
+    small = (small + held(small_other, *arrived[0])).astype(jnp.bfloat16)
+    in_query, out_query = small[:rows], small[rows:]
+    packs = by_distance(jnp.concatenate([in_query, eigvals], axis=1))
+
+    ready = [chunk for both in arrived for chunk in both] + packs[1:]
     mine_2 = jnp.concatenate(
-        [jnp.where(inner, held(here, *arrived), there) for here, there in mine_2], axis=1
+        [jnp.where(inner, held(there, *ready), here) for here, there in arrived], axis=1
     )
     theirs_1 = [
-        jnp.where(inner, held(there, mine_2), held(here, mine_2))
-        for here, there in zip(arrived[0:4:2], arrived[1:4:2])
+        jnp.where(inner, held(here, mine_2), held(there, mine_2)) for here, there in arrived
     ]
     theirs_2 = swapped(mine_2)
     mine_3 = along(mine_2)
 
-    part = add_sent(part, held(other, mine_2), split).astype(jnp.bfloat16)
-    in_query, out_query, grad_proj = part[:rows], part[rows:split], part[split:]
-    packs = by_distance(jnp.concatenate([in_query, eigvals], axis=1))
+    grad_half = (grad_half + held(grad_other, mine_2)).astype(jnp.bfloat16)
+    grad_other = lax.ppermute(grad_half, "rep", pair)
+    of_first = lax.axis_index("rep") == 0
+    grad_proj = jnp.concatenate(
+        [
+            jnp.where(of_first, grad_half, grad_other),
+            jnp.where(of_first, grad_other, grad_half),
+        ],
+        axis=0,
+    )
+    total_shape = jax.ShapeDtypeStruct((tokens, LANES), jnp.float32)
+    first_total, acts = call(
+        first_kernel,
+        [total_shape, pltpu.VMEM(acts.shape, acts.dtype)],
+        in_hbm(held(acts, grad_half)), *half, *other_half, *mine_1, *theirs_1,
+        in_specs=[pl.BlockSpec(memory_space=pl.ANY)]
+        + [pl.BlockSpec(memory_space=pltpu.VMEM)] * 8,
+        scratch_shapes=[pltpu.SemaphoreType.DMA((tokens // BLOCK, 2))],
+    )
+    acts = in_vmem(acts)
+
+    cut = mine_3.shape[1] // 2
+    left_3 = along(held(theirs_2, first_total)[:, :cut])
+    right_3 = swapped(held(mine_3, first_total)[:, cut:])
+    mixed_width = 2 * query_count * rows
     weights = call(
         functools.partial(weight_kernel, query_count),
-        jax.ShapeDtypeStruct((2, 2 * query_count * rows, width), jnp.bfloat16),
+        jax.ShapeDtypeStruct((2, mixed_width, width), jnp.bfloat16),
         *packs, out_query,
     )
-    mixed_width = 2 * query_count * rows
-    sums = call(
-        first_kernel,
-        jax.ShapeDtypeStruct((seq_count, mixed_width), jnp.float32),
-        acts, *half, *other_half, *mine_1, *theirs_1, weights, grad_proj, onehot,
-    )
-
-    cut = mine_3.shape[1] // 2
-    left_3 = along(held(theirs_2, sums)[:, :cut])
-    right_3 = swapped(held(mine_3, sums)[:, cut:])
-    total, mixed = call(
+    total, mixed, sums = call(
         mine_kernel,
-        [jax.ShapeDtypeStruct((tokens, size), jnp.float32) for size in (LANES, mixed_width)],
-        acts, mine_2, mine_3, weights, grad_proj,
+        [
+            total_shape,
+            jax.ShapeDtypeStruct((tokens, mixed_width), jnp.float32),
+            jax.ShapeDtypeStruct((seq_count, mixed_width), jnp.float32),
+        ],
+        acts, mine_2, mine_3, first_total, weights, grad_proj, onehot,
     )
     places = lax.axis_size("blk")
     return call(
@@ -395,14 +412,12 @@
 
 
 def plain_path(acts, out_grads, basis_in, basis_out, eigvals, query_out, query_in, onehot):
-    def whole_sum(part, send_as):
-        return swap_sum(swap_sum(part, "rep", jnp.float32), "eig", send_as).astype(jnp.bfloat16)
-
-    in_query = whole_sum(jnp.dot(basis_in, query_in, preferred_element_type=jnp.float32), jnp.float32)
-    out_query = whole_sum(
-        jnp.dot(basis_out, query_out, preferred_element_type=jnp.float32), jnp.float32
-    )
-    grad_proj = whole_sum(contract_last(out_grads, basis_out), jnp.bfloat16)
+    def whole_sum(part):
+        return swap_sum(swap_sum(part, "rep"), "eig").astype(jnp.bfloat16)
+
+    in_query = whole_sum(jnp.dot(basis_in, query_in, preferred_element_type=jnp.float32))
+    out_query = whole_sum(jnp.dot(basis_out, query_out, preferred_element_type=jnp.float32))
+    grad_proj = whole_sum(contract_last(out_grads, basis_out))
     pack = jnp.concatenate([in_query, eigvals], axis=1)
     scores = plain_scores(acts, basis_in, pack, out_query, grad_proj, onehot.astype(jnp.float32))
     queries, columns = scores.shape
@@ -421,6 +436,7 @@
     stepped = (
         all(lax.axis_size(axis) == size for axis, size in zip(AXES, (2, 4, 2, 2)))
         and 2 * rows == LANES
+        and (rows + basis_out.shape[0]) % 16 == acts.shape[0] % 32 == 0
         and features % (4 * LANES) == 0
         and acts.shape[0] % BLOCK == 0
         and pairs == basis_out.shape[0] == LANES

time: 67.8 us -> 65.3 us (0.963)
  waiting for transfers between devices: 11.2 us -> 6.72 us
  starting transfers between devices: 25 us -> 26.7 us
    ppermute x3, waiting for transfers between devices: 6.96 us -> 3.11 us  [by_distance(): lax.ppermute(value, axis, [(i, i ^ k) for i in range(size)])]
    ppermute x2 -> x4, starting transfers between devices: 1.63 us -> 3.76 us  [the longest x1 1.56 us: stepped_scores(): small_other = lax.ppermute(small, 'eig', pair)]
    ppermute x6, waiting for transfers between devices: 2.49 us -> 0.85 us  [along(): return lax.ppermute(value, 'blk', [(i, i ^ 1) for i in range(4)])]
    ppermute x2, waiting for transfers between devices: 1.71 us -> 2.74 us  [swapped(): return lax.ppermute(value, 'groups', pair)]
    ppermute x2, starting transfers between devices: 3.1 us -> 2.15 us  [swapped(): return lax.ppermute(value, 'groups', pair)]
    pallas_call x5 -> x4, Pallas kernels: 13.2 us -> 13.7 us  [call(): pl.pallas_call(kernel, out_shape=out_shape, compiler_params=pltpu.Compile...]
  transfers between devices with their start and end apart: 17 -> 19, of which waited for: 5 -> 4; matrix products, arithmetic and copies ran while one was open for 1% -> 1% of each run, Pallas kernels for 22% -> 24%
where the time goes in v8:
time: 65.3 us; the launch traced here: 65.1 us
  starting transfers between devices  26.7 us (41%)
  Pallas kernels  19.4 us (30%)
  blocking collectives  11 us (17%)
  waiting for transfers between devices  6.72 us (10%)
  other arithmetic  0.96 us (1%)
    pallas_call x4, Pallas kernels, call(): pl.pallas_call(kernel, out_shape=out_shape, compiler_params=pltpu.Compile...  13.7 us
    ppermute x6, starting transfers between devices, along(): return lax.ppermute(value, 'blk', [(i, i ^ 1) for i in range(4)])  12.6 us
    all_to_all x1, blocking collectives, on_device(): parts = lax.all_to_all(parts, ('blk', 'eig', 'rep'), 0, 0, tiled=True)  11 us
    ppermute x3, starting transfers between devices, by_distance(): lax.ppermute(value, axis, [(i, i ^ k) for i in range(size)])  5.12 us
    pallas_call x1, Pallas kernels, small_parts(): pl.pallas_call(parts_kernel, in_specs=[pl.BlockSpec(memory_space=pl.ANY)]...  4.48 us
    ppermute x3, waiting for transfers between devices, by_distance(): lax.ppermute(value, axis, [(i, i ^ k) for i in range(size)])  3.11 us
    ppermute x4, starting transfers between devices, across(): lax.ppermute(value, AXES, pairing(lambda g, b, e, r: (g, 3 - b, e, r) if...  3.04 us
    ppermute x2, waiting for transfers between devices, swapped(): return lax.ppermute(value, 'groups', pair)  2.74 us
  transfers between devices with their start and end apart: 19, of which 4 were waited for; matrix products, arithmetic and copies ran while one was open for 1% of the time, Pallas kernels for 24%

profile of v8, /device:TPU:0, one launch (start us, length us, event | category | flops | bytes accessed | tf_op | source)
XLA Modules:
  0.0 65.1 jit_solution(13147094692402787411)
XLA Ops:
  0.0 1.3 %shard_map.91 = (bf16[64,1792]{1,0:T(8,128)(2,1)S(1)}, bf16[64,1792]{1,0:T(8,128)(2,1)S(1)}, bf16[64,1792]{1,0:T(8,128)(2,1)S(1)}, bf16[64,1792]{1,0:T(8,128)(2,1)S(1)}) custom-call(bf16[64,7168]{1,0:T(8,128)(2,1)} %refs_2_), custom_call_target="tpu_custom_call" | custom-call | tf_op jit(solution)/shard_map/pallas_call | solution.py:86
  1.3 3.1 %collective-permute-start.1 = (bf16[64,1792]{1,0:T(8,128)(2,1)S(1)}, bf16[64,1792]{1,0:T(8,128)(2,1)S(1)}, u32[]{:S(2)}, u32[]{:S(2)}) collective-permute-start(bf16[64,1792]{1,0:T(8,128)(2,1)S(1)} %get-tuple-element.33.refs_0_), channel_id=1, source_target_pairs={{0,4},{4,0},{8,12},{12,8},{1,5},{5,1},{9,13},{13,9},{2,6},{6,2},{1... | collective-permute-start | bytes 688136 | tf_op jit(solution)/shard_map/ppermute | solution.py:318
  4.4 3.1 %collective-permute-start.2 = (bf16[64,1792]{1,0:T(8,128)(2,1)S(1)}, bf16[64,1792]{1,0:T(8,128)(2,1)S(1)}, u32[]{:S(2)}, u32[]{:S(2)}) collective-permute-start(bf16[64,1792]{1,0:T(8,128)(2,1)S(1)} %get-tuple-element.34.refs_1_), channel_id=1, source_target_pairs={{0,4},{4,0},{8,12},{12,8},{1,5},{5,1},{9,13},{13,9},{2,6},{6,2},{1... | collective-permute-start | bytes 688136 | tf_op jit(solution)/shard_map/ppermute | solution.py:318
  7.6 4.5 %shard_map.92 = (f32[576,128]{1,0:T(8,128)S(1)}, f32[576,128]{1,0:T(8,128)S(1)}) custom-call(bf16[128,2048]{1,0:T(8,128)(2,1)} %refs_0_.1, bf16[2048,128]{1,0:T(8,128)(2,1)} %refs_1_.1, bf16[64,7168]{1,0:T(8,128)(2,1)} %refs_2_, bf16[7168,128]{1,0:T(8,128)(2,1)} %refs_3_.1, bf16[768,2048]{1,0:T(8,128)(2,1)} %refs_4_.1), custom_call_target="tpu_custom_call" | custom-call | tf_op jit(solution)/shard_map/pallas_call | solution.py:135
  12.1 0.6 collective-permute-start
  12.6 0.1 select_reduce_fusion
  12.8 1.4 %collective-permute-start.7 = (bf16[64,1792]{1,0:T(8,128)(2,1)S(1)}, bf16[64,1792]{1,0:T(8,128)(2,1)S(1)}, u32[]{:S(2)}, u32[]{:S(2)}) collective-permute-start(bf16[64,1792]{1,0:T(8,128)(2,1)S(1)} %broadcast_select_fusion.5), channel_id=1, source_target_pairs={{0,4},{4,0},{8,12},{12,8},{1,5},{5,1},{9,13},{13,9},{2,6},{6,2},{1... | collective-permute-start | bytes 688136 | tf_op jit(solution)/shard_map/ppermute | solution.py:318
  14.1 1.5 %collective-permute-start.6 = (bf16[64,1792]{1,0:T(8,128)(2,1)S(1)}, bf16[64,1792]{1,0:T(8,128)(2,1)S(1)}, u32[]{:S(2)}, u32[]{:S(2)}) collective-permute-start(bf16[64,1792]{1,0:T(8,128)(2,1)S(1)} %collective-permute-done.1.refs_4_), channel_id=1, source_target_pairs={{0,16},{1,17},{2,18},{3,19},{4,8},{5,9},{6,10},{7,11},{8,4},{9,5},... | collective-permute-start | bytes 688136 | tf_op jit(solution)/shard_map/ppermute | solution.py:324
  15.7 1.6 %collective-permute-start.10 = (f32[192,128]{1,0:T(8,128)S(1)}, f32[192,128]{1,0:T(8,128)S(1)}, u32[]{:S(2)}, u32[]{:S(2)}) collective-permute-start(f32[192,128]{1,0:T(8,128)S(1)} %slice.25), channel_id=1, source_target_pairs={{0,2},{2,0},{1,3},{3,1},{4,6},{6,4},{5,7},{7,5},{8,10},{10,8},{9,1... | collective-permute-start | bytes 294920 | tf_op jit(solution)/shard_map/ppermute | solution.py:344
  17.3 2.9 %collective-permute-start.8 = (bf16[64,1792]{1,0:T(8,128)(2,1)S(1)}, bf16[64,1792]{1,0:T(8,128)(2,1)S(1)}, u32[]{:S(2)}, u32[]{:S(2)}) collective-permute-start(bf16[64,1792]{1,0:T(8,128)(2,1)S(1)} %broadcast_select_fusion.4), channel_id=1, source_target_pairs={{0,4},{4,0},{8,12},{12,8},{1,5},{5,1},{9,13},{13,9},{2,6},{6,2},{1... | collective-permute-start | bytes 688136 | tf_op jit(solution)/shard_map/ppermute | solution.py:318
  20.2 1.5 %collective-permute-start.9 = (bf16[64,1792]{1,0:T(8,128)(2,1)S(1)}, bf16[64,1792]{1,0:T(8,128)(2,1)S(1)}, u32[]{:S(2)}, u32[]{:S(2)}) collective-permute-start(bf16[64,1792]{1,0:T(8,128)(2,1)S(1)} %collective-permute-done.2.refs_5_), channel_id=1, source_target_pairs={{0,16},{1,17},{2,18},{3,19},{4,8},{5,9},{6,10},{7,11},{8,4},{9,5},... | collective-permute-start | bytes 688136 | tf_op jit(solution)/shard_map/ppermute | solution.py:324
  21.8 1.7 %collective-permute-start.11 = (bf16[64,256]{1,0:T(8,128)(2,1)S(1)}, bf16[64,256]{1,0:T(8,128)(2,1)S(1)}, u32[]{:S(2)}, u32[]{:S(2)}) collective-permute-start(bf16[64,256]{1,0:T(8,128)(2,1)S(1)} %pad_maximum_fusion.2.refs_0_), channel_id=1, source_target_pairs={{0,4},{4,0},{8,12},{12,8},{1,5},{5,1},{9,13},{13,9},{2,6},{6,2},{1... | collective-permute-start | bytes 98312 | tf_op jit(solution)/shard_map/ppermute | solution.py:46
  23.6 2.3 %collective-permute-start.12 = (bf16[64,256]{1,0:T(8,128)(2,1)S(1)}, bf16[64,256]{1,0:T(8,128)(2,1)S(1)}, u32[]{:S(2)}, u32[]{:S(2)}) collective-permute-start(bf16[64,256]{1,0:T(8,128)(2,1)S(1)} %pad_maximum_fusion.2.refs_0_), channel_id=1, source_target_pairs={{0,8},{4,12},{8,0},{12,4},{1,9},{5,13},{9,1},{13,5},{2,10},{6,14},... | collective-permute-start | bytes 98312 | tf_op jit(solution)/shard_map/ppermute | solution.py:46
  25.8 1.1 %collective-permute-start.13 = (bf16[64,256]{1,0:T(8,128)(2,1)S(1)}, bf16[64,256]{1,0:T(8,128)(2,1)S(1)}, u32[]{:S(2)}, u32[]{:S(2)}) collective-permute-start(bf16[64,256]{1,0:T(8,128)(2,1)S(1)} %pad_maximum_fusion.2.refs_0_), channel_id=1, source_target_pairs={{0,12},{4,8},{8,4},{12,0},{1,13},{5,9},{9,5},{13,1},{2,14},{6,10},... | collective-permute-start | bytes 98312 | tf_op jit(solution)/shard_map/ppermute | solution.py:46
  27.0 1.6 %collective-permute-start.5 = (f32[384,128]{1,0:T(8,128)S(1)}, f32[384,128]{1,0:T(8,128)S(1)}, u32[]{:S(2)}, u32[]{:S(2)}) collective-permute-start(f32[384,128]{1,0:T(8,128)S(1)} %slice.24), channel_id=1, source_target_pairs={{0,2},{2,0},{1,3},{3,1},{4,6},{6,4},{5,7},{7,5},{8,10},{10,8},{9,1... | collective-permute-start | bytes 589832 | tf_op jit(solution)/shard_map/ppermute | solution.py:345
  28.5 0.3 collective-permute-done.12.refs_2_
  28.8 2.8 %collective-permute-done.13.refs_3_ = bf16[64,256]{1,0:T(8,128)(2,1)S(1)} collective-permute-done((bf16[64,256]{1,0:T(8,128)(2,1)S(1)}, bf16[64,256]{1,0:T(8,128)(2,1)S(1)}, u32[]{:S(2)}, u32[]{:S(2)}) %collective-permute-start.13) | collective-permute-done | bytes 32800 | tf_op jit(solution)/shard_map/ppermute | solution.py:46
  31.7 0.5 shard_map.94.weights_ref
  32.1 0.0 collective-permute-done.8
  32.2 0.1 collective-permute-start.16
  32.3 1.3 %collective-permute-start.14 = (bf16[64,3584]{1,0:T(8,128)(2,1)S(1)}, bf16[64,3584]{1,0:T(8,128)(2,1)S(1)}, u32[]{:S(2)}, u32[]{:S(2)}) collective-permute-start(bf16[64,3584]{1,0:T(8,128)(2,1)S(1)} %pad_maximum_fusion.mine_2_ref), channel_id=1, source_target_pairs={{0,16},{16,0},{1,17},{17,1},{2,18},{18,2},{3,19},{19,3},{4,20},{20... | collective-permute-start | bytes 1376264 | tf_op jit(solution)/shard_map/ppermute | solution.py:321
  33.6 0.1 collective-permute-start.18
  33.7 0.1 broadcast_select_fusion
  33.8 8.2 %shard_map.93 = (f32[768,128]{1,0:T(8,128)S(1)}, bf16[768,7168]{1,0:T(8,128)(2,1)S(1)}) custom-call(bf16[768,7168]{1,0:T(8,128)(2,1)} %source_ref, bf16[64,1792]{1,0:T(8,128)(2,1)S(1)} %get-tuple-element.33.refs_0_, bf16[64,1792]{1,0:T(8,128)(2,1)S(1)} %get-tuple-element.34.refs_1_, bf16[64,1792]{1,0:T(8,128)(2,1)S(1)} %get-tuple-element.41.refs_2_, ...), custom_call_target="tpu_custom_call" | custom-call | flops 1 | bytes 1 | tf_op jit(solution)/shard_map/pallas_call | solution.py:272
  42.1 0.9 %collective-permute-start.17 = (bf16[64,1792]{1,0:T(8,128)(2,1)S(1)}, bf16[64,1792]{1,0:T(8,128)(2,1)S(1)}, u32[]{:S(2)}, u32[]{:S(2)}) collective-permute-start(bf16[64,1792]{1,0:T(8,128)(2,1)S(1)} %slice.22), channel_id=1, source_target_pairs={{0,16},{16,0},{1,17},{17,1},{2,18},{18,2},{3,19},{19,3},{4,20},{20... | collective-permute-start | bytes 688136 | tf_op jit(solution)/shard_map/ppermute | solution.py:321
  43.0 2.0 %collective-permute-start.15 = (bf16[64,1792]{1,0:T(8,128)(2,1)S(1)}, bf16[64,1792]{1,0:T(8,128)(2,1)S(1)}, u32[]{:S(2)}, u32[]{:S(2)}) collective-permute-start(bf16[64,1792]{1,0:T(8,128)(2,1)S(1)} %slice.21), channel_id=1, source_target_pairs={{0,4},{4,0},{8,12},{12,8},{1,5},{5,1},{9,13},{13,9},{2,6},{6,2},{1... | collective-permute-start | bytes 688136 | tf_op jit(solution)/shard_map/ppermute | solution.py:318
  45.0 2.4 %shard_map.95 = (f32[768,128]{1,0:T(8,128)S(1)}, f32[768,512]{1,0:T(8,128)S(1)}, f32[8,512]{1,0:T(8,128)S(1)}) custom-call(bf16[768,7168]{1,0:T(8,128)(2,1)S(1)} %get-tuple-element.54.acts_ref, bf16[64,3584]{1,0:T(8,128)(2,1)S(1)} %pad_maximum_fusion.mine_2_ref, bf16[64,3584]{1,0:T(8,128)(2,1)S(1)} %collective-permute-done.16.mine_3_ref, ...), custom_call_target="tpu_custom_call" | custom-call | flops 1 | bytes 1 | tf_op jit(solution)/shard_map/pallas_call | solution.py:272
  47.4 2.7 %collective-permute-done.17.right_ref = bf16[64,1792]{1,0:T(8,128)(2,1)S(1)} collective-permute-done((bf16[64,1792]{1,0:T(8,128)(2,1)S(1)}, bf16[64,1792]{1,0:T(8,128)(2,1)S(1)}, u32[]{:S(2)}, u32[]{:S(2)}) %collective-permute-start.17) | collective-permute-done | bytes 229408 | tf_op jit(solution)/shard_map/ppermute | solution.py:321
  50.1 0.8 %collective-permute-done.15.left_ref = bf16[64,1792]{1,0:T(8,128)(2,1)S(1)} collective-permute-done((bf16[64,1792]{1,0:T(8,128)(2,1)S(1)}, bf16[64,1792]{1,0:T(8,128)(2,1)S(1)}, u32[]{:S(2)}, u32[]{:S(2)}) %collective-permute-start.15) | collective-permute-done | bytes 229408 | tf_op jit(solution)/shard_map/ppermute | solution.py:318
  51.0 2.6 %shard_map.96 = f32[16,2]{1,0:T(8,128)S(1)} custom-call(bf16[768,7168]{1,0:T(8,128)(2,1)S(1)} %get-tuple-element.54.acts_ref, bf16[64,3584]{1,0:T(8,128)(2,1)S(1)} %collective-permute-done.14.theirs_2_ref, bf16[64,1792]{1,0:T(8,128)(2,1)S(1)} %collective-permute-done.15.left_ref, bf16[64,1792]{1,0:T(8,128)(2,1)S(1)} %collective-permute-done.17.right_ref, ...), custom_call_target="tpu_custom_call" | custom-call | flops 1 | bytes 1 | tf_op jit(solution)/shard_map/pallas_call | solution.py:272
  53.6 11.0 %all_to_all.9 = f32[16,1,2]{2,1,0:T(1,128)S(1)} all-to-all(f32[16,1,2]{2,1,0:T(1,128)S(1)} %bitcast.4), channel_id=1, replica_groups=mesh['groups'=2,'blk'=4,'eig'=2,'rep'=2] {'blk','eig','rep'}, dimensions={0} | all-to-all | bytes 256 | tf_op jit(solution)/shard_map/all_to_all | solution.py:448
  64.6 0.5 reduce_sum.21
  (40 shorter events, 0.4 us)
Async XLA Ops:
  1.3 11.4 %collective-permute-start.1 = (bf16[64,1792]{1,0:T(8,128)(2,1)S(1)}, bf16[64,1792]{1,0:T(8,128)(2,1)S(1)}, u32[]{:S(2)}, u32[]{:S(2)}) collective-permute-start(bf16[64,1792]{1,0:T(8,128)(2,1)S(1)} %get-tuple-element.33.refs_0_), channel_id=1, source_target_pairs={{0,4},{4,0},{8,12},{12,8},{1,5},{5,1},{9,13},{13,9},{2,6},{6,2},{1... | collective-permute-start | bytes 688136 | tf_op jit(solution)/shard_map/ppermute | solution.py:318
  4.4 8.3 %collective-permute-start.3 = (bf16[64,1792]{1,0:T(8,128)(2,1)S(1)}, bf16[64,1792]{1,0:T(8,128)(2,1)S(1)}, u32[]{:S(2)}, u32[]{:S(2)}) collective-permute-start(bf16[64,1792]{1,0:T(8,128)(2,1)S(1)} %get-tuple-element.33.refs_0_), channel_id=1, source_target_pairs={{0,1},{1,0},{2,3},{3,2},{4,8},{5,9},{6,10},{7,11},{8,4},{9,5},{10,... | collective-permute-start | bytes 688136 | tf_op jit(solution)/shard_map/ppermute | solution.py:324
  4.4 8.2 %copy-start.1 = (s32[768]{0:T(1024)S(1)}, s32[768]{0:T(1024)}, u32[]{:S(2)}) copy-start(s32[768]{0:T(1024)} %param.16) | copy-start | bytes 9220
  4.4 8.2 %copy-start.2 = (s32[8]{0:T(128)S(1)}, s32[8]{0:T(128)}, u32[]{:S(2)}) copy-start(s32[8]{0:T(128)} %param.17) | copy-start | bytes 100
  4.4 17.4 %copy-start = (bf16[64,128]{1,0:T(8,128)(2,1)S(1)}, bf16[64,128]{1,0:T(8,128)(2,1)}, u32[]{:S(2)}) copy-start(bf16[64,128]{1,0:T(8,128)(2,1)} %param.13) | copy-start | bytes 49156
  4.4 11.2 %collective-permute-start.2 = (bf16[64,1792]{1,0:T(8,128)(2,1)S(1)}, bf16[64,1792]{1,0:T(8,128)(2,1)S(1)}, u32[]{:S(2)}, u32[]{:S(2)}) collective-permute-start(bf16[64,1792]{1,0:T(8,128)(2,1)S(1)} %get-tuple-element.34.refs_1_), channel_id=1, source_target_pairs={{0,4},{4,0},{8,12},{12,8},{1,5},{5,1},{9,13},{13,9},{2,6},{6,2},{1... | collective-permute-start | bytes 688136 | tf_op jit(solution)/shard_map/ppermute | solution.py:318
  7.6 8.1 %collective-permute-start.4 = (bf16[64,1792]{1,0:T(8,128)(2,1)S(1)}, bf16[64,1792]{1,0:T(8,128)(2,1)S(1)}, u32[]{:S(2)}, u32[]{:S(2)}) collective-permute-start(bf16[64,1792]{1,0:T(8,128)(2,1)S(1)} %get-tuple-element.34.refs_1_), channel_id=1, source_target_pairs={{0,1},{1,0},{2,3},{3,2},{4,8},{5,9},{6,10},{7,11},{8,4},{9,5},{10,... | collective-permute-start | bytes 688136 | tf_op jit(solution)/shard_map/ppermute | solution.py:324
  12.1 3.6 %collective-permute-start = (f32[576,128]{1,0:T(8,128)S(1)}, f32[576,128]{1,0:T(8,128)S(1)}, u32[]{:S(2)}, u32[]{:S(2)}) collective-permute-start(f32[576,128]{1,0:T(8,128)S(1)} %get-tuple-element.37), channel_id=1, source_target_pairs={{0,1},{1,0},{2,3},{3,2},{4,5},{5,4},{6,7},{7,6},{8,9},{9,8},{10,11... | collective-permute-start | bytes 884744 | tf_op jit(solution)/shard_map/ppermute | solution.py:341
  12.8 9.0 %collective-permute-start.7 = (bf16[64,1792]{1,0:T(8,128)(2,1)S(1)}, bf16[64,1792]{1,0:T(8,128)(2,1)S(1)}, u32[]{:S(2)}, u32[]{:S(2)}) collective-permute-start(bf16[64,1792]{1,0:T(8,128)(2,1)S(1)} %broadcast_select_fusion.5), channel_id=1, source_target_pairs={{0,4},{4,0},{8,12},{12,8},{1,5},{5,1},{9,13},{13,9},{2,6},{6,2},{1... | collective-permute-start | bytes 688136 | tf_op jit(solution)/shard_map/ppermute | solution.py:318
  14.1 7.6 %collective-permute-start.6 = (bf16[64,1792]{1,0:T(8,128)(2,1)S(1)}, bf16[64,1792]{1,0:T(8,128)(2,1)S(1)}, u32[]{:S(2)}, u32[]{:S(2)}) collective-permute-start(bf16[64,1792]{1,0:T(8,128)(2,1)S(1)} %collective-permute-done.1.refs_4_), channel_id=1, source_target_pairs={{0,16},{1,17},{2,18},{3,19},{4,8},{5,9},{6,10},{7,11},{8,4},{9,5},... | collective-permute-start | bytes 688136 | tf_op jit(solution)/shard_map/ppermute | solution.py:324
  15.7 6.0 %collective-permute-start.10 = (f32[192,128]{1,0:T(8,128)S(1)}, f32[192,128]{1,0:T(8,128)S(1)}, u32[]{:S(2)}, u32[]{:S(2)}) collective-permute-start(f32[192,128]{1,0:T(8,128)S(1)} %slice.25), channel_id=1, source_target_pairs={{0,2},{2,0},{1,3},{3,1},{4,6},{6,4},{5,7},{7,5},{8,10},{10,8},{9,1... | collective-permute-start | bytes 294920 | tf_op jit(solution)/shard_map/ppermute | solution.py:344
  17.3 14.8 %collective-permute-start.8 = (bf16[64,1792]{1,0:T(8,128)(2,1)S(1)}, bf16[64,1792]{1,0:T(8,128)(2,1)S(1)}, u32[]{:S(2)}, u32[]{:S(2)}) collective-permute-start(bf16[64,1792]{1,0:T(8,128)(2,1)S(1)} %broadcast_select_fusion.4), channel_id=1, source_target_pairs={{0,4},{4,0},{8,12},{12,8},{1,5},{5,1},{9,13},{13,9},{2,6},{6,2},{1... | collective-permute-start | bytes 688136 | tf_op jit(solution)/shard_map/ppermute | solution.py:318
  20.2 11.9 %collective-permute-start.9 = (bf16[64,1792]{1,0:T(8,128)(2,1)S(1)}, bf16[64,1792]{1,0:T(8,128)(2,1)S(1)}, u32[]{:S(2)}, u32[]{:S(2)}) collective-permute-start(bf16[64,1792]{1,0:T(8,128)(2,1)S(1)} %collective-permute-done.2.refs_5_), channel_id=1, source_target_pairs={{0,16},{1,17},{2,18},{3,19},{4,8},{5,9},{6,10},{7,11},{8,4},{9,5},... | collective-permute-start | bytes 688136 | tf_op jit(solution)/shard_map/ppermute | solution.py:324
  21.8 5.2 %collective-permute-start.11 = (bf16[64,256]{1,0:T(8,128)(2,1)S(1)}, bf16[64,256]{1,0:T(8,128)(2,1)S(1)}, u32[]{:S(2)}, u32[]{:S(2)}) collective-permute-start(bf16[64,256]{1,0:T(8,128)(2,1)S(1)} %pad_maximum_fusion.2.refs_0_), channel_id=1, source_target_pairs={{0,4},{4,0},{8,12},{12,8},{1,5},{5,1},{9,13},{13,9},{2,6},{6,2},{1... | collective-permute-start | bytes 98312 | tf_op jit(solution)/shard_map/ppermute | solution.py:46
  23.6 5.3 %collective-permute-start.12 = (bf16[64,256]{1,0:T(8,128)(2,1)S(1)}, bf16[64,256]{1,0:T(8,128)(2,1)S(1)}, u32[]{:S(2)}, u32[]{:S(2)}) collective-permute-start(bf16[64,256]{1,0:T(8,128)(2,1)S(1)} %pad_maximum_fusion.2.refs_0_), channel_id=1, source_target_pairs={{0,8},{4,12},{8,0},{12,4},{1,9},{5,13},{9,1},{13,5},{2,10},{6,14},... | collective-permute-start | bytes 98312 | tf_op jit(solution)/shard_map/ppermute | solution.py:46
  25.8 5.8 %collective-permute-start.13 = (bf16[64,256]{1,0:T(8,128)(2,1)S(1)}, bf16[64,256]{1,0:T(8,128)(2,1)S(1)}, u32[]{:S(2)}, u32[]{:S(2)}) collective-permute-start(bf16[64,256]{1,0:T(8,128)(2,1)S(1)} %pad_maximum_fusion.2.refs_0_), channel_id=1, source_target_pairs={{0,12},{4,8},{8,4},{12,0},{1,13},{5,9},{9,5},{13,1},{2,14},{6,10},... | collective-permute-start | bytes 98312 | tf_op jit(solution)/shard_map/ppermute | solution.py:46
  27.0 6.6 %collective-permute-start.5 = (f32[384,128]{1,0:T(8,128)S(1)}, f32[384,128]{1,0:T(8,128)S(1)}, u32[]{:S(2)}, u32[]{:S(2)}) collective-permute-start(f32[384,128]{1,0:T(8,128)S(1)} %slice.24), channel_id=1, source_target_pairs={{0,2},{2,0},{1,3},{3,1},{4,6},{6,4},{5,7},{7,5},{8,10},{10,8},{9,1... | collective-permute-start | bytes 589832 | tf_op jit(solution)/shard_map/ppermute | solution.py:345
  32.2 9.8 %collective-permute-start.16 = (bf16[64,3584]{1,0:T(8,128)(2,1)S(1)}, bf16[64,3584]{1,0:T(8,128)(2,1)S(1)}, u32[]{:S(2)}, u32[]{:S(2)}) collective-permute-start(bf16[64,3584]{1,0:T(8,128)(2,1)S(1)} %pad_maximum_fusion.mine_2_ref), channel_id=1, source_target_pairs={{0,4},{4,0},{8,12},{12,8},{1,5},{5,1},{9,13},{13,9},{2,6},{6,2},{1... | collective-permute-start | bytes 1376264 | tf_op jit(solution)/shard_map/ppermute | solution.py:318
  32.3 10.6 %collective-permute-start.14 = (bf16[64,3584]{1,0:T(8,128)(2,1)S(1)}, bf16[64,3584]{1,0:T(8,128)(2,1)S(1)}, u32[]{:S(2)}, u32[]{:S(2)}) collective-permute-start(bf16[64,3584]{1,0:T(8,128)(2,1)S(1)} %pad_maximum_fusion.mine_2_ref), channel_id=1, source_target_pairs={{0,16},{16,0},{1,17},{17,1},{2,18},{18,2},{3,19},{19,3},{4,20},{20... | collective-permute-start | bytes 1376264 | tf_op jit(solution)/shard_map/ppermute | solution.py:321
  33.6 11.4 %collective-permute-start.18 = (bf16[384,128]{1,0:T(8,128)(2,1)S(1)}, bf16[384,128]{1,0:T(8,128)(2,1)S(1)}, u32[]{:S(2)}, u32[]{:S(2)}) collective-permute-start(bf16[384,128]{1,0:T(8,128)(2,1)S(1)} %add_convert_fusion), channel_id=1, source_target_pairs={{0,1},{1,0},{2,3},{3,2},{4,5},{5,4},{6,7},{7,6},{8,9},{9,8},{10,11... | collective-permute-start | bytes 294920 | tf_op jit(solution)/shard_map/ppermute | solution.py:368
  42.1 8.1 %collective-permute-start.17 = (bf16[64,1792]{1,0:T(8,128)(2,1)S(1)}, bf16[64,1792]{1,0:T(8,128)(2,1)S(1)}, u32[]{:S(2)}, u32[]{:S(2)}) collective-permute-start(bf16[64,1792]{1,0:T(8,128)(2,1)S(1)} %slice.22), channel_id=1, source_target_pairs={{0,16},{16,0},{1,17},{17,1},{2,18},{18,2},{3,19},{19,3},{4,20},{20... | collective-permute-start | bytes 688136 | tf_op jit(solution)/shard_map/ppermute | solution.py:321
  43.0 8.0 %collective-permute-start.15 = (bf16[64,1792]{1,0:T(8,128)(2,1)S(1)}, bf16[64,1792]{1,0:T(8,128)(2,1)S(1)}, u32[]{:S(2)}, u32[]{:S(2)}) collective-permute-start(bf16[64,1792]{1,0:T(8,128)(2,1)S(1)} %slice.21), channel_id=1, source_target_pairs={{0,4},{4,0},{8,12},{12,8},{1,5},{5,1},{9,13},{13,9},{2,6},{6,2},{1... | collective-permute-start | bytes 688136 | tf_op jit(solution)/shard_map/ppermute | solution.py:318

commit v9 on v8

--- a/solution.py
+++ b/solution.py
@@ -91,26 +91,40 @@
     )(in_hbm(whole))
 
 
+def cut_copies(source, target, copied, parts):
+    size = source.shape[0] // parts
+    places = [pl.ds(part * size, size) for part in range(parts)]
+    return [
+        pltpu.make_async_copy(source.at[place], target.at[place], copied.at[part])
+        for part, place in enumerate(places)
+    ]
+
+
 def parts_kernel(*refs):
     sources, keep_ref, send_ref, copied = refs[:5], refs[5], refs[6], refs[-1]
     held_refs = out_ref, out_query_ref, in_ref, in_query_ref, grads_ref = refs[7:-2]
     sum_ref = refs[-2]
     copies = [
-        pltpu.make_async_copy(source, target, copied.at[place])
-        for place, (source, target) in enumerate(zip(sources, held_refs))
+        cut_copies(source, target, copied.at[place], parts)
+        for place, (source, target, parts) in enumerate(zip(sources, held_refs, (1, 1, 2, 4, 8)))
     ]
-    for copy in copies:
-        copy.start()
+    for group in copies:
+        for copy in group:
+            copy.start()
+
+    def wait(*places):
+        for place in places:
+            for copy in copies[place]:
+                copy.wait()
+
     rows, width = in_ref.shape[0], out_ref.shape[0]
-    copies[0].wait()
-    copies[1].wait()
+    wait(0, 1)
     sum_ref[rows : rows + width] = jnp.dot(
         out_ref[...], out_query_ref[...], preferred_element_type=jnp.float32
     )
-    copies[2].wait()
-    copies[3].wait()
+    wait(2, 3)
     sum_ref[:rows] = jnp.dot(in_ref[...], in_query_ref[...], preferred_element_type=jnp.float32)
-    copies[4].wait()
+    wait(4)
 
     @pl.loop(0, grads_ref.shape[0] // BLOCK)
     def _(step):
@@ -137,7 +151,7 @@
         in_specs=[pl.BlockSpec(memory_space=pl.ANY)] * len(sources),
         out_shape=[half, half],
         scratch_shapes=[pltpu.VMEM(source.shape, source.dtype) for source in sources]
-        + [pltpu.VMEM((high, pairs), jnp.float32), pltpu.SemaphoreType.DMA((len(sources),))],
+        + [pltpu.VMEM((high, pairs), jnp.float32), pltpu.SemaphoreType.DMA((len(sources), 8))],
         compiler_params=pltpu.CompilerParams(vmem_limit_bytes=VMEM_LIMIT),
     )(*[in_hbm(source) for source in sources])
 
@@ -195,7 +209,7 @@
     columns = slots[0].shape[1]
     group = lax.axis_index("groups")
     steps = acts_ref.shape[0] // BLOCK
-    parts = 2
+    parts = 8
 
     def copies(step):
         size = BLOCK // parts
@@ -340,9 +354,7 @@
     keep, send = small_parts(held(basis_in, *half), query_in, basis_out, query_out, out_grads)
     other = lax.ppermute(send, "rep", pair)
     keep = keep + held(other, *mine_1, *middle_3)
-    small, grad_half = keep[:split], keep[split:]
-    small_other = lax.ppermute(small, "eig", pair)
-    grad_other = lax.ppermute(grad_half, "eig", pair)
+    other = lax.ppermute(keep, "eig", pair)
 
     arrived = []
     for after, first, middle, rest in zip((half[0], keep), mine_1, middle_3, other_half):
@@ -350,11 +362,7 @@
         from_across = across(held(first, middle, after), over_y)
         arrived.append((from_pair, from_across))
 
-    small = (small + held(small_other, *arrived[0])).astype(jnp.bfloat16)
-    in_query, out_query = small[:rows], small[rows:]
-    packs = by_distance(jnp.concatenate([in_query, eigvals], axis=1))
-
-    ready = [chunk for both in arrived for chunk in both] + packs[1:]
+    ready = [chunk for both in arrived for chunk in both]
     mine_2 = jnp.concatenate(
         [jnp.where(inner, held(there, *ready), here) for here, there in arrived], axis=1
     )
@@ -364,7 +372,9 @@
     theirs_2 = swapped(mine_2)
     mine_3 = along(mine_2)
 
-    grad_half = (grad_half + held(grad_other, mine_2)).astype(jnp.bfloat16)
+    small = (keep + held(other, mine_2)).astype(jnp.bfloat16)
+    in_query, out_query, grad_half = small[:rows], small[rows:split], small[split:]
+    packs = by_distance(jnp.concatenate([in_query, eigvals], axis=1))
     grad_other = lax.ppermute(grad_half, "rep", pair)
     of_first = lax.axis_index("rep") == 0
     grad_proj = jnp.concatenate(
@@ -381,13 +391,13 @@
         in_hbm(held(acts, grad_half)), *half, *other_half, *mine_1, *theirs_1,
         in_specs=[pl.BlockSpec(memory_space=pl.ANY)]
         + [pl.BlockSpec(memory_space=pltpu.VMEM)] * 8,
-        scratch_shapes=[pltpu.SemaphoreType.DMA((tokens // BLOCK, 2))],
+        scratch_shapes=[pltpu.SemaphoreType.DMA((tokens // BLOCK, 8))],
     )
     acts = in_vmem(acts)
 
     cut = mine_3.shape[1] // 2
-    left_3 = along(held(theirs_2, first_total)[:, :cut])
-    right_3 = swapped(held(mine_3, first_total)[:, cut:])
+    left_3 = along(held(theirs_2, first_total, *packs[1:])[:, :cut])
+    right_3 = swapped(held(mine_3, first_total, *packs[1:])[:, cut:])
     mixed_width = 2 * query_count * rows
     weights = call(
         functools.partial(weight_kernel, query_count),

time: 65.3 us -> 65.8 us (level)
  waiting for transfers between devices: 6.72 us -> 9.98 us
  starting transfers between devices: 26.7 us -> 23.7 us
    ppermute x3, waiting for transfers between devices: 3.11 us -> 0.01 us  [by_distance(): lax.ppermute(value, axis, [(i, i ^ k) for i in range(size)])]
    ppermute x6, waiting for transfers between devices: 0.85 us -> 3.71 us  [along(): return lax.ppermute(value, 'blk', [(i, i ^ 1) for i in range(4)])]
    ppermute x2, waiting for transfers between devices: 2.74 us -> 4.46 us  [swapped(): return lax.ppermute(value, 'groups', pair)]
    ppermute x2 -> x1, starting transfers between devices: 3.11 us -> 1.56 us  [stepped_scores(): other = lax.ppermute(keep, 'eig', pair)]
    ppermute x2 -> x1, waiting for transfers between devices: 0.01 us -> 1.3 us  [stepped_scores(): other = lax.ppermute(keep, 'eig', pair)]
    ppermute x2, starting transfers between devices: 2.15 us -> 1.29 us  [swapped(): return lax.ppermute(value, 'groups', pair)]
    ppermute x6, starting transfers between devices: 12.6 us -> 11.8 us  [along(): return lax.ppermute(value, 'blk', [(i, i ^ 1) for i in range(4)])]
  transfers between devices with their start and end apart: 19 -> 18, of which waited for: 4 -> 6; matrix products, arithmetic and copies ran while one was open for 1% -> 1% of each run, Pallas kernels for 24% -> 24%
where the time goes in v9:
time: 65.8 us; the launch traced here: 65.6 us
  starting transfers between devices  23.7 us (36%)
  Pallas kernels  19.8 us (30%)
  blocking collectives  10.9 us (17%)
  waiting for transfers between devices  9.98 us (15%)
  other arithmetic  0.92 us (1%)
    pallas_call x4, Pallas kernels, call(): pl.pallas_call(kernel, out_shape=out_shape, compiler_params=pltpu.Compile...  13.7 us
    ppermute x6, starting transfers between devices, along(): return lax.ppermute(value, 'blk', [(i, i ^ 1) for i in range(4)])  11.8 us
    all_to_all x1, blocking collectives, on_device(): parts = lax.all_to_all(parts, ('blk', 'eig', 'rep'), 0, 0, tiled=True)  10.9 us
    ppermute x3, starting transfers between devices, by_distance(): lax.ppermute(value, axis, [(i, i ^ k) for i in range(size)])  5.46 us
    pallas_call x1, Pallas kernels, small_parts(): pl.pallas_call(parts_kernel, in_specs=[pl.BlockSpec(memory_space=pl.ANY)]...  4.79 us
    ppermute x2, waiting for transfers between devices, swapped(): return lax.ppermute(value, 'groups', pair)  4.46 us
    ppermute x6, waiting for transfers between devices, along(): return lax.ppermute(value, 'blk', [(i, i ^ 1) for i in range(4)])  3.71 us
    ppermute x4, starting transfers between devices, across(): lax.ppermute(value, AXES, pairing(lambda g, b, e, r: (g, 3 - b, e, r) if...  3.04 us
  transfers between devices with their start and end apart: 18, of which 6 were waited for; matrix products, arithmetic and copies ran while one was open for 1% of the time, Pallas kernels for 24%

profile of v9, /device:TPU:0, one launch (start us, length us, event | category | flops | bytes accessed | tf_op | source)
XLA Modules:
  0.0 65.6 jit_solution(17950251485015270903)
XLA Ops:
  0.0 1.3 %shard_map.91 = (bf16[64,1792]{1,0:T(8,128)(2,1)S(1)}, bf16[64,1792]{1,0:T(8,128)(2,1)S(1)}, bf16[64,1792]{1,0:T(8,128)(2,1)S(1)}, bf16[64,1792]{1,0:T(8,128)(2,1)S(1)}) custom-call(bf16[64,7168]{1,0:T(8,128)(2,1)} %refs_2_), custom_call_target="tpu_custom_call" | custom-call | tf_op jit(solution)/shard_map/pallas_call | solution.py:86
  1.3 3.1 %collective-permute-start.1 = (bf16[64,1792]{1,0:T(8,128)(2,1)S(1)}, bf16[64,1792]{1,0:T(8,128)(2,1)S(1)}, u32[]{:S(2)}, u32[]{:S(2)}) collective-permute-start(bf16[64,1792]{1,0:T(8,128)(2,1)S(1)} %get-tuple-element.32.refs_0_), channel_id=1, source_target_pairs={{0,4},{4,0},{8,12},{12,8},{1,5},{5,1},{9,13},{13,9},{2,6},{6,2},{1... | collective-permute-start | bytes 688136 | tf_op jit(solution)/shard_map/ppermute | solution.py:332
  4.4 3.1 %collective-permute-start.2 = (bf16[64,1792]{1,0:T(8,128)(2,1)S(1)}, bf16[64,1792]{1,0:T(8,128)(2,1)S(1)}, u32[]{:S(2)}, u32[]{:S(2)}) collective-permute-start(bf16[64,1792]{1,0:T(8,128)(2,1)S(1)} %get-tuple-element.33.refs_1_), channel_id=1, source_target_pairs={{0,4},{4,0},{8,12},{12,8},{1,5},{5,1},{9,13},{13,9},{2,6},{6,2},{1... | collective-permute-start | bytes 688136 | tf_op jit(solution)/shard_map/ppermute | solution.py:332
  7.6 4.8 %shard_map.92 = (f32[576,128]{1,0:T(8,128)S(1)}, f32[576,128]{1,0:T(8,128)S(1)}) custom-call(bf16[128,2048]{1,0:T(8,128)(2,1)} %refs_0_.1, bf16[2048,128]{1,0:T(8,128)(2,1)} %refs_1_.1, bf16[64,7168]{1,0:T(8,128)(2,1)} %refs_2_, bf16[7168,128]{1,0:T(8,128)(2,1)} %refs_3_.1, bf16[768,2048]{1,0:T(8,128)(2,1)} %refs_4_.1), custom_call_target="tpu_custom_call" | custom-call | tf_op jit(solution)/shard_map/pallas_call | solution.py:149
  12.4 0.0 copy-start
  12.4 0.6 collective-permute-start
  13.0 1.1 %collective-permute-start.7 = (bf16[64,1792]{1,0:T(8,128)(2,1)S(1)}, bf16[64,1792]{1,0:T(8,128)(2,1)S(1)}, u32[]{:S(2)}, u32[]{:S(2)}) collective-permute-start(bf16[64,1792]{1,0:T(8,128)(2,1)S(1)} %broadcast_select_fusion.5), channel_id=1, source_target_pairs={{0,4},{4,0},{8,12},{12,8},{1,5},{5,1},{9,13},{13,9},{2,6},{6,2},{1... | collective-permute-start | bytes 688136 | tf_op jit(solution)/shard_map/ppermute | solution.py:332
  14.1 1.5 %collective-permute-start.6 = (bf16[64,1792]{1,0:T(8,128)(2,1)S(1)}, bf16[64,1792]{1,0:T(8,128)(2,1)S(1)}, u32[]{:S(2)}, u32[]{:S(2)}) collective-permute-start(bf16[64,1792]{1,0:T(8,128)(2,1)S(1)} %collective-permute-done.1.refs_4_), channel_id=1, source_target_pairs={{0,16},{1,17},{2,18},{3,19},{4,8},{5,9},{6,10},{7,11},{8,4},{9,5},... | collective-permute-start | bytes 688136 | tf_op jit(solution)/shard_map/ppermute | solution.py:338
  15.7 2.9 %collective-permute-start.8 = (bf16[64,1792]{1,0:T(8,128)(2,1)S(1)}, bf16[64,1792]{1,0:T(8,128)(2,1)S(1)}, u32[]{:S(2)}, u32[]{:S(2)}) collective-permute-start(bf16[64,1792]{1,0:T(8,128)(2,1)S(1)} %broadcast_select_fusion.4), channel_id=1, source_target_pairs={{0,4},{4,0},{8,12},{12,8},{1,5},{5,1},{9,13},{13,9},{2,6},{6,2},{1... | collective-permute-start | bytes 688136 | tf_op jit(solution)/shard_map/ppermute | solution.py:332
  18.7 1.5 %collective-permute-start.9 = (bf16[64,1792]{1,0:T(8,128)(2,1)S(1)}, bf16[64,1792]{1,0:T(8,128)(2,1)S(1)}, u32[]{:S(2)}, u32[]{:S(2)}) collective-permute-start(bf16[64,1792]{1,0:T(8,128)(2,1)S(1)} %collective-permute-done.2.refs_5_), channel_id=1, source_target_pairs={{0,16},{1,17},{2,18},{3,19},{4,8},{5,9},{6,10},{7,11},{8,4},{9,5},... | collective-permute-start | bytes 688136 | tf_op jit(solution)/shard_map/ppermute | solution.py:338
  20.2 0.1 select_reduce_fusion
  20.3 1.6 %collective-permute-start.5 = (f32[576,128]{1,0:T(8,128)S(1)}, f32[576,128]{1,0:T(8,128)S(1)}, u32[]{:S(2)}, u32[]{:S(2)}) collective-permute-start(f32[576,128]{1,0:T(8,128)S(1)} %add.6), channel_id=1, source_target_pairs={{0,2},{2,0},{1,3},{3,1},{4,6},{6,4},{5,7},{7,5},{8,10},{10,8},{9,1... | collective-permute-start | bytes 884744 | tf_op jit(solution)/shard_map/ppermute | solution.py:357
  21.8 0.4 collective-permute-done.6
  22.2 3.3 %collective-permute-done.8 = bf16[64,1792]{1,0:T(8,128)(2,1)S(1)} collective-permute-done((bf16[64,1792]{1,0:T(8,128)(2,1)S(1)}, bf16[64,1792]{1,0:T(8,128)(2,1)S(1)}, u32[]{:S(2)}, u32[]{:S(2)}) %collective-permute-start.8) | collective-permute-done | bytes 229408 | tf_op jit(solution)/shard_map/ppermute | solution.py:332
  25.5 0.1 collective-permute-done.9
  25.8 1.3 %collective-permute-done.5 = f32[576,128]{1,0:T(8,128)S(1)} collective-permute-done((f32[576,128]{1,0:T(8,128)S(1)}, f32[576,128]{1,0:T(8,128)S(1)}, u32[]{:S(2)}, u32[]{:S(2)}) %collective-permute-start.5) | collective-permute-done | bytes 294944 | tf_op jit(solution)/shard_map/ppermute | solution.py:357
  27.1 1.1 %collective-permute-start.11 = (bf16[64,256]{1,0:T(8,128)(2,1)S(1)}, bf16[64,256]{1,0:T(8,128)(2,1)S(1)}, u32[]{:S(2)}, u32[]{:S(2)}) collective-permute-start(bf16[64,256]{1,0:T(8,128)(2,1)S(1)} %pad_maximum_fusion.2.refs_0_), channel_id=1, source_target_pairs={{0,4},{4,0},{8,12},{12,8},{1,5},{5,1},{9,13},{13,9},{2,6},{6,2},{1... | collective-permute-start | bytes 98312 | tf_op jit(solution)/shard_map/ppermute | solution.py:46
  28.2 1.0 %collective-permute-start.15 = (bf16[64,3584]{1,0:T(8,128)(2,1)S(1)}, bf16[64,3584]{1,0:T(8,128)(2,1)S(1)}, u32[]{:S(2)}, u32[]{:S(2)}) collective-permute-start(bf16[64,3584]{1,0:T(8,128)(2,1)S(1)} %pad_maximum_fusion.mine_2_ref), channel_id=1, source_target_pairs={{0,4},{4,0},{8,12},{12,8},{1,5},{5,1},{9,13},{13,9},{2,6},{6,2},{1... | collective-permute-start | bytes 1376264 | tf_op jit(solution)/shard_map/ppermute | solution.py:332
  29.2 0.6 collective-permute-start.10
  29.9 2.8 %collective-permute-start.12 = (bf16[64,256]{1,0:T(8,128)(2,1)S(1)}, bf16[64,256]{1,0:T(8,128)(2,1)S(1)}, u32[]{:S(2)}, u32[]{:S(2)}) collective-permute-start(bf16[64,256]{1,0:T(8,128)(2,1)S(1)} %pad_maximum_fusion.2.refs_0_), channel_id=1, source_target_pairs={{0,8},{4,12},{8,0},{12,4},{1,9},{5,13},{9,1},{13,5},{2,10},{6,14},... | collective-permute-start | bytes 98312 | tf_op jit(solution)/shard_map/ppermute | solution.py:46
  32.7 1.5 %collective-permute-start.13 = (bf16[64,256]{1,0:T(8,128)(2,1)S(1)}, bf16[64,256]{1,0:T(8,128)(2,1)S(1)}, u32[]{:S(2)}, u32[]{:S(2)}) collective-permute-start(bf16[64,256]{1,0:T(8,128)(2,1)S(1)} %pad_maximum_fusion.2.refs_0_), channel_id=1, source_target_pairs={{0,12},{4,8},{8,4},{12,0},{1,13},{5,9},{9,5},{13,1},{2,14},{6,10},... | collective-permute-start | bytes 98312 | tf_op jit(solution)/shard_map/ppermute | solution.py:46
  34.3 8.3 %shard_map.93 = (f32[768,128]{1,0:T(8,128)S(1)}, bf16[768,7168]{1,0:T(8,128)(2,1)S(1)}) custom-call(bf16[768,7168]{1,0:T(8,128)(2,1)} %source_ref, bf16[64,1792]{1,0:T(8,128)(2,1)S(1)} %get-tuple-element.32.refs_0_, bf16[64,1792]{1,0:T(8,128)(2,1)S(1)} %get-tuple-element.33.refs_1_, bf16[64,1792]{1,0:T(8,128)(2,1)S(1)} %get-tuple-element.40.refs_2_, ...), custom_call_target="tpu_custom_call" | custom-call | flops 1 | bytes 1 | tf_op jit(solution)/shard_map/pallas_call | solution.py:286
  42.6 0.5 shard_map.94.weights_ref
  43.1 0.0 collective-permute-done.15.mine_3_ref
  43.1 0.7 %collective-permute-start.16 = (bf16[64,1792]{1,0:T(8,128)(2,1)S(1)}, bf16[64,1792]{1,0:T(8,128)(2,1)S(1)}, u32[]{:S(2)}, u32[]{:S(2)}) collective-permute-start(bf16[64,1792]{1,0:T(8,128)(2,1)S(1)} %slice.18), channel_id=1, source_target_pairs={{0,16},{16,0},{1,17},{17,1},{2,18},{18,2},{3,19},{19,3},{4,20},{20... | collective-permute-start | bytes 688136 | tf_op jit(solution)/shard_map/ppermute | solution.py:335
  43.8 0.5 collective-permute-start.14
  44.4 2.4 %shard_map.95 = (f32[768,128]{1,0:T(8,128)S(1)}, f32[768,512]{1,0:T(8,128)S(1)}, f32[8,512]{1,0:T(8,128)S(1)}) custom-call(bf16[768,7168]{1,0:T(8,128)(2,1)S(1)} %get-tuple-element.52.acts_ref, bf16[64,3584]{1,0:T(8,128)(2,1)S(1)} %pad_maximum_fusion.mine_2_ref, bf16[64,3584]{1,0:T(8,128)(2,1)S(1)} %collective-permute-done.15.mine_3_ref, ...), custom_call_target="tpu_custom_call" | custom-call | flops 1 | bytes 1 | tf_op jit(solution)/shard_map/pallas_call | solution.py:286
  46.7 4.5 %collective-permute-done.16.right_ref = bf16[64,1792]{1,0:T(8,128)(2,1)S(1)} collective-permute-done((bf16[64,1792]{1,0:T(8,128)(2,1)S(1)}, bf16[64,1792]{1,0:T(8,128)(2,1)S(1)}, u32[]{:S(2)}, u32[]{:S(2)}) %collective-permute-start.16) | collective-permute-done | bytes 229408 | tf_op jit(solution)/shard_map/ppermute | solution.py:335
  51.2 0.4 collective-permute-done.14.left_ref
  51.5 2.6 %shard_map.96 = f32[16,2]{1,0:T(8,128)S(1)} custom-call(bf16[768,7168]{1,0:T(8,128)(2,1)S(1)} %get-tuple-element.52.acts_ref, bf16[64,3584]{1,0:T(8,128)(2,1)S(1)} %collective-permute-done.10.theirs_2_ref, bf16[64,1792]{1,0:T(8,128)(2,1)S(1)} %collective-permute-done.14.left_ref, bf16[64,1792]{1,0:T(8,128)(2,1)S(1)} %collective-permute-done.16.right_ref, ...), custom_call_target="tpu_custom_call" | custom-call | flops 1 | bytes 1 | tf_op jit(solution)/shard_map/pallas_call | solution.py:286
  54.1 10.9 %all_to_all.9 = f32[16,1,2]{2,1,0:T(1,128)S(1)} all-to-all(f32[16,1,2]{2,1,0:T(1,128)S(1)} %bitcast.4), channel_id=1, replica_groups=mesh['groups'=2,'blk'=4,'eig'=2,'rep'=2] {'blk','eig','rep'}, dimensions={0} | all-to-all | bytes 256 | tf_op jit(solution)/shard_map/all_to_all | solution.py:458
  65.0 0.5 reduce_sum.21
  (36 shorter events, 0.4 us)
Async XLA Ops:
  1.3 11.6 %collective-permute-start.1 = (bf16[64,1792]{1,0:T(8,128)(2,1)S(1)}, bf16[64,1792]{1,0:T(8,128)(2,1)S(1)}, u32[]{:S(2)}, u32[]{:S(2)}) collective-permute-start(bf16[64,1792]{1,0:T(8,128)(2,1)S(1)} %get-tuple-element.32.refs_0_), channel_id=1, source_target_pairs={{0,4},{4,0},{8,12},{12,8},{1,5},{5,1},{9,13},{13,9},{2,6},{6,2},{1... | collective-permute-start | bytes 688136 | tf_op jit(solution)/shard_map/ppermute | solution.py:332
  4.4 8.5 %collective-permute-start.3 = (bf16[64,1792]{1,0:T(8,128)(2,1)S(1)}, bf16[64,1792]{1,0:T(8,128)(2,1)S(1)}, u32[]{:S(2)}, u32[]{:S(2)}) collective-permute-start(bf16[64,1792]{1,0:T(8,128)(2,1)S(1)} %get-tuple-element.32.refs_0_), channel_id=1, source_target_pairs={{0,1},{1,0},{2,3},{3,2},{4,8},{5,9},{6,10},{7,11},{8,4},{9,5},{10,... | collective-permute-start | bytes 688136 | tf_op jit(solution)/shard_map/ppermute | solution.py:338
  4.4 15.8 %copy-start.1 = (s32[768]{0:T(1024)S(1)}, s32[768]{0:T(1024)}, u32[]{:S(2)}) copy-start(s32[768]{0:T(1024)} %param.16) | copy-start | bytes 9220
  4.4 15.8 %copy-start.2 = (s32[8]{0:T(128)S(1)}, s32[8]{0:T(128)}, u32[]{:S(2)}) copy-start(s32[8]{0:T(128)} %param.17) | copy-start | bytes 100
  4.4 11.2 %collective-permute-start.2 = (bf16[64,1792]{1,0:T(8,128)(2,1)S(1)}, bf16[64,1792]{1,0:T(8,128)(2,1)S(1)}, u32[]{:S(2)}, u32[]{:S(2)}) collective-permute-start(bf16[64,1792]{1,0:T(8,128)(2,1)S(1)} %get-tuple-element.33.refs_1_), channel_id=1, source_target_pairs={{0,4},{4,0},{8,12},{12,8},{1,5},{5,1},{9,13},{13,9},{2,6},{6,2},{1... | collective-permute-start | bytes 688136 | tf_op jit(solution)/shard_map/ppermute | solution.py:332
  7.6 8.1 %collective-permute-start.4 = (bf16[64,1792]{1,0:T(8,128)(2,1)S(1)}, bf16[64,1792]{1,0:T(8,128)(2,1)S(1)}, u32[]{:S(2)}, u32[]{:S(2)}) collective-permute-start(bf16[64,1792]{1,0:T(8,128)(2,1)S(1)} %get-tuple-element.33.refs_1_), channel_id=1, source_target_pairs={{0,1},{1,0},{2,3},{3,2},{4,8},{5,9},{6,10},{7,11},{8,4},{9,5},{10,... | collective-permute-start | bytes 688136 | tf_op jit(solution)/shard_map/ppermute | solution.py:338
  12.4 14.7 %copy-start = (bf16[64,128]{1,0:T(8,128)(2,1)S(1)}, bf16[64,128]{1,0:T(8,128)(2,1)}, u32[]{:S(2)}) copy-start(bf16[64,128]{1,0:T(8,128)(2,1)} %param.13) | copy-start | bytes 49156
  12.4 3.3 %collective-permute-start = (f32[576,128]{1,0:T(8,128)S(1)}, f32[576,128]{1,0:T(8,128)S(1)}, u32[]{:S(2)}, u32[]{:S(2)}) collective-permute-start(f32[576,128]{1,0:T(8,128)S(1)} %get-tuple-element.36), channel_id=1, source_target_pairs={{0,1},{1,0},{2,3},{3,2},{4,5},{5,4},{6,7},{7,6},{8,9},{9,8},{10,11... | collective-permute-start | bytes 884744 | tf_op jit(solution)/shard_map/ppermute | solution.py:355
  13.0 8.8 %collective-permute-start.7 = (bf16[64,1792]{1,0:T(8,128)(2,1)S(1)}, bf16[64,1792]{1,0:T(8,128)(2,1)S(1)}, u32[]{:S(2)}, u32[]{:S(2)}) collective-permute-start(bf16[64,1792]{1,0:T(8,128)(2,1)S(1)} %broadcast_select_fusion.5), channel_id=1, source_target_pairs={{0,4},{4,0},{8,12},{12,8},{1,5},{5,1},{9,13},{13,9},{2,6},{6,2},{1... | collective-permute-start | bytes 688136 | tf_op jit(solution)/shard_map/ppermute | solution.py:332
  14.1 8.1 %collective-permute-start.6 = (bf16[64,1792]{1,0:T(8,128)(2,1)S(1)}, bf16[64,1792]{1,0:T(8,128)(2,1)S(1)}, u32[]{:S(2)}, u32[]{:S(2)}) collective-permute-start(bf16[64,1792]{1,0:T(8,128)(2,1)S(1)} %collective-permute-done.1.refs_4_), channel_id=1, source_target_pairs={{0,16},{1,17},{2,18},{3,19},{4,8},{5,9},{6,10},{7,11},{8,4},{9,5},... | collective-permute-start | bytes 688136 | tf_op jit(solution)/shard_map/ppermute | solution.py:338
  15.7 9.8 %collective-permute-start.8 = (bf16[64,1792]{1,0:T(8,128)(2,1)S(1)}, bf16[64,1792]{1,0:T(8,128)(2,1)S(1)}, u32[]{:S(2)}, u32[]{:S(2)}) collective-permute-start(bf16[64,1792]{1,0:T(8,128)(2,1)S(1)} %broadcast_select_fusion.4), channel_id=1, source_target_pairs={{0,4},{4,0},{8,12},{12,8},{1,5},{5,1},{9,13},{13,9},{2,6},{6,2},{1... | collective-permute-start | bytes 688136 | tf_op jit(solution)/shard_map/ppermute | solution.py:332
  18.7 7.0 %collective-permute-start.9 = (bf16[64,1792]{1,0:T(8,128)(2,1)S(1)}, bf16[64,1792]{1,0:T(8,128)(2,1)S(1)}, u32[]{:S(2)}, u32[]{:S(2)}) collective-permute-start(bf16[64,1792]{1,0:T(8,128)(2,1)S(1)} %collective-permute-done.2.refs_5_), channel_id=1, source_target_pairs={{0,16},{1,17},{2,18},{3,19},{4,8},{5,9},{6,10},{7,11},{8,4},{9,5},... | collective-permute-start | bytes 688136 | tf_op jit(solution)/shard_map/ppermute | solution.py:338
  20.3 6.8 %collective-permute-start.5 = (f32[576,128]{1,0:T(8,128)S(1)}, f32[576,128]{1,0:T(8,128)S(1)}, u32[]{:S(2)}, u32[]{:S(2)}) collective-permute-start(f32[576,128]{1,0:T(8,128)S(1)} %add.6), channel_id=1, source_target_pairs={{0,2},{2,0},{1,3},{3,1},{4,6},{6,4},{5,7},{7,5},{8,10},{10,8},{9,1... | collective-permute-start | bytes 884744 | tf_op jit(solution)/shard_map/ppermute | solution.py:357
  27.1 7.1 %collective-permute-start.11 = (bf16[64,256]{1,0:T(8,128)(2,1)S(1)}, bf16[64,256]{1,0:T(8,128)(2,1)S(1)}, u32[]{:S(2)}, u32[]{:S(2)}) collective-permute-start(bf16[64,256]{1,0:T(8,128)(2,1)S(1)} %pad_maximum_fusion.2.refs_0_), channel_id=1, source_target_pairs={{0,4},{4,0},{8,12},{12,8},{1,5},{5,1},{9,13},{13,9},{2,6},{6,2},{1... | collective-permute-start | bytes 98312 | tf_op jit(solution)/shard_map/ppermute | solution.py:46
  28.2 14.8 %collective-permute-start.15 = (bf16[64,3584]{1,0:T(8,128)(2,1)S(1)}, bf16[64,3584]{1,0:T(8,128)(2,1)S(1)}, u32[]{:S(2)}, u32[]{:S(2)}) collective-permute-start(bf16[64,3584]{1,0:T(8,128)(2,1)S(1)} %pad_maximum_fusion.mine_2_ref), channel_id=1, source_target_pairs={{0,4},{4,0},{8,12},{12,8},{1,5},{5,1},{9,13},{13,9},{2,6},{6,2},{1... | collective-permute-start | bytes 1376264 | tf_op jit(solution)/shard_map/ppermute | solution.py:332
  29.2 14.5 %collective-permute-start.10 = (bf16[64,3584]{1,0:T(8,128)(2,1)S(1)}, bf16[64,3584]{1,0:T(8,128)(2,1)S(1)}, u32[]{:S(2)}, u32[]{:S(2)}) collective-permute-start(bf16[64,3584]{1,0:T(8,128)(2,1)S(1)} %pad_maximum_fusion.mine_2_ref), channel_id=1, source_target_pairs={{0,16},{16,0},{1,17},{17,1},{2,18},{18,2},{3,19},{19,3},{4,20},{20... | collective-permute-start | bytes 1376264 | tf_op jit(solution)/shard_map/ppermute | solution.py:335
  29.9 12.7 %collective-permute-start.12 = (bf16[64,256]{1,0:T(8,128)(2,1)S(1)}, bf16[64,256]{1,0:T(8,128)(2,1)S(1)}, u32[]{:S(2)}, u32[]{:S(2)}) collective-permute-start(bf16[64,256]{1,0:T(8,128)(2,1)S(1)} %pad_maximum_fusion.2.refs_0_), channel_id=1, source_target_pairs={{0,8},{4,12},{8,0},{12,4},{1,9},{5,13},{9,1},{13,5},{2,10},{6,14},... | collective-permute-start | bytes 98312 | tf_op jit(solution)/shard_map/ppermute | solution.py:46
  32.7 9.9 %collective-permute-start.13 = (bf16[64,256]{1,0:T(8,128)(2,1)S(1)}, bf16[64,256]{1,0:T(8,128)(2,1)S(1)}, u32[]{:S(2)}, u32[]{:S(2)}) collective-permute-start(bf16[64,256]{1,0:T(8,128)(2,1)S(1)} %pad_maximum_fusion.2.refs_0_), channel_id=1, source_target_pairs={{0,12},{4,8},{8,4},{12,0},{1,13},{5,9},{9,5},{13,1},{2,14},{6,10},... | collective-permute-start | bytes 98312 | tf_op jit(solution)/shard_map/ppermute | solution.py:46
  34.2 10.1 %collective-permute-start.17 = (bf16[384,128]{1,0:T(8,128)(2,1)S(1)}, bf16[384,128]{1,0:T(8,128)(2,1)S(1)}, u32[]{:S(2)}, u32[]{:S(2)}) collective-permute-start(bf16[384,128]{1,0:T(8,128)(2,1)S(1)} %slice.20), channel_id=1, source_target_pairs={{0,1},{1,0},{2,3},{3,2},{4,5},{5,4},{6,7},{7,6},{8,9},{9,8},{10,11... | collective-permute-start | bytes 294920 | tf_op jit(solution)/shard_map/ppermute | solution.py:378
  43.1 8.1 %collective-permute-start.16 = (bf16[64,1792]{1,0:T(8,128)(2,1)S(1)}, bf16[64,1792]{1,0:T(8,128)(2,1)S(1)}, u32[]{:S(2)}, u32[]{:S(2)}) collective-permute-start(bf16[64,1792]{1,0:T(8,128)(2,1)S(1)} %slice.18), channel_id=1, source_target_pairs={{0,16},{16,0},{1,17},{17,1},{2,18},{18,2},{3,19},{19,3},{4,20},{20... | collective-permute-start | bytes 688136 | tf_op jit(solution)/shard_map/ppermute | solution.py:335
  43.8 7.8 %collective-permute-start.14 = (bf16[64,1792]{1,0:T(8,128)(2,1)S(1)}, bf16[64,1792]{1,0:T(8,128)(2,1)S(1)}, u32[]{:S(2)}, u32[]{:S(2)}) collective-permute-start(bf16[64,1792]{1,0:T(8,128)(2,1)S(1)} %slice.17), channel_id=1, source_target_pairs={{0,4},{4,0},{8,12},{12,8},{1,5},{5,1},{9,13},{13,9},{2,6},{6,2},{1... | collective-permute-start | bytes 688136 | tf_op jit(solution)/shard_map/ppermute | solution.py:332

commit v10 on v9

--- a/solution.py
+++ b/solution.py
@@ -106,7 +106,7 @@
     sum_ref = refs[-2]
     copies = [
         cut_copies(source, target, copied.at[place], parts)
-        for place, (source, target, parts) in enumerate(zip(sources, held_refs, (1, 1, 2, 4, 8)))
+        for place, (source, target, parts) in enumerate(zip(sources, held_refs, (1, 1, 2, 4, 4)))
     ]
     for group in copies:
         for copy in group:
@@ -124,13 +124,18 @@
     )
     wait(2, 3)
     sum_ref[:rows] = jnp.dot(in_ref[...], in_query_ref[...], preferred_element_type=jnp.float32)
-    wait(4)
-
-    @pl.loop(0, grads_ref.shape[0] // BLOCK)
+    blocks_copied = copies[4]
+    size = grads_ref.shape[0] // len(blocks_copied)
+
+    @pl.loop(0, len(blocks_copied))
     def _(step):
-        start = pl.multiple_of(step * BLOCK, LANES)
-        sum_ref[pl.ds(rows + width + start, BLOCK), :] = contract_last(
-            grads_ref[pl.ds(start, BLOCK), :], out_ref[...]
+        start = pl.multiple_of(step * size, 16)
+        place = pl.ds(start, size)
+        pltpu.make_async_copy(
+            sources[4].at[place], grads_ref.at[place], copied.at[4, step]
+        ).wait()
+        sum_ref[pl.ds(rows + width + start, size), :] = contract_last(
+            grads_ref[place, :], out_ref[...]
         )
 
     core, split = lax.axis_index("rep"), rows + width
@@ -213,7 +218,8 @@
 
     def copies(step):
         size = BLOCK // parts
-        places = [pl.ds(step * BLOCK + part * size, size) for part in range(parts)]
+        begin = pl.multiple_of(step * BLOCK, BLOCK)
+        places = [pl.ds(begin + part * size, size) for part in range(parts)]
         return [
             pltpu.make_async_copy(source_ref.at[place], acts_ref.at[place], copied.at[step, part])
             for part, place in enumerate(places)
@@ -221,13 +227,18 @@
 
     for copy in copies(0):
         copy.start()
-    for step in range(steps):
+
+    @pl.loop(0, steps)
+    def _(step):
         for copy in copies(step):
             copy.wait()
-        if step + 1 < steps:
+
+        @pl.when(step + 1 < steps)
+        def _():
             for copy in copies(step + 1):
                 copy.start()
-        start = step * BLOCK
+
+        start = pl.multiple_of(step * BLOCK, LANES)
         total = 0.0
         for place in range(4):
             half = group if place < 2 else 1 - group
@@ -353,16 +364,17 @@
     split = rows + width
     keep, send = small_parts(held(basis_in, *half), query_in, basis_out, query_out, out_grads)
     other = lax.ppermute(send, "rep", pair)
-    keep = keep + held(other, *mine_1, *middle_3)
+    keep = keep + held(other, mine_1[0], middle_3[0])
     other = lax.ppermute(keep, "eig", pair)
 
     arrived = []
-    for after, first, middle, rest in zip((half[0], keep), mine_1, middle_3, other_half):
-        from_pair = along(jnp.where(inner, middle, held(rest, first, after)))
-        from_across = across(held(first, middle, after), over_y)
+    for first, middle, rest in zip(mine_1, middle_3, other_half):
+        from_pair = along(jnp.where(inner, middle, held(rest, first, keep)))
+        from_across = across(held(first, middle, keep), over_y)
         arrived.append((from_pair, from_across))
 
-    ready = [chunk for both in arrived for chunk in both]
+    small = (keep + held(other, *arrived[0])).astype(jnp.bfloat16)
+    ready = [chunk for both in arrived for chunk in both] + [small]
     mine_2 = jnp.concatenate(
         [jnp.where(inner, held(there, *ready), here) for here, there in arrived], axis=1
     )
@@ -372,7 +384,6 @@
     theirs_2 = swapped(mine_2)
     mine_3 = along(mine_2)
 
-    small = (keep + held(other, mine_2)).astype(jnp.bfloat16)
     in_query, out_query, grad_half = small[:rows], small[rows:split], small[split:]
     packs = by_distance(jnp.concatenate([in_query, eigvals], axis=1))
     grad_other = lax.ppermute(grad_half, "rep", pair)

time: 65.8 us -> 61.5 us (0.935)
  blocking collectives: 10.9 us -> 8.98 us
  Pallas kernels: 19.8 us -> 18.4 us
  waiting for transfers between devices: 9.98 us -> 8.93 us
    all_to_all x1, blocking collectives: 10.9 us -> 8.98 us  [on_device(): parts = lax.all_to_all(parts, ('blk', 'eig', 'rep'), 0, 0, tiled=True)]
    ppermute x2, waiting for transfers between devices: 4.46 us -> 2.75 us  [swapped(): return lax.ppermute(value, 'groups', pair)]
    ppermute x2, starting transfers between devices: 1.29 us -> 2.74 us  [swapped(): return lax.ppermute(value, 'groups', pair)]
    ppermute x1, waiting for transfers between devices: 1.3 us -> 0.01 us  [stepped_scores(): other = lax.ppermute(keep, 'eig', pair)]
    ppermute x1, waiting for transfers between devices: 0.01 us -> 1.07 us  [stepped_scores(): other = lax.ppermute(send, 'rep', pair)]
    ppermute x3, starting transfers between devices: 5.46 us -> 4.45 us  [by_distance(): lax.ppermute(value, axis, [(i, i ^ k) for i in range(size)])]
    ppermute x6, waiting for transfers between devices: 3.71 us -> 4.68 us  [along(): return lax.ppermute(value, 'blk', [(i, i ^ 1) for i in range(4)])]
    pallas_call x4, Pallas kernels: 13.7 us -> 12.8 us  [call(): pl.pallas_call(kernel, out_shape=out_shape, compiler_params=pltpu.Compile...]
  transfers between devices with their start and end apart: 18 -> 18, of which waited for: 6 -> 5; matrix products, arithmetic and copies ran while one was open for 1% -> 1% of each run, Pallas kernels for 24% -> 24%
where the time goes in v10:
time: 61.5 us; the launch traced here: 61.3 us
  starting transfers between devices  23.8 us (39%)
  Pallas kernels  18.4 us (30%)
  blocking collectives  8.98 us (15%)
  waiting for transfers between devices  8.93 us (15%)
  other arithmetic  0.95 us (2%)
    pallas_call x4, Pallas kernels, call(): pl.pallas_call(kernel, out_shape=out_shape, compiler_params=pltpu.Compile...  12.8 us
    ppermute x6, starting transfers between devices, along(): return lax.ppermute(value, 'blk', [(i, i ^ 1) for i in range(4)])  11.4 us
    all_to_all x1, blocking collectives, on_device(): parts = lax.all_to_all(parts, ('blk', 'eig', 'rep'), 0, 0, tiled=True)  8.98 us
    ppermute x6, waiting for transfers between devices, along(): return lax.ppermute(value, 'blk', [(i, i ^ 1) for i in range(4)])  4.68 us
    ppermute x3, starting transfers between devices, by_distance(): lax.ppermute(value, axis, [(i, i ^ k) for i in range(size)])  4.45 us
    pallas_call x1, Pallas kernels, small_parts(): pl.pallas_call(parts_kernel, in_specs=[pl.BlockSpec(memory_space=pl.ANY)]...  4.31 us
    ppermute x4, starting transfers between devices, across(): lax.ppermute(value, AXES, pairing(lambda g, b, e, r: (g, 3 - b, e, r) if...  3.05 us
    ppermute x2, waiting for transfers between devices, swapped(): return lax.ppermute(value, 'groups', pair)  2.75 us
  transfers between devices with their start and end apart: 18, of which 5 were waited for; matrix products, arithmetic and copies ran while one was open for 1% of the time, Pallas kernels for 24%

profile of v10, /device:TPU:0, one launch (start us, length us, event | category | flops | bytes accessed | tf_op | source)
XLA Modules:
  0.0 61.3 jit_solution(14969254425265754409)
XLA Ops:
  0.0 1.3 %shard_map.91 = (bf16[64,1792]{1,0:T(8,128)(2,1)S(1)}, bf16[64,1792]{1,0:T(8,128)(2,1)S(1)}, bf16[64,1792]{1,0:T(8,128)(2,1)S(1)}, bf16[64,1792]{1,0:T(8,128)(2,1)S(1)}) custom-call(bf16[64,7168]{1,0:T(8,128)(2,1)} %refs_2_), custom_call_target="tpu_custom_call" | custom-call | tf_op jit(solution)/shard_map/pallas_call | solution.py:86
  1.3 3.1 %collective-permute-start.1 = (bf16[64,1792]{1,0:T(8,128)(2,1)S(1)}, bf16[64,1792]{1,0:T(8,128)(2,1)S(1)}, u32[]{:S(2)}, u32[]{:S(2)}) collective-permute-start(bf16[64,1792]{1,0:T(8,128)(2,1)S(1)} %get-tuple-element.32.refs_0_), channel_id=1, source_target_pairs={{0,4},{4,0},{8,12},{12,8},{1,5},{5,1},{9,13},{13,9},{2,6},{6,2},{1... | collective-permute-start | bytes 688136 | tf_op jit(solution)/shard_map/ppermute | solution.py:343
  4.4 3.1 %collective-permute-start.6 = (bf16[64,1792]{1,0:T(8,128)(2,1)S(1)}, bf16[64,1792]{1,0:T(8,128)(2,1)S(1)}, u32[]{:S(2)}, u32[]{:S(2)}) collective-permute-start(bf16[64,1792]{1,0:T(8,128)(2,1)S(1)} %get-tuple-element.33.refs_1_), channel_id=1, source_target_pairs={{0,4},{4,0},{8,12},{12,8},{1,5},{5,1},{9,13},{13,9},{2,6},{6,2},{1... | collective-permute-start | bytes 688136 | tf_op jit(solution)/shard_map/ppermute | solution.py:343
  7.6 4.3 %shard_map.92 = (f32[576,128]{1,0:T(8,128)S(1)}, f32[576,128]{1,0:T(8,128)S(1)}) custom-call(bf16[128,2048]{1,0:T(8,128)(2,1)} %refs_0_.1, bf16[2048,128]{1,0:T(8,128)(2,1)} %refs_1_.1, bf16[64,7168]{1,0:T(8,128)(2,1)} %refs_2_, bf16[7168,128]{1,0:T(8,128)(2,1)} %refs_3_.1, bf16[768,2048]{1,0:T(8,128)(2,1)} %refs_4_.1), custom_call_target="tpu_custom_call" | custom-call | tf_op jit(solution)/shard_map/pallas_call | solution.py:154
  11.9 0.6 collective-permute-start
  12.5 0.1 select_reduce_fusion
  12.6 1.1 %collective-permute-done = f32[576,128]{1,0:T(8,128)S(1)} collective-permute-done((f32[576,128]{1,0:T(8,128)S(1)}, f32[576,128]{1,0:T(8,128)S(1)}, u32[]{:S(2)}, u32[]{:S(2)}) %collective-permute-start) | collective-permute-done | bytes 294944 | tf_op jit(solution)/shard_map/ppermute | solution.py:366
  13.7 1.6 %collective-permute-start.3 = (f32[576,128]{1,0:T(8,128)S(1)}, f32[576,128]{1,0:T(8,128)S(1)}, u32[]{:S(2)}, u32[]{:S(2)}) collective-permute-start(f32[576,128]{1,0:T(8,128)S(1)} %add.6), channel_id=1, source_target_pairs={{0,2},{2,0},{1,3},{3,1},{4,6},{6,4},{5,7},{7,5},{8,10},{10,8},{9,1... | collective-permute-start | bytes 884744 | tf_op jit(solution)/shard_map/ppermute | solution.py:368
  15.3 0.4 collective-permute-start.4
  15.7 1.5 %collective-permute-start.5 = (bf16[64,1792]{1,0:T(8,128)(2,1)S(1)}, bf16[64,1792]{1,0:T(8,128)(2,1)S(1)}, u32[]{:S(2)}, u32[]{:S(2)}) collective-permute-start(bf16[64,1792]{1,0:T(8,128)(2,1)S(1)} %collective-permute-done.1.refs_4_), channel_id=1, source_target_pairs={{0,16},{1,17},{2,18},{3,19},{4,8},{5,9},{6,10},{7,11},{8,4},{9,5},... | collective-permute-start | bytes 688136 | tf_op jit(solution)/shard_map/ppermute | solution.py:349
  17.3 0.0 collective-permute-done.6.refs_5_
  17.3 0.7 %collective-permute-start.8 = (bf16[64,1792]{1,0:T(8,128)(2,1)S(1)}, bf16[64,1792]{1,0:T(8,128)(2,1)S(1)}, u32[]{:S(2)}, u32[]{:S(2)}) collective-permute-start(bf16[64,1792]{1,0:T(8,128)(2,1)S(1)} %broadcast_select_fusion.4), channel_id=1, source_target_pairs={{0,4},{4,0},{8,12},{12,8},{1,5},{5,1},{9,13},{13,9},{2,6},{6,2},{1... | collective-permute-start | bytes 688136 | tf_op jit(solution)/shard_map/ppermute | solution.py:343
  18.0 1.5 %collective-permute-start.9 = (bf16[64,1792]{1,0:T(8,128)(2,1)S(1)}, bf16[64,1792]{1,0:T(8,128)(2,1)S(1)}, u32[]{:S(2)}, u32[]{:S(2)}) collective-permute-start(bf16[64,1792]{1,0:T(8,128)(2,1)S(1)} %collective-permute-done.6.refs_5_), channel_id=1, source_target_pairs={{0,16},{1,17},{2,18},{3,19},{4,8},{5,9},{6,10},{7,11},{8,4},{9,5},... | collective-permute-start | bytes 688136 | tf_op jit(solution)/shard_map/ppermute | solution.py:349
  19.5 4.4 %collective-permute-done.4 = bf16[64,1792]{1,0:T(8,128)(2,1)S(1)} collective-permute-done((bf16[64,1792]{1,0:T(8,128)(2,1)S(1)}, bf16[64,1792]{1,0:T(8,128)(2,1)S(1)}, u32[]{:S(2)}, u32[]{:S(2)}) %collective-permute-start.4) | collective-permute-done | bytes 229408 | tf_op jit(solution)/shard_map/ppermute | solution.py:343
  23.8 0.4 collective-permute-done.5
  24.3 1.7 %collective-permute-start.11 = (bf16[64,256]{1,0:T(8,128)(2,1)S(1)}, bf16[64,256]{1,0:T(8,128)(2,1)S(1)}, u32[]{:S(2)}, u32[]{:S(2)}) collective-permute-start(bf16[64,256]{1,0:T(8,128)(2,1)S(1)} %pad_maximum_fusion.2.refs_0_), channel_id=1, source_target_pairs={{0,4},{4,0},{8,12},{12,8},{1,5},{5,1},{9,13},{13,9},{2,6},{6,2},{1... | collective-permute-start | bytes 98312 | tf_op jit(solution)/shard_map/ppermute | solution.py:46
  26.1 1.9 %collective-permute-start.12 = (bf16[64,256]{1,0:T(8,128)(2,1)S(1)}, bf16[64,256]{1,0:T(8,128)(2,1)S(1)}, u32[]{:S(2)}, u32[]{:S(2)}) collective-permute-start(bf16[64,256]{1,0:T(8,128)(2,1)S(1)} %pad_maximum_fusion.2.refs_0_), channel_id=1, source_target_pairs={{0,8},{4,12},{8,0},{12,4},{1,9},{5,13},{9,1},{13,5},{2,10},{6,14},... | collective-permute-start | bytes 98312 | tf_op jit(solution)/shard_map/ppermute | solution.py:46
  27.9 0.8 %collective-permute-start.13 = (bf16[64,256]{1,0:T(8,128)(2,1)S(1)}, bf16[64,256]{1,0:T(8,128)(2,1)S(1)}, u32[]{:S(2)}, u32[]{:S(2)}) collective-permute-start(bf16[64,256]{1,0:T(8,128)(2,1)S(1)} %pad_maximum_fusion.2.refs_0_), channel_id=1, source_target_pairs={{0,12},{4,8},{8,4},{12,0},{1,13},{5,9},{9,5},{13,1},{2,14},{6,10},... | collective-permute-start | bytes 98312 | tf_op jit(solution)/shard_map/ppermute | solution.py:46
  28.9 2.4 %collective-permute-start.15 = (bf16[64,3584]{1,0:T(8,128)(2,1)S(1)}, bf16[64,3584]{1,0:T(8,128)(2,1)S(1)}, u32[]{:S(2)}, u32[]{:S(2)}) collective-permute-start(bf16[64,3584]{1,0:T(8,128)(2,1)S(1)} %pad_maximum_fusion.mine_2_ref), channel_id=1, source_target_pairs={{0,4},{4,0},{8,12},{12,8},{1,5},{5,1},{9,13},{13,9},{2,6},{6,2},{1... | collective-permute-start | bytes 1376264 | tf_op jit(solution)/shard_map/ppermute | solution.py:343
  31.4 1.5 %collective-permute-start.10 = (bf16[64,3584]{1,0:T(8,128)(2,1)S(1)}, bf16[64,3584]{1,0:T(8,128)(2,1)S(1)}, u32[]{:S(2)}, u32[]{:S(2)}) collective-permute-start(bf16[64,3584]{1,0:T(8,128)(2,1)S(1)} %pad_maximum_fusion.mine_2_ref), channel_id=1, source_target_pairs={{0,16},{16,0},{1,17},{17,1},{2,18},{18,2},{3,19},{19,3},{4,20},{20... | collective-permute-start | bytes 1376264 | tf_op jit(solution)/shard_map/ppermute | solution.py:346
  32.9 0.1 broadcast_select_fusion
  33.0 7.3 %shard_map.93 = (f32[768,128]{1,0:T(8,128)S(1)}, bf16[768,7168]{1,0:T(8,128)(2,1)S(1)}) custom-call(bf16[768,7168]{1,0:T(8,128)(2,1)} %source_ref, bf16[64,1792]{1,0:T(8,128)(2,1)S(1)} %get-tuple-element.32.refs_0_, bf16[64,1792]{1,0:T(8,128)(2,1)S(1)} %get-tuple-element.33.refs_1_, bf16[64,1792]{1,0:T(8,128)(2,1)S(1)} %get-tuple-element.39.refs_2_, ...), custom_call_target="tpu_custom_call" | custom-call | flops 1 | bytes 1 | tf_op jit(solution)/shard_map/pallas_call | solution.py:297
  40.3 0.5 shard_map.94.weights_ref
  40.8 0.0 collective-permute-done.15.mine_3_ref
  40.8 1.2 %collective-permute-start.16 = (bf16[64,1792]{1,0:T(8,128)(2,1)S(1)}, bf16[64,1792]{1,0:T(8,128)(2,1)S(1)}, u32[]{:S(2)}, u32[]{:S(2)}) collective-permute-start(bf16[64,1792]{1,0:T(8,128)(2,1)S(1)} %slice.18), channel_id=1, source_target_pairs={{0,16},{16,0},{1,17},{17,1},{2,18},{18,2},{3,19},{19,3},{4,20},{20... | collective-permute-start | bytes 688136 | tf_op jit(solution)/shard_map/ppermute | solution.py:346
  42.1 1.7 %collective-permute-start.14 = (bf16[64,1792]{1,0:T(8,128)(2,1)S(1)}, bf16[64,1792]{1,0:T(8,128)(2,1)S(1)}, u32[]{:S(2)}, u32[]{:S(2)}) collective-permute-start(bf16[64,1792]{1,0:T(8,128)(2,1)S(1)} %slice.17), channel_id=1, source_target_pairs={{0,4},{4,0},{8,12},{12,8},{1,5},{5,1},{9,13},{13,9},{2,6},{6,2},{1... | collective-permute-start | bytes 688136 | tf_op jit(solution)/shard_map/ppermute | solution.py:343
  43.8 2.4 %shard_map.95 = (f32[768,128]{1,0:T(8,128)S(1)}, f32[768,512]{1,0:T(8,128)S(1)}, f32[8,512]{1,0:T(8,128)S(1)}) custom-call(bf16[768,7168]{1,0:T(8,128)(2,1)S(1)} %get-tuple-element.52.acts_ref, bf16[64,3584]{1,0:T(8,128)(2,1)S(1)} %pad_maximum_fusion.mine_2_ref, bf16[64,3584]{1,0:T(8,128)(2,1)S(1)} %collective-permute-done.15.mine_3_ref, ...), custom_call_target="tpu_custom_call" | custom-call | flops 1 | bytes 1 | tf_op jit(solution)/shard_map/pallas_call | solution.py:297
  46.1 2.7 %collective-permute-done.16.right_ref = bf16[64,1792]{1,0:T(8,128)(2,1)S(1)} collective-permute-done((bf16[64,1792]{1,0:T(8,128)(2,1)S(1)}, bf16[64,1792]{1,0:T(8,128)(2,1)S(1)}, u32[]{:S(2)}, u32[]{:S(2)}) %collective-permute-start.16) | collective-permute-done | bytes 229408 | tf_op jit(solution)/shard_map/ppermute | solution.py:346
  48.9 0.3 collective-permute-done.14.left_ref
  49.2 2.6 %shard_map.96 = f32[16,2]{1,0:T(8,128)S(1)} custom-call(bf16[768,7168]{1,0:T(8,128)(2,1)S(1)} %get-tuple-element.52.acts_ref, bf16[64,3584]{1,0:T(8,128)(2,1)S(1)} %collective-permute-done.10.theirs_2_ref, bf16[64,1792]{1,0:T(8,128)(2,1)S(1)} %collective-permute-done.14.left_ref, bf16[64,1792]{1,0:T(8,128)(2,1)S(1)} %collective-permute-done.16.right_ref, ...), custom_call_target="tpu_custom_call" | custom-call | flops 1 | bytes 1 | tf_op jit(solution)/shard_map/pallas_call | solution.py:297
  51.8 9.0 %all_to_all.9 = f32[16,1,2]{2,1,0:T(1,128)S(1)} all-to-all(f32[16,1,2]{2,1,0:T(1,128)S(1)} %bitcast.4), channel_id=1, replica_groups=mesh['groups'=2,'blk'=4,'eig'=2,'rep'=2] {'blk','eig','rep'}, dimensions={0} | all-to-all | bytes 256 | tf_op jit(solution)/shard_map/all_to_all | solution.py:469
  60.8 0.5 reduce_sum.21
  (36 shorter events, 0.4 us)
Async XLA Ops:
  1.3 11.3 %collective-permute-start.1 = (bf16[64,1792]{1,0:T(8,128)(2,1)S(1)}, bf16[64,1792]{1,0:T(8,128)(2,1)S(1)}, u32[]{:S(2)}, u32[]{:S(2)}) collective-permute-start(bf16[64,1792]{1,0:T(8,128)(2,1)S(1)} %get-tuple-element.32.refs_0_), channel_id=1, source_target_pairs={{0,4},{4,0},{8,12},{12,8},{1,5},{5,1},{9,13},{13,9},{2,6},{6,2},{1... | collective-permute-start | bytes 688136 | tf_op jit(solution)/shard_map/ppermute | solution.py:343
  4.4 8.2 %collective-permute-start.2 = (bf16[64,1792]{1,0:T(8,128)(2,1)S(1)}, bf16[64,1792]{1,0:T(8,128)(2,1)S(1)}, u32[]{:S(2)}, u32[]{:S(2)}) collective-permute-start(bf16[64,1792]{1,0:T(8,128)(2,1)S(1)} %get-tuple-element.32.refs_0_), channel_id=1, source_target_pairs={{0,1},{1,0},{2,3},{3,2},{4,8},{5,9},{6,10},{7,11},{8,4},{9,5},{10,... | collective-permute-start | bytes 688136 | tf_op jit(solution)/shard_map/ppermute | solution.py:349
  4.4 8.1 %copy-start.1 = (s32[768]{0:T(1024)S(1)}, s32[768]{0:T(1024)}, u32[]{:S(2)}) copy-start(s32[768]{0:T(1024)} %param.16) | copy-start | bytes 9220
  4.4 8.1 %copy-start.2 = (s32[8]{0:T(128)S(1)}, s32[8]{0:T(128)}, u32[]{:S(2)}) copy-start(s32[8]{0:T(128)} %param.17) | copy-start | bytes 100
  4.4 19.9 %copy-start = (bf16[64,128]{1,0:T(8,128)(2,1)S(1)}, bf16[64,128]{1,0:T(8,128)(2,1)}, u32[]{:S(2)}) copy-start(bf16[64,128]{1,0:T(8,128)(2,1)} %param.13) | copy-start | bytes 49156
  4.4 12.8 %collective-permute-start.6 = (bf16[64,1792]{1,0:T(8,128)(2,1)S(1)}, bf16[64,1792]{1,0:T(8,128)(2,1)S(1)}, u32[]{:S(2)}, u32[]{:S(2)}) collective-permute-start(bf16[64,1792]{1,0:T(8,128)(2,1)S(1)} %get-tuple-element.33.refs_1_), channel_id=1, source_target_pairs={{0,4},{4,0},{8,12},{12,8},{1,5},{5,1},{9,13},{13,9},{2,6},{6,2},{1... | collective-permute-start | bytes 688136 | tf_op jit(solution)/shard_map/ppermute | solution.py:343
  7.6 9.7 %collective-permute-start.7 = (bf16[64,1792]{1,0:T(8,128)(2,1)S(1)}, bf16[64,1792]{1,0:T(8,128)(2,1)S(1)}, u32[]{:S(2)}, u32[]{:S(2)}) collective-permute-start(bf16[64,1792]{1,0:T(8,128)(2,1)S(1)} %get-tuple-element.33.refs_1_), channel_id=1, source_target_pairs={{0,1},{1,0},{2,3},{3,2},{4,8},{5,9},{6,10},{7,11},{8,4},{9,5},{10,... | collective-permute-start | bytes 688136 | tf_op jit(solution)/shard_map/ppermute | solution.py:349
  11.9 1.8 %collective-permute-start = (f32[576,128]{1,0:T(8,128)S(1)}, f32[576,128]{1,0:T(8,128)S(1)}, u32[]{:S(2)}, u32[]{:S(2)}) collective-permute-start(f32[576,128]{1,0:T(8,128)S(1)} %get-tuple-element.36), channel_id=1, source_target_pairs={{0,1},{1,0},{2,3},{3,2},{4,5},{5,4},{6,7},{7,6},{8,9},{9,8},{10,11... | collective-permute-start | bytes 884744 | tf_op jit(solution)/shard_map/ppermute | solution.py:366
  13.7 10.5 %collective-permute-start.3 = (f32[576,128]{1,0:T(8,128)S(1)}, f32[576,128]{1,0:T(8,128)S(1)}, u32[]{:S(2)}, u32[]{:S(2)}) collective-permute-start(f32[576,128]{1,0:T(8,128)S(1)} %add.6), channel_id=1, source_target_pairs={{0,2},{2,0},{1,3},{3,1},{4,6},{6,4},{5,7},{7,5},{8,10},{10,8},{9,1... | collective-permute-start | bytes 884744 | tf_op jit(solution)/shard_map/ppermute | solution.py:368
  15.3 8.5 %collective-permute-start.4 = (bf16[64,1792]{1,0:T(8,128)(2,1)S(1)}, bf16[64,1792]{1,0:T(8,128)(2,1)S(1)}, u32[]{:S(2)}, u32[]{:S(2)}) collective-permute-start(bf16[64,1792]{1,0:T(8,128)(2,1)S(1)} %broadcast_select_fusion.5), channel_id=1, source_target_pairs={{0,4},{4,0},{8,12},{12,8},{1,5},{5,1},{9,13},{13,9},{2,6},{6,2},{1... | collective-permute-start | bytes 688136 | tf_op jit(solution)/shard_map/ppermute | solution.py:343
  15.7 8.5 %collective-permute-start.5 = (bf16[64,1792]{1,0:T(8,128)(2,1)S(1)}, bf16[64,1792]{1,0:T(8,128)(2,1)S(1)}, u32[]{:S(2)}, u32[]{:S(2)}) collective-permute-start(bf16[64,1792]{1,0:T(8,128)(2,1)S(1)} %collective-permute-done.1.refs_4_), channel_id=1, source_target_pairs={{0,16},{1,17},{2,18},{3,19},{4,8},{5,9},{6,10},{7,11},{8,4},{9,5},... | collective-permute-start | bytes 688136 | tf_op jit(solution)/shard_map/ppermute | solution.py:349
  17.3 11.5 %collective-permute-start.8 = (bf16[64,1792]{1,0:T(8,128)(2,1)S(1)}, bf16[64,1792]{1,0:T(8,128)(2,1)S(1)}, u32[]{:S(2)}, u32[]{:S(2)}) collective-permute-start(bf16[64,1792]{1,0:T(8,128)(2,1)S(1)} %broadcast_select_fusion.4), channel_id=1, source_target_pairs={{0,4},{4,0},{8,12},{12,8},{1,5},{5,1},{9,13},{13,9},{2,6},{6,2},{1... | collective-permute-start | bytes 688136 | tf_op jit(solution)/shard_map/ppermute | solution.py:343
  18.0 10.8 %collective-permute-start.9 = (bf16[64,1792]{1,0:T(8,128)(2,1)S(1)}, bf16[64,1792]{1,0:T(8,128)(2,1)S(1)}, u32[]{:S(2)}, u32[]{:S(2)}) collective-permute-start(bf16[64,1792]{1,0:T(8,128)(2,1)S(1)} %collective-permute-done.6.refs_5_), channel_id=1, source_target_pairs={{0,16},{1,17},{2,18},{3,19},{4,8},{5,9},{6,10},{7,11},{8,4},{9,5},... | collective-permute-start | bytes 688136 | tf_op jit(solution)/shard_map/ppermute | solution.py:349
  24.3 8.6 %collective-permute-start.11 = (bf16[64,256]{1,0:T(8,128)(2,1)S(1)}, bf16[64,256]{1,0:T(8,128)(2,1)S(1)}, u32[]{:S(2)}, u32[]{:S(2)}) collective-permute-start(bf16[64,256]{1,0:T(8,128)(2,1)S(1)} %pad_maximum_fusion.2.refs_0_), channel_id=1, source_target_pairs={{0,4},{4,0},{8,12},{12,8},{1,5},{5,1},{9,13},{13,9},{2,6},{6,2},{1... | collective-permute-start | bytes 98312 | tf_op jit(solution)/shard_map/ppermute | solution.py:46
  26.1 14.3 %collective-permute-start.12 = (bf16[64,256]{1,0:T(8,128)(2,1)S(1)}, bf16[64,256]{1,0:T(8,128)(2,1)S(1)}, u32[]{:S(2)}, u32[]{:S(2)}) collective-permute-start(bf16[64,256]{1,0:T(8,128)(2,1)S(1)} %pad_maximum_fusion.2.refs_0_), channel_id=1, source_target_pairs={{0,8},{4,12},{8,0},{12,4},{1,9},{5,13},{9,1},{13,5},{2,10},{6,14},... | collective-permute-start | bytes 98312 | tf_op jit(solution)/shard_map/ppermute | solution.py:46
  27.9 12.4 %collective-permute-start.13 = (bf16[64,256]{1,0:T(8,128)(2,1)S(1)}, bf16[64,256]{1,0:T(8,128)(2,1)S(1)}, u32[]{:S(2)}, u32[]{:S(2)}) collective-permute-start(bf16[64,256]{1,0:T(8,128)(2,1)S(1)} %pad_maximum_fusion.2.refs_0_), channel_id=1, source_target_pairs={{0,12},{4,8},{8,4},{12,0},{1,13},{5,9},{9,5},{13,1},{2,14},{6,10},... | collective-permute-start | bytes 98312 | tf_op jit(solution)/shard_map/ppermute | solution.py:46
  28.9 11.9 %collective-permute-start.15 = (bf16[64,3584]{1,0:T(8,128)(2,1)S(1)}, bf16[64,3584]{1,0:T(8,128)(2,1)S(1)}, u32[]{:S(2)}, u32[]{:S(2)}) collective-permute-start(bf16[64,3584]{1,0:T(8,128)(2,1)S(1)} %pad_maximum_fusion.mine_2_ref), channel_id=1, source_target_pairs={{0,4},{4,0},{8,12},{12,8},{1,5},{5,1},{9,13},{13,9},{2,6},{6,2},{1... | collective-permute-start | bytes 1376264 | tf_op jit(solution)/shard_map/ppermute | solution.py:343
  31.4 10.7 %collective-permute-start.10 = (bf16[64,3584]{1,0:T(8,128)(2,1)S(1)}, bf16[64,3584]{1,0:T(8,128)(2,1)S(1)}, u32[]{:S(2)}, u32[]{:S(2)}) collective-permute-start(bf16[64,3584]{1,0:T(8,128)(2,1)S(1)} %pad_maximum_fusion.mine_2_ref), channel_id=1, source_target_pairs={{0,16},{16,0},{1,17},{17,1},{2,18},{18,2},{3,19},{19,3},{4,20},{20... | collective-permute-start | bytes 1376264 | tf_op jit(solution)/shard_map/ppermute | solution.py:346
  32.9 10.8 %collective-permute-start.17 = (bf16[384,128]{1,0:T(8,128)(2,1)S(1)}, bf16[384,128]{1,0:T(8,128)(2,1)S(1)}, u32[]{:S(2)}, u32[]{:S(2)}) collective-permute-start(bf16[384,128]{1,0:T(8,128)(2,1)S(1)} %slice.20), channel_id=1, source_target_pairs={{0,1},{1,0},{2,3},{3,2},{4,5},{5,4},{6,7},{7,6},{8,9},{9,8},{10,11... | collective-permute-start | bytes 294920 | tf_op jit(solution)/shard_map/ppermute | solution.py:389
  40.8 8.1 %collective-permute-start.16 = (bf16[64,1792]{1,0:T(8,128)(2,1)S(1)}, bf16[64,1792]{1,0:T(8,128)(2,1)S(1)}, u32[]{:S(2)}, u32[]{:S(2)}) collective-permute-start(bf16[64,1792]{1,0:T(8,128)(2,1)S(1)} %slice.18), channel_id=1, source_target_pairs={{0,16},{16,0},{1,17},{17,1},{2,18},{18,2},{3,19},{19,3},{4,20},{20... | collective-permute-start | bytes 688136 | tf_op jit(solution)/shard_map/ppermute | solution.py:346
  42.1 7.1 %collective-permute-start.14 = (bf16[64,1792]{1,0:T(8,128)(2,1)S(1)}, bf16[64,1792]{1,0:T(8,128)(2,1)S(1)}, u32[]{:S(2)}, u32[]{:S(2)}) collective-permute-start(bf16[64,1792]{1,0:T(8,128)(2,1)S(1)} %slice.17), channel_id=1, source_target_pairs={{0,4},{4,0},{8,12},{12,8},{1,5},{5,1},{9,13},{13,9},{2,6},{6,2},{1... | collective-permute-start | bytes 688136 | tf_op jit(solution)/shard_map/ppermute | solution.py:343

commit v11 on v10

--- a/solution.py
+++ b/solution.py
@@ -209,36 +209,20 @@
     weigh(query_count, packs, out_query_ref[...], weights_ref)
 
 
-def first_kernel(source_ref, *refs):
-    slots, (total_ref, acts_ref, copied) = refs[:8], refs[8:]
+def load_kernel(source_ref, acts_ref, copied):
+    copies = cut_copies(source_ref, acts_ref, copied, copied.shape[0])
+    for copy in copies:
+        copy.start()
+    for copy in copies:
+        copy.wait()
+
+
+def first_kernel(acts_ref, *refs):
+    slots, total_ref = refs[:8], refs[8]
     columns = slots[0].shape[1]
     group = lax.axis_index("groups")
-    steps = acts_ref.shape[0] // BLOCK
-    parts = 8
-
-    def copies(step):
-        size = BLOCK // parts
-        begin = pl.multiple_of(step * BLOCK, BLOCK)
-        places = [pl.ds(begin + part * size, size) for part in range(parts)]
-        return [
-            pltpu.make_async_copy(source_ref.at[place], acts_ref.at[place], copied.at[step, part])
-            for part, place in enumerate(places)
-        ]
-
-    for copy in copies(0):
-        copy.start()
-
-    @pl.loop(0, steps)
-    def _(step):
-        for copy in copies(step):
-            copy.wait()
-
-        @pl.when(step + 1 < steps)
-        def _():
-            for copy in copies(step + 1):
-                copy.start()
-
-        start = pl.multiple_of(step * BLOCK, LANES)
+
+    def body(start, carry):
         total = 0.0
         for place in range(4):
             half = group if place < 2 else 1 - group
@@ -246,6 +230,9 @@
                 acts_ref, start, (slots[place], slots[4 + place]), half, place % 2 * columns
             )
         total_ref[pl.ds(start, BLOCK), :] = total
+        return carry
+
+    blocks(acts_ref.shape[0], body, 0)
 
 
 def mine_kernel(
@@ -364,17 +351,24 @@
     split = rows + width
     keep, send = small_parts(held(basis_in, *half), query_in, basis_out, query_out, out_grads)
     other = lax.ppermute(send, "rep", pair)
-    keep = keep + held(other, mine_1[0], middle_3[0])
+    keep = keep + held(other, *mine_1, *middle_3)
     other = lax.ppermute(keep, "eig", pair)
 
     arrived = []
-    for first, middle, rest in zip(mine_1, middle_3, other_half):
-        from_pair = along(jnp.where(inner, middle, held(rest, first, keep)))
-        from_across = across(held(first, middle, keep), over_y)
+    for after, first, middle, rest in zip((half[0], keep), mine_1, middle_3, other_half):
+        from_pair = along(jnp.where(inner, middle, held(rest, first, after)))
+        from_across = across(held(first, middle, after), over_y)
         arrived.append((from_pair, from_across))
 
-    small = (keep + held(other, *arrived[0])).astype(jnp.bfloat16)
-    ready = [chunk for both in arrived for chunk in both] + [small]
+    acts = call(
+        load_kernel,
+        pltpu.VMEM(acts.shape, acts.dtype),
+        in_hbm(held(acts, keep)),
+        in_specs=[pl.BlockSpec(memory_space=pl.ANY)],
+        scratch_shapes=[pltpu.SemaphoreType.DMA((8,))],
+    )
+    acts = in_vmem(acts)
+    ready = [chunk for both in arrived for chunk in both] + [acts]
     mine_2 = jnp.concatenate(
         [jnp.where(inner, held(there, *ready), here) for here, there in arrived], axis=1
     )
@@ -384,6 +378,7 @@
     theirs_2 = swapped(mine_2)
     mine_3 = along(mine_2)
 
+    small = (keep + held(other, mine_2)).astype(jnp.bfloat16)
     in_query, out_query, grad_half = small[:rows], small[rows:split], small[split:]
     packs = by_distance(jnp.concatenate([in_query, eigvals], axis=1))
     grad_other = lax.ppermute(grad_half, "rep", pair)
@@ -396,15 +391,9 @@
         axis=0,
     )
     total_shape = jax.ShapeDtypeStruct((tokens, LANES), jnp.float32)
-    first_total, acts = call(
-        first_kernel,
-        [total_shape, pltpu.VMEM(acts.shape, acts.dtype)],
-        in_hbm(held(acts, grad_half)), *half, *other_half, *mine_1, *theirs_1,
-        in_specs=[pl.BlockSpec(memory_space=pl.ANY)]
-        + [pl.BlockSpec(memory_space=pltpu.VMEM)] * 8,
-        scratch_shapes=[pltpu.SemaphoreType.DMA((tokens // BLOCK, 8))],
-    )
-    acts = in_vmem(acts)
+    first_total = call(
+        first_kernel, total_shape, acts, *half, *other_half, *mine_1, *theirs_1
+    )
 
     cut = mine_3.shape[1] // 2
     left_3 = along(held(theirs_2, first_total, *packs[1:])[:, :cut])

time: 61.5 us -> 74.4 us (1.21)
  local copies, waits for them, and re-layouts: 0.06 us -> 13.1 us
  waiting for transfers between devices: 8.93 us -> 4.85 us
  other arithmetic: 0.95 us -> 2.59 us
  blocking collectives: 8.98 us -> 9.96 us
    unnamed x6 -> x44, local copies, waits for them, and re-layouts: 0.01 us -> 12.1 us
    ppermute x6, waiting for transfers between devices: 4.68 us -> 0.38 us  [along(): return lax.ppermute(value, 'blk', [(i, i ^ 1) for i in range(4)])]
    ppermute x2, waiting for transfers between devices: 2.75 us -> 4.45 us  [swapped(): return lax.ppermute(value, 'groups', pair)]
    ppermute x2, starting transfers between devices: 2.74 us -> 1.21 us  [swapped(): return lax.ppermute(value, 'groups', pair)]
    ppermute x1, waiting for transfers between devices: 1.07 us -> 0.01 us  [stepped_scores(): other = lax.ppermute(send, 'rep', pair)]
    select_n x1, other arithmetic: 0.06 us -> 1.1 us  [stepped_scores(): jnp.where(inner, held(here, mine_2), held(there, mine_2))]
    ppermute x6, starting transfers between devices: 11.4 us -> 12.4 us  [along(): return lax.ppermute(value, 'blk', [(i, i ^ 1) for i in range(4)])]
    all_to_all x1, blocking collectives: 8.98 us -> 9.96 us  [on_device(): parts = lax.all_to_all(parts, ('blk', 'eig', 'rep'), 0, 0, tiled=True)]
  transfers between devices with their start and end apart: 18 -> 18, of which waited for: 5 -> 2; matrix products, arithmetic and copies ran while one was open for 1% -> 3% of each run, Pallas kernels for 24% -> 20%
where the time goes in v11:
time: 74.4 us; the launch traced here: 74 us
  starting transfers between devices  24.1 us (32%)
  Pallas kernels  19 us (26%)
  local copies, waits for them, and re-layouts  13.1 us (18%)
  blocking collectives  9.96 us (13%)
  waiting for transfers between devices  4.85 us (7%)
  other arithmetic  2.59 us (3%)
    pallas_call x5, Pallas kernels, call(): pl.pallas_call(kernel, out_shape=out_shape, compiler_params=pltpu.Compile...  13.4 us
    ppermute x6, starting transfers between devices, along(): return lax.ppermute(value, 'blk', [(i, i ^ 1) for i in range(4)])  12.4 us
    unnamed x44, local copies, waits for them, and re-layouts  12.1 us
    all_to_all x1, blocking collectives, on_device(): parts = lax.all_to_all(parts, ('blk', 'eig', 'rep'), 0, 0, tiled=True)  9.96 us
    ppermute x3, starting transfers between devices, by_distance(): lax.ppermute(value, axis, [(i, i ^ k) for i in range(size)])  5.32 us
    ppermute x2, waiting for transfers between devices, swapped(): return lax.ppermute(value, 'groups', pair)  4.45 us
    pallas_call x1, Pallas kernels, small_parts(): pl.pallas_call(parts_kernel, in_specs=[pl.BlockSpec(memory_space=pl.ANY)]...  4.31 us
    ppermute x4, starting transfers between devices, across(): lax.ppermute(value, AXES, pairing(lambda g, b, e, r: (g, 3 - b, e, r) if...  3.05 us
  transfers between devices with their start and end apart: 18, of which 2 were waited for; matrix products, arithmetic and copies ran while one was open for 3% of the time, Pallas kernels for 20%

profile of v11, /device:TPU:0, one launch (start us, length us, event | category | flops | bytes accessed | tf_op | source)
XLA Modules:
  0.0 74.0 jit_solution(4403875293448317952)
XLA Ops:
  0.0 1.3 %shard_map.91 = (bf16[64,1792]{1,0:T(8,128)(2,1)S(1)}, bf16[64,1792]{1,0:T(8,128)(2,1)S(1)}, bf16[64,1792]{1,0:T(8,128)(2,1)S(1)}, bf16[64,1792]{1,0:T(8,128)(2,1)S(1)}) custom-call(bf16[64,7168]{1,0:T(8,128)(2,1)} %refs_2_), custom_call_target="tpu_custom_call" | custom-call | tf_op jit(solution)/shard_map/pallas_call | solution.py:86
  1.3 3.1 %collective-permute-start.1 = (bf16[64,1792]{1,0:T(8,128)(2,1)S(1)}, bf16[64,1792]{1,0:T(8,128)(2,1)S(1)}, u32[]{:S(2)}, u32[]{:S(2)}) collective-permute-start(bf16[64,1792]{1,0:T(8,128)(2,1)S(1)} %get-tuple-element.30.refs_0_), channel_id=1, source_target_pairs={{0,4},{4,0},{8,12},{12,8},{1,5},{5,1},{9,13},{13,9},{2,6},{6,2},{1... | collective-permute-start | bytes 688136 | tf_op jit(solution)/shard_map/ppermute | solution.py:330
  4.4 3.1 %collective-permute-start.2 = (bf16[64,1792]{1,0:T(8,128)(2,1)S(1)}, bf16[64,1792]{1,0:T(8,128)(2,1)S(1)}, u32[]{:S(2)}, u32[]{:S(2)}) collective-permute-start(bf16[64,1792]{1,0:T(8,128)(2,1)S(1)} %get-tuple-element.31.refs_1_), channel_id=1, source_target_pairs={{0,4},{4,0},{8,12},{12,8},{1,5},{5,1},{9,13},{13,9},{2,6},{6,2},{1... | collective-permute-start | bytes 688136 | tf_op jit(solution)/shard_map/ppermute | solution.py:330
  7.6 4.3 %shard_map.92 = (f32[576,128]{1,0:T(8,128)S(1)}, f32[576,128]{1,0:T(8,128)S(1)}) custom-call(bf16[128,2048]{1,0:T(8,128)(2,1)} %refs_0_.1, bf16[2048,128]{1,0:T(8,128)(2,1)} %refs_1_.1, bf16[64,7168]{1,0:T(8,128)(2,1)} %refs_2_, bf16[7168,128]{1,0:T(8,128)(2,1)} %refs_3_.1, bf16[768,2048]{1,0:T(8,128)(2,1)} %refs_4_.1), custom_call_target="tpu_custom_call" | custom-call | tf_op jit(solution)/shard_map/pallas_call | solution.py:154
  11.9 0.6 collective-permute-start
  12.6 1.6 %collective-permute-start.6 = (bf16[64,1792]{1,0:T(8,128)(2,1)S(1)}, bf16[64,1792]{1,0:T(8,128)(2,1)S(1)}, u32[]{:S(2)}, u32[]{:S(2)}) collective-permute-start(bf16[64,1792]{1,0:T(8,128)(2,1)S(1)} %broadcast_select_fusion.5), channel_id=1, source_target_pairs={{0,4},{4,0},{8,12},{12,8},{1,5},{5,1},{9,13},{13,9},{2,6},{6,2},{1... | collective-permute-start | bytes 688136 | tf_op jit(solution)/shard_map/ppermute | solution.py:330
  14.1 1.5 %collective-permute-start.5 = (bf16[64,1792]{1,0:T(8,128)(2,1)S(1)}, bf16[64,1792]{1,0:T(8,128)(2,1)S(1)}, u32[]{:S(2)}, u32[]{:S(2)}) collective-permute-start(bf16[64,1792]{1,0:T(8,128)(2,1)S(1)} %collective-permute-done.1.refs_4_), channel_id=1, source_target_pairs={{0,16},{1,17},{2,18},{3,19},{4,8},{5,9},{6,10},{7,11},{8,4},{9,5},... | collective-permute-start | bytes 688136 | tf_op jit(solution)/shard_map/ppermute | solution.py:336
  15.8 2.9 %collective-permute-start.7 = (bf16[64,1792]{1,0:T(8,128)(2,1)S(1)}, bf16[64,1792]{1,0:T(8,128)(2,1)S(1)}, u32[]{:S(2)}, u32[]{:S(2)}) collective-permute-start(bf16[64,1792]{1,0:T(8,128)(2,1)S(1)} %broadcast_select_fusion.4), channel_id=1, source_target_pairs={{0,4},{4,0},{8,12},{12,8},{1,5},{5,1},{9,13},{13,9},{2,6},{6,2},{1... | collective-permute-start | bytes 688136 | tf_op jit(solution)/shard_map/ppermute | solution.py:330
  18.7 1.5 %collective-permute-start.8 = (bf16[64,1792]{1,0:T(8,128)(2,1)S(1)}, bf16[64,1792]{1,0:T(8,128)(2,1)S(1)}, u32[]{:S(2)}, u32[]{:S(2)}) collective-permute-start(bf16[64,1792]{1,0:T(8,128)(2,1)S(1)} %collective-permute-done.2.refs_5_), channel_id=1, source_target_pairs={{0,16},{1,17},{2,18},{3,19},{4,8},{5,9},{6,10},{7,11},{8,4},{9,5},... | collective-permute-start | bytes 688136 | tf_op jit(solution)/shard_map/ppermute | solution.py:336
  20.3 1.6 %collective-permute-start.10 = (f32[576,128]{1,0:T(8,128)S(1)}, f32[576,128]{1,0:T(8,128)S(1)}, u32[]{:S(2)}, u32[]{:S(2)}) collective-permute-start(f32[576,128]{1,0:T(8,128)S(1)} %add.6), channel_id=1, source_target_pairs={{0,2},{2,0},{1,3},{3,1},{4,6},{6,4},{5,7},{7,5},{8,10},{10,8},{9,1... | collective-permute-start | bytes 884744 | tf_op jit(solution)/shard_map/ppermute | solution.py:355
  21.9 4.2 %shard_map.93.acts_ref = bf16[768,7168]{1,0:T(8,128)(2,1)S(1)} custom-call(bf16[768,7168]{1,0:T(8,128)(2,1)} %source_ref), custom_call_target="tpu_custom_call" | custom-call | flops 1 | bytes 1 | tf_op jit(solution)/shard_map/pallas_call | solution.py:284
  26.2 4.2 %copy-done = bf16[768,7168]{1,0:T(8,128)(2,1)} copy-done((bf16[768,7168]{1,0:T(8,128)(2,1)}, bf16[768,7168]{1,0:T(8,128)(2,1)S(1)}, u32[]{:S(2)}) %copy-start) | copy-done | bytes 11010072
  30.6 0.6 pad_maximum_fusion.2.refs_0_
  31.2 1.0 %collective-permute-start.11 = (bf16[64,256]{1,0:T(8,128)(2,1)}, bf16[64,256]{1,0:T(8,128)(2,1)}, u32[]{:S(2)}, u32[]{:S(2)}) collective-permute-start(bf16[64,256]{1,0:T(8,128)(2,1)} %pad_maximum_fusion.2.refs_0_), channel_id=1, source_target_pairs={{0,4},{4,0},{8,12},{12,8},{1,5},{5,1},{9,13},{13,9},{2,6},{6,2},{1... | collective-permute-start | bytes 98312 | tf_op jit(solution)/shard_map/ppermute | solution.py:46
  32.3 1.1 %collective-permute-start.15 = (bf16[64,3584]{1,0:T(8,128)(2,1)S(1)}, bf16[64,3584]{1,0:T(8,128)(2,1)S(1)}, u32[]{:S(2)}, u32[]{:S(2)}) collective-permute-start(bf16[64,3584]{1,0:T(8,128)(2,1)S(1)} %pad_maximum_fusion.mine_2_ref), channel_id=1, source_target_pairs={{0,4},{4,0},{8,12},{12,8},{1,5},{5,1},{9,13},{13,9},{2,6},{6,2},{1... | collective-permute-start | bytes 1376264 | tf_op jit(solution)/shard_map/ppermute | solution.py:330
  33.4 0.6 collective-permute-start.9
  33.9 0.9 %slice.22 = bf16[384,128]{1,0:T(8,128)(2,1)S(1)} slice(bf16[576,128]{1,0:T(8,128)(2,1)} %copy-done.10), slice={[192:576], [0:128]} | slice | bytes 196608 | tf_op jit(solution)/shard_map/slice | solution.py:382
  34.8 1.9 %collective-permute-start.12 = (bf16[64,256]{1,0:T(8,128)(2,1)}, bf16[64,256]{1,0:T(8,128)(2,1)S(1)}, u32[]{:S(2)}, u32[]{:S(2)}) collective-permute-start(bf16[64,256]{1,0:T(8,128)(2,1)} %pad_maximum_fusion.2.refs_0_), channel_id=1, source_target_pairs={{0,8},{4,12},{8,0},{12,4},{1,9},{5,13},{9,1},{13,5},{2,10},{6,14},... | collective-permute-start | bytes 98312 | tf_op jit(solution)/shard_map/ppermute | solution.py:46
  36.7 2.4 %collective-permute-start.13 = (bf16[64,256]{1,0:T(8,128)(2,1)}, bf16[64,256]{1,0:T(8,128)(2,1)S(1)}, u32[]{:S(2)}, u32[]{:S(2)}) collective-permute-start(bf16[64,256]{1,0:T(8,128)(2,1)} %pad_maximum_fusion.2.refs_0_), channel_id=1, source_target_pairs={{0,12},{4,8},{8,4},{12,0},{1,13},{5,9},{9,5},{13,1},{2,14},{6,10},... | collective-permute-start | bytes 98312 | tf_op jit(solution)/shard_map/ppermute | solution.py:46
  39.2 1.1 %broadcast_select_fusion = (bf16[64,1792]{1,0:T(8,128)(2,1)S(1)}, bf16[64,1792]{1,0:T(8,128)(2,1)S(1)}) fusion(bf16[64,1792]{1,0:T(8,128)(2,1)} %copy-done.14, bf16[64,1792]{1,0:T(8,128)(2,1)} %copy-done.15, pred[]{:T(512)S(6)} %or.3, bf16[64,1792]{1,0:T(8,128)(2,1)} %copy-done.12, bf16[64,1792]{1,0:T(8,128)(2,1)} %copy-done.13), kind=kLoop, calls=%fused_computation.2 | loop fusion | flops 229376 | bytes 1376257 | tf_op jit(solution)/shard_map/jit(_where)/select_n | solution.py:376
  40.3 4.1 %copy-done.1 = bf16[768,7168]{1,0:T(8,128)(2,1)S(1)} copy-done((bf16[768,7168]{1,0:T(8,128)(2,1)S(1)}, bf16[768,7168]{1,0:T(8,128)(2,1)}, u32[]{:S(2)}) %copy-start.1) | copy-done | bytes 11010072
  44.4 0.9 %copy-done.3 = bf16[64,1792]{1,0:T(8,128)(2,1)S(1)} copy-done((bf16[64,1792]{1,0:T(8,128)(2,1)S(1)}, bf16[64,1792]{1,0:T(8,128)(2,1)}, u32[]{:S(2)}) %copy-start.3) | copy-done | bytes 229400
  45.3 0.9 %copy-done.5 = bf16[64,1792]{1,0:T(8,128)(2,1)S(1)} copy-done((bf16[64,1792]{1,0:T(8,128)(2,1)S(1)}, bf16[64,1792]{1,0:T(8,128)(2,1)}, u32[]{:S(2)}) %copy-start.5) | copy-done | bytes 229400
  46.3 0.9 %copy-done.7 = bf16[64,1792]{1,0:T(8,128)(2,1)S(1)} copy-done((bf16[64,1792]{1,0:T(8,128)(2,1)S(1)}, bf16[64,1792]{1,0:T(8,128)(2,1)}, u32[]{:S(2)}) %copy-start.7) | copy-done | bytes 229400
  47.2 0.9 %copy-done.9 = bf16[64,1792]{1,0:T(8,128)(2,1)S(1)} copy-done((bf16[64,1792]{1,0:T(8,128)(2,1)S(1)}, bf16[64,1792]{1,0:T(8,128)(2,1)}, u32[]{:S(2)}) %copy-start.9) | copy-done | bytes 229400
  48.2 3.0 %shard_map.94.first_ref = f32[768,128]{1,0:T(8,128)S(1)} custom-call(bf16[768,7168]{1,0:T(8,128)(2,1)S(1)} %copy-done.1, bf16[64,1792]{1,0:T(8,128)(2,1)S(1)} %copy-done.3, bf16[64,1792]{1,0:T(8,128)(2,1)S(1)} %copy-done.5, bf16[64,1792]{1,0:T(8,128)(2,1)S(1)} %get-tuple-element.39.refs_2_, bf16[64,1792]{1,0:T(8,128)(2,1)S(1)} %get-tuple-element.41.refs_3_, ...), custom_call_target="tpu_custom_call" | custom-call | flops 1 | bytes 1 | tf_op jit(solution)/shard_map/pallas_call | solution.py:284
  51.2 1.2 %shard_map.95.weights_ref = bf16[2,512,128]{2,1,0:T(8,128)(2,1)S(1)} custom-call(bf16[64,256]{1,0:T(8,128)(2,1)} %pad_maximum_fusion.2.refs_0_, bf16[64,256]{1,0:T(8,128)(2,1)} %collective-permute-done.11.refs_1_, bf16[64,256]{1,0:T(8,128)(2,1)S(1)} %collective-permute-done.12.refs_2_, bf16[64,256]{1,0:T(8,128)(2,1)S(1)} %collective-permute-done.13.refs_3_, ...), custom_call_target="tpu_custom_call" | custom-call | flops 1 | bytes 1 | tf_op jit(solution)/shard_map/pallas_call | solution.py:284
  52.5 0.6 collective-permute-start.16
  53.8 2.3 %shard_map.96 = (f32[768,128]{1,0:T(8,128)S(1)}, f32[768,512]{1,0:T(8,128)S(1)}, f32[8,512]{1,0:T(8,128)S(1)}) custom-call(bf16[768,7168]{1,0:T(8,128)(2,1)S(1)} %bitcast.5, bf16[64,3584]{1,0:T(8,128)(2,1)S(1)} %pad_maximum_fusion.mine_2_ref, bf16[64,3584]{1,0:T(8,128)(2,1)S(1)} %collective-permute-done.15.mine_3_ref, f32[768,128]{1,0:T(8,128)S(1)} %shard_map.94.first_ref, ...), custom_call_target="tpu_custom_call" | custom-call | flops 1 | bytes 1 | tf_op jit(solution)/shard_map/pallas_call | solution.py:284
  56.1 4.4 %collective-permute-done.16.right_ref = bf16[64,1792]{1,0:T(8,128)(2,1)S(1)} collective-permute-done((bf16[64,1792]{1,0:T(8,128)(2,1)S(1)}, bf16[64,1792]{1,0:T(8,128)(2,1)S(1)}, u32[]{:S(2)}, u32[]{:S(2)}) %collective-permute-start.16) | collective-permute-done | bytes 229408 | tf_op jit(solution)/shard_map/ppermute | solution.py:333
  60.9 2.6 %shard_map.97 = f32[16,2]{1,0:T(8,128)S(1)} custom-call(bf16[768,7168]{1,0:T(8,128)(2,1)S(1)} %bitcast.5, bf16[64,3584]{1,0:T(8,128)(2,1)S(1)} %collective-permute-done.9.theirs_2_ref, bf16[64,1792]{1,0:T(8,128)(2,1)S(1)} %collective-permute-done.14.left_ref, bf16[64,1792]{1,0:T(8,128)(2,1)S(1)} %collective-permute-done.16.right_ref, ...), custom_call_target="tpu_custom_call" | custom-call | flops 1 | bytes 1 | tf_op jit(solution)/shard_map/pallas_call | solution.py:284
  63.5 10.0 %all_to_all.9 = f32[16,1,2]{2,1,0:T(1,128)S(1)} all-to-all(f32[16,1,2]{2,1,0:T(1,128)S(1)} %bitcast.6), channel_id=1, replica_groups=mesh['groups'=2,'blk'=4,'eig'=2,'rep'=2] {'blk','eig','rep'}, dimensions={0} | all-to-all | bytes 256 | tf_op jit(solution)/shard_map/all_to_all | solution.py:458
  (76 shorter events, 2.0 us)
Async XLA Ops:
  1.3 10.6 %copy-start.2 = (bf16[64,1792]{1,0:T(8,128)(2,1)}, bf16[64,1792]{1,0:T(8,128)(2,1)S(1)}, u32[]{:S(2)}) copy-start(bf16[64,1792]{1,0:T(8,128)(2,1)S(1)} %get-tuple-element.30.refs_0_) | copy-start | bytes 688132
  1.3 10.6 %copy-start.4 = (bf16[64,1792]{1,0:T(8,128)(2,1)}, bf16[64,1792]{1,0:T(8,128)(2,1)S(1)}, u32[]{:S(2)}) copy-start(bf16[64,1792]{1,0:T(8,128)(2,1)S(1)} %get-tuple-element.31.refs_1_) | copy-start | bytes 688132
  1.3 11.2 %collective-permute-start.1 = (bf16[64,1792]{1,0:T(8,128)(2,1)S(1)}, bf16[64,1792]{1,0:T(8,128)(2,1)S(1)}, u32[]{:S(2)}, u32[]{:S(2)}) collective-permute-start(bf16[64,1792]{1,0:T(8,128)(2,1)S(1)} %get-tuple-element.30.refs_0_), channel_id=1, source_target_pairs={{0,4},{4,0},{8,12},{12,8},{1,5},{5,1},{9,13},{13,9},{2,6},{6,2},{1... | collective-permute-start | bytes 688136 | tf_op jit(solution)/shard_map/ppermute | solution.py:330
  4.4 8.1 %collective-permute-start.3 = (bf16[64,1792]{1,0:T(8,128)(2,1)S(1)}, bf16[64,1792]{1,0:T(8,128)(2,1)S(1)}, u32[]{:S(2)}, u32[]{:S(2)}) collective-permute-start(bf16[64,1792]{1,0:T(8,128)(2,1)S(1)} %get-tuple-element.30.refs_0_), channel_id=1, source_target_pairs={{0,1},{1,0},{2,3},{3,2},{4,8},{5,9},{6,10},{7,11},{8,4},{9,5},{10,... | collective-permute-start | bytes 688136 | tf_op jit(solution)/shard_map/ppermute | solution.py:336
  4.4 15.8 %copy-start.17 = (s32[768]{0:T(1024)S(1)}, s32[768]{0:T(1024)}, u32[]{:S(2)}) copy-start(s32[768]{0:T(1024)} %param.16) | copy-start | bytes 9220
  4.4 15.8 %copy-start.18 = (s32[8]{0:T(128)S(1)}, s32[8]{0:T(128)}, u32[]{:S(2)}) copy-start(s32[8]{0:T(128)} %param.17) | copy-start | bytes 100
  4.4 11.2 %collective-permute-start.2 = (bf16[64,1792]{1,0:T(8,128)(2,1)S(1)}, bf16[64,1792]{1,0:T(8,128)(2,1)S(1)}, u32[]{:S(2)}, u32[]{:S(2)}) collective-permute-start(bf16[64,1792]{1,0:T(8,128)(2,1)S(1)} %get-tuple-element.31.refs_1_), channel_id=1, source_target_pairs={{0,4},{4,0},{8,12},{12,8},{1,5},{5,1},{9,13},{13,9},{2,6},{6,2},{1... | collective-permute-start | bytes 688136 | tf_op jit(solution)/shard_map/ppermute | solution.py:330
  7.6 8.1 %collective-permute-start.4 = (bf16[64,1792]{1,0:T(8,128)(2,1)S(1)}, bf16[64,1792]{1,0:T(8,128)(2,1)S(1)}, u32[]{:S(2)}, u32[]{:S(2)}) collective-permute-start(bf16[64,1792]{1,0:T(8,128)(2,1)S(1)} %get-tuple-element.31.refs_1_), channel_id=1, source_target_pairs={{0,1},{1,0},{2,3},{3,2},{4,8},{5,9},{6,10},{7,11},{8,4},{9,5},{10,... | collective-permute-start | bytes 688136 | tf_op jit(solution)/shard_map/ppermute | solution.py:336
  11.9 3.7 %collective-permute-start = (f32[576,128]{1,0:T(8,128)S(1)}, f32[576,128]{1,0:T(8,128)S(1)}, u32[]{:S(2)}, u32[]{:S(2)}) collective-permute-start(f32[576,128]{1,0:T(8,128)S(1)} %get-tuple-element.34), channel_id=1, source_target_pairs={{0,1},{1,0},{2,3},{3,2},{4,5},{5,4},{6,7},{7,6},{8,9},{9,8},{10,11... | collective-permute-start | bytes 884744 | tf_op jit(solution)/shard_map/ppermute | solution.py:353
  12.5 13.6 %copy-start.6 = (bf16[64,1792]{1,0:T(8,128)(2,1)}, bf16[64,1792]{1,0:T(8,128)(2,1)S(1)}, u32[]{:S(2)}) copy-start(bf16[64,1792]{1,0:T(8,128)(2,1)S(1)} %collective-permute-done.1.refs_4_) | copy-start | bytes 688132
  12.6 17.8 %collective-permute-start.6 = (bf16[64,1792]{1,0:T(8,128)(2,1)S(1)}, bf16[64,1792]{1,0:T(8,128)(2,1)S(1)}, u32[]{:S(2)}, u32[]{:S(2)}) collective-permute-start(bf16[64,1792]{1,0:T(8,128)(2,1)S(1)} %broadcast_select_fusion.5), channel_id=1, source_target_pairs={{0,4},{4,0},{8,12},{12,8},{1,5},{5,1},{9,13},{13,9},{2,6},{6,2},{1... | collective-permute-start | bytes 688136 | tf_op jit(solution)/shard_map/ppermute | solution.py:330
  14.1 16.2 %collective-permute-start.5 = (bf16[64,1792]{1,0:T(8,128)(2,1)S(1)}, bf16[64,1792]{1,0:T(8,128)(2,1)S(1)}, u32[]{:S(2)}, u32[]{:S(2)}) collective-permute-start(bf16[64,1792]{1,0:T(8,128)(2,1)S(1)} %collective-permute-done.1.refs_4_), channel_id=1, source_target_pairs={{0,16},{1,17},{2,18},{3,19},{4,8},{5,9},{6,10},{7,11},{8,4},{9,5},... | collective-permute-start | bytes 688136 | tf_op jit(solution)/shard_map/ppermute | solution.py:336
  15.7 10.5 %copy-start.8 = (bf16[64,1792]{1,0:T(8,128)(2,1)}, bf16[64,1792]{1,0:T(8,128)(2,1)S(1)}, u32[]{:S(2)}) copy-start(bf16[64,1792]{1,0:T(8,128)(2,1)S(1)} %collective-permute-done.2.refs_5_) | copy-start | bytes 688132
  15.8 14.6 %collective-permute-start.7 = (bf16[64,1792]{1,0:T(8,128)(2,1)S(1)}, bf16[64,1792]{1,0:T(8,128)(2,1)S(1)}, u32[]{:S(2)}, u32[]{:S(2)}) collective-permute-start(bf16[64,1792]{1,0:T(8,128)(2,1)S(1)} %broadcast_select_fusion.4), channel_id=1, source_target_pairs={{0,4},{4,0},{8,12},{12,8},{1,5},{5,1},{9,13},{13,9},{2,6},{6,2},{1... | collective-permute-start | bytes 688136 | tf_op jit(solution)/shard_map/ppermute | solution.py:330
  18.7 11.7 %collective-permute-start.8 = (bf16[64,1792]{1,0:T(8,128)(2,1)S(1)}, bf16[64,1792]{1,0:T(8,128)(2,1)S(1)}, u32[]{:S(2)}, u32[]{:S(2)}) collective-permute-start(bf16[64,1792]{1,0:T(8,128)(2,1)S(1)} %collective-permute-done.2.refs_5_), channel_id=1, source_target_pairs={{0,16},{1,17},{2,18},{3,19},{4,8},{5,9},{6,10},{7,11},{8,4},{9,5},... | collective-permute-start | bytes 688136 | tf_op jit(solution)/shard_map/ppermute | solution.py:336
  20.3 10.3 %copy-start.16 = (bf16[64,128]{1,0:T(8,128)(2,1)S(1)}, bf16[64,128]{1,0:T(8,128)(2,1)}, u32[]{:S(2)}) copy-start(bf16[64,128]{1,0:T(8,128)(2,1)} %param.13) | copy-start | bytes 49156
  20.3 10.2 %collective-permute-start.10 = (f32[576,128]{1,0:T(8,128)S(1)}, f32[576,128]{1,0:T(8,128)S(1)}, u32[]{:S(2)}, u32[]{:S(2)}) collective-permute-start(f32[576,128]{1,0:T(8,128)S(1)} %add.6), channel_id=1, source_target_pairs={{0,2},{2,0},{1,3},{3,1},{4,6},{6,4},{5,7},{7,5},{8,10},{10,8},{9,1... | collective-permute-start | bytes 884744 | tf_op jit(solution)/shard_map/ppermute | solution.py:355
  26.2 4.2 %copy-start = (bf16[768,7168]{1,0:T(8,128)(2,1)}, bf16[768,7168]{1,0:T(8,128)(2,1)S(1)}, u32[]{:S(2)}) copy-start(bf16[768,7168]{1,0:T(8,128)(2,1)S(1)} %shard_map.93.acts_ref) | copy-start | bytes 33030148
  30.3 1.9 %copy-start.12 = (bf16[64,1792]{1,0:T(8,128)(2,1)}, bf16[64,1792]{1,0:T(8,128)(2,1)S(1)}, u32[]{:S(2)}) copy-start(bf16[64,1792]{1,0:T(8,128)(2,1)S(1)} %collective-permute-done.6) | copy-start | bytes 688132
  30.4 23.4 %slice-start = ((s8[11010048]{0:T(1024)(128)(4,1)}), s8[2621440]{0:T(1024)(128)(4,1)S(1)}, s32[]{:S(2)}) async-start(s8[11010048]{0:T(1024)(128)(4,1)} %bitcast.4), calls=%async_computation.1 | async-start | bytes 5242880
  31.2 7.9 %collective-permute-start.11 = (bf16[64,256]{1,0:T(8,128)(2,1)}, bf16[64,256]{1,0:T(8,128)(2,1)}, u32[]{:S(2)}, u32[]{:S(2)}) collective-permute-start(bf16[64,256]{1,0:T(8,128)(2,1)} %pad_maximum_fusion.2.refs_0_), channel_id=1, source_target_pairs={{0,4},{4,0},{8,12},{12,8},{1,5},{5,1},{9,13},{13,9},{2,6},{6,2},{1... | collective-permute-start | bytes 98312 | tf_op jit(solution)/shard_map/ppermute | solution.py:46
  32.3 20.2 %collective-permute-start.15 = (bf16[64,3584]{1,0:T(8,128)(2,1)S(1)}, bf16[64,3584]{1,0:T(8,128)(2,1)S(1)}, u32[]{:S(2)}, u32[]{:S(2)}) collective-permute-start(bf16[64,3584]{1,0:T(8,128)(2,1)S(1)} %pad_maximum_fusion.mine_2_ref), channel_id=1, source_target_pairs={{0,4},{4,0},{8,12},{12,8},{1,5},{5,1},{9,13},{13,9},{2,6},{6,2},{1... | collective-permute-start | bytes 1376264 | tf_op jit(solution)/shard_map/ppermute | solution.py:330
  33.4 19.8 %collective-permute-start.9 = (bf16[64,3584]{1,0:T(8,128)(2,1)S(1)}, bf16[64,3584]{1,0:T(8,128)(2,1)S(1)}, u32[]{:S(2)}, u32[]{:S(2)}) collective-permute-start(bf16[64,3584]{1,0:T(8,128)(2,1)S(1)} %pad_maximum_fusion.mine_2_ref), channel_id=1, source_target_pairs={{0,16},{16,0},{1,17},{17,1},{2,18},{18,2},{3,19},{19,3},{4,20},{20... | collective-permute-start | bytes 1376264 | tf_op jit(solution)/shard_map/ppermute | solution.py:333
  34.8 16.4 %collective-permute-start.12 = (bf16[64,256]{1,0:T(8,128)(2,1)}, bf16[64,256]{1,0:T(8,128)(2,1)S(1)}, u32[]{:S(2)}, u32[]{:S(2)}) collective-permute-start(bf16[64,256]{1,0:T(8,128)(2,1)} %pad_maximum_fusion.2.refs_0_), channel_id=1, source_target_pairs={{0,8},{4,12},{8,0},{12,4},{1,9},{5,13},{9,1},{13,5},{2,10},{6,14},... | collective-permute-start | bytes 98312 | tf_op jit(solution)/shard_map/ppermute | solution.py:46
  36.7 14.5 %collective-permute-start.13 = (bf16[64,256]{1,0:T(8,128)(2,1)}, bf16[64,256]{1,0:T(8,128)(2,1)S(1)}, u32[]{:S(2)}, u32[]{:S(2)}) collective-permute-start(bf16[64,256]{1,0:T(8,128)(2,1)} %pad_maximum_fusion.2.refs_0_), channel_id=1, source_target_pairs={{0,12},{4,8},{8,4},{12,0},{1,13},{5,9},{9,5},{13,1},{2,14},{6,10},... | collective-permute-start | bytes 98312 | tf_op jit(solution)/shard_map/ppermute | solution.py:46
  39.2 14.6 %collective-permute-start.17 = (bf16[384,128]{1,0:T(8,128)(2,1)S(1)}, bf16[384,128]{1,0:T(8,128)(2,1)S(1)}, u32[]{:S(2)}, u32[]{:S(2)}) collective-permute-start(bf16[384,128]{1,0:T(8,128)(2,1)S(1)} %slice.22), channel_id=1, source_target_pairs={{0,1},{1,0},{2,3},{3,2},{4,5},{5,4},{6,7},{7,6},{8,9},{9,8},{10,11... | collective-permute-start | bytes 294920 | tf_op jit(solution)/shard_map/ppermute | solution.py:384
  40.3 4.1 %copy-start.1 = (bf16[768,7168]{1,0:T(8,128)(2,1)S(1)}, bf16[768,7168]{1,0:T(8,128)(2,1)}, u32[]{:S(2)}) copy-start(bf16[768,7168]{1,0:T(8,128)(2,1)} %copy-done) | copy-start | bytes 33030148
  48.1 3.0 %copy-start.11 = (bf16[576,128]{1,0:T(8,128)(2,1)S(1)}, bf16[576,128]{1,0:T(8,128)(2,1)}, u32[]{:S(2)}) copy-start(bf16[576,128]{1,0:T(8,128)(2,1)} %copy-done.10) | copy-start | bytes 442372
  48.1 5.6 %slice-start.1 = ((s8[11010048]{0:T(1024)(128)(4,1)}), s8[4194304]{0:T(1024)(128)(4,1)S(1)}, s32[]{:S(2)}) async-start(s8[11010048]{0:T(1024)(128)(4,1)} %bitcast.4), calls=%async_computation.2 | async-start | bytes 8388608
  48.2 5.6 %slice-start.2 = ((s8[11010048]{0:T(1024)(128)(4,1)}), s8[4194304]{0:T(1024)(128)(4,1)S(1)}, s32[]{:S(2)}) async-start(s8[11010048]{0:T(1024)(128)(4,1)} %bitcast.4), calls=%async_computation.3 | async-start | bytes 8388608
  52.5 8.1 %collective-permute-start.16 = (bf16[64,1792]{1,0:T(8,128)(2,1)S(1)}, bf16[64,1792]{1,0:T(8,128)(2,1)S(1)}, u32[]{:S(2)}, u32[]{:S(2)}) collective-permute-start(bf16[64,1792]{1,0:T(8,128)(2,1)S(1)} %slice.17), channel_id=1, source_target_pairs={{0,16},{16,0},{1,17},{17,1},{2,18},{18,2},{3,19},{19,3},{4,20},{20... | collective-permute-start | bytes 688136 | tf_op jit(solution)/shard_map/ppermute | solution.py:333
  53.1 7.8 %collective-permute-start.14 = (bf16[64,1792]{1,0:T(8,128)(2,1)S(1)}, bf16[64,1792]{1,0:T(8,128)(2,1)S(1)}, u32[]{:S(2)}, u32[]{:S(2)}) collective-permute-start(bf16[64,1792]{1,0:T(8,128)(2,1)S(1)} %slice.16), channel_id=1, source_target_pairs={{0,4},{4,0},{8,12},{12,8},{1,5},{5,1},{9,13},{13,9},{2,6},{6,2},{1... | collective-permute-start | bytes 688136 | tf_op jit(solution)/shard_map/ppermute | solution.py:330
  (8 other events, 10.1 us)

commit v12 on v11

--- a/solution.py
+++ b/solution.py
@@ -325,6 +325,7 @@
     pair = [(0, 1), (1, 0)]
     place = lax.axis_index("blk")
     inner = (place == 1) | (place == 2)
+    of_first = lax.axis_index("rep") == 0
 
     def along(value):
         return lax.ppermute(value, "blk", [(i, i ^ 1) for i in range(4)])
@@ -349,7 +350,8 @@
         mine_1.append(along(chunk))
 
     split = rows + width
-    keep, send = small_parts(held(basis_in, *half), query_in, basis_out, query_out, out_grads)
+    early, inner, of_first, _ = lax.optimization_barrier((basis_in, inner, of_first, half))
+    keep, send = small_parts(early, query_in, basis_out, query_out, out_grads)
     other = lax.ppermute(send, "rep", pair)
     keep = keep + held(other, *mine_1, *middle_3)
     other = lax.ppermute(keep, "eig", pair)
@@ -382,7 +384,6 @@
     in_query, out_query, grad_half = small[:rows], small[rows:split], small[split:]
     packs = by_distance(jnp.concatenate([in_query, eigvals], axis=1))
     grad_other = lax.ppermute(grad_half, "rep", pair)
-    of_first = lax.axis_index("rep") == 0
     grad_proj = jnp.concatenate(
         [
             jnp.where(of_first, grad_half, grad_other),

time: 74.4 us -> 63.6 us (0.85)
  local copies, waits for them, and re-layouts: 13.1 us -> 0.06 us
  waiting for transfers between devices: 4.85 us -> 8.6 us
  other arithmetic: 2.59 us -> 0.92 us
  starting transfers between devices: 24.1 us -> 24.9 us
    unnamed x44 -> x6, local copies, waits for them, and re-layouts: 12.1 us -> 0.01 us
    ppermute x3, waiting for transfers between devices: 0.01 us -> 4.35 us  [by_distance(): lax.ppermute(value, axis, [(i, i ^ k) for i in range(size)])]
    ppermute x2, waiting for transfers between devices: 4.45 us -> 1.78 us  [swapped(): return lax.ppermute(value, 'groups', pair)]
    ppermute x6, waiting for transfers between devices: 0.38 us -> 1.62 us  [along(): return lax.ppermute(value, 'blk', [(i, i ^ 1) for i in range(4)])]
    select_n x1, other arithmetic: 1.1 us -> 0.05 us  [stepped_scores(): jnp.where(inner, held(here, mine_2), held(there, mine_2))]
    ppermute x2, starting transfers between devices: 1.21 us -> 2.17 us  [swapped(): return lax.ppermute(value, 'groups', pair)]
    slice x1, local copies, waits for them, and re-layouts: 0.9 us -> 0.01 us  [stepped_scores(): small[split:]]
    ppermute x1, waiting for transfers between devices: 0.01 us -> 0.84 us  [stepped_scores(): other = lax.ppermute(keep, 'eig', pair)]
  transfers between devices with their start and end apart: 18 -> 18, of which waited for: 2 -> 5; matrix products, arithmetic and copies ran while one was open for 3% -> 1% of each run, Pallas kernels for 20% -> 23%
where the time goes in v12:
time: 63.6 us; the launch traced here: 63.4 us
  starting transfers between devices  24.9 us (39%)
  Pallas kernels  18.3 us (29%)
  blocking collectives  10.4 us (16%)
  waiting for transfers between devices  8.6 us (14%)
  other arithmetic  0.92 us (1%)
    pallas_call x5, Pallas kernels, call(): pl.pallas_call(kernel, out_shape=out_shape, compiler_params=pltpu.Compile...  12.7 us
    ppermute x6, starting transfers between devices, along(): return lax.ppermute(value, 'blk', [(i, i ^ 1) for i in range(4)])  12.1 us
    all_to_all x1, blocking collectives, on_device(): parts = lax.all_to_all(parts, ('blk', 'eig', 'rep'), 0, 0, tiled=True)  10.4 us
    ppermute x3, starting transfers between devices, by_distance(): lax.ppermute(value, axis, [(i, i ^ k) for i in range(size)])  5.43 us
    ppermute x3, waiting for transfers between devices, by_distance(): lax.ppermute(value, axis, [(i, i ^ k) for i in range(size)])  4.35 us
    pallas_call x1, Pallas kernels, small_parts(): pl.pallas_call(parts_kernel, in_specs=[pl.BlockSpec(memory_space=pl.ANY)]...  4.34 us
    ppermute x4, starting transfers between devices, across(): lax.ppermute(value, AXES, pairing(lambda g, b, e, r: (g, 3 - b, e, r) if...  3.04 us
    ppermute x2, starting transfers between devices, swapped(): return lax.ppermute(value, 'groups', pair)  2.17 us
  transfers between devices with their start and end apart: 18, of which 5 were waited for; matrix products, arithmetic and copies ran while one was open for 1% of the time, Pallas kernels for 23%

profile of v12, /device:TPU:0, one launch (start us, length us, event | category | flops | bytes accessed | tf_op | source)
XLA Modules:
  0.0 63.4 jit_solution(8209207811983065878)
XLA Ops:
  0.0 1.3 %shard_map.91 = (bf16[64,1792]{1,0:T(8,128)(2,1)S(1)}, bf16[64,1792]{1,0:T(8,128)(2,1)S(1)}, bf16[64,1792]{1,0:T(8,128)(2,1)S(1)}, bf16[64,1792]{1,0:T(8,128)(2,1)S(1)}) custom-call(bf16[64,7168]{1,0:T(8,128)(2,1)} %refs_2_), custom_call_target="tpu_custom_call" | custom-call | tf_op jit(solution)/shard_map/pallas_call | solution.py:86
  1.3 3.1 %collective-permute-start.1 = (bf16[64,1792]{1,0:T(8,128)(2,1)S(1)}, bf16[64,1792]{1,0:T(8,128)(2,1)S(1)}, u32[]{:S(2)}, u32[]{:S(2)}) collective-permute-start(bf16[64,1792]{1,0:T(8,128)(2,1)S(1)} %get-tuple-element.32.refs_0_), channel_id=1, source_target_pairs={{0,4},{4,0},{8,12},{12,8},{1,5},{5,1},{9,13},{13,9},{2,6},{6,2},{1... | collective-permute-start | bytes 688136 | tf_op jit(solution)/shard_map/ppermute | solution.py:331
  4.4 3.1 %collective-permute-start.2 = (bf16[64,1792]{1,0:T(8,128)(2,1)S(1)}, bf16[64,1792]{1,0:T(8,128)(2,1)S(1)}, u32[]{:S(2)}, u32[]{:S(2)}) collective-permute-start(bf16[64,1792]{1,0:T(8,128)(2,1)S(1)} %get-tuple-element.33.refs_1_), channel_id=1, source_target_pairs={{0,4},{4,0},{8,12},{12,8},{1,5},{5,1},{9,13},{13,9},{2,6},{6,2},{1... | collective-permute-start | bytes 688136 | tf_op jit(solution)/shard_map/ppermute | solution.py:331
  7.6 4.3 %shard_map.92 = (f32[576,128]{1,0:T(8,128)S(1)}, f32[576,128]{1,0:T(8,128)S(1)}) custom-call(bf16[128,2048]{1,0:T(8,128)(2,1)} %refs_0_.1, bf16[2048,128]{1,0:T(8,128)(2,1)} %refs_1_.1, bf16[64,7168]{1,0:T(8,128)(2,1)} %refs_2_, bf16[7168,128]{1,0:T(8,128)(2,1)} %refs_3_.1, bf16[768,2048]{1,0:T(8,128)(2,1)} %refs_4_.1), custom_call_target="tpu_custom_call" | custom-call | tf_op jit(solution)/shard_map/pallas_call | solution.py:154
  11.9 0.6 collective-permute-start
  12.5 1.6 %collective-permute-start.6 = (bf16[64,1792]{1,0:T(8,128)(2,1)S(1)}, bf16[64,1792]{1,0:T(8,128)(2,1)S(1)}, u32[]{:S(2)}, u32[]{:S(2)}) collective-permute-start(bf16[64,1792]{1,0:T(8,128)(2,1)S(1)} %broadcast_select_fusion.5), channel_id=1, source_target_pairs={{0,4},{4,0},{8,12},{12,8},{1,5},{5,1},{9,13},{13,9},{2,6},{6,2},{1... | collective-permute-start | bytes 688136 | tf_op jit(solution)/shard_map/ppermute | solution.py:331
  14.1 1.5 %collective-permute-start.5 = (bf16[64,1792]{1,0:T(8,128)(2,1)S(1)}, bf16[64,1792]{1,0:T(8,128)(2,1)S(1)}, u32[]{:S(2)}, u32[]{:S(2)}) collective-permute-start(bf16[64,1792]{1,0:T(8,128)(2,1)S(1)} %collective-permute-done.1.refs_4_), channel_id=1, source_target_pairs={{0,16},{1,17},{2,18},{3,19},{4,8},{5,9},{6,10},{7,11},{8,4},{9,5},... | collective-permute-start | bytes 688136 | tf_op jit(solution)/shard_map/ppermute | solution.py:337
  15.7 3.0 %collective-permute-start.7 = (bf16[64,1792]{1,0:T(8,128)(2,1)S(1)}, bf16[64,1792]{1,0:T(8,128)(2,1)S(1)}, u32[]{:S(2)}, u32[]{:S(2)}) collective-permute-start(bf16[64,1792]{1,0:T(8,128)(2,1)S(1)} %broadcast_select_fusion.4), channel_id=1, source_target_pairs={{0,4},{4,0},{8,12},{12,8},{1,5},{5,1},{9,13},{13,9},{2,6},{6,2},{1... | collective-permute-start | bytes 688136 | tf_op jit(solution)/shard_map/ppermute | solution.py:331
  18.7 1.5 %collective-permute-start.8 = (bf16[64,1792]{1,0:T(8,128)(2,1)S(1)}, bf16[64,1792]{1,0:T(8,128)(2,1)S(1)}, u32[]{:S(2)}, u32[]{:S(2)}) collective-permute-start(bf16[64,1792]{1,0:T(8,128)(2,1)S(1)} %collective-permute-done.2.refs_5_), channel_id=1, source_target_pairs={{0,16},{1,17},{2,18},{3,19},{4,8},{5,9},{6,10},{7,11},{8,4},{9,5},... | collective-permute-start | bytes 688136 | tf_op jit(solution)/shard_map/ppermute | solution.py:337
  20.2 0.1 select_reduce_fusion
  20.3 0.0 copy-start
  20.3 1.6 %collective-permute-start.10 = (f32[576,128]{1,0:T(8,128)S(1)}, f32[576,128]{1,0:T(8,128)S(1)}, u32[]{:S(2)}, u32[]{:S(2)}) collective-permute-start(f32[576,128]{1,0:T(8,128)S(1)} %add.6), channel_id=1, source_target_pairs={{0,2},{2,0},{1,3},{3,1},{4,6},{6,4},{5,7},{7,5},{8,10},{10,8},{9,1... | collective-permute-start | bytes 884744 | tf_op jit(solution)/shard_map/ppermute | solution.py:357
  21.9 4.2 %shard_map.93.acts_ref = bf16[768,7168]{1,0:T(8,128)(2,1)S(1)} custom-call(bf16[768,7168]{1,0:T(8,128)(2,1)} %source_ref), custom_call_target="tpu_custom_call" | custom-call | flops 1 | bytes 1 | tf_op jit(solution)/shard_map/pallas_call | solution.py:284
  26.3 0.8 %collective-permute-done.10 = f32[576,128]{1,0:T(8,128)S(1)} collective-permute-done((f32[576,128]{1,0:T(8,128)S(1)}, f32[576,128]{1,0:T(8,128)S(1)}, u32[]{:S(2)}, u32[]{:S(2)}) %collective-permute-start.10) | collective-permute-done | bytes 294944 | tf_op jit(solution)/shard_map/ppermute | solution.py:357
  27.2 1.1 %collective-permute-start.11 = (bf16[64,256]{1,0:T(8,128)(2,1)S(1)}, bf16[64,256]{1,0:T(8,128)(2,1)S(1)}, u32[]{:S(2)}, u32[]{:S(2)}) collective-permute-start(bf16[64,256]{1,0:T(8,128)(2,1)S(1)} %pad_maximum_fusion.2.refs_0_), channel_id=1, source_target_pairs={{0,4},{4,0},{8,12},{12,8},{1,5},{5,1},{9,13},{13,9},{2,6},{6,2},{1... | collective-permute-start | bytes 98312 | tf_op jit(solution)/shard_map/ppermute | solution.py:46
  28.3 1.0 %collective-permute-start.15 = (bf16[64,3584]{1,0:T(8,128)(2,1)S(1)}, bf16[64,3584]{1,0:T(8,128)(2,1)S(1)}, u32[]{:S(2)}, u32[]{:S(2)}) collective-permute-start(bf16[64,3584]{1,0:T(8,128)(2,1)S(1)} %pad_maximum_fusion.mine_2_ref), channel_id=1, source_target_pairs={{0,4},{4,0},{8,12},{12,8},{1,5},{5,1},{9,13},{13,9},{2,6},{6,2},{1... | collective-permute-start | bytes 1376264 | tf_op jit(solution)/shard_map/ppermute | solution.py:331
  29.3 0.6 collective-permute-start.9
  29.9 2.8 %collective-permute-start.12 = (bf16[64,256]{1,0:T(8,128)(2,1)S(1)}, bf16[64,256]{1,0:T(8,128)(2,1)S(1)}, u32[]{:S(2)}, u32[]{:S(2)}) collective-permute-start(bf16[64,256]{1,0:T(8,128)(2,1)S(1)} %pad_maximum_fusion.2.refs_0_), channel_id=1, source_target_pairs={{0,8},{4,12},{8,0},{12,4},{1,9},{5,13},{9,1},{13,5},{2,10},{6,14},... | collective-permute-start | bytes 98312 | tf_op jit(solution)/shard_map/ppermute | solution.py:46
  32.7 1.5 %collective-permute-start.13 = (bf16[64,256]{1,0:T(8,128)(2,1)S(1)}, bf16[64,256]{1,0:T(8,128)(2,1)S(1)}, u32[]{:S(2)}, u32[]{:S(2)}) collective-permute-start(bf16[64,256]{1,0:T(8,128)(2,1)S(1)} %pad_maximum_fusion.2.refs_0_), channel_id=1, source_target_pairs={{0,12},{4,8},{8,4},{12,0},{1,13},{5,9},{9,5},{13,1},{2,14},{6,10},... | collective-permute-start | bytes 98312 | tf_op jit(solution)/shard_map/ppermute | solution.py:46
  34.3 3.0 %shard_map.94.first_ref = f32[768,128]{1,0:T(8,128)S(1)} custom-call(bf16[768,7168]{1,0:T(8,128)(2,1)S(1)} %shard_map.93.acts_ref, bf16[64,1792]{1,0:T(8,128)(2,1)S(1)} %get-tuple-element.32.refs_0_, bf16[64,1792]{1,0:T(8,128)(2,1)S(1)} %get-tuple-element.33.refs_1_, bf16[64,1792]{1,0:T(8,128)(2,1)S(1)} %get-tuple-element.42.refs_2_, ...), custom_call_target="tpu_custom_call" | custom-call | flops 1 | bytes 1 | tf_op jit(solution)/shard_map/pallas_call | solution.py:284
  37.3 1.6 %collective-permute-done.12.refs_2_ = bf16[64,256]{1,0:T(8,128)(2,1)S(1)} collective-permute-done((bf16[64,256]{1,0:T(8,128)(2,1)S(1)}, bf16[64,256]{1,0:T(8,128)(2,1)S(1)}, u32[]{:S(2)}, u32[]{:S(2)}) %collective-permute-start.12) | collective-permute-done | bytes 32800 | tf_op jit(solution)/shard_map/ppermute | solution.py:46
  38.9 2.7 %collective-permute-done.13.refs_3_ = bf16[64,256]{1,0:T(8,128)(2,1)S(1)} collective-permute-done((bf16[64,256]{1,0:T(8,128)(2,1)S(1)}, bf16[64,256]{1,0:T(8,128)(2,1)S(1)}, u32[]{:S(2)}, u32[]{:S(2)}) %collective-permute-start.13) | collective-permute-done | bytes 32800 | tf_op jit(solution)/shard_map/ppermute | solution.py:46
  41.7 0.5 shard_map.95.weights_ref
  42.1 0.0 collective-permute-done.15.mine_3_ref
  42.2 1.6 %collective-permute-start.16 = (bf16[64,1792]{1,0:T(8,128)(2,1)S(1)}, bf16[64,1792]{1,0:T(8,128)(2,1)S(1)}, u32[]{:S(2)}, u32[]{:S(2)}) collective-permute-start(bf16[64,1792]{1,0:T(8,128)(2,1)S(1)} %slice.17), channel_id=1, source_target_pairs={{0,16},{16,0},{1,17},{17,1},{2,18},{18,2},{3,19},{19,3},{4,20},{20... | collective-permute-start | bytes 688136 | tf_op jit(solution)/shard_map/ppermute | solution.py:334
  43.8 0.3 collective-permute-start.14
  44.1 2.4 %shard_map.96 = (f32[768,128]{1,0:T(8,128)S(1)}, f32[768,512]{1,0:T(8,128)S(1)}, f32[8,512]{1,0:T(8,128)S(1)}) custom-call(bf16[768,7168]{1,0:T(8,128)(2,1)S(1)} %shard_map.93.acts_ref, bf16[64,3584]{1,0:T(8,128)(2,1)S(1)} %pad_maximum_fusion.mine_2_ref, bf16[64,3584]{1,0:T(8,128)(2,1)S(1)} %collective-permute-done.15.mine_3_ref, ...), custom_call_target="tpu_custom_call" | custom-call | flops 1 | bytes 1 | tf_op jit(solution)/shard_map/pallas_call | solution.py:284
  46.5 1.8 %collective-permute-done.16.right_ref = bf16[64,1792]{1,0:T(8,128)(2,1)S(1)} collective-permute-done((bf16[64,1792]{1,0:T(8,128)(2,1)S(1)}, bf16[64,1792]{1,0:T(8,128)(2,1)S(1)}, u32[]{:S(2)}, u32[]{:S(2)}) %collective-permute-start.16) | collective-permute-done | bytes 229408 | tf_op jit(solution)/shard_map/ppermute | solution.py:334
  48.3 1.6 %collective-permute-done.14.left_ref = bf16[64,1792]{1,0:T(8,128)(2,1)S(1)} collective-permute-done((bf16[64,1792]{1,0:T(8,128)(2,1)S(1)}, bf16[64,1792]{1,0:T(8,128)(2,1)S(1)}, u32[]{:S(2)}, u32[]{:S(2)}) %collective-permute-start.14) | collective-permute-done | bytes 229408 | tf_op jit(solution)/shard_map/ppermute | solution.py:331
  49.9 2.6 %shard_map.97 = f32[16,2]{1,0:T(8,128)S(1)} custom-call(bf16[768,7168]{1,0:T(8,128)(2,1)S(1)} %shard_map.93.acts_ref, bf16[64,3584]{1,0:T(8,128)(2,1)S(1)} %collective-permute-done.9.theirs_2_ref, bf16[64,1792]{1,0:T(8,128)(2,1)S(1)} %collective-permute-done.14.left_ref, bf16[64,1792]{1,0:T(8,128)(2,1)S(1)} %collective-permute-done.16.right_ref, ...), custom_call_target="tpu_custom_call" | custom-call | flops 1 | bytes 1 | tf_op jit(solution)/shard_map/pallas_call | solution.py:284
  52.5 10.4 %all_to_all.9 = f32[16,1,2]{2,1,0:T(1,128)S(1)} all-to-all(f32[16,1,2]{2,1,0:T(1,128)S(1)} %bitcast.4), channel_id=1, replica_groups=mesh['groups'=2,'blk'=4,'eig'=2,'rep'=2] {'blk','eig','rep'}, dimensions={0} | all-to-all | bytes 256 | tf_op jit(solution)/shard_map/all_to_all | solution.py:459
  62.9 0.5 reduce_sum.21
  (37 shorter events, 0.4 us)
Async XLA Ops:
  1.3 11.2 %collective-permute-start.1 = (bf16[64,1792]{1,0:T(8,128)(2,1)S(1)}, bf16[64,1792]{1,0:T(8,128)(2,1)S(1)}, u32[]{:S(2)}, u32[]{:S(2)}) collective-permute-start(bf16[64,1792]{1,0:T(8,128)(2,1)S(1)} %get-tuple-element.32.refs_0_), channel_id=1, source_target_pairs={{0,4},{4,0},{8,12},{12,8},{1,5},{5,1},{9,13},{13,9},{2,6},{6,2},{1... | collective-permute-start | bytes 688136 | tf_op jit(solution)/shard_map/ppermute | solution.py:331
  4.4 8.1 %collective-permute-start.3 = (bf16[64,1792]{1,0:T(8,128)(2,1)S(1)}, bf16[64,1792]{1,0:T(8,128)(2,1)S(1)}, u32[]{:S(2)}, u32[]{:S(2)}) collective-permute-start(bf16[64,1792]{1,0:T(8,128)(2,1)S(1)} %get-tuple-element.32.refs_0_), channel_id=1, source_target_pairs={{0,1},{1,0},{2,3},{3,2},{4,8},{5,9},{6,10},{7,11},{8,4},{9,5},{10,... | collective-permute-start | bytes 688136 | tf_op jit(solution)/shard_map/ppermute | solution.py:337
  4.4 11.2 %collective-permute-start.2 = (bf16[64,1792]{1,0:T(8,128)(2,1)S(1)}, bf16[64,1792]{1,0:T(8,128)(2,1)S(1)}, u32[]{:S(2)}, u32[]{:S(2)}) collective-permute-start(bf16[64,1792]{1,0:T(8,128)(2,1)S(1)} %get-tuple-element.33.refs_1_), channel_id=1, source_target_pairs={{0,4},{4,0},{8,12},{12,8},{1,5},{5,1},{9,13},{13,9},{2,6},{6,2},{1... | collective-permute-start | bytes 688136 | tf_op jit(solution)/shard_map/ppermute | solution.py:331
  7.6 8.1 %collective-permute-start.4 = (bf16[64,1792]{1,0:T(8,128)(2,1)S(1)}, bf16[64,1792]{1,0:T(8,128)(2,1)S(1)}, u32[]{:S(2)}, u32[]{:S(2)}) collective-permute-start(bf16[64,1792]{1,0:T(8,128)(2,1)S(1)} %get-tuple-element.33.refs_1_), channel_id=1, source_target_pairs={{0,1},{1,0},{2,3},{3,2},{4,8},{5,9},{6,10},{7,11},{8,4},{9,5},{10,... | collective-permute-start | bytes 688136 | tf_op jit(solution)/shard_map/ppermute | solution.py:337
  7.6 12.7 %copy-start.1 = (s32[768]{0:T(1024)S(1)}, s32[768]{0:T(1024)}, u32[]{:S(2)}) copy-start(s32[768]{0:T(1024)} %param.16) | copy-start | bytes 9220
  7.6 12.7 %copy-start.2 = (s32[8]{0:T(128)S(1)}, s32[8]{0:T(128)}, u32[]{:S(2)}) copy-start(s32[8]{0:T(128)} %param.17) | copy-start | bytes 100
  11.9 3.7 %collective-permute-start = (f32[576,128]{1,0:T(8,128)S(1)}, f32[576,128]{1,0:T(8,128)S(1)}, u32[]{:S(2)}, u32[]{:S(2)}) collective-permute-start(f32[576,128]{1,0:T(8,128)S(1)} %get-tuple-element.36), channel_id=1, source_target_pairs={{0,1},{1,0},{2,3},{3,2},{4,5},{5,4},{6,7},{7,6},{8,9},{9,8},{10,11... | collective-permute-start | bytes 884744 | tf_op jit(solution)/shard_map/ppermute | solution.py:355
  12.5 13.6 %collective-permute-start.6 = (bf16[64,1792]{1,0:T(8,128)(2,1)S(1)}, bf16[64,1792]{1,0:T(8,128)(2,1)S(1)}, u32[]{:S(2)}, u32[]{:S(2)}) collective-permute-start(bf16[64,1792]{1,0:T(8,128)(2,1)S(1)} %broadcast_select_fusion.5), channel_id=1, source_target_pairs={{0,4},{4,0},{8,12},{12,8},{1,5},{5,1},{9,13},{13,9},{2,6},{6,2},{1... | collective-permute-start | bytes 688136 | tf_op jit(solution)/shard_map/ppermute | solution.py:331
  14.1 12.0 %collective-permute-start.5 = (bf16[64,1792]{1,0:T(8,128)(2,1)S(1)}, bf16[64,1792]{1,0:T(8,128)(2,1)S(1)}, u32[]{:S(2)}, u32[]{:S(2)}) collective-permute-start(bf16[64,1792]{1,0:T(8,128)(2,1)S(1)} %collective-permute-done.1.refs_4_), channel_id=1, source_target_pairs={{0,16},{1,17},{2,18},{3,19},{4,8},{5,9},{6,10},{7,11},{8,4},{9,5},... | collective-permute-start | bytes 688136 | tf_op jit(solution)/shard_map/ppermute | solution.py:337
  15.7 10.4 %collective-permute-start.7 = (bf16[64,1792]{1,0:T(8,128)(2,1)S(1)}, bf16[64,1792]{1,0:T(8,128)(2,1)S(1)}, u32[]{:S(2)}, u32[]{:S(2)}) collective-permute-start(bf16[64,1792]{1,0:T(8,128)(2,1)S(1)} %broadcast_select_fusion.4), channel_id=1, source_target_pairs={{0,4},{4,0},{8,12},{12,8},{1,5},{5,1},{9,13},{13,9},{2,6},{6,2},{1... | collective-permute-start | bytes 688136 | tf_op jit(solution)/shard_map/ppermute | solution.py:331
  18.7 7.5 %collective-permute-start.8 = (bf16[64,1792]{1,0:T(8,128)(2,1)S(1)}, bf16[64,1792]{1,0:T(8,128)(2,1)S(1)}, u32[]{:S(2)}, u32[]{:S(2)}) collective-permute-start(bf16[64,1792]{1,0:T(8,128)(2,1)S(1)} %collective-permute-done.2.refs_5_), channel_id=1, source_target_pairs={{0,16},{1,17},{2,18},{3,19},{4,8},{5,9},{6,10},{7,11},{8,4},{9,5},... | collective-permute-start | bytes 688136 | tf_op jit(solution)/shard_map/ppermute | solution.py:337
  20.3 6.8 %copy-start = (bf16[64,128]{1,0:T(8,128)(2,1)S(1)}, bf16[64,128]{1,0:T(8,128)(2,1)}, u32[]{:S(2)}) copy-start(bf16[64,128]{1,0:T(8,128)(2,1)} %param.13) | copy-start | bytes 49156
  20.3 6.8 %collective-permute-start.10 = (f32[576,128]{1,0:T(8,128)S(1)}, f32[576,128]{1,0:T(8,128)S(1)}, u32[]{:S(2)}, u32[]{:S(2)}) collective-permute-start(f32[576,128]{1,0:T(8,128)S(1)} %add.6), channel_id=1, source_target_pairs={{0,2},{2,0},{1,3},{3,1},{4,6},{6,4},{5,7},{7,5},{8,10},{10,8},{9,1... | collective-permute-start | bytes 884744 | tf_op jit(solution)/shard_map/ppermute | solution.py:357
  27.2 7.1 %collective-permute-start.11 = (bf16[64,256]{1,0:T(8,128)(2,1)S(1)}, bf16[64,256]{1,0:T(8,128)(2,1)S(1)}, u32[]{:S(2)}, u32[]{:S(2)}) collective-permute-start(bf16[64,256]{1,0:T(8,128)(2,1)S(1)} %pad_maximum_fusion.2.refs_0_), channel_id=1, source_target_pairs={{0,4},{4,0},{8,12},{12,8},{1,5},{5,1},{9,13},{13,9},{2,6},{6,2},{1... | collective-permute-start | bytes 98312 | tf_op jit(solution)/shard_map/ppermute | solution.py:46
  28.3 13.9 %collective-permute-start.15 = (bf16[64,3584]{1,0:T(8,128)(2,1)S(1)}, bf16[64,3584]{1,0:T(8,128)(2,1)S(1)}, u32[]{:S(2)}, u32[]{:S(2)}) collective-permute-start(bf16[64,3584]{1,0:T(8,128)(2,1)S(1)} %pad_maximum_fusion.mine_2_ref), channel_id=1, source_target_pairs={{0,4},{4,0},{8,12},{12,8},{1,5},{5,1},{9,13},{13,9},{2,6},{6,2},{1... | collective-permute-start | bytes 1376264 | tf_op jit(solution)/shard_map/ppermute | solution.py:331
  29.3 14.5 %collective-permute-start.9 = (bf16[64,3584]{1,0:T(8,128)(2,1)S(1)}, bf16[64,3584]{1,0:T(8,128)(2,1)S(1)}, u32[]{:S(2)}, u32[]{:S(2)}) collective-permute-start(bf16[64,3584]{1,0:T(8,128)(2,1)S(1)} %pad_maximum_fusion.mine_2_ref), channel_id=1, source_target_pairs={{0,16},{16,0},{1,17},{17,1},{2,18},{18,2},{3,19},{19,3},{4,20},{20... | collective-permute-start | bytes 1376264 | tf_op jit(solution)/shard_map/ppermute | solution.py:334
  29.9 9.1 %collective-permute-start.12 = (bf16[64,256]{1,0:T(8,128)(2,1)S(1)}, bf16[64,256]{1,0:T(8,128)(2,1)S(1)}, u32[]{:S(2)}, u32[]{:S(2)}) collective-permute-start(bf16[64,256]{1,0:T(8,128)(2,1)S(1)} %pad_maximum_fusion.2.refs_0_), channel_id=1, source_target_pairs={{0,8},{4,12},{8,0},{12,4},{1,9},{5,13},{9,1},{13,5},{2,10},{6,14},... | collective-permute-start | bytes 98312 | tf_op jit(solution)/shard_map/ppermute | solution.py:46
  32.7 9.0 %collective-permute-start.13 = (bf16[64,256]{1,0:T(8,128)(2,1)S(1)}, bf16[64,256]{1,0:T(8,128)(2,1)S(1)}, u32[]{:S(2)}, u32[]{:S(2)}) collective-permute-start(bf16[64,256]{1,0:T(8,128)(2,1)S(1)} %pad_maximum_fusion.2.refs_0_), channel_id=1, source_target_pairs={{0,12},{4,8},{8,4},{12,0},{1,13},{5,9},{9,5},{13,1},{2,14},{6,10},... | collective-permute-start | bytes 98312 | tf_op jit(solution)/shard_map/ppermute | solution.py:46
  34.2 9.8 %collective-permute-start.17 = (bf16[384,128]{1,0:T(8,128)(2,1)S(1)}, bf16[384,128]{1,0:T(8,128)(2,1)S(1)}, u32[]{:S(2)}, u32[]{:S(2)}) collective-permute-start(bf16[384,128]{1,0:T(8,128)(2,1)S(1)} %slice.22), channel_id=1, source_target_pairs={{0,1},{1,0},{2,3},{3,2},{4,5},{5,4},{6,7},{7,6},{8,9},{9,8},{10,11... | collective-permute-start | bytes 294920 | tf_op jit(solution)/shard_map/ppermute | solution.py:386
  42.2 6.1 %collective-permute-start.16 = (bf16[64,1792]{1,0:T(8,128)(2,1)S(1)}, bf16[64,1792]{1,0:T(8,128)(2,1)S(1)}, u32[]{:S(2)}, u32[]{:S(2)}) collective-permute-start(bf16[64,1792]{1,0:T(8,128)(2,1)S(1)} %slice.17), channel_id=1, source_target_pairs={{0,16},{16,0},{1,17},{17,1},{2,18},{18,2},{3,19},{19,3},{4,20},{20... | collective-permute-start | bytes 688136 | tf_op jit(solution)/shard_map/ppermute | solution.py:334
  43.8 6.1 %collective-permute-start.14 = (bf16[64,1792]{1,0:T(8,128)(2,1)S(1)}, bf16[64,1792]{1,0:T(8,128)(2,1)S(1)}, u32[]{:S(2)}, u32[]{:S(2)}) collective-permute-start(bf16[64,1792]{1,0:T(8,128)(2,1)S(1)} %slice.16), channel_id=1, source_target_pairs={{0,4},{4,0},{8,12},{12,8},{1,5},{5,1},{9,13},{13,9},{2,6},{6,2},{1... | collective-permute-start | bytes 688136 | tf_op jit(solution)/shard_map/ppermute | solution.py:331

commit v13 on v10

--- a/solution.py
+++ b/solution.py
@@ -10,7 +10,7 @@
 
 R = 32
 LANES = 128
-BLOCK = 256
+BLOCK = 384
 VMEM_LIMIT = 16 * 1024 * 1024
 AXES = ("groups", "blk", "eig", "rep")
 

time: 61.5 us -> 62.3 us (1.013)
  transfers between devices with their start and end apart: 18 -> 18, of which waited for: 5 -> 6; matrix products, arithmetic and copies ran while one was open for 1% -> 1% of each run, Pallas kernels for 24% -> 23%
where the time goes in v13:
time: 62.3 us; the launch traced here: 62.1 us
  starting transfers between devices  24.2 us (39%)
  Pallas kernels  18.9 us (30%)
  blocking collectives  9.25 us (15%)
  waiting for transfers between devices  8.54 us (14%)
  other arithmetic  0.95 us (2%)
    pallas_call x4, Pallas kernels, call(): pl.pallas_call(kernel, out_shape=out_shape, compiler_params=pltpu.Compile...  13.3 us
    ppermute x6, starting transfers between devices, along(): return lax.ppermute(value, 'blk', [(i, i ^ 1) for i in range(4)])  11.4 us
    all_to_all x1, blocking collectives, on_device(): parts = lax.all_to_all(parts, ('blk', 'eig', 'rep'), 0, 0, tiled=True)  9.25 us
    ppermute x6, waiting for transfers between devices, along(): return lax.ppermute(value, 'blk', [(i, i ^ 1) for i in range(4)])  4.81 us
    ppermute x3, starting transfers between devices, by_distance(): lax.ppermute(value, axis, [(i, i ^ k) for i in range(size)])  4.45 us
    pallas_call x1, Pallas kernels, small_parts(): pl.pallas_call(parts_kernel, in_specs=[pl.BlockSpec(memory_space=pl.ANY)]...  4.31 us
    ppermute x2, starting transfers between devices, swapped(): return lax.ppermute(value, 'groups', pair)  3.1 us
    ppermute x4, starting transfers between devices, across(): lax.ppermute(value, AXES, pairing(lambda g, b, e, r: (g, 3 - b, e, r) if...  3.05 us
  transfers between devices with their start and end apart: 18, of which 6 were waited for; matrix products, arithmetic and copies ran while one was open for 1% of the time, Pallas kernels for 23%

profile of v13, /device:TPU:0, one launch (start us, length us, event | category | flops | bytes accessed | tf_op | source)
XLA Modules:
  0.0 62.1 jit_solution(2175859289394031682)
XLA Ops:
  0.0 1.3 %shard_map.91 = (bf16[64,1792]{1,0:T(8,128)(2,1)S(1)}, bf16[64,1792]{1,0:T(8,128)(2,1)S(1)}, bf16[64,1792]{1,0:T(8,128)(2,1)S(1)}, bf16[64,1792]{1,0:T(8,128)(2,1)S(1)}) custom-call(bf16[64,7168]{1,0:T(8,128)(2,1)} %refs_2_), custom_call_target="tpu_custom_call" | custom-call | tf_op jit(solution)/shard_map/pallas_call | solution.py:86
  1.3 3.1 %collective-permute-start.1 = (bf16[64,1792]{1,0:T(8,128)(2,1)S(1)}, bf16[64,1792]{1,0:T(8,128)(2,1)S(1)}, u32[]{:S(2)}, u32[]{:S(2)}) collective-permute-start(bf16[64,1792]{1,0:T(8,128)(2,1)S(1)} %get-tuple-element.32.refs_0_), channel_id=1, source_target_pairs={{0,4},{4,0},{8,12},{12,8},{1,5},{5,1},{9,13},{13,9},{2,6},{6,2},{1... | collective-permute-start | bytes 688136 | tf_op jit(solution)/shard_map/ppermute | solution.py:343
  4.4 0.0 collective-permute-start.2
  4.4 3.1 %collective-permute-start.6 = (bf16[64,1792]{1,0:T(8,128)(2,1)S(1)}, bf16[64,1792]{1,0:T(8,128)(2,1)S(1)}, u32[]{:S(2)}, u32[]{:S(2)}) collective-permute-start(bf16[64,1792]{1,0:T(8,128)(2,1)S(1)} %get-tuple-element.33.refs_1_), channel_id=1, source_target_pairs={{0,4},{4,0},{8,12},{12,8},{1,5},{5,1},{9,13},{13,9},{2,6},{6,2},{1... | collective-permute-start | bytes 688136 | tf_op jit(solution)/shard_map/ppermute | solution.py:343
  7.6 4.3 %shard_map.92 = (f32[576,128]{1,0:T(8,128)S(1)}, f32[576,128]{1,0:T(8,128)S(1)}) custom-call(bf16[128,2048]{1,0:T(8,128)(2,1)} %refs_0_.1, bf16[2048,128]{1,0:T(8,128)(2,1)} %refs_1_.1, bf16[64,7168]{1,0:T(8,128)(2,1)} %refs_2_, bf16[7168,128]{1,0:T(8,128)(2,1)} %refs_3_.1, bf16[768,2048]{1,0:T(8,128)(2,1)} %refs_4_.1), custom_call_target="tpu_custom_call" | custom-call | tf_op jit(solution)/shard_map/pallas_call | solution.py:154
  11.9 0.6 collective-permute-start
  12.5 0.1 select_reduce_fusion
  12.6 1.1 %collective-permute-done = f32[576,128]{1,0:T(8,128)S(1)} collective-permute-done((f32[576,128]{1,0:T(8,128)S(1)}, f32[576,128]{1,0:T(8,128)S(1)}, u32[]{:S(2)}, u32[]{:S(2)}) %collective-permute-start) | collective-permute-done | bytes 294944 | tf_op jit(solution)/shard_map/ppermute | solution.py:366
  13.7 1.6 %collective-permute-start.3 = (f32[576,128]{1,0:T(8,128)S(1)}, f32[576,128]{1,0:T(8,128)S(1)}, u32[]{:S(2)}, u32[]{:S(2)}) collective-permute-start(f32[576,128]{1,0:T(8,128)S(1)} %add.6), channel_id=1, source_target_pairs={{0,2},{2,0},{1,3},{3,1},{4,6},{6,4},{5,7},{7,5},{8,10},{10,8},{9,1... | collective-permute-start | bytes 884744 | tf_op jit(solution)/shard_map/ppermute | solution.py:368
  15.3 0.4 collective-permute-start.4
  15.7 1.5 %collective-permute-start.5 = (bf16[64,1792]{1,0:T(8,128)(2,1)S(1)}, bf16[64,1792]{1,0:T(8,128)(2,1)S(1)}, u32[]{:S(2)}, u32[]{:S(2)}) collective-permute-start(bf16[64,1792]{1,0:T(8,128)(2,1)S(1)} %collective-permute-done.1.refs_4_), channel_id=1, source_target_pairs={{0,16},{1,17},{2,18},{3,19},{4,8},{5,9},{6,10},{7,11},{8,4},{9,5},... | collective-permute-start | bytes 688136 | tf_op jit(solution)/shard_map/ppermute | solution.py:349
  17.3 0.7 %collective-permute-start.8 = (bf16[64,1792]{1,0:T(8,128)(2,1)S(1)}, bf16[64,1792]{1,0:T(8,128)(2,1)S(1)}, u32[]{:S(2)}, u32[]{:S(2)}) collective-permute-start(bf16[64,1792]{1,0:T(8,128)(2,1)S(1)} %broadcast_select_fusion.4), channel_id=1, source_target_pairs={{0,4},{4,0},{8,12},{12,8},{1,5},{5,1},{9,13},{13,9},{2,6},{6,2},{1... | collective-permute-start | bytes 688136 | tf_op jit(solution)/shard_map/ppermute | solution.py:343
  18.0 1.5 %collective-permute-start.9 = (bf16[64,1792]{1,0:T(8,128)(2,1)S(1)}, bf16[64,1792]{1,0:T(8,128)(2,1)S(1)}, u32[]{:S(2)}, u32[]{:S(2)}) collective-permute-start(bf16[64,1792]{1,0:T(8,128)(2,1)S(1)} %collective-permute-done.6.refs_5_), channel_id=1, source_target_pairs={{0,16},{1,17},{2,18},{3,19},{4,8},{5,9},{6,10},{7,11},{8,4},{9,5},... | collective-permute-start | bytes 688136 | tf_op jit(solution)/shard_map/ppermute | solution.py:349
  19.5 4.4 %collective-permute-done.4 = bf16[64,1792]{1,0:T(8,128)(2,1)S(1)} collective-permute-done((bf16[64,1792]{1,0:T(8,128)(2,1)S(1)}, bf16[64,1792]{1,0:T(8,128)(2,1)S(1)}, u32[]{:S(2)}, u32[]{:S(2)}) %collective-permute-start.4) | collective-permute-done | bytes 229408 | tf_op jit(solution)/shard_map/ppermute | solution.py:343
  23.8 0.4 collective-permute-done.5
  24.3 1.7 %collective-permute-start.11 = (bf16[64,256]{1,0:T(8,128)(2,1)S(1)}, bf16[64,256]{1,0:T(8,128)(2,1)S(1)}, u32[]{:S(2)}, u32[]{:S(2)}) collective-permute-start(bf16[64,256]{1,0:T(8,128)(2,1)S(1)} %pad_maximum_fusion.2.refs_0_), channel_id=1, source_target_pairs={{0,4},{4,0},{8,12},{12,8},{1,5},{5,1},{9,13},{13,9},{2,6},{6,2},{1... | collective-permute-start | bytes 98312 | tf_op jit(solution)/shard_map/ppermute | solution.py:46
  26.1 1.9 %collective-permute-start.12 = (bf16[64,256]{1,0:T(8,128)(2,1)S(1)}, bf16[64,256]{1,0:T(8,128)(2,1)S(1)}, u32[]{:S(2)}, u32[]{:S(2)}) collective-permute-start(bf16[64,256]{1,0:T(8,128)(2,1)S(1)} %pad_maximum_fusion.2.refs_0_), channel_id=1, source_target_pairs={{0,8},{4,12},{8,0},{12,4},{1,9},{5,13},{9,1},{13,5},{2,10},{6,14},... | collective-permute-start | bytes 98312 | tf_op jit(solution)/shard_map/ppermute | solution.py:46
  27.9 0.8 %collective-permute-start.13 = (bf16[64,256]{1,0:T(8,128)(2,1)S(1)}, bf16[64,256]{1,0:T(8,128)(2,1)S(1)}, u32[]{:S(2)}, u32[]{:S(2)}) collective-permute-start(bf16[64,256]{1,0:T(8,128)(2,1)S(1)} %pad_maximum_fusion.2.refs_0_), channel_id=1, source_target_pairs={{0,12},{4,8},{8,4},{12,0},{1,13},{5,9},{9,5},{13,1},{2,14},{6,10},... | collective-permute-start | bytes 98312 | tf_op jit(solution)/shard_map/ppermute | solution.py:46
  28.9 2.4 %collective-permute-start.15 = (bf16[64,3584]{1,0:T(8,128)(2,1)S(1)}, bf16[64,3584]{1,0:T(8,128)(2,1)S(1)}, u32[]{:S(2)}, u32[]{:S(2)}) collective-permute-start(bf16[64,3584]{1,0:T(8,128)(2,1)S(1)} %pad_maximum_fusion.mine_2_ref), channel_id=1, source_target_pairs={{0,4},{4,0},{8,12},{12,8},{1,5},{5,1},{9,13},{13,9},{2,6},{6,2},{1... | collective-permute-start | bytes 1376264 | tf_op jit(solution)/shard_map/ppermute | solution.py:343
  31.4 1.5 %collective-permute-start.10 = (bf16[64,3584]{1,0:T(8,128)(2,1)S(1)}, bf16[64,3584]{1,0:T(8,128)(2,1)S(1)}, u32[]{:S(2)}, u32[]{:S(2)}) collective-permute-start(bf16[64,3584]{1,0:T(8,128)(2,1)S(1)} %pad_maximum_fusion.mine_2_ref), channel_id=1, source_target_pairs={{0,16},{16,0},{1,17},{17,1},{2,18},{18,2},{3,19},{19,3},{4,20},{20... | collective-permute-start | bytes 1376264 | tf_op jit(solution)/shard_map/ppermute | solution.py:346
  32.9 0.1 broadcast_select_fusion
  33.0 6.9 %shard_map.93 = (f32[768,128]{1,0:T(8,128)S(1)}, bf16[768,7168]{1,0:T(8,128)(2,1)S(1)}) custom-call(bf16[768,7168]{1,0:T(8,128)(2,1)} %source_ref, bf16[64,1792]{1,0:T(8,128)(2,1)S(1)} %get-tuple-element.32.refs_0_, bf16[64,1792]{1,0:T(8,128)(2,1)S(1)} %get-tuple-element.33.refs_1_, bf16[64,1792]{1,0:T(8,128)(2,1)S(1)} %get-tuple-element.39.refs_2_, ...), custom_call_target="tpu_custom_call" | custom-call | flops 1 | bytes 1 | tf_op jit(solution)/shard_map/pallas_call | solution.py:297
  39.9 0.5 shard_map.94.weights_ref
  40.3 0.1 collective-permute-done.15.mine_3_ref
  40.5 1.6 %collective-permute-start.16 = (bf16[64,1792]{1,0:T(8,128)(2,1)S(1)}, bf16[64,1792]{1,0:T(8,128)(2,1)S(1)}, u32[]{:S(2)}, u32[]{:S(2)}) collective-permute-start(bf16[64,1792]{1,0:T(8,128)(2,1)S(1)} %slice.18), channel_id=1, source_target_pairs={{0,16},{16,0},{1,17},{17,1},{2,18},{18,2},{3,19},{19,3},{4,20},{20... | collective-permute-start | bytes 688136 | tf_op jit(solution)/shard_map/ppermute | solution.py:346
  42.1 1.7 %collective-permute-start.14 = (bf16[64,1792]{1,0:T(8,128)(2,1)S(1)}, bf16[64,1792]{1,0:T(8,128)(2,1)S(1)}, u32[]{:S(2)}, u32[]{:S(2)}) collective-permute-start(bf16[64,1792]{1,0:T(8,128)(2,1)S(1)} %slice.17), channel_id=1, source_target_pairs={{0,4},{4,0},{8,12},{12,8},{1,5},{5,1},{9,13},{13,9},{2,6},{6,2},{1... | collective-permute-start | bytes 688136 | tf_op jit(solution)/shard_map/ppermute | solution.py:343
  43.8 2.4 %shard_map.95 = (f32[768,128]{1,0:T(8,128)S(1)}, f32[768,512]{1,0:T(8,128)S(1)}, f32[8,512]{1,0:T(8,128)S(1)}) custom-call(bf16[768,7168]{1,0:T(8,128)(2,1)S(1)} %get-tuple-element.52.acts_ref, bf16[64,3584]{1,0:T(8,128)(2,1)S(1)} %pad_maximum_fusion.mine_2_ref, bf16[64,3584]{1,0:T(8,128)(2,1)S(1)} %collective-permute-done.15.mine_3_ref, ...), custom_call_target="tpu_custom_call" | custom-call | flops 1 | bytes 1 | tf_op jit(solution)/shard_map/pallas_call | solution.py:297
  46.2 2.2 %collective-permute-done.16.right_ref = bf16[64,1792]{1,0:T(8,128)(2,1)S(1)} collective-permute-done((bf16[64,1792]{1,0:T(8,128)(2,1)S(1)}, bf16[64,1792]{1,0:T(8,128)(2,1)S(1)}, u32[]{:S(2)}, u32[]{:S(2)}) %collective-permute-start.16) | collective-permute-done | bytes 229408 | tf_op jit(solution)/shard_map/ppermute | solution.py:346
  48.4 0.3 collective-permute-done.14.left_ref
  48.7 3.5 %shard_map.96 = f32[16,2]{1,0:T(8,128)S(1)} custom-call(bf16[768,7168]{1,0:T(8,128)(2,1)S(1)} %get-tuple-element.52.acts_ref, bf16[64,3584]{1,0:T(8,128)(2,1)S(1)} %collective-permute-done.10.theirs_2_ref, bf16[64,1792]{1,0:T(8,128)(2,1)S(1)} %collective-permute-done.14.left_ref, bf16[64,1792]{1,0:T(8,128)(2,1)S(1)} %collective-permute-done.16.right_ref, ...), custom_call_target="tpu_custom_call" | custom-call | flops 1 | bytes 1 | tf_op jit(solution)/shard_map/pallas_call | solution.py:297
  52.3 9.3 %all_to_all.9 = f32[16,1,2]{2,1,0:T(1,128)S(1)} all-to-all(f32[16,1,2]{2,1,0:T(1,128)S(1)} %bitcast.4), channel_id=1, replica_groups=mesh['groups'=2,'blk'=4,'eig'=2,'rep'=2] {'blk','eig','rep'}, dimensions={0} | all-to-all | bytes 256 | tf_op jit(solution)/shard_map/all_to_all | solution.py:469
  61.5 0.5 reduce_sum.21
  (36 shorter events, 0.4 us)
Async XLA Ops:
  1.3 11.3 %collective-permute-start.1 = (bf16[64,1792]{1,0:T(8,128)(2,1)S(1)}, bf16[64,1792]{1,0:T(8,128)(2,1)S(1)}, u32[]{:S(2)}, u32[]{:S(2)}) collective-permute-start(bf16[64,1792]{1,0:T(8,128)(2,1)S(1)} %get-tuple-element.32.refs_0_), channel_id=1, source_target_pairs={{0,4},{4,0},{8,12},{12,8},{1,5},{5,1},{9,13},{13,9},{2,6},{6,2},{1... | collective-permute-start | bytes 688136 | tf_op jit(solution)/shard_map/ppermute | solution.py:343
  4.4 8.2 %collective-permute-start.2 = (bf16[64,1792]{1,0:T(8,128)(2,1)S(1)}, bf16[64,1792]{1,0:T(8,128)(2,1)S(1)}, u32[]{:S(2)}, u32[]{:S(2)}) collective-permute-start(bf16[64,1792]{1,0:T(8,128)(2,1)S(1)} %get-tuple-element.32.refs_0_), channel_id=1, source_target_pairs={{0,1},{1,0},{2,3},{3,2},{4,8},{5,9},{6,10},{7,11},{8,4},{9,5},{10,... | collective-permute-start | bytes 688136 | tf_op jit(solution)/shard_map/ppermute | solution.py:349
  4.4 8.1 %copy-start.1 = (s32[768]{0:T(1024)S(1)}, s32[768]{0:T(1024)}, u32[]{:S(2)}) copy-start(s32[768]{0:T(1024)} %param.16) | copy-start | bytes 9220
  4.4 8.1 %copy-start.2 = (s32[8]{0:T(128)S(1)}, s32[8]{0:T(128)}, u32[]{:S(2)}) copy-start(s32[8]{0:T(128)} %param.17) | copy-start | bytes 100
  4.4 19.9 %copy-start = (bf16[64,128]{1,0:T(8,128)(2,1)S(1)}, bf16[64,128]{1,0:T(8,128)(2,1)}, u32[]{:S(2)}) copy-start(bf16[64,128]{1,0:T(8,128)(2,1)} %param.13) | copy-start | bytes 49156
  4.4 12.8 %collective-permute-start.6 = (bf16[64,1792]{1,0:T(8,128)(2,1)S(1)}, bf16[64,1792]{1,0:T(8,128)(2,1)S(1)}, u32[]{:S(2)}, u32[]{:S(2)}) collective-permute-start(bf16[64,1792]{1,0:T(8,128)(2,1)S(1)} %get-tuple-element.33.refs_1_), channel_id=1, source_target_pairs={{0,4},{4,0},{8,12},{12,8},{1,5},{5,1},{9,13},{13,9},{2,6},{6,2},{1... | collective-permute-start | bytes 688136 | tf_op jit(solution)/shard_map/ppermute | solution.py:343
  7.6 9.7 %collective-permute-start.7 = (bf16[64,1792]{1,0:T(8,128)(2,1)S(1)}, bf16[64,1792]{1,0:T(8,128)(2,1)S(1)}, u32[]{:S(2)}, u32[]{:S(2)}) collective-permute-start(bf16[64,1792]{1,0:T(8,128)(2,1)S(1)} %get-tuple-element.33.refs_1_), channel_id=1, source_target_pairs={{0,1},{1,0},{2,3},{3,2},{4,8},{5,9},{6,10},{7,11},{8,4},{9,5},{10,... | collective-permute-start | bytes 688136 | tf_op jit(solution)/shard_map/ppermute | solution.py:349
  11.9 1.8 %collective-permute-start = (f32[576,128]{1,0:T(8,128)S(1)}, f32[576,128]{1,0:T(8,128)S(1)}, u32[]{:S(2)}, u32[]{:S(2)}) collective-permute-start(f32[576,128]{1,0:T(8,128)S(1)} %get-tuple-element.36), channel_id=1, source_target_pairs={{0,1},{1,0},{2,3},{3,2},{4,5},{5,4},{6,7},{7,6},{8,9},{9,8},{10,11... | collective-permute-start | bytes 884744 | tf_op jit(solution)/shard_map/ppermute | solution.py:366
  13.7 10.5 %collective-permute-start.3 = (f32[576,128]{1,0:T(8,128)S(1)}, f32[576,128]{1,0:T(8,128)S(1)}, u32[]{:S(2)}, u32[]{:S(2)}) collective-permute-start(f32[576,128]{1,0:T(8,128)S(1)} %add.6), channel_id=1, source_target_pairs={{0,2},{2,0},{1,3},{3,1},{4,6},{6,4},{5,7},{7,5},{8,10},{10,8},{9,1... | collective-permute-start | bytes 884744 | tf_op jit(solution)/shard_map/ppermute | solution.py:368
  15.3 8.5 %collective-permute-start.4 = (bf16[64,1792]{1,0:T(8,128)(2,1)S(1)}, bf16[64,1792]{1,0:T(8,128)(2,1)S(1)}, u32[]{:S(2)}, u32[]{:S(2)}) collective-permute-start(bf16[64,1792]{1,0:T(8,128)(2,1)S(1)} %broadcast_select_fusion.5), channel_id=1, source_target_pairs={{0,4},{4,0},{8,12},{12,8},{1,5},{5,1},{9,13},{13,9},{2,6},{6,2},{1... | collective-permute-start | bytes 688136 | tf_op jit(solution)/shard_map/ppermute | solution.py:343
  15.7 8.5 %collective-permute-start.5 = (bf16[64,1792]{1,0:T(8,128)(2,1)S(1)}, bf16[64,1792]{1,0:T(8,128)(2,1)S(1)}, u32[]{:S(2)}, u32[]{:S(2)}) collective-permute-start(bf16[64,1792]{1,0:T(8,128)(2,1)S(1)} %collective-permute-done.1.refs_4_), channel_id=1, source_target_pairs={{0,16},{1,17},{2,18},{3,19},{4,8},{5,9},{6,10},{7,11},{8,4},{9,5},... | collective-permute-start | bytes 688136 | tf_op jit(solution)/shard_map/ppermute | solution.py:349
  17.3 11.5 %collective-permute-start.8 = (bf16[64,1792]{1,0:T(8,128)(2,1)S(1)}, bf16[64,1792]{1,0:T(8,128)(2,1)S(1)}, u32[]{:S(2)}, u32[]{:S(2)}) collective-permute-start(bf16[64,1792]{1,0:T(8,128)(2,1)S(1)} %broadcast_select_fusion.4), channel_id=1, source_target_pairs={{0,4},{4,0},{8,12},{12,8},{1,5},{5,1},{9,13},{13,9},{2,6},{6,2},{1... | collective-permute-start | bytes 688136 | tf_op jit(solution)/shard_map/ppermute | solution.py:343
  18.0 10.8 %collective-permute-start.9 = (bf16[64,1792]{1,0:T(8,128)(2,1)S(1)}, bf16[64,1792]{1,0:T(8,128)(2,1)S(1)}, u32[]{:S(2)}, u32[]{:S(2)}) collective-permute-start(bf16[64,1792]{1,0:T(8,128)(2,1)S(1)} %collective-permute-done.6.refs_5_), channel_id=1, source_target_pairs={{0,16},{1,17},{2,18},{3,19},{4,8},{5,9},{6,10},{7,11},{8,4},{9,5},... | collective-permute-start | bytes 688136 | tf_op jit(solution)/shard_map/ppermute | solution.py:349
  24.3 8.6 %collective-permute-start.11 = (bf16[64,256]{1,0:T(8,128)(2,1)S(1)}, bf16[64,256]{1,0:T(8,128)(2,1)S(1)}, u32[]{:S(2)}, u32[]{:S(2)}) collective-permute-start(bf16[64,256]{1,0:T(8,128)(2,1)S(1)} %pad_maximum_fusion.2.refs_0_), channel_id=1, source_target_pairs={{0,4},{4,0},{8,12},{12,8},{1,5},{5,1},{9,13},{13,9},{2,6},{6,2},{1... | collective-permute-start | bytes 98312 | tf_op jit(solution)/shard_map/ppermute | solution.py:46
  26.1 13.8 %collective-permute-start.12 = (bf16[64,256]{1,0:T(8,128)(2,1)S(1)}, bf16[64,256]{1,0:T(8,128)(2,1)S(1)}, u32[]{:S(2)}, u32[]{:S(2)}) collective-permute-start(bf16[64,256]{1,0:T(8,128)(2,1)S(1)} %pad_maximum_fusion.2.refs_0_), channel_id=1, source_target_pairs={{0,8},{4,12},{8,0},{12,4},{1,9},{5,13},{9,1},{13,5},{2,10},{6,14},... | collective-permute-start | bytes 98312 | tf_op jit(solution)/shard_map/ppermute | solution.py:46
  27.9 11.9 %collective-permute-start.13 = (bf16[64,256]{1,0:T(8,128)(2,1)S(1)}, bf16[64,256]{1,0:T(8,128)(2,1)S(1)}, u32[]{:S(2)}, u32[]{:S(2)}) collective-permute-start(bf16[64,256]{1,0:T(8,128)(2,1)S(1)} %pad_maximum_fusion.2.refs_0_), channel_id=1, source_target_pairs={{0,12},{4,8},{8,4},{12,0},{1,13},{5,9},{9,5},{13,1},{2,14},{6,10},... | collective-permute-start | bytes 98312 | tf_op jit(solution)/shard_map/ppermute | solution.py:46
  28.9 11.5 %collective-permute-start.15 = (bf16[64,3584]{1,0:T(8,128)(2,1)S(1)}, bf16[64,3584]{1,0:T(8,128)(2,1)S(1)}, u32[]{:S(2)}, u32[]{:S(2)}) collective-permute-start(bf16[64,3584]{1,0:T(8,128)(2,1)S(1)} %pad_maximum_fusion.mine_2_ref), channel_id=1, source_target_pairs={{0,4},{4,0},{8,12},{12,8},{1,5},{5,1},{9,13},{13,9},{2,6},{6,2},{1... | collective-permute-start | bytes 1376264 | tf_op jit(solution)/shard_map/ppermute | solution.py:343
  31.4 10.7 %collective-permute-start.10 = (bf16[64,3584]{1,0:T(8,128)(2,1)S(1)}, bf16[64,3584]{1,0:T(8,128)(2,1)S(1)}, u32[]{:S(2)}, u32[]{:S(2)}) collective-permute-start(bf16[64,3584]{1,0:T(8,128)(2,1)S(1)} %pad_maximum_fusion.mine_2_ref), channel_id=1, source_target_pairs={{0,16},{16,0},{1,17},{17,1},{2,18},{18,2},{3,19},{19,3},{4,20},{20... | collective-permute-start | bytes 1376264 | tf_op jit(solution)/shard_map/ppermute | solution.py:346
  32.9 10.8 %collective-permute-start.17 = (bf16[384,128]{1,0:T(8,128)(2,1)S(1)}, bf16[384,128]{1,0:T(8,128)(2,1)S(1)}, u32[]{:S(2)}, u32[]{:S(2)}) collective-permute-start(bf16[384,128]{1,0:T(8,128)(2,1)S(1)} %slice.20), channel_id=1, source_target_pairs={{0,1},{1,0},{2,3},{3,2},{4,5},{5,4},{6,7},{7,6},{8,9},{9,8},{10,11... | collective-permute-start | bytes 294920 | tf_op jit(solution)/shard_map/ppermute | solution.py:389
  40.5 8.0 %collective-permute-start.16 = (bf16[64,1792]{1,0:T(8,128)(2,1)S(1)}, bf16[64,1792]{1,0:T(8,128)(2,1)S(1)}, u32[]{:S(2)}, u32[]{:S(2)}) collective-permute-start(bf16[64,1792]{1,0:T(8,128)(2,1)S(1)} %slice.18), channel_id=1, source_target_pairs={{0,16},{16,0},{1,17},{17,1},{2,18},{18,2},{3,19},{19,3},{4,20},{20... | collective-permute-start | bytes 688136 | tf_op jit(solution)/shard_map/ppermute | solution.py:346
  42.1 6.7 %collective-permute-start.14 = (bf16[64,1792]{1,0:T(8,128)(2,1)S(1)}, bf16[64,1792]{1,0:T(8,128)(2,1)S(1)}, u32[]{:S(2)}, u32[]{:S(2)}) collective-permute-start(bf16[64,1792]{1,0:T(8,128)(2,1)S(1)} %slice.17), channel_id=1, source_target_pairs={{0,4},{4,0},{8,12},{12,8},{1,5},{5,1},{9,13},{13,9},{2,6},{6,2},{1... | collective-permute-start | bytes 688136 | tf_op jit(solution)/shard_map/ppermute | solution.py:343

commit v14 on v10

--- a/solution.py
+++ b/solution.py
@@ -175,33 +175,33 @@
             ).astype(jnp.bfloat16)
 
 
-def project(acts_ref, start, pieces, group, first=0):
+def project(acts_ref, start, pieces, group, first=0, size=BLOCK):
     columns = pl.ds(
         pl.multiple_of(group * (acts_ref.shape[1] // 2) + first, LANES), pieces[0].shape[1]
     )
     stacked = jnp.concatenate([piece[...] for piece in pieces], axis=0)
-    return contract_last(acts_ref[pl.ds(start, BLOCK), columns], stacked)
+    return contract_last(acts_ref[pl.ds(start, size), columns], stacked)
 
 
 def mixing(start, weights, grad_ref):
     return contract_last(grad_ref[pl.ds(start, BLOCK), :], weights)
 
 
-def mix(start, projected, mixed, onehot_ref):
+def mix(start, projected, mixed, onehot_ref, size=BLOCK):
     product = jnp.concatenate([projected] * (mixed.shape[1] // LANES), axis=1) * mixed
     high = product.astype(jnp.bfloat16)
     low = (product - high.astype(jnp.float32)).astype(jnp.bfloat16)
-    onehot = onehot_ref[:, pl.ds(start, BLOCK)]
+    onehot = onehot_ref[:, pl.ds(start, size)]
     return jnp.dot(onehot, high, preferred_element_type=jnp.float32) + jnp.dot(
         onehot, low, preferred_element_type=jnp.float32
     )
 
 
-def blocks(tokens, body, initial):
+def blocks(tokens, body, initial, size=BLOCK):
     def step(index, carry):
-        return body(pl.multiple_of(index * BLOCK, LANES), carry)
-
-    return lax.fori_loop(0, tokens // BLOCK, step, initial, unroll=True)
+        return body(pl.multiple_of(index * size, LANES), carry)
+
+    return lax.fori_loop(0, tokens // size, step, initial, unroll=True)
 
 
 def weight_kernel(query_count, *refs):
@@ -271,17 +271,19 @@
     other = 1 - lax.axis_index("groups")
     cut = left_ref.shape[1]
 
+    size = LANES
+
     def body(start, sums):
-        total = total_ref[pl.ds(start, BLOCK), :]
+        total = total_ref[pl.ds(start, size), :]
         total = total + project(
-            acts_ref, start, (theirs_2_ref.at[:, :cut], left_ref), other
+            acts_ref, start, (theirs_2_ref.at[:, :cut], left_ref), other, 0, size
         )
         total = total + project(
-            acts_ref, start, (theirs_2_ref.at[:, cut:], right_ref), other, cut
+            acts_ref, start, (theirs_2_ref.at[:, cut:], right_ref), other, cut, size
         )
-        return sums + mix(start, total, mixed_ref[pl.ds(start, BLOCK), :], onehot_ref)
-
-    sums = blocks(acts_ref.shape[0], body, before_ref[...])
+        return sums + mix(start, total, mixed_ref[pl.ds(start, size), :], onehot_ref, size)
+
+    sums = blocks(acts_ref.shape[0], body, before_ref[...], size)
     width = sums.shape[1]
     query_of = lax.broadcasted_iota(jnp.int32, (query_count, width), 1) // (width // query_count)
     chosen = query_of == lax.broadcasted_iota(jnp.int32, (query_count, width), 0)

time: 61.5 us -> 62.1 us (level)
  transfers between devices with their start and end apart: 18 -> 18, of which waited for: 5 -> 5; matrix products, arithmetic and copies ran while one was open for 1% -> 1% of each run, Pallas kernels for 24% -> 23%
where the time goes in v14:
time: 62.1 us; the launch traced here: 61.9 us
  starting transfers between devices  23.8 us (38%)
  Pallas kernels  18.9 us (30%)
  blocking collectives  9.04 us (15%)
  waiting for transfers between devices  8.93 us (14%)
  other arithmetic  0.95 us (2%)
    pallas_call x4, Pallas kernels, call(): pl.pallas_call(kernel, out_shape=out_shape, compiler_params=pltpu.Compile...  13.2 us
    ppermute x6, starting transfers between devices, along(): return lax.ppermute(value, 'blk', [(i, i ^ 1) for i in range(4)])  11.4 us
    all_to_all x1, blocking collectives, on_device(): parts = lax.all_to_all(parts, ('blk', 'eig', 'rep'), 0, 0, tiled=True)  9.04 us
    ppermute x6, waiting for transfers between devices, along(): return lax.ppermute(value, 'blk', [(i, i ^ 1) for i in range(4)])  4.68 us
    ppermute x3, starting transfers between devices, by_distance(): lax.ppermute(value, axis, [(i, i ^ k) for i in range(size)])  4.45 us
    pallas_call x1, Pallas kernels, small_parts(): pl.pallas_call(parts_kernel, in_specs=[pl.BlockSpec(memory_space=pl.ANY)]...  4.31 us
    ppermute x4, starting transfers between devices, across(): lax.ppermute(value, AXES, pairing(lambda g, b, e, r: (g, 3 - b, e, r) if...  3.05 us
    ppermute x2, waiting for transfers between devices, swapped(): return lax.ppermute(value, 'groups', pair)  2.75 us
  transfers between devices with their start and end apart: 18, of which 5 were waited for; matrix products, arithmetic and copies ran while one was open for 1% of the time, Pallas kernels for 23%

profile of v14, /device:TPU:0, one launch (start us, length us, event | category | flops | bytes accessed | tf_op | source)
XLA Modules:
  0.0 61.9 jit_solution(15124003794332349574)
XLA Ops:
  0.0 1.3 %shard_map.91 = (bf16[64,1792]{1,0:T(8,128)(2,1)S(1)}, bf16[64,1792]{1,0:T(8,128)(2,1)S(1)}, bf16[64,1792]{1,0:T(8,128)(2,1)S(1)}, bf16[64,1792]{1,0:T(8,128)(2,1)S(1)}) custom-call(bf16[64,7168]{1,0:T(8,128)(2,1)} %refs_2_), custom_call_target="tpu_custom_call" | custom-call | tf_op jit(solution)/shard_map/pallas_call | solution.py:86
  1.3 3.1 %collective-permute-start.1 = (bf16[64,1792]{1,0:T(8,128)(2,1)S(1)}, bf16[64,1792]{1,0:T(8,128)(2,1)S(1)}, u32[]{:S(2)}, u32[]{:S(2)}) collective-permute-start(bf16[64,1792]{1,0:T(8,128)(2,1)S(1)} %get-tuple-element.32.refs_0_), channel_id=1, source_target_pairs={{0,4},{4,0},{8,12},{12,8},{1,5},{5,1},{9,13},{13,9},{2,6},{6,2},{1... | collective-permute-start | bytes 688136 | tf_op jit(solution)/shard_map/ppermute | solution.py:345
  4.4 0.0 collective-permute-start.2
  4.4 3.1 %collective-permute-start.6 = (bf16[64,1792]{1,0:T(8,128)(2,1)S(1)}, bf16[64,1792]{1,0:T(8,128)(2,1)S(1)}, u32[]{:S(2)}, u32[]{:S(2)}) collective-permute-start(bf16[64,1792]{1,0:T(8,128)(2,1)S(1)} %get-tuple-element.33.refs_1_), channel_id=1, source_target_pairs={{0,4},{4,0},{8,12},{12,8},{1,5},{5,1},{9,13},{13,9},{2,6},{6,2},{1... | collective-permute-start | bytes 688136 | tf_op jit(solution)/shard_map/ppermute | solution.py:345
  7.6 4.3 %shard_map.92 = (f32[576,128]{1,0:T(8,128)S(1)}, f32[576,128]{1,0:T(8,128)S(1)}) custom-call(bf16[128,2048]{1,0:T(8,128)(2,1)} %refs_0_.1, bf16[2048,128]{1,0:T(8,128)(2,1)} %refs_1_.1, bf16[64,7168]{1,0:T(8,128)(2,1)} %refs_2_, bf16[7168,128]{1,0:T(8,128)(2,1)} %refs_3_.1, bf16[768,2048]{1,0:T(8,128)(2,1)} %refs_4_.1), custom_call_target="tpu_custom_call" | custom-call | tf_op jit(solution)/shard_map/pallas_call | solution.py:154
  11.9 0.6 collective-permute-start
  12.5 0.1 select_reduce_fusion
  12.6 1.1 %collective-permute-done = f32[576,128]{1,0:T(8,128)S(1)} collective-permute-done((f32[576,128]{1,0:T(8,128)S(1)}, f32[576,128]{1,0:T(8,128)S(1)}, u32[]{:S(2)}, u32[]{:S(2)}) %collective-permute-start) | collective-permute-done | bytes 294944 | tf_op jit(solution)/shard_map/ppermute | solution.py:368
  13.7 1.6 %collective-permute-start.3 = (f32[576,128]{1,0:T(8,128)S(1)}, f32[576,128]{1,0:T(8,128)S(1)}, u32[]{:S(2)}, u32[]{:S(2)}) collective-permute-start(f32[576,128]{1,0:T(8,128)S(1)} %add.6), channel_id=1, source_target_pairs={{0,2},{2,0},{1,3},{3,1},{4,6},{6,4},{5,7},{7,5},{8,10},{10,8},{9,1... | collective-permute-start | bytes 884744 | tf_op jit(solution)/shard_map/ppermute | solution.py:370
  15.3 0.4 collective-permute-start.4
  15.7 1.5 %collective-permute-start.5 = (bf16[64,1792]{1,0:T(8,128)(2,1)S(1)}, bf16[64,1792]{1,0:T(8,128)(2,1)S(1)}, u32[]{:S(2)}, u32[]{:S(2)}) collective-permute-start(bf16[64,1792]{1,0:T(8,128)(2,1)S(1)} %collective-permute-done.1.refs_4_), channel_id=1, source_target_pairs={{0,16},{1,17},{2,18},{3,19},{4,8},{5,9},{6,10},{7,11},{8,4},{9,5},... | collective-permute-start | bytes 688136 | tf_op jit(solution)/shard_map/ppermute | solution.py:351
  17.3 0.7 %collective-permute-start.8 = (bf16[64,1792]{1,0:T(8,128)(2,1)S(1)}, bf16[64,1792]{1,0:T(8,128)(2,1)S(1)}, u32[]{:S(2)}, u32[]{:S(2)}) collective-permute-start(bf16[64,1792]{1,0:T(8,128)(2,1)S(1)} %broadcast_select_fusion.4), channel_id=1, source_target_pairs={{0,4},{4,0},{8,12},{12,8},{1,5},{5,1},{9,13},{13,9},{2,6},{6,2},{1... | collective-permute-start | bytes 688136 | tf_op jit(solution)/shard_map/ppermute | solution.py:345
  18.0 1.5 %collective-permute-start.9 = (bf16[64,1792]{1,0:T(8,128)(2,1)S(1)}, bf16[64,1792]{1,0:T(8,128)(2,1)S(1)}, u32[]{:S(2)}, u32[]{:S(2)}) collective-permute-start(bf16[64,1792]{1,0:T(8,128)(2,1)S(1)} %collective-permute-done.6.refs_5_), channel_id=1, source_target_pairs={{0,16},{1,17},{2,18},{3,19},{4,8},{5,9},{6,10},{7,11},{8,4},{9,5},... | collective-permute-start | bytes 688136 | tf_op jit(solution)/shard_map/ppermute | solution.py:351
  19.5 4.4 %collective-permute-done.4 = bf16[64,1792]{1,0:T(8,128)(2,1)S(1)} collective-permute-done((bf16[64,1792]{1,0:T(8,128)(2,1)S(1)}, bf16[64,1792]{1,0:T(8,128)(2,1)S(1)}, u32[]{:S(2)}, u32[]{:S(2)}) %collective-permute-start.4) | collective-permute-done | bytes 229408 | tf_op jit(solution)/shard_map/ppermute | solution.py:345
  23.8 0.4 collective-permute-done.5
  24.3 1.7 %collective-permute-start.11 = (bf16[64,256]{1,0:T(8,128)(2,1)S(1)}, bf16[64,256]{1,0:T(8,128)(2,1)S(1)}, u32[]{:S(2)}, u32[]{:S(2)}) collective-permute-start(bf16[64,256]{1,0:T(8,128)(2,1)S(1)} %pad_maximum_fusion.2.refs_0_), channel_id=1, source_target_pairs={{0,4},{4,0},{8,12},{12,8},{1,5},{5,1},{9,13},{13,9},{2,6},{6,2},{1... | collective-permute-start | bytes 98312 | tf_op jit(solution)/shard_map/ppermute | solution.py:46
  26.1 1.9 %collective-permute-start.12 = (bf16[64,256]{1,0:T(8,128)(2,1)S(1)}, bf16[64,256]{1,0:T(8,128)(2,1)S(1)}, u32[]{:S(2)}, u32[]{:S(2)}) collective-permute-start(bf16[64,256]{1,0:T(8,128)(2,1)S(1)} %pad_maximum_fusion.2.refs_0_), channel_id=1, source_target_pairs={{0,8},{4,12},{8,0},{12,4},{1,9},{5,13},{9,1},{13,5},{2,10},{6,14},... | collective-permute-start | bytes 98312 | tf_op jit(solution)/shard_map/ppermute | solution.py:46
  27.9 0.8 %collective-permute-start.13 = (bf16[64,256]{1,0:T(8,128)(2,1)S(1)}, bf16[64,256]{1,0:T(8,128)(2,1)S(1)}, u32[]{:S(2)}, u32[]{:S(2)}) collective-permute-start(bf16[64,256]{1,0:T(8,128)(2,1)S(1)} %pad_maximum_fusion.2.refs_0_), channel_id=1, source_target_pairs={{0,12},{4,8},{8,4},{12,0},{1,13},{5,9},{9,5},{13,1},{2,14},{6,10},... | collective-permute-start | bytes 98312 | tf_op jit(solution)/shard_map/ppermute | solution.py:46
  28.9 2.4 %collective-permute-start.15 = (bf16[64,3584]{1,0:T(8,128)(2,1)S(1)}, bf16[64,3584]{1,0:T(8,128)(2,1)S(1)}, u32[]{:S(2)}, u32[]{:S(2)}) collective-permute-start(bf16[64,3584]{1,0:T(8,128)(2,1)S(1)} %pad_maximum_fusion.mine_2_ref), channel_id=1, source_target_pairs={{0,4},{4,0},{8,12},{12,8},{1,5},{5,1},{9,13},{13,9},{2,6},{6,2},{1... | collective-permute-start | bytes 1376264 | tf_op jit(solution)/shard_map/ppermute | solution.py:345
  31.4 1.5 %collective-permute-start.10 = (bf16[64,3584]{1,0:T(8,128)(2,1)S(1)}, bf16[64,3584]{1,0:T(8,128)(2,1)S(1)}, u32[]{:S(2)}, u32[]{:S(2)}) collective-permute-start(bf16[64,3584]{1,0:T(8,128)(2,1)S(1)} %pad_maximum_fusion.mine_2_ref), channel_id=1, source_target_pairs={{0,16},{16,0},{1,17},{17,1},{2,18},{18,2},{3,19},{19,3},{4,20},{20... | collective-permute-start | bytes 1376264 | tf_op jit(solution)/shard_map/ppermute | solution.py:348
  32.9 0.1 broadcast_select_fusion
  33.0 7.3 %shard_map.93 = (f32[768,128]{1,0:T(8,128)S(1)}, bf16[768,7168]{1,0:T(8,128)(2,1)S(1)}) custom-call(bf16[768,7168]{1,0:T(8,128)(2,1)} %source_ref, bf16[64,1792]{1,0:T(8,128)(2,1)S(1)} %get-tuple-element.32.refs_0_, bf16[64,1792]{1,0:T(8,128)(2,1)S(1)} %get-tuple-element.33.refs_1_, bf16[64,1792]{1,0:T(8,128)(2,1)S(1)} %get-tuple-element.39.refs_2_, ...), custom_call_target="tpu_custom_call" | custom-call | flops 1 | bytes 1 | tf_op jit(solution)/shard_map/pallas_call | solution.py:299
  40.3 0.5 shard_map.94.weights_ref
  40.8 0.0 collective-permute-done.15.mine_3_ref
  40.8 1.2 %collective-permute-start.16 = (bf16[64,1792]{1,0:T(8,128)(2,1)S(1)}, bf16[64,1792]{1,0:T(8,128)(2,1)S(1)}, u32[]{:S(2)}, u32[]{:S(2)}) collective-permute-start(bf16[64,1792]{1,0:T(8,128)(2,1)S(1)} %slice.18), channel_id=1, source_target_pairs={{0,16},{16,0},{1,17},{17,1},{2,18},{18,2},{3,19},{19,3},{4,20},{20... | collective-permute-start | bytes 688136 | tf_op jit(solution)/shard_map/ppermute | solution.py:348
  42.1 1.7 %collective-permute-start.14 = (bf16[64,1792]{1,0:T(8,128)(2,1)S(1)}, bf16[64,1792]{1,0:T(8,128)(2,1)S(1)}, u32[]{:S(2)}, u32[]{:S(2)}) collective-permute-start(bf16[64,1792]{1,0:T(8,128)(2,1)S(1)} %slice.17), channel_id=1, source_target_pairs={{0,4},{4,0},{8,12},{12,8},{1,5},{5,1},{9,13},{13,9},{2,6},{6,2},{1... | collective-permute-start | bytes 688136 | tf_op jit(solution)/shard_map/ppermute | solution.py:345
  43.8 2.4 %shard_map.95 = (f32[768,128]{1,0:T(8,128)S(1)}, f32[768,512]{1,0:T(8,128)S(1)}, f32[8,512]{1,0:T(8,128)S(1)}) custom-call(bf16[768,7168]{1,0:T(8,128)(2,1)S(1)} %get-tuple-element.52.acts_ref, bf16[64,3584]{1,0:T(8,128)(2,1)S(1)} %pad_maximum_fusion.mine_2_ref, bf16[64,3584]{1,0:T(8,128)(2,1)S(1)} %collective-permute-done.15.mine_3_ref, ...), custom_call_target="tpu_custom_call" | custom-call | flops 1 | bytes 1 | tf_op jit(solution)/shard_map/pallas_call | solution.py:299
  46.1 2.7 %collective-permute-done.16.right_ref = bf16[64,1792]{1,0:T(8,128)(2,1)S(1)} collective-permute-done((bf16[64,1792]{1,0:T(8,128)(2,1)S(1)}, bf16[64,1792]{1,0:T(8,128)(2,1)S(1)}, u32[]{:S(2)}, u32[]{:S(2)}) %collective-permute-start.16) | collective-permute-done | bytes 229408 | tf_op jit(solution)/shard_map/ppermute | solution.py:348
  48.9 0.3 collective-permute-done.14.left_ref
  49.2 3.1 %shard_map.96 = f32[16,2]{1,0:T(8,128)S(1)} custom-call(bf16[768,7168]{1,0:T(8,128)(2,1)S(1)} %get-tuple-element.52.acts_ref, bf16[64,3584]{1,0:T(8,128)(2,1)S(1)} %collective-permute-done.10.theirs_2_ref, bf16[64,1792]{1,0:T(8,128)(2,1)S(1)} %collective-permute-done.14.left_ref, bf16[64,1792]{1,0:T(8,128)(2,1)S(1)} %collective-permute-done.16.right_ref, ...), custom_call_target="tpu_custom_call" | custom-call | flops 1 | bytes 1 | tf_op jit(solution)/shard_map/pallas_call | solution.py:299
  52.3 9.0 %all_to_all.9 = f32[16,1,2]{2,1,0:T(1,128)S(1)} all-to-all(f32[16,1,2]{2,1,0:T(1,128)S(1)} %bitcast.4), channel_id=1, replica_groups=mesh['groups'=2,'blk'=4,'eig'=2,'rep'=2] {'blk','eig','rep'}, dimensions={0} | all-to-all | bytes 256 | tf_op jit(solution)/shard_map/all_to_all | solution.py:471
  61.3 0.5 reduce_sum.21
  (36 shorter events, 0.4 us)
Async XLA Ops:
  1.3 11.3 %collective-permute-start.1 = (bf16[64,1792]{1,0:T(8,128)(2,1)S(1)}, bf16[64,1792]{1,0:T(8,128)(2,1)S(1)}, u32[]{:S(2)}, u32[]{:S(2)}) collective-permute-start(bf16[64,1792]{1,0:T(8,128)(2,1)S(1)} %get-tuple-element.32.refs_0_), channel_id=1, source_target_pairs={{0,4},{4,0},{8,12},{12,8},{1,5},{5,1},{9,13},{13,9},{2,6},{6,2},{1... | collective-permute-start | bytes 688136 | tf_op jit(solution)/shard_map/ppermute | solution.py:345
  4.4 8.2 %collective-permute-start.2 = (bf16[64,1792]{1,0:T(8,128)(2,1)S(1)}, bf16[64,1792]{1,0:T(8,128)(2,1)S(1)}, u32[]{:S(2)}, u32[]{:S(2)}) collective-permute-start(bf16[64,1792]{1,0:T(8,128)(2,1)S(1)} %get-tuple-element.32.refs_0_), channel_id=1, source_target_pairs={{0,1},{1,0},{2,3},{3,2},{4,8},{5,9},{6,10},{7,11},{8,4},{9,5},{10,... | collective-permute-start | bytes 688136 | tf_op jit(solution)/shard_map/ppermute | solution.py:351
  4.4 8.1 %copy-start.1 = (s32[768]{0:T(1024)S(1)}, s32[768]{0:T(1024)}, u32[]{:S(2)}) copy-start(s32[768]{0:T(1024)} %param.16) | copy-start | bytes 9220
  4.4 8.1 %copy-start.2 = (s32[8]{0:T(128)S(1)}, s32[8]{0:T(128)}, u32[]{:S(2)}) copy-start(s32[8]{0:T(128)} %param.17) | copy-start | bytes 100
  4.4 19.9 %copy-start = (bf16[64,128]{1,0:T(8,128)(2,1)S(1)}, bf16[64,128]{1,0:T(8,128)(2,1)}, u32[]{:S(2)}) copy-start(bf16[64,128]{1,0:T(8,128)(2,1)} %param.13) | copy-start | bytes 49156
  4.4 12.8 %collective-permute-start.6 = (bf16[64,1792]{1,0:T(8,128)(2,1)S(1)}, bf16[64,1792]{1,0:T(8,128)(2,1)S(1)}, u32[]{:S(2)}, u32[]{:S(2)}) collective-permute-start(bf16[64,1792]{1,0:T(8,128)(2,1)S(1)} %get-tuple-element.33.refs_1_), channel_id=1, source_target_pairs={{0,4},{4,0},{8,12},{12,8},{1,5},{5,1},{9,13},{13,9},{2,6},{6,2},{1... | collective-permute-start | bytes 688136 | tf_op jit(solution)/shard_map/ppermute | solution.py:345
  7.6 9.7 %collective-permute-start.7 = (bf16[64,1792]{1,0:T(8,128)(2,1)S(1)}, bf16[64,1792]{1,0:T(8,128)(2,1)S(1)}, u32[]{:S(2)}, u32[]{:S(2)}) collective-permute-start(bf16[64,1792]{1,0:T(8,128)(2,1)S(1)} %get-tuple-element.33.refs_1_), channel_id=1, source_target_pairs={{0,1},{1,0},{2,3},{3,2},{4,8},{5,9},{6,10},{7,11},{8,4},{9,5},{10,... | collective-permute-start | bytes 688136 | tf_op jit(solution)/shard_map/ppermute | solution.py:351
  11.9 1.8 %collective-permute-start = (f32[576,128]{1,0:T(8,128)S(1)}, f32[576,128]{1,0:T(8,128)S(1)}, u32[]{:S(2)}, u32[]{:S(2)}) collective-permute-start(f32[576,128]{1,0:T(8,128)S(1)} %get-tuple-element.36), channel_id=1, source_target_pairs={{0,1},{1,0},{2,3},{3,2},{4,5},{5,4},{6,7},{7,6},{8,9},{9,8},{10,11... | collective-permute-start | bytes 884744 | tf_op jit(solution)/shard_map/ppermute | solution.py:368
  13.7 10.5 %collective-permute-start.3 = (f32[576,128]{1,0:T(8,128)S(1)}, f32[576,128]{1,0:T(8,128)S(1)}, u32[]{:S(2)}, u32[]{:S(2)}) collective-permute-start(f32[576,128]{1,0:T(8,128)S(1)} %add.6), channel_id=1, source_target_pairs={{0,2},{2,0},{1,3},{3,1},{4,6},{6,4},{5,7},{7,5},{8,10},{10,8},{9,1... | collective-permute-start | bytes 884744 | tf_op jit(solution)/shard_map/ppermute | solution.py:370
  15.3 8.5 %collective-permute-start.4 = (bf16[64,1792]{1,0:T(8,128)(2,1)S(1)}, bf16[64,1792]{1,0:T(8,128)(2,1)S(1)}, u32[]{:S(2)}, u32[]{:S(2)}) collective-permute-start(bf16[64,1792]{1,0:T(8,128)(2,1)S(1)} %broadcast_select_fusion.5), channel_id=1, source_target_pairs={{0,4},{4,0},{8,12},{12,8},{1,5},{5,1},{9,13},{13,9},{2,6},{6,2},{1... | collective-permute-start | bytes 688136 | tf_op jit(solution)/shard_map/ppermute | solution.py:345
  15.7 8.5 %collective-permute-start.5 = (bf16[64,1792]{1,0:T(8,128)(2,1)S(1)}, bf16[64,1792]{1,0:T(8,128)(2,1)S(1)}, u32[]{:S(2)}, u32[]{:S(2)}) collective-permute-start(bf16[64,1792]{1,0:T(8,128)(2,1)S(1)} %collective-permute-done.1.refs_4_), channel_id=1, source_target_pairs={{0,16},{1,17},{2,18},{3,19},{4,8},{5,9},{6,10},{7,11},{8,4},{9,5},... | collective-permute-start | bytes 688136 | tf_op jit(solution)/shard_map/ppermute | solution.py:351
  17.3 11.5 %collective-permute-start.8 = (bf16[64,1792]{1,0:T(8,128)(2,1)S(1)}, bf16[64,1792]{1,0:T(8,128)(2,1)S(1)}, u32[]{:S(2)}, u32[]{:S(2)}) collective-permute-start(bf16[64,1792]{1,0:T(8,128)(2,1)S(1)} %broadcast_select_fusion.4), channel_id=1, source_target_pairs={{0,4},{4,0},{8,12},{12,8},{1,5},{5,1},{9,13},{13,9},{2,6},{6,2},{1... | collective-permute-start | bytes 688136 | tf_op jit(solution)/shard_map/ppermute | solution.py:345
  18.0 10.8 %collective-permute-start.9 = (bf16[64,1792]{1,0:T(8,128)(2,1)S(1)}, bf16[64,1792]{1,0:T(8,128)(2,1)S(1)}, u32[]{:S(2)}, u32[]{:S(2)}) collective-permute-start(bf16[64,1792]{1,0:T(8,128)(2,1)S(1)} %collective-permute-done.6.refs_5_), channel_id=1, source_target_pairs={{0,16},{1,17},{2,18},{3,19},{4,8},{5,9},{6,10},{7,11},{8,4},{9,5},... | collective-permute-start | bytes 688136 | tf_op jit(solution)/shard_map/ppermute | solution.py:351
  24.3 8.6 %collective-permute-start.11 = (bf16[64,256]{1,0:T(8,128)(2,1)S(1)}, bf16[64,256]{1,0:T(8,128)(2,1)S(1)}, u32[]{:S(2)}, u32[]{:S(2)}) collective-permute-start(bf16[64,256]{1,0:T(8,128)(2,1)S(1)} %pad_maximum_fusion.2.refs_0_), channel_id=1, source_target_pairs={{0,4},{4,0},{8,12},{12,8},{1,5},{5,1},{9,13},{13,9},{2,6},{6,2},{1... | collective-permute-start | bytes 98312 | tf_op jit(solution)/shard_map/ppermute | solution.py:46
  26.1 14.3 %collective-permute-start.12 = (bf16[64,256]{1,0:T(8,128)(2,1)S(1)}, bf16[64,256]{1,0:T(8,128)(2,1)S(1)}, u32[]{:S(2)}, u32[]{:S(2)}) collective-permute-start(bf16[64,256]{1,0:T(8,128)(2,1)S(1)} %pad_maximum_fusion.2.refs_0_), channel_id=1, source_target_pairs={{0,8},{4,12},{8,0},{12,4},{1,9},{5,13},{9,1},{13,5},{2,10},{6,14},... | collective-permute-start | bytes 98312 | tf_op jit(solution)/shard_map/ppermute | solution.py:46
  27.9 12.4 %collective-permute-start.13 = (bf16[64,256]{1,0:T(8,128)(2,1)S(1)}, bf16[64,256]{1,0:T(8,128)(2,1)S(1)}, u32[]{:S(2)}, u32[]{:S(2)}) collective-permute-start(bf16[64,256]{1,0:T(8,128)(2,1)S(1)} %pad_maximum_fusion.2.refs_0_), channel_id=1, source_target_pairs={{0,12},{4,8},{8,4},{12,0},{1,13},{5,9},{9,5},{13,1},{2,14},{6,10},... | collective-permute-start | bytes 98312 | tf_op jit(solution)/shard_map/ppermute | solution.py:46
  28.9 11.9 %collective-permute-start.15 = (bf16[64,3584]{1,0:T(8,128)(2,1)S(1)}, bf16[64,3584]{1,0:T(8,128)(2,1)S(1)}, u32[]{:S(2)}, u32[]{:S(2)}) collective-permute-start(bf16[64,3584]{1,0:T(8,128)(2,1)S(1)} %pad_maximum_fusion.mine_2_ref), channel_id=1, source_target_pairs={{0,4},{4,0},{8,12},{12,8},{1,5},{5,1},{9,13},{13,9},{2,6},{6,2},{1... | collective-permute-start | bytes 1376264 | tf_op jit(solution)/shard_map/ppermute | solution.py:345
  31.4 10.7 %collective-permute-start.10 = (bf16[64,3584]{1,0:T(8,128)(2,1)S(1)}, bf16[64,3584]{1,0:T(8,128)(2,1)S(1)}, u32[]{:S(2)}, u32[]{:S(2)}) collective-permute-start(bf16[64,3584]{1,0:T(8,128)(2,1)S(1)} %pad_maximum_fusion.mine_2_ref), channel_id=1, source_target_pairs={{0,16},{16,0},{1,17},{17,1},{2,18},{18,2},{3,19},{19,3},{4,20},{20... | collective-permute-start | bytes 1376264 | tf_op jit(solution)/shard_map/ppermute | solution.py:348
  32.9 10.8 %collective-permute-start.17 = (bf16[384,128]{1,0:T(8,128)(2,1)S(1)}, bf16[384,128]{1,0:T(8,128)(2,1)S(1)}, u32[]{:S(2)}, u32[]{:S(2)}) collective-permute-start(bf16[384,128]{1,0:T(8,128)(2,1)S(1)} %slice.20), channel_id=1, source_target_pairs={{0,1},{1,0},{2,3},{3,2},{4,5},{5,4},{6,7},{7,6},{8,9},{9,8},{10,11... | collective-permute-start | bytes 294920 | tf_op jit(solution)/shard_map/ppermute | solution.py:391
  40.8 8.1 %collective-permute-start.16 = (bf16[64,1792]{1,0:T(8,128)(2,1)S(1)}, bf16[64,1792]{1,0:T(8,128)(2,1)S(1)}, u32[]{:S(2)}, u32[]{:S(2)}) collective-permute-start(bf16[64,1792]{1,0:T(8,128)(2,1)S(1)} %slice.18), channel_id=1, source_target_pairs={{0,16},{16,0},{1,17},{17,1},{2,18},{18,2},{3,19},{19,3},{4,20},{20... | collective-permute-start | bytes 688136 | tf_op jit(solution)/shard_map/ppermute | solution.py:348
  42.1 7.1 %collective-permute-start.14 = (bf16[64,1792]{1,0:T(8,128)(2,1)S(1)}, bf16[64,1792]{1,0:T(8,128)(2,1)S(1)}, u32[]{:S(2)}, u32[]{:S(2)}) collective-permute-start(bf16[64,1792]{1,0:T(8,128)(2,1)S(1)} %slice.17), channel_id=1, source_target_pairs={{0,4},{4,0},{8,12},{12,8},{1,5},{5,1},{9,13},{13,9},{2,6},{6,2},{1... | collective-permute-start | bytes 688136 | tf_op jit(solution)/shard_map/ppermute | solution.py:345

commit v15 on v12

--- a/solution.py
+++ b/solution.py
@@ -353,15 +353,16 @@
     early, inner, of_first, _ = lax.optimization_barrier((basis_in, inner, of_first, half))
     keep, send = small_parts(early, query_in, basis_out, query_out, out_grads)
     other = lax.ppermute(send, "rep", pair)
-    keep = keep + held(other, *mine_1, *middle_3)
+    keep = keep + held(other, mine_1[0], middle_3[0])
     other = lax.ppermute(keep, "eig", pair)
 
     arrived = []
-    for after, first, middle, rest in zip((half[0], keep), mine_1, middle_3, other_half):
-        from_pair = along(jnp.where(inner, middle, held(rest, first, after)))
-        from_across = across(held(first, middle, after), over_y)
+    for first, middle, rest in zip(mine_1, middle_3, other_half):
+        from_pair = along(jnp.where(inner, middle, held(rest, first, keep)))
+        from_across = across(held(first, middle, keep), over_y)
         arrived.append((from_pair, from_across))
 
+    small = (keep + held(other, *arrived[0])).astype(jnp.bfloat16)
     acts = call(
         load_kernel,
         pltpu.VMEM(acts.shape, acts.dtype),
@@ -370,7 +371,7 @@
         scratch_shapes=[pltpu.SemaphoreType.DMA((8,))],
     )
     acts = in_vmem(acts)
-    ready = [chunk for both in arrived for chunk in both] + [acts]
+    ready = [chunk for both in arrived for chunk in both] + [small, acts]
     mine_2 = jnp.concatenate(
         [jnp.where(inner, held(there, *ready), here) for here, there in arrived], axis=1
     )
@@ -380,7 +381,6 @@
     theirs_2 = swapped(mine_2)
     mine_3 = along(mine_2)
 
-    small = (keep + held(other, mine_2)).astype(jnp.bfloat16)
     in_query, out_query, grad_half = small[:rows], small[rows:split], small[split:]
     packs = by_distance(jnp.concatenate([in_query, eigvals], axis=1))
     grad_other = lax.ppermute(grad_half, "rep", pair)

time: 63.6 us -> 61.3 us (0.964)
  starting transfers between devices: 24.9 us -> 24 us
  waiting for transfers between devices: 8.6 us -> 7.85 us
  blocking collectives: 10.4 us -> 9.73 us
    ppermute x3, waiting for transfers between devices: 4.35 us -> 0.01 us  [by_distance(): lax.ppermute(value, axis, [(i, i ^ k) for i in range(size)])]
    ppermute x6, waiting for transfers between devices: 1.62 us -> 5.68 us  [along(): return lax.ppermute(value, 'blk', [(i, i ^ 1) for i in range(4)])]
    ppermute x1, waiting for transfers between devices: 0.01 us -> 1.09 us  [stepped_scores(): other = lax.ppermute(send, 'rep', pair)]
    ppermute x2, waiting for transfers between devices: 1.78 us -> 0.71 us  [swapped(): return lax.ppermute(value, 'groups', pair)]
    ppermute x3, starting transfers between devices: 5.43 us -> 4.45 us  [by_distance(): lax.ppermute(value, axis, [(i, i ^ k) for i in range(size)])]
    ppermute x1, waiting for transfers between devices: 0.84 us -> 0.01 us  [stepped_scores(): other = lax.ppermute(keep, 'eig', pair)]
    all_to_all x1, blocking collectives: 10.4 us -> 9.73 us  [on_device(): parts = lax.all_to_all(parts, ('blk', 'eig', 'rep'), 0, 0, tiled=True)]
    ppermute x2, starting transfers between devices: 2.17 us -> 2.81 us  [swapped(): return lax.ppermute(value, 'groups', pair)]
  transfers between devices with their start and end apart: 18 -> 18, of which waited for: 5 -> 6; matrix products, arithmetic and copies ran while one was open for 1% -> 1% of each run, Pallas kernels for 23% -> 24%
where the time goes in v15:
time: 61.3 us; the launch traced here: 61.1 us
  starting transfers between devices  24 us (39%)
  Pallas kernels  18.3 us (30%)
  blocking collectives  9.73 us (16%)
  waiting for transfers between devices  7.85 us (13%)
  other arithmetic  0.93 us (2%)
    pallas_call x5, Pallas kernels, call(): pl.pallas_call(kernel, out_shape=out_shape, compiler_params=pltpu.Compile...  12.7 us
    ppermute x6, starting transfers between devices, along(): return lax.ppermute(value, 'blk', [(i, i ^ 1) for i in range(4)])  11.5 us
    all_to_all x1, blocking collectives, on_device(): parts = lax.all_to_all(parts, ('blk', 'eig', 'rep'), 0, 0, tiled=True)  9.73 us
    ppermute x6, waiting for transfers between devices, along(): return lax.ppermute(value, 'blk', [(i, i ^ 1) for i in range(4)])  5.68 us
    ppermute x3, starting transfers between devices, by_distance(): lax.ppermute(value, axis, [(i, i ^ k) for i in range(size)])  4.45 us
    pallas_call x1, Pallas kernels, small_parts(): pl.pallas_call(parts_kernel, in_specs=[pl.BlockSpec(memory_space=pl.ANY)]...  4.34 us
    ppermute x4, starting transfers between devices, across(): lax.ppermute(value, AXES, pairing(lambda g, b, e, r: (g, 3 - b, e, r) if...  3.04 us
    ppermute x2, starting transfers between devices, swapped(): return lax.ppermute(value, 'groups', pair)  2.81 us
  transfers between devices with their start and end apart: 18, of which 6 were waited for; matrix products, arithmetic and copies ran while one was open for 1% of the time, Pallas kernels for 24%

profile of v15, /device:TPU:0, one launch (start us, length us, event | category | flops | bytes accessed | tf_op | source)
XLA Modules:
  0.0 61.1 jit_solution(1635821138876371438)
XLA Ops:
  0.0 1.3 %shard_map.91 = (bf16[64,1792]{1,0:T(8,128)(2,1)S(1)}, bf16[64,1792]{1,0:T(8,128)(2,1)S(1)}, bf16[64,1792]{1,0:T(8,128)(2,1)S(1)}, bf16[64,1792]{1,0:T(8,128)(2,1)S(1)}) custom-call(bf16[64,7168]{1,0:T(8,128)(2,1)} %refs_2_), custom_call_target="tpu_custom_call" | custom-call | tf_op jit(solution)/shard_map/pallas_call | solution.py:86
  1.3 3.1 %collective-permute-start.1 = (bf16[64,1792]{1,0:T(8,128)(2,1)S(1)}, bf16[64,1792]{1,0:T(8,128)(2,1)S(1)}, u32[]{:S(2)}, u32[]{:S(2)}) collective-permute-start(bf16[64,1792]{1,0:T(8,128)(2,1)S(1)} %get-tuple-element.32.refs_0_), channel_id=1, source_target_pairs={{0,4},{4,0},{8,12},{12,8},{1,5},{5,1},{9,13},{13,9},{2,6},{6,2},{1... | collective-permute-start | bytes 688136 | tf_op jit(solution)/shard_map/ppermute | solution.py:331
  4.4 3.1 %collective-permute-start.6 = (bf16[64,1792]{1,0:T(8,128)(2,1)S(1)}, bf16[64,1792]{1,0:T(8,128)(2,1)S(1)}, u32[]{:S(2)}, u32[]{:S(2)}) collective-permute-start(bf16[64,1792]{1,0:T(8,128)(2,1)S(1)} %get-tuple-element.33.refs_1_), channel_id=1, source_target_pairs={{0,4},{4,0},{8,12},{12,8},{1,5},{5,1},{9,13},{13,9},{2,6},{6,2},{1... | collective-permute-start | bytes 688136 | tf_op jit(solution)/shard_map/ppermute | solution.py:331
  7.6 4.3 %shard_map.92 = (f32[576,128]{1,0:T(8,128)S(1)}, f32[576,128]{1,0:T(8,128)S(1)}) custom-call(bf16[128,2048]{1,0:T(8,128)(2,1)} %refs_0_.1, bf16[2048,128]{1,0:T(8,128)(2,1)} %refs_1_.1, bf16[64,7168]{1,0:T(8,128)(2,1)} %refs_2_, bf16[7168,128]{1,0:T(8,128)(2,1)} %refs_3_.1, bf16[768,2048]{1,0:T(8,128)(2,1)} %refs_4_.1), custom_call_target="tpu_custom_call" | custom-call | tf_op jit(solution)/shard_map/pallas_call | solution.py:154
  11.9 0.6 collective-permute-start
  12.5 0.1 select_reduce_fusion
  12.6 1.1 %collective-permute-done = f32[576,128]{1,0:T(8,128)S(1)} collective-permute-done((f32[576,128]{1,0:T(8,128)S(1)}, f32[576,128]{1,0:T(8,128)S(1)}, u32[]{:S(2)}, u32[]{:S(2)}) %collective-permute-start) | collective-permute-done | bytes 294944 | tf_op jit(solution)/shard_map/ppermute | solution.py:355
  13.7 1.6 %collective-permute-start.9 = (f32[576,128]{1,0:T(8,128)S(1)}, f32[576,128]{1,0:T(8,128)S(1)}, u32[]{:S(2)}, u32[]{:S(2)}) collective-permute-start(f32[576,128]{1,0:T(8,128)S(1)} %add.6), channel_id=1, source_target_pairs={{0,2},{2,0},{1,3},{3,1},{4,6},{6,4},{5,7},{7,5},{8,10},{10,8},{9,1... | collective-permute-start | bytes 884744 | tf_op jit(solution)/shard_map/ppermute | solution.py:357
  15.3 0.4 collective-permute-start.4
  15.7 1.5 %collective-permute-start.3 = (bf16[64,1792]{1,0:T(8,128)(2,1)S(1)}, bf16[64,1792]{1,0:T(8,128)(2,1)S(1)}, u32[]{:S(2)}, u32[]{:S(2)}) collective-permute-start(bf16[64,1792]{1,0:T(8,128)(2,1)S(1)} %collective-permute-done.1.refs_4_), channel_id=1, source_target_pairs={{0,16},{1,17},{2,18},{3,19},{4,8},{5,9},{6,10},{7,11},{8,4},{9,5},... | collective-permute-start | bytes 688136 | tf_op jit(solution)/shard_map/ppermute | solution.py:337
  17.3 0.0 copy-start
  17.3 0.7 %collective-permute-start.7 = (bf16[64,1792]{1,0:T(8,128)(2,1)S(1)}, bf16[64,1792]{1,0:T(8,128)(2,1)S(1)}, u32[]{:S(2)}, u32[]{:S(2)}) collective-permute-start(bf16[64,1792]{1,0:T(8,128)(2,1)S(1)} %broadcast_select_fusion.4), channel_id=1, source_target_pairs={{0,4},{4,0},{8,12},{12,8},{1,5},{5,1},{9,13},{13,9},{2,6},{6,2},{1... | collective-permute-start | bytes 688136 | tf_op jit(solution)/shard_map/ppermute | solution.py:331
  18.0 1.5 %collective-permute-start.8 = (bf16[64,1792]{1,0:T(8,128)(2,1)S(1)}, bf16[64,1792]{1,0:T(8,128)(2,1)S(1)}, u32[]{:S(2)}, u32[]{:S(2)}) collective-permute-start(bf16[64,1792]{1,0:T(8,128)(2,1)S(1)} %collective-permute-done.6.refs_5_), channel_id=1, source_target_pairs={{0,16},{1,17},{2,18},{3,19},{4,8},{5,9},{6,10},{7,11},{8,4},{9,5},... | collective-permute-start | bytes 688136 | tf_op jit(solution)/shard_map/ppermute | solution.py:337
  19.5 4.2 %shard_map.93.acts_ref = bf16[768,7168]{1,0:T(8,128)(2,1)S(1)} custom-call(bf16[768,7168]{1,0:T(8,128)(2,1)} %source_ref), custom_call_target="tpu_custom_call" | custom-call | flops 1 | bytes 1 | tf_op jit(solution)/shard_map/pallas_call | solution.py:284
  23.7 0.1 collective-permute-done.4
  23.9 0.4 collective-permute-done.3
  24.3 1.8 %collective-permute-start.11 = (bf16[64,256]{1,0:T(8,128)(2,1)S(1)}, bf16[64,256]{1,0:T(8,128)(2,1)S(1)}, u32[]{:S(2)}, u32[]{:S(2)}) collective-permute-start(bf16[64,256]{1,0:T(8,128)(2,1)S(1)} %pad_maximum_fusion.2.refs_0_), channel_id=1, source_target_pairs={{0,4},{4,0},{8,12},{12,8},{1,5},{5,1},{9,13},{13,9},{2,6},{6,2},{1... | collective-permute-start | bytes 98312 | tf_op jit(solution)/shard_map/ppermute | solution.py:46
  26.1 1.9 %collective-permute-start.12 = (bf16[64,256]{1,0:T(8,128)(2,1)S(1)}, bf16[64,256]{1,0:T(8,128)(2,1)S(1)}, u32[]{:S(2)}, u32[]{:S(2)}) collective-permute-start(bf16[64,256]{1,0:T(8,128)(2,1)S(1)} %pad_maximum_fusion.2.refs_0_), channel_id=1, source_target_pairs={{0,8},{4,12},{8,0},{12,4},{1,9},{5,13},{9,1},{13,5},{2,10},{6,14},... | collective-permute-start | bytes 98312 | tf_op jit(solution)/shard_map/ppermute | solution.py:46
  28.0 0.8 %collective-permute-start.13 = (bf16[64,256]{1,0:T(8,128)(2,1)S(1)}, bf16[64,256]{1,0:T(8,128)(2,1)S(1)}, u32[]{:S(2)}, u32[]{:S(2)}) collective-permute-start(bf16[64,256]{1,0:T(8,128)(2,1)S(1)} %pad_maximum_fusion.2.refs_0_), channel_id=1, source_target_pairs={{0,12},{4,8},{8,4},{12,0},{1,13},{5,9},{9,5},{13,1},{2,14},{6,10},... | collective-permute-start | bytes 98312 | tf_op jit(solution)/shard_map/ppermute | solution.py:46
  28.9 2.6 %collective-permute-start.15 = (bf16[64,3584]{1,0:T(8,128)(2,1)S(1)}, bf16[64,3584]{1,0:T(8,128)(2,1)S(1)}, u32[]{:S(2)}, u32[]{:S(2)}) collective-permute-start(bf16[64,3584]{1,0:T(8,128)(2,1)S(1)} %pad_maximum_fusion.mine_2_ref), channel_id=1, source_target_pairs={{0,4},{4,0},{8,12},{12,8},{1,5},{5,1},{9,13},{13,9},{2,6},{6,2},{1... | collective-permute-start | bytes 1376264 | tf_op jit(solution)/shard_map/ppermute | solution.py:331
  31.5 1.5 %collective-permute-start.10 = (bf16[64,3584]{1,0:T(8,128)(2,1)S(1)}, bf16[64,3584]{1,0:T(8,128)(2,1)S(1)}, u32[]{:S(2)}, u32[]{:S(2)}) collective-permute-start(bf16[64,3584]{1,0:T(8,128)(2,1)S(1)} %pad_maximum_fusion.mine_2_ref), channel_id=1, source_target_pairs={{0,16},{16,0},{1,17},{17,1},{2,18},{18,2},{3,19},{19,3},{4,20},{20... | collective-permute-start | bytes 1376264 | tf_op jit(solution)/shard_map/ppermute | solution.py:334
  33.0 3.0 %shard_map.94.first_ref = f32[768,128]{1,0:T(8,128)S(1)} custom-call(bf16[768,7168]{1,0:T(8,128)(2,1)S(1)} %shard_map.93.acts_ref, bf16[64,1792]{1,0:T(8,128)(2,1)S(1)} %get-tuple-element.32.refs_0_, bf16[64,1792]{1,0:T(8,128)(2,1)S(1)} %get-tuple-element.33.refs_1_, bf16[64,1792]{1,0:T(8,128)(2,1)S(1)} %get-tuple-element.42.refs_2_, ...), custom_call_target="tpu_custom_call" | custom-call | flops 1 | bytes 1 | tf_op jit(solution)/shard_map/pallas_call | solution.py:284
  36.1 0.5 shard_map.95.weights_ref
  36.5 4.2 %collective-permute-done.15.mine_3_ref = bf16[64,3584]{1,0:T(8,128)(2,1)S(1)} collective-permute-done((bf16[64,3584]{1,0:T(8,128)(2,1)S(1)}, bf16[64,3584]{1,0:T(8,128)(2,1)S(1)}, u32[]{:S(2)}, u32[]{:S(2)}) %collective-permute-start.15) | collective-permute-done | bytes 458784 | tf_op jit(solution)/shard_map/ppermute | solution.py:331
  40.8 1.3 %collective-permute-start.16 = (bf16[64,1792]{1,0:T(8,128)(2,1)S(1)}, bf16[64,1792]{1,0:T(8,128)(2,1)S(1)}, u32[]{:S(2)}, u32[]{:S(2)}) collective-permute-start(bf16[64,1792]{1,0:T(8,128)(2,1)S(1)} %slice.17), channel_id=1, source_target_pairs={{0,16},{16,0},{1,17},{17,1},{2,18},{18,2},{3,19},{19,3},{4,20},{20... | collective-permute-start | bytes 688136 | tf_op jit(solution)/shard_map/ppermute | solution.py:334
  42.1 1.6 %collective-permute-start.14 = (bf16[64,1792]{1,0:T(8,128)(2,1)S(1)}, bf16[64,1792]{1,0:T(8,128)(2,1)S(1)}, u32[]{:S(2)}, u32[]{:S(2)}) collective-permute-start(bf16[64,1792]{1,0:T(8,128)(2,1)S(1)} %slice.16), channel_id=1, source_target_pairs={{0,4},{4,0},{8,12},{12,8},{1,5},{5,1},{9,13},{13,9},{2,6},{6,2},{1... | collective-permute-start | bytes 688136 | tf_op jit(solution)/shard_map/ppermute | solution.py:331
  43.8 2.4 %shard_map.96 = (f32[768,128]{1,0:T(8,128)S(1)}, f32[768,512]{1,0:T(8,128)S(1)}, f32[8,512]{1,0:T(8,128)S(1)}) custom-call(bf16[768,7168]{1,0:T(8,128)(2,1)S(1)} %shard_map.93.acts_ref, bf16[64,3584]{1,0:T(8,128)(2,1)S(1)} %pad_maximum_fusion.mine_2_ref, bf16[64,3584]{1,0:T(8,128)(2,1)S(1)} %collective-permute-done.15.mine_3_ref, ...), custom_call_target="tpu_custom_call" | custom-call | flops 1 | bytes 1 | tf_op jit(solution)/shard_map/pallas_call | solution.py:284
  46.2 0.7 %collective-permute-done.16.right_ref = bf16[64,1792]{1,0:T(8,128)(2,1)S(1)} collective-permute-done((bf16[64,1792]{1,0:T(8,128)(2,1)S(1)}, bf16[64,1792]{1,0:T(8,128)(2,1)S(1)}, u32[]{:S(2)}, u32[]{:S(2)}) %collective-permute-start.16) | collective-permute-done | bytes 229408 | tf_op jit(solution)/shard_map/ppermute | solution.py:334
  46.9 1.3 %collective-permute-done.14.left_ref = bf16[64,1792]{1,0:T(8,128)(2,1)S(1)} collective-permute-done((bf16[64,1792]{1,0:T(8,128)(2,1)S(1)}, bf16[64,1792]{1,0:T(8,128)(2,1)S(1)}, u32[]{:S(2)}, u32[]{:S(2)}) %collective-permute-start.14) | collective-permute-done | bytes 229408 | tf_op jit(solution)/shard_map/ppermute | solution.py:331
  48.2 2.6 %shard_map.97 = f32[16,2]{1,0:T(8,128)S(1)} custom-call(bf16[768,7168]{1,0:T(8,128)(2,1)S(1)} %shard_map.93.acts_ref, bf16[64,3584]{1,0:T(8,128)(2,1)S(1)} %collective-permute-done.10.theirs_2_ref, bf16[64,1792]{1,0:T(8,128)(2,1)S(1)} %collective-permute-done.14.left_ref, bf16[64,1792]{1,0:T(8,128)(2,1)S(1)} %collective-permute-done.16.right_ref, ...), custom_call_target="tpu_custom_call" | custom-call | flops 1 | bytes 1 | tf_op jit(solution)/shard_map/pallas_call | solution.py:284
  50.8 9.7 %all_to_all.9 = f32[16,1,2]{2,1,0:T(1,128)S(1)} all-to-all(f32[16,1,2]{2,1,0:T(1,128)S(1)} %bitcast.4), channel_id=1, replica_groups=mesh['groups'=2,'blk'=4,'eig'=2,'rep'=2] {'blk','eig','rep'}, dimensions={0} | all-to-all | bytes 256 | tf_op jit(solution)/shard_map/all_to_all | solution.py:459
  60.5 0.5 reduce_sum.21
  (37 shorter events, 0.4 us)
Async XLA Ops:
  1.3 11.3 %collective-permute-start.1 = (bf16[64,1792]{1,0:T(8,128)(2,1)S(1)}, bf16[64,1792]{1,0:T(8,128)(2,1)S(1)}, u32[]{:S(2)}, u32[]{:S(2)}) collective-permute-start(bf16[64,1792]{1,0:T(8,128)(2,1)S(1)} %get-tuple-element.32.refs_0_), channel_id=1, source_target_pairs={{0,4},{4,0},{8,12},{12,8},{1,5},{5,1},{9,13},{13,9},{2,6},{6,2},{1... | collective-permute-start | bytes 688136 | tf_op jit(solution)/shard_map/ppermute | solution.py:331
  4.4 8.2 %collective-permute-start.2 = (bf16[64,1792]{1,0:T(8,128)(2,1)S(1)}, bf16[64,1792]{1,0:T(8,128)(2,1)S(1)}, u32[]{:S(2)}, u32[]{:S(2)}) collective-permute-start(bf16[64,1792]{1,0:T(8,128)(2,1)S(1)} %get-tuple-element.32.refs_0_), channel_id=1, source_target_pairs={{0,1},{1,0},{2,3},{3,2},{4,8},{5,9},{6,10},{7,11},{8,4},{9,5},{10,... | collective-permute-start | bytes 688136 | tf_op jit(solution)/shard_map/ppermute | solution.py:337
  4.4 12.8 %collective-permute-start.6 = (bf16[64,1792]{1,0:T(8,128)(2,1)S(1)}, bf16[64,1792]{1,0:T(8,128)(2,1)S(1)}, u32[]{:S(2)}, u32[]{:S(2)}) collective-permute-start(bf16[64,1792]{1,0:T(8,128)(2,1)S(1)} %get-tuple-element.33.refs_1_), channel_id=1, source_target_pairs={{0,4},{4,0},{8,12},{12,8},{1,5},{5,1},{9,13},{13,9},{2,6},{6,2},{1... | collective-permute-start | bytes 688136 | tf_op jit(solution)/shard_map/ppermute | solution.py:331
  7.6 9.7 %collective-permute-start.5 = (bf16[64,1792]{1,0:T(8,128)(2,1)S(1)}, bf16[64,1792]{1,0:T(8,128)(2,1)S(1)}, u32[]{:S(2)}, u32[]{:S(2)}) collective-permute-start(bf16[64,1792]{1,0:T(8,128)(2,1)S(1)} %get-tuple-element.33.refs_1_), channel_id=1, source_target_pairs={{0,1},{1,0},{2,3},{3,2},{4,8},{5,9},{6,10},{7,11},{8,4},{9,5},{10,... | collective-permute-start | bytes 688136 | tf_op jit(solution)/shard_map/ppermute | solution.py:337
  7.6 4.9 %copy-start.1 = (s32[768]{0:T(1024)S(1)}, s32[768]{0:T(1024)}, u32[]{:S(2)}) copy-start(s32[768]{0:T(1024)} %param.16) | copy-start | bytes 9220
  7.6 4.9 %copy-start.2 = (s32[8]{0:T(128)S(1)}, s32[8]{0:T(128)}, u32[]{:S(2)}) copy-start(s32[8]{0:T(128)} %param.17) | copy-start | bytes 100
  11.9 1.8 %collective-permute-start = (f32[576,128]{1,0:T(8,128)S(1)}, f32[576,128]{1,0:T(8,128)S(1)}, u32[]{:S(2)}, u32[]{:S(2)}) collective-permute-start(f32[576,128]{1,0:T(8,128)S(1)} %get-tuple-element.36), channel_id=1, source_target_pairs={{0,1},{1,0},{2,3},{3,2},{4,5},{5,4},{6,7},{7,6},{8,9},{9,8},{10,11... | collective-permute-start | bytes 884744 | tf_op jit(solution)/shard_map/ppermute | solution.py:355
  13.7 10.5 %collective-permute-start.9 = (f32[576,128]{1,0:T(8,128)S(1)}, f32[576,128]{1,0:T(8,128)S(1)}, u32[]{:S(2)}, u32[]{:S(2)}) collective-permute-start(f32[576,128]{1,0:T(8,128)S(1)} %add.6), channel_id=1, source_target_pairs={{0,2},{2,0},{1,3},{3,1},{4,6},{6,4},{5,7},{7,5},{8,10},{10,8},{9,1... | collective-permute-start | bytes 884744 | tf_op jit(solution)/shard_map/ppermute | solution.py:357
  15.3 8.5 %collective-permute-start.4 = (bf16[64,1792]{1,0:T(8,128)(2,1)S(1)}, bf16[64,1792]{1,0:T(8,128)(2,1)S(1)}, u32[]{:S(2)}, u32[]{:S(2)}) collective-permute-start(bf16[64,1792]{1,0:T(8,128)(2,1)S(1)} %broadcast_select_fusion.5), channel_id=1, source_target_pairs={{0,4},{4,0},{8,12},{12,8},{1,5},{5,1},{9,13},{13,9},{2,6},{6,2},{1... | collective-permute-start | bytes 688136 | tf_op jit(solution)/shard_map/ppermute | solution.py:331
  15.7 8.5 %collective-permute-start.3 = (bf16[64,1792]{1,0:T(8,128)(2,1)S(1)}, bf16[64,1792]{1,0:T(8,128)(2,1)S(1)}, u32[]{:S(2)}, u32[]{:S(2)}) collective-permute-start(bf16[64,1792]{1,0:T(8,128)(2,1)S(1)} %collective-permute-done.1.refs_4_), channel_id=1, source_target_pairs={{0,16},{1,17},{2,18},{3,19},{4,8},{5,9},{6,10},{7,11},{8,4},{9,5},... | collective-permute-start | bytes 688136 | tf_op jit(solution)/shard_map/ppermute | solution.py:337
  17.3 7.0 %copy-start = (bf16[64,128]{1,0:T(8,128)(2,1)S(1)}, bf16[64,128]{1,0:T(8,128)(2,1)}, u32[]{:S(2)}) copy-start(bf16[64,128]{1,0:T(8,128)(2,1)} %param.13) | copy-start | bytes 49156
  17.3 11.5 %collective-permute-start.7 = (bf16[64,1792]{1,0:T(8,128)(2,1)S(1)}, bf16[64,1792]{1,0:T(8,128)(2,1)S(1)}, u32[]{:S(2)}, u32[]{:S(2)}) collective-permute-start(bf16[64,1792]{1,0:T(8,128)(2,1)S(1)} %broadcast_select_fusion.4), channel_id=1, source_target_pairs={{0,4},{4,0},{8,12},{12,8},{1,5},{5,1},{9,13},{13,9},{2,6},{6,2},{1... | collective-permute-start | bytes 688136 | tf_op jit(solution)/shard_map/ppermute | solution.py:331
  18.0 10.8 %collective-permute-start.8 = (bf16[64,1792]{1,0:T(8,128)(2,1)S(1)}, bf16[64,1792]{1,0:T(8,128)(2,1)S(1)}, u32[]{:S(2)}, u32[]{:S(2)}) collective-permute-start(bf16[64,1792]{1,0:T(8,128)(2,1)S(1)} %collective-permute-done.6.refs_5_), channel_id=1, source_target_pairs={{0,16},{1,17},{2,18},{3,19},{4,8},{5,9},{6,10},{7,11},{8,4},{9,5},... | collective-permute-start | bytes 688136 | tf_op jit(solution)/shard_map/ppermute | solution.py:337
  24.3 8.7 %collective-permute-start.11 = (bf16[64,256]{1,0:T(8,128)(2,1)S(1)}, bf16[64,256]{1,0:T(8,128)(2,1)S(1)}, u32[]{:S(2)}, u32[]{:S(2)}) collective-permute-start(bf16[64,256]{1,0:T(8,128)(2,1)S(1)} %pad_maximum_fusion.2.refs_0_), channel_id=1, source_target_pairs={{0,4},{4,0},{8,12},{12,8},{1,5},{5,1},{9,13},{13,9},{2,6},{6,2},{1... | collective-permute-start | bytes 98312 | tf_op jit(solution)/shard_map/ppermute | solution.py:46
  26.1 10.0 %collective-permute-start.12 = (bf16[64,256]{1,0:T(8,128)(2,1)S(1)}, bf16[64,256]{1,0:T(8,128)(2,1)S(1)}, u32[]{:S(2)}, u32[]{:S(2)}) collective-permute-start(bf16[64,256]{1,0:T(8,128)(2,1)S(1)} %pad_maximum_fusion.2.refs_0_), channel_id=1, source_target_pairs={{0,8},{4,12},{8,0},{12,4},{1,9},{5,13},{9,1},{13,5},{2,10},{6,14},... | collective-permute-start | bytes 98312 | tf_op jit(solution)/shard_map/ppermute | solution.py:46
  28.0 8.1 %collective-permute-start.13 = (bf16[64,256]{1,0:T(8,128)(2,1)S(1)}, bf16[64,256]{1,0:T(8,128)(2,1)S(1)}, u32[]{:S(2)}, u32[]{:S(2)}) collective-permute-start(bf16[64,256]{1,0:T(8,128)(2,1)S(1)} %pad_maximum_fusion.2.refs_0_), channel_id=1, source_target_pairs={{0,12},{4,8},{8,4},{12,0},{1,13},{5,9},{9,5},{13,1},{2,14},{6,10},... | collective-permute-start | bytes 98312 | tf_op jit(solution)/shard_map/ppermute | solution.py:46
  28.9 11.9 %collective-permute-start.15 = (bf16[64,3584]{1,0:T(8,128)(2,1)S(1)}, bf16[64,3584]{1,0:T(8,128)(2,1)S(1)}, u32[]{:S(2)}, u32[]{:S(2)}) collective-permute-start(bf16[64,3584]{1,0:T(8,128)(2,1)S(1)} %pad_maximum_fusion.mine_2_ref), channel_id=1, source_target_pairs={{0,4},{4,0},{8,12},{12,8},{1,5},{5,1},{9,13},{13,9},{2,6},{6,2},{1... | collective-permute-start | bytes 1376264 | tf_op jit(solution)/shard_map/ppermute | solution.py:331
  31.5 10.6 %collective-permute-start.10 = (bf16[64,3584]{1,0:T(8,128)(2,1)S(1)}, bf16[64,3584]{1,0:T(8,128)(2,1)S(1)}, u32[]{:S(2)}, u32[]{:S(2)}) collective-permute-start(bf16[64,3584]{1,0:T(8,128)(2,1)S(1)} %pad_maximum_fusion.mine_2_ref), channel_id=1, source_target_pairs={{0,16},{16,0},{1,17},{17,1},{2,18},{18,2},{3,19},{19,3},{4,20},{20... | collective-permute-start | bytes 1376264 | tf_op jit(solution)/shard_map/ppermute | solution.py:334
  33.0 10.8 %collective-permute-start.17 = (bf16[384,128]{1,0:T(8,128)(2,1)S(1)}, bf16[384,128]{1,0:T(8,128)(2,1)S(1)}, u32[]{:S(2)}, u32[]{:S(2)}) collective-permute-start(bf16[384,128]{1,0:T(8,128)(2,1)S(1)} %slice.22), channel_id=1, source_target_pairs={{0,1},{1,0},{2,3},{3,2},{4,5},{5,4},{6,7},{7,6},{8,9},{9,8},{10,11... | collective-permute-start | bytes 294920 | tf_op jit(solution)/shard_map/ppermute | solution.py:386
  40.8 6.1 %collective-permute-start.16 = (bf16[64,1792]{1,0:T(8,128)(2,1)S(1)}, bf16[64,1792]{1,0:T(8,128)(2,1)S(1)}, u32[]{:S(2)}, u32[]{:S(2)}) collective-permute-start(bf16[64,1792]{1,0:T(8,128)(2,1)S(1)} %slice.17), channel_id=1, source_target_pairs={{0,16},{16,0},{1,17},{17,1},{2,18},{18,2},{3,19},{19,3},{4,20},{20... | collective-permute-start | bytes 688136 | tf_op jit(solution)/shard_map/ppermute | solution.py:334
  42.1 6.1 %collective-permute-start.14 = (bf16[64,1792]{1,0:T(8,128)(2,1)S(1)}, bf16[64,1792]{1,0:T(8,128)(2,1)S(1)}, u32[]{:S(2)}, u32[]{:S(2)}) collective-permute-start(bf16[64,1792]{1,0:T(8,128)(2,1)S(1)} %slice.16), channel_id=1, source_target_pairs={{0,4},{4,0},{8,12},{12,8},{1,5},{5,1},{9,13},{13,9},{2,6},{6,2},{1... | collective-permute-start | bytes 688136 | tf_op jit(solution)/shard_map/ppermute | solution.py:331

commit v16 on v15

--- a/solution.py
+++ b/solution.py
@@ -187,9 +187,12 @@
     return contract_last(grad_ref[pl.ds(start, BLOCK), :], weights)
 
 
-def mix(start, projected, mixed, onehot_ref):
+def mix(start, projected, mixed, onehot_ref, once=False):
     product = jnp.concatenate([projected] * (mixed.shape[1] // LANES), axis=1) * mixed
     high = product.astype(jnp.bfloat16)
+    onehot = onehot_ref[:, pl.ds(start, BLOCK)]
+    if once:
+        return jnp.dot(onehot, high, preferred_element_type=jnp.float32)
     low = (product - high.astype(jnp.float32)).astype(jnp.bfloat16)
     onehot = onehot_ref[:, pl.ds(start, BLOCK)]
     return jnp.dot(onehot, high, preferred_element_type=jnp.float32) + jnp.dot(
@@ -266,7 +269,7 @@
         total = total + project(
             acts_ref, start, (theirs_2_ref.at[:, cut:], right_ref), other, cut
         )
-        return sums + mix(start, total, mixed_ref[pl.ds(start, BLOCK), :], onehot_ref)
+        return sums + mix(start, total, mixed_ref[pl.ds(start, BLOCK), :], onehot_ref, once=True)
 
     sums = blocks(acts_ref.shape[0], body, before_ref[...])
     width = sums.shape[1]

time: 61.3 us -> 61 us (level)
  no operation moved by 1% of the time
where the time goes in v16:
time: 61 us; the launch traced here: 60.8 us
  starting transfers between devices  24 us (39%)
  Pallas kernels  18.1 us (30%)
  blocking collectives  9.72 us (16%)
  waiting for transfers between devices  7.85 us (13%)
  other arithmetic  0.93 us (2%)
    pallas_call x5, Pallas kernels, call(): pl.pallas_call(kernel, out_shape=out_shape, compiler_params=pltpu.Compile...  12.4 us
    ppermute x6, starting transfers between devices, along(): return lax.ppermute(value, 'blk', [(i, i ^ 1) for i in range(4)])  11.5 us
    all_to_all x1, blocking collectives, on_device(): parts = lax.all_to_all(parts, ('blk', 'eig', 'rep'), 0, 0, tiled=True)  9.72 us
    ppermute x6, waiting for transfers between devices, along(): return lax.ppermute(value, 'blk', [(i, i ^ 1) for i in range(4)])  5.68 us
    ppermute x3, starting transfers between devices, by_distance(): lax.ppermute(value, axis, [(i, i ^ k) for i in range(size)])  4.45 us
    pallas_call x1, Pallas kernels, small_parts(): pl.pallas_call(parts_kernel, in_specs=[pl.BlockSpec(memory_space=pl.ANY)]...  4.34 us
    ppermute x4, starting transfers between devices, across(): lax.ppermute(value, AXES, pairing(lambda g, b, e, r: (g, 3 - b, e, r) if...  3.04 us
    ppermute x2, starting transfers between devices, swapped(): return lax.ppermute(value, 'groups', pair)  2.81 us
  transfers between devices with their start and end apart: 18, of which 6 were waited for; matrix products, arithmetic and copies ran while one was open for 1% of the time, Pallas kernels for 24%

profile of v16, /device:TPU:0, one launch (start us, length us, event | category | flops | bytes accessed | tf_op | source)
XLA Modules:
  0.0 60.8 jit_solution(12266887436245670028)
XLA Ops:
  0.0 1.3 %shard_map.91 = (bf16[64,1792]{1,0:T(8,128)(2,1)S(1)}, bf16[64,1792]{1,0:T(8,128)(2,1)S(1)}, bf16[64,1792]{1,0:T(8,128)(2,1)S(1)}, bf16[64,1792]{1,0:T(8,128)(2,1)S(1)}) custom-call(bf16[64,7168]{1,0:T(8,128)(2,1)} %refs_2_), custom_call_target="tpu_custom_call" | custom-call | tf_op jit(solution)/shard_map/pallas_call | solution.py:86
  1.3 3.1 %collective-permute-start.1 = (bf16[64,1792]{1,0:T(8,128)(2,1)S(1)}, bf16[64,1792]{1,0:T(8,128)(2,1)S(1)}, u32[]{:S(2)}, u32[]{:S(2)}) collective-permute-start(bf16[64,1792]{1,0:T(8,128)(2,1)S(1)} %get-tuple-element.32.refs_0_), channel_id=1, source_target_pairs={{0,4},{4,0},{8,12},{12,8},{1,5},{5,1},{9,13},{13,9},{2,6},{6,2},{1... | collective-permute-start | bytes 688136 | tf_op jit(solution)/shard_map/ppermute | solution.py:334
  4.4 3.1 %collective-permute-start.6 = (bf16[64,1792]{1,0:T(8,128)(2,1)S(1)}, bf16[64,1792]{1,0:T(8,128)(2,1)S(1)}, u32[]{:S(2)}, u32[]{:S(2)}) collective-permute-start(bf16[64,1792]{1,0:T(8,128)(2,1)S(1)} %get-tuple-element.33.refs_1_), channel_id=1, source_target_pairs={{0,4},{4,0},{8,12},{12,8},{1,5},{5,1},{9,13},{13,9},{2,6},{6,2},{1... | collective-permute-start | bytes 688136 | tf_op jit(solution)/shard_map/ppermute | solution.py:334
  7.6 4.3 %shard_map.92 = (f32[576,128]{1,0:T(8,128)S(1)}, f32[576,128]{1,0:T(8,128)S(1)}) custom-call(bf16[128,2048]{1,0:T(8,128)(2,1)} %refs_0_.1, bf16[2048,128]{1,0:T(8,128)(2,1)} %refs_1_.1, bf16[64,7168]{1,0:T(8,128)(2,1)} %refs_2_, bf16[7168,128]{1,0:T(8,128)(2,1)} %refs_3_.1, bf16[768,2048]{1,0:T(8,128)(2,1)} %refs_4_.1), custom_call_target="tpu_custom_call" | custom-call | tf_op jit(solution)/shard_map/pallas_call | solution.py:154
  11.9 0.6 collective-permute-start
  12.5 0.1 select_reduce_fusion
  12.6 1.1 %collective-permute-done = f32[576,128]{1,0:T(8,128)S(1)} collective-permute-done((f32[576,128]{1,0:T(8,128)S(1)}, f32[576,128]{1,0:T(8,128)S(1)}, u32[]{:S(2)}, u32[]{:S(2)}) %collective-permute-start) | collective-permute-done | bytes 294944 | tf_op jit(solution)/shard_map/ppermute | solution.py:358
  13.7 1.6 %collective-permute-start.9 = (f32[576,128]{1,0:T(8,128)S(1)}, f32[576,128]{1,0:T(8,128)S(1)}, u32[]{:S(2)}, u32[]{:S(2)}) collective-permute-start(f32[576,128]{1,0:T(8,128)S(1)} %add.6), channel_id=1, source_target_pairs={{0,2},{2,0},{1,3},{3,1},{4,6},{6,4},{5,7},{7,5},{8,10},{10,8},{9,1... | collective-permute-start | bytes 884744 | tf_op jit(solution)/shard_map/ppermute | solution.py:360
  15.3 0.4 collective-permute-start.4
  15.7 1.5 %collective-permute-start.3 = (bf16[64,1792]{1,0:T(8,128)(2,1)S(1)}, bf16[64,1792]{1,0:T(8,128)(2,1)S(1)}, u32[]{:S(2)}, u32[]{:S(2)}) collective-permute-start(bf16[64,1792]{1,0:T(8,128)(2,1)S(1)} %collective-permute-done.1.refs_4_), channel_id=1, source_target_pairs={{0,16},{1,17},{2,18},{3,19},{4,8},{5,9},{6,10},{7,11},{8,4},{9,5},... | collective-permute-start | bytes 688136 | tf_op jit(solution)/shard_map/ppermute | solution.py:340
  17.3 0.0 copy-start
  17.3 0.7 %collective-permute-start.7 = (bf16[64,1792]{1,0:T(8,128)(2,1)S(1)}, bf16[64,1792]{1,0:T(8,128)(2,1)S(1)}, u32[]{:S(2)}, u32[]{:S(2)}) collective-permute-start(bf16[64,1792]{1,0:T(8,128)(2,1)S(1)} %broadcast_select_fusion.4), channel_id=1, source_target_pairs={{0,4},{4,0},{8,12},{12,8},{1,5},{5,1},{9,13},{13,9},{2,6},{6,2},{1... | collective-permute-start | bytes 688136 | tf_op jit(solution)/shard_map/ppermute | solution.py:334
  18.0 1.5 %collective-permute-start.8 = (bf16[64,1792]{1,0:T(8,128)(2,1)S(1)}, bf16[64,1792]{1,0:T(8,128)(2,1)S(1)}, u32[]{:S(2)}, u32[]{:S(2)}) collective-permute-start(bf16[64,1792]{1,0:T(8,128)(2,1)S(1)} %collective-permute-done.6.refs_5_), channel_id=1, source_target_pairs={{0,16},{1,17},{2,18},{3,19},{4,8},{5,9},{6,10},{7,11},{8,4},{9,5},... | collective-permute-start | bytes 688136 | tf_op jit(solution)/shard_map/ppermute | solution.py:340
  19.5 4.2 %shard_map.93.acts_ref = bf16[768,7168]{1,0:T(8,128)(2,1)S(1)} custom-call(bf16[768,7168]{1,0:T(8,128)(2,1)} %source_ref), custom_call_target="tpu_custom_call" | custom-call | flops 1 | bytes 1 | tf_op jit(solution)/shard_map/pallas_call | solution.py:287
  23.7 0.1 collective-permute-done.4
  23.9 0.4 collective-permute-done.3
  24.3 1.8 %collective-permute-start.11 = (bf16[64,256]{1,0:T(8,128)(2,1)S(1)}, bf16[64,256]{1,0:T(8,128)(2,1)S(1)}, u32[]{:S(2)}, u32[]{:S(2)}) collective-permute-start(bf16[64,256]{1,0:T(8,128)(2,1)S(1)} %pad_maximum_fusion.2.refs_0_), channel_id=1, source_target_pairs={{0,4},{4,0},{8,12},{12,8},{1,5},{5,1},{9,13},{13,9},{2,6},{6,2},{1... | collective-permute-start | bytes 98312 | tf_op jit(solution)/shard_map/ppermute | solution.py:46
  26.1 1.9 %collective-permute-start.12 = (bf16[64,256]{1,0:T(8,128)(2,1)S(1)}, bf16[64,256]{1,0:T(8,128)(2,1)S(1)}, u32[]{:S(2)}, u32[]{:S(2)}) collective-permute-start(bf16[64,256]{1,0:T(8,128)(2,1)S(1)} %pad_maximum_fusion.2.refs_0_), channel_id=1, source_target_pairs={{0,8},{4,12},{8,0},{12,4},{1,9},{5,13},{9,1},{13,5},{2,10},{6,14},... | collective-permute-start | bytes 98312 | tf_op jit(solution)/shard_map/ppermute | solution.py:46
  28.0 0.8 %collective-permute-start.13 = (bf16[64,256]{1,0:T(8,128)(2,1)S(1)}, bf16[64,256]{1,0:T(8,128)(2,1)S(1)}, u32[]{:S(2)}, u32[]{:S(2)}) collective-permute-start(bf16[64,256]{1,0:T(8,128)(2,1)S(1)} %pad_maximum_fusion.2.refs_0_), channel_id=1, source_target_pairs={{0,12},{4,8},{8,4},{12,0},{1,13},{5,9},{9,5},{13,1},{2,14},{6,10},... | collective-permute-start | bytes 98312 | tf_op jit(solution)/shard_map/ppermute | solution.py:46
  28.9 2.6 %collective-permute-start.15 = (bf16[64,3584]{1,0:T(8,128)(2,1)S(1)}, bf16[64,3584]{1,0:T(8,128)(2,1)S(1)}, u32[]{:S(2)}, u32[]{:S(2)}) collective-permute-start(bf16[64,3584]{1,0:T(8,128)(2,1)S(1)} %pad_maximum_fusion.mine_2_ref), channel_id=1, source_target_pairs={{0,4},{4,0},{8,12},{12,8},{1,5},{5,1},{9,13},{13,9},{2,6},{6,2},{1... | collective-permute-start | bytes 1376264 | tf_op jit(solution)/shard_map/ppermute | solution.py:334
  31.5 1.5 %collective-permute-start.10 = (bf16[64,3584]{1,0:T(8,128)(2,1)S(1)}, bf16[64,3584]{1,0:T(8,128)(2,1)S(1)}, u32[]{:S(2)}, u32[]{:S(2)}) collective-permute-start(bf16[64,3584]{1,0:T(8,128)(2,1)S(1)} %pad_maximum_fusion.mine_2_ref), channel_id=1, source_target_pairs={{0,16},{16,0},{1,17},{17,1},{2,18},{18,2},{3,19},{19,3},{4,20},{20... | collective-permute-start | bytes 1376264 | tf_op jit(solution)/shard_map/ppermute | solution.py:337
  33.0 3.0 %shard_map.94.first_ref = f32[768,128]{1,0:T(8,128)S(1)} custom-call(bf16[768,7168]{1,0:T(8,128)(2,1)S(1)} %shard_map.93.acts_ref, bf16[64,1792]{1,0:T(8,128)(2,1)S(1)} %get-tuple-element.32.refs_0_, bf16[64,1792]{1,0:T(8,128)(2,1)S(1)} %get-tuple-element.33.refs_1_, bf16[64,1792]{1,0:T(8,128)(2,1)S(1)} %get-tuple-element.42.refs_2_, ...), custom_call_target="tpu_custom_call" | custom-call | flops 1 | bytes 1 | tf_op jit(solution)/shard_map/pallas_call | solution.py:287
  36.1 0.5 shard_map.95.weights_ref
  36.5 4.2 %collective-permute-done.15.mine_3_ref = bf16[64,3584]{1,0:T(8,128)(2,1)S(1)} collective-permute-done((bf16[64,3584]{1,0:T(8,128)(2,1)S(1)}, bf16[64,3584]{1,0:T(8,128)(2,1)S(1)}, u32[]{:S(2)}, u32[]{:S(2)}) %collective-permute-start.15) | collective-permute-done | bytes 458784 | tf_op jit(solution)/shard_map/ppermute | solution.py:334
  40.8 1.3 %collective-permute-start.16 = (bf16[64,1792]{1,0:T(8,128)(2,1)S(1)}, bf16[64,1792]{1,0:T(8,128)(2,1)S(1)}, u32[]{:S(2)}, u32[]{:S(2)}) collective-permute-start(bf16[64,1792]{1,0:T(8,128)(2,1)S(1)} %slice.17), channel_id=1, source_target_pairs={{0,16},{16,0},{1,17},{17,1},{2,18},{18,2},{3,19},{19,3},{4,20},{20... | collective-permute-start | bytes 688136 | tf_op jit(solution)/shard_map/ppermute | solution.py:337
  42.1 1.6 %collective-permute-start.14 = (bf16[64,1792]{1,0:T(8,128)(2,1)S(1)}, bf16[64,1792]{1,0:T(8,128)(2,1)S(1)}, u32[]{:S(2)}, u32[]{:S(2)}) collective-permute-start(bf16[64,1792]{1,0:T(8,128)(2,1)S(1)} %slice.16), channel_id=1, source_target_pairs={{0,4},{4,0},{8,12},{12,8},{1,5},{5,1},{9,13},{13,9},{2,6},{6,2},{1... | collective-permute-start | bytes 688136 | tf_op jit(solution)/shard_map/ppermute | solution.py:334
  43.8 2.4 %shard_map.96 = (f32[768,128]{1,0:T(8,128)S(1)}, f32[768,512]{1,0:T(8,128)S(1)}, f32[8,512]{1,0:T(8,128)S(1)}) custom-call(bf16[768,7168]{1,0:T(8,128)(2,1)S(1)} %shard_map.93.acts_ref, bf16[64,3584]{1,0:T(8,128)(2,1)S(1)} %pad_maximum_fusion.mine_2_ref, bf16[64,3584]{1,0:T(8,128)(2,1)S(1)} %collective-permute-done.15.mine_3_ref, ...), custom_call_target="tpu_custom_call" | custom-call | flops 1 | bytes 1 | tf_op jit(solution)/shard_map/pallas_call | solution.py:287
  46.2 0.7 %collective-permute-done.16.right_ref = bf16[64,1792]{1,0:T(8,128)(2,1)S(1)} collective-permute-done((bf16[64,1792]{1,0:T(8,128)(2,1)S(1)}, bf16[64,1792]{1,0:T(8,128)(2,1)S(1)}, u32[]{:S(2)}, u32[]{:S(2)}) %collective-permute-start.16) | collective-permute-done | bytes 229408 | tf_op jit(solution)/shard_map/ppermute | solution.py:337
  46.9 1.3 %collective-permute-done.14.left_ref = bf16[64,1792]{1,0:T(8,128)(2,1)S(1)} collective-permute-done((bf16[64,1792]{1,0:T(8,128)(2,1)S(1)}, bf16[64,1792]{1,0:T(8,128)(2,1)S(1)}, u32[]{:S(2)}, u32[]{:S(2)}) %collective-permute-start.14) | collective-permute-done | bytes 229408 | tf_op jit(solution)/shard_map/ppermute | solution.py:334
  48.2 2.3 %shard_map.97 = f32[16,2]{1,0:T(8,128)S(1)} custom-call(bf16[768,7168]{1,0:T(8,128)(2,1)S(1)} %shard_map.93.acts_ref, bf16[64,3584]{1,0:T(8,128)(2,1)S(1)} %collective-permute-done.10.theirs_2_ref, bf16[64,1792]{1,0:T(8,128)(2,1)S(1)} %collective-permute-done.14.left_ref, bf16[64,1792]{1,0:T(8,128)(2,1)S(1)} %collective-permute-done.16.right_ref, ...), custom_call_target="tpu_custom_call" | custom-call | flops 1 | bytes 1 | tf_op jit(solution)/shard_map/pallas_call | solution.py:287
  50.5 9.7 %all_to_all.9 = f32[16,1,2]{2,1,0:T(1,128)S(1)} all-to-all(f32[16,1,2]{2,1,0:T(1,128)S(1)} %bitcast.4), channel_id=1, replica_groups=mesh['groups'=2,'blk'=4,'eig'=2,'rep'=2] {'blk','eig','rep'}, dimensions={0} | all-to-all | bytes 256 | tf_op jit(solution)/shard_map/all_to_all | solution.py:462
  60.2 0.5 reduce_sum.21
  (37 shorter events, 0.4 us)
Async XLA Ops:
  1.3 11.3 %collective-permute-start.1 = (bf16[64,1792]{1,0:T(8,128)(2,1)S(1)}, bf16[64,1792]{1,0:T(8,128)(2,1)S(1)}, u32[]{:S(2)}, u32[]{:S(2)}) collective-permute-start(bf16[64,1792]{1,0:T(8,128)(2,1)S(1)} %get-tuple-element.32.refs_0_), channel_id=1, source_target_pairs={{0,4},{4,0},{8,12},{12,8},{1,5},{5,1},{9,13},{13,9},{2,6},{6,2},{1... | collective-permute-start | bytes 688136 | tf_op jit(solution)/shard_map/ppermute | solution.py:334
  4.4 8.2 %collective-permute-start.2 = (bf16[64,1792]{1,0:T(8,128)(2,1)S(1)}, bf16[64,1792]{1,0:T(8,128)(2,1)S(1)}, u32[]{:S(2)}, u32[]{:S(2)}) collective-permute-start(bf16[64,1792]{1,0:T(8,128)(2,1)S(1)} %get-tuple-element.32.refs_0_), channel_id=1, source_target_pairs={{0,1},{1,0},{2,3},{3,2},{4,8},{5,9},{6,10},{7,11},{8,4},{9,5},{10,... | collective-permute-start | bytes 688136 | tf_op jit(solution)/shard_map/ppermute | solution.py:340
  4.4 12.8 %collective-permute-start.6 = (bf16[64,1792]{1,0:T(8,128)(2,1)S(1)}, bf16[64,1792]{1,0:T(8,128)(2,1)S(1)}, u32[]{:S(2)}, u32[]{:S(2)}) collective-permute-start(bf16[64,1792]{1,0:T(8,128)(2,1)S(1)} %get-tuple-element.33.refs_1_), channel_id=1, source_target_pairs={{0,4},{4,0},{8,12},{12,8},{1,5},{5,1},{9,13},{13,9},{2,6},{6,2},{1... | collective-permute-start | bytes 688136 | tf_op jit(solution)/shard_map/ppermute | solution.py:334
  7.6 9.7 %collective-permute-start.5 = (bf16[64,1792]{1,0:T(8,128)(2,1)S(1)}, bf16[64,1792]{1,0:T(8,128)(2,1)S(1)}, u32[]{:S(2)}, u32[]{:S(2)}) collective-permute-start(bf16[64,1792]{1,0:T(8,128)(2,1)S(1)} %get-tuple-element.33.refs_1_), channel_id=1, source_target_pairs={{0,1},{1,0},{2,3},{3,2},{4,8},{5,9},{6,10},{7,11},{8,4},{9,5},{10,... | collective-permute-start | bytes 688136 | tf_op jit(solution)/shard_map/ppermute | solution.py:340
  7.6 4.9 %copy-start.1 = (s32[768]{0:T(1024)S(1)}, s32[768]{0:T(1024)}, u32[]{:S(2)}) copy-start(s32[768]{0:T(1024)} %param.16) | copy-start | bytes 9220
  7.6 4.9 %copy-start.2 = (s32[8]{0:T(128)S(1)}, s32[8]{0:T(128)}, u32[]{:S(2)}) copy-start(s32[8]{0:T(128)} %param.17) | copy-start | bytes 100
  11.9 1.8 %collective-permute-start = (f32[576,128]{1,0:T(8,128)S(1)}, f32[576,128]{1,0:T(8,128)S(1)}, u32[]{:S(2)}, u32[]{:S(2)}) collective-permute-start(f32[576,128]{1,0:T(8,128)S(1)} %get-tuple-element.36), channel_id=1, source_target_pairs={{0,1},{1,0},{2,3},{3,2},{4,5},{5,4},{6,7},{7,6},{8,9},{9,8},{10,11... | collective-permute-start | bytes 884744 | tf_op jit(solution)/shard_map/ppermute | solution.py:358
  13.7 10.5 %collective-permute-start.9 = (f32[576,128]{1,0:T(8,128)S(1)}, f32[576,128]{1,0:T(8,128)S(1)}, u32[]{:S(2)}, u32[]{:S(2)}) collective-permute-start(f32[576,128]{1,0:T(8,128)S(1)} %add.6), channel_id=1, source_target_pairs={{0,2},{2,0},{1,3},{3,1},{4,6},{6,4},{5,7},{7,5},{8,10},{10,8},{9,1... | collective-permute-start | bytes 884744 | tf_op jit(solution)/shard_map/ppermute | solution.py:360
  15.3 8.5 %collective-permute-start.4 = (bf16[64,1792]{1,0:T(8,128)(2,1)S(1)}, bf16[64,1792]{1,0:T(8,128)(2,1)S(1)}, u32[]{:S(2)}, u32[]{:S(2)}) collective-permute-start(bf16[64,1792]{1,0:T(8,128)(2,1)S(1)} %broadcast_select_fusion.5), channel_id=1, source_target_pairs={{0,4},{4,0},{8,12},{12,8},{1,5},{5,1},{9,13},{13,9},{2,6},{6,2},{1... | collective-permute-start | bytes 688136 | tf_op jit(solution)/shard_map/ppermute | solution.py:334
  15.7 8.5 %collective-permute-start.3 = (bf16[64,1792]{1,0:T(8,128)(2,1)S(1)}, bf16[64,1792]{1,0:T(8,128)(2,1)S(1)}, u32[]{:S(2)}, u32[]{:S(2)}) collective-permute-start(bf16[64,1792]{1,0:T(8,128)(2,1)S(1)} %collective-permute-done.1.refs_4_), channel_id=1, source_target_pairs={{0,16},{1,17},{2,18},{3,19},{4,8},{5,9},{6,10},{7,11},{8,4},{9,5},... | collective-permute-start | bytes 688136 | tf_op jit(solution)/shard_map/ppermute | solution.py:340
  17.3 7.0 %copy-start = (bf16[64,128]{1,0:T(8,128)(2,1)S(1)}, bf16[64,128]{1,0:T(8,128)(2,1)}, u32[]{:S(2)}) copy-start(bf16[64,128]{1,0:T(8,128)(2,1)} %param.13) | copy-start | bytes 49156
  17.3 11.5 %collective-permute-start.7 = (bf16[64,1792]{1,0:T(8,128)(2,1)S(1)}, bf16[64,1792]{1,0:T(8,128)(2,1)S(1)}, u32[]{:S(2)}, u32[]{:S(2)}) collective-permute-start(bf16[64,1792]{1,0:T(8,128)(2,1)S(1)} %broadcast_select_fusion.4), channel_id=1, source_target_pairs={{0,4},{4,0},{8,12},{12,8},{1,5},{5,1},{9,13},{13,9},{2,6},{6,2},{1... | collective-permute-start | bytes 688136 | tf_op jit(solution)/shard_map/ppermute | solution.py:334
  18.0 10.8 %collective-permute-start.8 = (bf16[64,1792]{1,0:T(8,128)(2,1)S(1)}, bf16[64,1792]{1,0:T(8,128)(2,1)S(1)}, u32[]{:S(2)}, u32[]{:S(2)}) collective-permute-start(bf16[64,1792]{1,0:T(8,128)(2,1)S(1)} %collective-permute-done.6.refs_5_), channel_id=1, source_target_pairs={{0,16},{1,17},{2,18},{3,19},{4,8},{5,9},{6,10},{7,11},{8,4},{9,5},... | collective-permute-start | bytes 688136 | tf_op jit(solution)/shard_map/ppermute | solution.py:340
  24.3 8.7 %collective-permute-start.11 = (bf16[64,256]{1,0:T(8,128)(2,1)S(1)}, bf16[64,256]{1,0:T(8,128)(2,1)S(1)}, u32[]{:S(2)}, u32[]{:S(2)}) collective-permute-start(bf16[64,256]{1,0:T(8,128)(2,1)S(1)} %pad_maximum_fusion.2.refs_0_), channel_id=1, source_target_pairs={{0,4},{4,0},{8,12},{12,8},{1,5},{5,1},{9,13},{13,9},{2,6},{6,2},{1... | collective-permute-start | bytes 98312 | tf_op jit(solution)/shard_map/ppermute | solution.py:46
  26.1 10.0 %collective-permute-start.12 = (bf16[64,256]{1,0:T(8,128)(2,1)S(1)}, bf16[64,256]{1,0:T(8,128)(2,1)S(1)}, u32[]{:S(2)}, u32[]{:S(2)}) collective-permute-start(bf16[64,256]{1,0:T(8,128)(2,1)S(1)} %pad_maximum_fusion.2.refs_0_), channel_id=1, source_target_pairs={{0,8},{4,12},{8,0},{12,4},{1,9},{5,13},{9,1},{13,5},{2,10},{6,14},... | collective-permute-start | bytes 98312 | tf_op jit(solution)/shard_map/ppermute | solution.py:46
  28.0 8.1 %collective-permute-start.13 = (bf16[64,256]{1,0:T(8,128)(2,1)S(1)}, bf16[64,256]{1,0:T(8,128)(2,1)S(1)}, u32[]{:S(2)}, u32[]{:S(2)}) collective-permute-start(bf16[64,256]{1,0:T(8,128)(2,1)S(1)} %pad_maximum_fusion.2.refs_0_), channel_id=1, source_target_pairs={{0,12},{4,8},{8,4},{12,0},{1,13},{5,9},{9,5},{13,1},{2,14},{6,10},... | collective-permute-start | bytes 98312 | tf_op jit(solution)/shard_map/ppermute | solution.py:46
  28.9 11.9 %collective-permute-start.15 = (bf16[64,3584]{1,0:T(8,128)(2,1)S(1)}, bf16[64,3584]{1,0:T(8,128)(2,1)S(1)}, u32[]{:S(2)}, u32[]{:S(2)}) collective-permute-start(bf16[64,3584]{1,0:T(8,128)(2,1)S(1)} %pad_maximum_fusion.mine_2_ref), channel_id=1, source_target_pairs={{0,4},{4,0},{8,12},{12,8},{1,5},{5,1},{9,13},{13,9},{2,6},{6,2},{1... | collective-permute-start | bytes 1376264 | tf_op jit(solution)/shard_map/ppermute | solution.py:334
  31.5 10.6 %collective-permute-start.10 = (bf16[64,3584]{1,0:T(8,128)(2,1)S(1)}, bf16[64,3584]{1,0:T(8,128)(2,1)S(1)}, u32[]{:S(2)}, u32[]{:S(2)}) collective-permute-start(bf16[64,3584]{1,0:T(8,128)(2,1)S(1)} %pad_maximum_fusion.mine_2_ref), channel_id=1, source_target_pairs={{0,16},{16,0},{1,17},{17,1},{2,18},{18,2},{3,19},{19,3},{4,20},{20... | collective-permute-start | bytes 1376264 | tf_op jit(solution)/shard_map/ppermute | solution.py:337
  33.0 10.8 %collective-permute-start.17 = (bf16[384,128]{1,0:T(8,128)(2,1)S(1)}, bf16[384,128]{1,0:T(8,128)(2,1)S(1)}, u32[]{:S(2)}, u32[]{:S(2)}) collective-permute-start(bf16[384,128]{1,0:T(8,128)(2,1)S(1)} %slice.22), channel_id=1, source_target_pairs={{0,1},{1,0},{2,3},{3,2},{4,5},{5,4},{6,7},{7,6},{8,9},{9,8},{10,11... | collective-permute-start | bytes 294920 | tf_op jit(solution)/shard_map/ppermute | solution.py:389
  40.8 6.1 %collective-permute-start.16 = (bf16[64,1792]{1,0:T(8,128)(2,1)S(1)}, bf16[64,1792]{1,0:T(8,128)(2,1)S(1)}, u32[]{:S(2)}, u32[]{:S(2)}) collective-permute-start(bf16[64,1792]{1,0:T(8,128)(2,1)S(1)} %slice.17), channel_id=1, source_target_pairs={{0,16},{16,0},{1,17},{17,1},{2,18},{18,2},{3,19},{19,3},{4,20},{20... | collective-permute-start | bytes 688136 | tf_op jit(solution)/shard_map/ppermute | solution.py:337
  42.1 6.1 %collective-permute-start.14 = (bf16[64,1792]{1,0:T(8,128)(2,1)S(1)}, bf16[64,1792]{1,0:T(8,128)(2,1)S(1)}, u32[]{:S(2)}, u32[]{:S(2)}) collective-permute-start(bf16[64,1792]{1,0:T(8,128)(2,1)S(1)} %slice.16), channel_id=1, source_target_pairs={{0,4},{4,0},{8,12},{12,8},{1,5},{5,1},{9,13},{13,9},{2,6},{6,2},{1... | collective-permute-start | bytes 688136 | tf_op jit(solution)/shard_map/ppermute | solution.py:334
